TPU v7x, 256 devices: a whole 4x4x8 slice. The times are simulated.
256 devices in a mesh: gz: 64 (over z, x, core), gy: 4 (over y).
Axes of the slice: x: 4, y: 4, z: 8, core: 2. Of those that a mesh axis runs over, the one named last changes fastest.
Arguments:
- pressure: float32 [512, 256, 256], P('gz', 'gy'), may hold values from -6 to 6
- velocity: float32 [3, 512, 256, 256], P(None, 'gz', 'gy'), may hold values from -6 to 6
- bulk: float32 [512, 256, 256], P('gz', 'gy'), may hold values from 0.15 to 0.6
- buoyancy: float32 [512, 256, 256], P('gz', 'gy'), may hold values from 0.15 to 0.6
- tiles: bfloat16 [2048, 16, 32, 32], P(('gz', 'gy')), may hold values from -3 to 3
- tile_corner: int32 [2048, 3], replicated, may hold values from 0 to 511, as said below
- live_count: int32 [256], replicated, may hold values from 1 to 8, 1024 in all
Outputs:
- new_pressure: float32 [512, 256, 256], P('gz', 'gy')
- new_velocity: float32 [3, 512, 256, 256], P(None, 'gz', 'gy')
Inputs may be any that keep to these rules, and one draw needn't show every extreme that they name: `tile_corner`: row s belongs to slot s % 8 of device s // 8, devices numbered with gz major and gy minor. Its z0 lies in that device's own slab of 8 planes, its y0 in that device's own block of 64 rows; x0 is any column. `live_count`: entry d counts the live slots of device d (the first ones); later slots of that device are ignored.
All inputs are finite; a program needn't handle non-finite values.
Results may differ from a plain program's by a relative error of at most 0.0015.
Values may be sent and summed in bfloat16 or wider, within the bound.
No kernel may reach another device: no remote copies, remote signals or barrier semaphores. Data moves between devices by JAX's collectives and lax.ppermute only.
A program may use at most 64 MiB of HBM per device.

v0:
```python
import math

import jax
import jax.numpy as jnp
from jax import lax
from jax.sharding import PartitionSpec as P

NY = 256


kappa_courant = 0.3
highest = lax.Precision.HIGHEST


def from_behind(x, axis, by):
    peers = lax.axis_size(axis)
    return lax.ppermute(x, axis, [(i, (i + by) % peers) for i in range(peers)])


def rotation(product, period, orientation):
    angles = 2.0 * math.pi / period * (product % period).astype(jnp.float32)
    cosine = jnp.cos(angles)
    sine_part = orientation * jnp.sin(angles)
    return jnp.stack([jnp.stack([cosine, sine_part]), jnp.stack([-sine_part, cosine])])


def outer_index(count_a, count_b):
    return (
        jnp.arange(count_a, dtype=jnp.int32)[:, None]
        * jnp.arange(count_b, dtype=jnp.int32)[None, :]
    )


def wavenumber(position, length):
    signed = jnp.where(position < length // 2, position, position - length)
    return signed.astype(jnp.float32) * (2.0 * math.pi / length)


def derivative(wave_grid, orientation):
    return (
        -orientation * wave_grid * jnp.sin(0.5 * wave_grid),
        wave_grid * jnp.cos(0.5 * wave_grid),
    )


def complex_times(real_part, imag_part, factor):
    factor_real, factor_imag = factor
    return (
        real_part * factor_real - imag_part * factor_imag,
        real_part * factor_imag + imag_part * factor_real,
    )


def twiddle_index(rows_y, slabs_z, plane_group):
    plane = (
        jnp.arange(rows_y, dtype=jnp.int32)[:, None, None] * plane_group
        + jnp.arange(plane_group, dtype=jnp.int32)[None, None, :]
    )
    return plane * jnp.arange(slabs_z, dtype=jnp.int32)[None, :, None]


def forward_xy(fields):
    pieces = lax.all_to_all(fields, "gy", split_axis=1, concat_axis=2, tiled=True)
    grid_y = pieces.shape[2]
    grid_x = pieces.shape[3]
    half_x = grid_x // 2
    x_table = rotation(outer_index(grid_x, half_x), grid_x, -1.0)[0]
    spectrum = jnp.einsum("fqyx,dxk->fdqyk", pieces, x_table, precision=highest)
    y_table = rotation(outer_index(grid_y, grid_y), grid_y, -1.0)
    return jnp.einsum("fcqyk,cdyl->fdqkl", spectrum, y_table, precision=highest)


def forward_z(spectrum):
    fields, _, plane_group, half_x, grid_y = spectrum.shape
    slabs_z = lax.axis_size("gz")
    rows_y = lax.axis_size("gy")
    width = half_x * grid_y // (slabs_z * rows_y)
    slab_planes = plane_group * rows_y
    grid_z = slab_planes * slabs_z
    blocks = spectrum.reshape(fields, 2, plane_group, rows_y, slabs_z, width)
    planes = lax.all_to_all(
        lax.all_to_all(blocks, "gz", split_axis=4, concat_axis=2, tiled=True),
        "gy",
        split_axis=3,
        concat_axis=2,
        tiled=True,
    )
    planes = planes.reshape(fields, 2, rows_y, slabs_z, plane_group, width)
    slab_table = rotation(outer_index(slabs_z, slabs_z), slabs_z, -1.0)
    sectioned = jnp.einsum("fcjgqm,cdga->fdjaqm", planes, slab_table, precision=highest)
    turns = rotation(twiddle_index(rows_y, slabs_z, plane_group), grid_z, -1.0)
    sectioned = jnp.einsum("fcjaqm,cdjaq->fdjaqm", sectioned, turns, precision=highest)
    plane_table = rotation(outer_index(slab_planes, slab_planes), slab_planes, -1.0).reshape(
        2, 2, rows_y, plane_group, slab_planes
    )
    return jnp.einsum("fcjaqm,cdjqb->fdabm", sectioned, plane_table, precision=highest)


def inverse_z(spectrum):
    fields, _, slabs_z, slab_planes, width = spectrum.shape
    rows_y = lax.axis_size("gy")
    plane_group = slab_planes // rows_y
    grid_z = slab_planes * slabs_z
    plane_table = rotation(outer_index(slab_planes, slab_planes), slab_planes, 1.0).reshape(
        2, 2, slab_planes, rows_y, plane_group
    )
    sectioned = jnp.einsum("fcabm,cdbjq->fdajqm", spectrum, plane_table, precision=highest)
    turns = rotation(twiddle_index(rows_y, slabs_z, plane_group), grid_z, 1.0)
    sectioned = jnp.einsum("fcajqm,cdjaq->fdajqm", sectioned, turns, precision=highest)
    slab_table = rotation(outer_index(slabs_z, slabs_z), slabs_z, 1.0)
    sectioned = jnp.einsum("fcajqm,cdag->fdgjqm", sectioned, slab_table, precision=highest)
    sectioned = sectioned.reshape(fields, 2, grid_z, 1, 1, width)
    blocks = lax.all_to_all(
        lax.all_to_all(sectioned, "gz", split_axis=2, concat_axis=4, tiled=True),
        "gy",
        split_axis=2,
        concat_axis=3,
        tiled=True,
    )
    half_x = rows_y * slabs_z * width // NY
    return blocks.reshape(fields, 2, plane_group, half_x, NY)


def inverse_xy(spectrum, inverse_scale):
    half_x = spectrum.shape[3]
    grid_y = spectrum.shape[4]
    grid_x = 2 * half_x
    y_table = rotation(outer_index(grid_y, grid_y), grid_y, 1.0)
    spectrum = jnp.einsum("fcqkl,cdly->fdqky", spectrum, y_table, precision=highest)
    x_table = rotation(outer_index(half_x, grid_x), grid_x, 1.0)[:, 0]
    weight = jnp.where(jnp.arange(half_x) == 0, 1.0, 2.0).astype(jnp.float32) * inverse_scale
    pieces = jnp.einsum(
        "fcqky,ckx->fqyx", spectrum, x_table * weight[None, :, None], precision=highest
    )
    return lax.all_to_all(pieces, "gy", split_axis=2, concat_axis=1, tiled=True)


def one_hot_place(extent, start, span):
    target = jnp.arange(extent, dtype=jnp.int32)[None, :, None]
    wanted = start[:, None, None] + jnp.arange(span, dtype=jnp.int32)[None, None, :]
    return (target == wanted).astype(jnp.bfloat16)


def place_tiles(buffer, blocks, plane_start, row_start, column_start):
    planes, rows, columns = buffer.shape
    tile_z, tile_y, tile_x = (blocks.shape[1], blocks.shape[2], blocks.shape[3])
    column_hot = one_hot_place(columns, column_start, tile_x)
    across = jnp.einsum(
        "sabc,sxc->sabx", blocks, column_hot, preferred_element_type=jnp.float32
    ).astype(jnp.bfloat16)
    plane_hot = one_hot_place(planes, plane_start, tile_z)
    lifted = jnp.einsum(
        "sAa,sabx->sAbx", plane_hot, across, preferred_element_type=jnp.float32
    ).astype(jnp.bfloat16)
    row_hot = one_hot_place(rows, row_start, tile_y)
    return buffer + jnp.einsum("sAbx,srb->Arx", lifted, row_hot, preferred_element_type=jnp.float32)


def fold_columns(buffer, grid_x, tile_x):
    return buffer[..., :grid_x].at[..., :tile_x].add(buffer[..., grid_x:])


def local(pressure, velocity, bulk, buoyancy, tiles, tile_corner, live_count):
    slabs_z = lax.axis_size("gz")
    rows_y = lax.axis_size("gy")
    slab_index = lax.axis_index("gz")
    row_block = lax.axis_index("gy")
    slab_planes, row_count, grid_x = pressure.shape
    half_x = grid_x // 2
    grid_z = slab_planes * slabs_z
    width = half_x * NY // (slabs_z * rows_y)
    inverse_scale = 1.0 / (grid_x * NY * grid_z)
    plane_wave = (
        jnp.arange(slabs_z, dtype=jnp.int32)[:, None, None]
        + slabs_z * jnp.arange(slab_planes, dtype=jnp.int32)[None, :, None]
    )
    column = (
        row_block * (slabs_z * width)
        + slab_index * width
        + jnp.arange(width, dtype=jnp.int32)[None, None, :]
    )
    wave_z = wavenumber(plane_wave, grid_z)
    wave_x = wavenumber(column // NY, grid_x)
    wave_y = wavenumber(column % NY, NY)
    magnitude = jnp.sqrt(wave_x * wave_x + wave_y * wave_y + wave_z * wave_z)
    kappa_factor = jnp.sinc(kappa_courant * magnitude / (2.0 * math.pi))
    pressure_spectrum = forward_z(forward_xy(pressure[None]))[0]
    scaled_real = pressure_spectrum[0] * kappa_factor
    scaled_imag = pressure_spectrum[1] * kappa_factor
    slope_spectra = [
        jnp.stack(complex_times(scaled_real, scaled_imag, derivative(wave_grid, 1.0)))
        for wave_grid in (wave_x, wave_y, wave_z)
    ]
    slopes = inverse_xy(inverse_z(jnp.stack(slope_spectra)), inverse_scale)
    new_velocity = velocity - buoyancy[None] * slopes
    velocity_spectrum = forward_z(forward_xy(new_velocity))
    summed_real = jnp.zeros_like(scaled_real)
    summed_imag = jnp.zeros_like(scaled_imag)
    for direction, wave_grid in enumerate((wave_x, wave_y, wave_z)):
        part_real, part_imag = complex_times(
            velocity_spectrum[direction, 0],
            velocity_spectrum[direction, 1],
            derivative(wave_grid, -1.0),
        )
        summed_real = summed_real + part_real
        summed_imag = summed_imag + part_imag
    divergence_spectrum = jnp.stack([summed_real * kappa_factor, summed_imag * kappa_factor])
    divergence = inverse_xy(inverse_z(divergence_spectrum[None]), inverse_scale)[0]
    slot_count, tile_z, tile_y, tile_x = tiles.shape
    slab_reach = (slab_planes + tile_z - 2) // slab_planes + 1
    own_device = slab_index * rows_y + row_block
    own_corners = lax.dynamic_slice_in_dim(tile_corner, own_device * slot_count, slot_count, 0)
    live_mask = (jnp.arange(slot_count, dtype=jnp.int32) < live_count[own_device]).astype(
        jnp.bfloat16
    )
    masked = tiles * live_mask[:, None, None, None]
    plane_offset = own_corners[:, 0] - slab_index * slab_planes
    padded = jnp.pad(masked, ((0, 0), (slab_planes, slab_planes), (0, 0), (0, 0)))
    window = jnp.zeros((slab_planes, 2 * row_count, grid_x + tile_x), jnp.float32)
    zero_start = jnp.zeros((slot_count,), jnp.int32)
    for step_index in range(slab_reach):
        first_plane = step_index * slab_planes - plane_offset + slab_planes
        blocks = jax.vmap(
            lambda tile_block, first_index: lax.dynamic_slice_in_dim(
                tile_block, first_index, slab_planes, 0
            )
        )(padded, first_plane)
        corners = own_corners
        if step_index > 0:
            blocks = from_behind(blocks, "gz", step_index)
            sender = (slab_index - step_index) % slabs_z * rows_y + row_block
            corners = lax.dynamic_slice_in_dim(tile_corner, sender * slot_count, slot_count, 0)
        window = place_tiles(
            window, blocks, zero_start, corners[:, 1] - row_block * row_count, corners[:, 2]
        )
    window = fold_columns(window, grid_x, tile_x)
    source = window[:, :row_count] + from_behind(
        window[:, row_count:].astype(jnp.bfloat16), "gy", 1
    ).astype(jnp.float32)
    new_pressure = pressure - bulk * divergence + source
    return (new_pressure, new_velocity)


def solution(mesh):
    in_specs = (
        P("gz", "gy", None),
        P(None, "gz", "gy", None),
        P("gz", "gy", None),
        P("gz", "gy", None),
        P(("gz", "gy"), None, None, None),
        P(),
        P(),
    )
    out_specs = (P("gz", "gy", None), P(None, "gz", "gy", None))
    return jax.shard_map(local, mesh=mesh, in_specs=in_specs, out_specs=out_specs, check_vma=False)
```

profile of v0, /device:TPU:1, one launch (start us, length us, event | category | flops | bytes accessed | tf_op | source)
XLA Modules:
  0.0 393.6 jit_solution(7370794767797964418)
XLA Ops:
  0.6 5.0 %all-to-all-start = ((f32[1,8,64,256]{3,2,0,1:T(8,128)}), f32[1,8,64,256]{3,2,0,1:T(8,128)S(1)}, u32[]{:S(2)}, u32[]{:S(2)}) async-start(f32[1,8,64,256]{3,2,0,1:T(8,128)} %bitcast.516), calls=%async_computation | async-start | bytes 1048576 | tf_op jit(solution)/shard_map/all_to_all | solution.py:63
  16.3 14.4 %all-to-all-start.1 = ((f32[1,2,2,4,64,128]{5,3,2,1,0,4:T(4,128)}), f32[1,2,2,4,64,128]{5,3,2,1,0,4:T(4,128)S(1)}, u32[]{:S(2)}, u32[]{:S(2)}) async-start(f32[1,2,2,4,64,128]{5,3,2,1,0,4:T(4,128)} %copy.291), calls=%async_computation.1 | async-start | bytes 1048576 | tf_op jit(solution)/shard_map/all_to_all | solution.py:82
  32.5 15.9 %all-to-all-done.1 = f32[1,2,2,4,64,128]{5,3,2,1,0,4:T(4,128)S(1)} async-done(((f32[1,2,2,4,64,128]{5,3,2,1,0,4:T(4,128)}), f32[1,2,2,4,64,128]{5,3,2,1,0,4:T(4,128)S(1)}, u32[]{:S(2)}, u32[]{:S(2)}) %all-to-all-start.1) | async-done | bytes 524320 | tf_op jit(solution)/shard_map/all_to_all | solution.py:82
  55.1 7.2 %all-to-all-done.2 = f32[1,2,128,4,1,128]{5,2,1,4,0,3:T(8,128)S(1)} async-done(((f32[1,2,128,4,1,128]{5,2,1,4,0,3:T(8,128)}), f32[1,2,128,4,1,128]{5,2,1,4,0,3:T(8,128)S(1)}, u32[]{:S(2)}, u32[]{:S(2)}) %all-to-all-start.2) | async-done | bytes 524320 | tf_op jit(solution)/shard_map/all_to_all | solution.py:81
  63.0 3.7 convolution_bitcast_fusion.9
  72.1 7.7 %fusion.48 = f32[3,2,64,4,2,128]{5,1,0,4,3,2:T(2,128)S(1)} fusion(f32[2,2,4,64,2,1]{0,1,5,4,2,3:T(2,128)S(1)} %copy.367, f32[3,2,64,4,2,128]{5,3,2,0,4,1:T(4,128)S(1)} %fusion.54), kind=kOutput, calls=%fused_computation.50 | convolution fusion | flops 9437184 | bytes 3153920 | tf_op jit(solution)/shard_map/fcajqm,cdjaq->fdajqm/dot_general | solution.py:109
  84.1 45.0 %all_to_all.198 = f32[3,2,512,1,1,128]{5,1,0,4,3,2:T(2,128)S(1)} all-to-all(f32[3,2,512,1,1,128]{5,1,0,4,3,2:T(2,128)S(1)} %copy.308), channel_id=1, replica_groups=mesh['gz'=64,'gy'=4] {'gz'}, dimensions={2} | all-to-all | bytes 3145728 | tf_op jit(solution)/shard_map/all_to_all | solution.py:114
  130.7 4.0 %all-to-all-start.4 = ((f32[3,2,8,1,64,128]{5,4,1,0,3,2:T(8,128)}), f32[3,2,8,1,64,128]{5,4,1,0,3,2:T(8,128)S(1)}, u32[]{:S(2)}, u32[]{:S(2)}) async-start(f32[3,2,8,1,64,128]{5,4,1,0,3,2:T(8,128)} %bitcast.505), calls=%async_computation.4 | async-start | bytes 3145728 | tf_op jit(solution)/shard_map/all_to_all | solution.py:113
  136.5 17.3 %all-to-all-done.4 = f32[3,2,8,1,64,128]{5,4,1,0,3,2:T(8,128)S(1)} async-done(((f32[3,2,8,1,64,128]{5,4,1,0,3,2:T(8,128)}), f32[3,2,8,1,64,128]{5,4,1,0,3,2:T(8,128)S(1)}, u32[]{:S(2)}, u32[]{:S(2)}) %all-to-all-start.4) | async-done | bytes 1572896 | tf_op jit(solution)/shard_map/all_to_all | solution.py:113
  154.6 4.0 %fusion.2 = f32[2,256,3,2,128,1]{4,1,0,5,3,2:T(8,128)S(1)} fusion(f32[3,2,2,128,256,1]{4,3,1,2,0,5:T(8,128)S(1)} %reshape.1517, f32[1,2,256,256]{2,3,1,0:T(8,128)} %get-tuple-element.39, f32[1,2,256,256]{2,3,1,0:T(8,128)} %get-tuple-element.36), kind=kOutput, calls=%fused_computation.11 | convolution fusion | flops 2416181248 | bytes 4194304 | tf_op jit(solution)/shard_map/fcqkl,cdly->fdqky/dot_general | solution.py:129
  161.4 20.7 %all_to_all.199 = f32[3,2,256,256]{3,1,0,2:T(2,128)S(1)} all-to-all(f32[3,2,256,256]{3,1,0,2:T(2,128)S(1)} %copy.315), channel_id=1, replica_groups=mesh['gz'=64,'gy'=4] {'gy'}, dimensions={2} | all-to-all | bytes 3145728 | tf_op jit(solution)/shard_map/all_to_all | solution.py:135
  183.9 19.6 %all_to_all.200 = f32[3,8,64,256]{3,2,0,1:T(8,128)S(1)} all-to-all(f32[3,8,64,256]{3,2,0,1:T(8,128)S(1)} %fusion.15), channel_id=1, replica_groups=mesh['gz'=64,'gy'=4] {'gy'}, dimensions={1} | all-to-all | bytes 3145728 | tf_op jit(solution)/shard_map/all_to_all | solution.py:63
  206.0 3.9 fusion.42
  216.6 13.6 %all-to-all-start.7 = ((f32[3,2,2,4,64,128]{5,3,2,1,0,4:T(4,128)}), f32[3,2,2,4,64,128]{5,3,2,1,0,4:T(4,128)S(1)}, u32[]{:S(2)}, u32[]{:S(2)}) async-start(f32[3,2,2,4,64,128]{5,3,2,1,0,4:T(4,128)} %copy.322), calls=%async_computation.7 | async-start | bytes 3145728 | tf_op jit(solution)/shard_map/all_to_all | solution.py:82
  254.7 16.0 %all-to-all-done.7 = f32[3,2,2,4,64,128]{5,3,2,1,0,4:T(4,128)S(1)} async-done(((f32[3,2,2,4,64,128]{5,3,2,1,0,4:T(4,128)}), f32[3,2,2,4,64,128]{5,3,2,1,0,4:T(4,128)S(1)}, u32[]{:S(2)}, u32[]{:S(2)}) %all-to-all-start.7) | async-done | bytes 1572896 | tf_op jit(solution)/shard_map/all_to_all | solution.py:82
  277.2 19.9 %all-to-all-done.8 = f32[3,2,128,4,1,128]{5,2,1,0,4,3:T(8,128)S(1)} async-done(((f32[3,2,128,4,1,128]{5,2,1,0,4,3:T(8,128)}), f32[3,2,128,4,1,128]{5,2,1,0,4,3:T(8,128)S(1)}, u32[]{:S(2)}, u32[]{:S(2)}) %all-to-all-start.8) | async-done | bytes 1572896 | tf_op jit(solution)/shard_map/all_to_all | solution.py:81
  298.9 7.8 %fusion.51 = f32[3,2,4,64,2,128,1]{5,1,0,4,3,2,6:T(2,128)S(1)} fusion(f32[2,2,4,64,2,1]{0,1,5,4,3,2:T(2,128)S(1)} %copy-done.27, f32[3,2,4,64,2,128]{5,3,4,2,0,1:T(8,128)S(1)} %fusion.36), kind=kOutput, calls=%fused_computation.51 | convolution fusion | flops 9437184 | bytes 3153920 | tf_op jit(solution)/shard_map/fcjaqm,cdjaq->fdjaqm/dot_general | solution.py:92
  306.8 3.8 fusion.39
  319.0 5.7 %all-to-all-start.9 = ((f32[1,2,512,1,1,128]{5,1,4,3,0,2:T(2,128)}), f32[1,2,512,1,1,128]{5,1,4,3,0,2:T(2,128)}, u32[]{:S(2)}, u32[]{:S(2)}) async-start(f32[1,2,512,1,1,128]{5,1,4,3,0,2:T(2,128)} %copy.338), calls=%async_computation.9 | async-start | bytes 1048576 | tf_op jit(solution)/shard_map/all_to_all | solution.py:114
  331.1 11.3 %all-to-all-done.9 = f32[1,2,512,1,1,128]{5,1,4,3,0,2:T(2,128)} async-done(((f32[1,2,512,1,1,128]{5,1,4,3,0,2:T(2,128)}), f32[1,2,512,1,1,128]{5,1,4,3,0,2:T(2,128)}, u32[]{:S(2)}, u32[]{:S(2)}) %all-to-all-start.9) | async-done | bytes 524320 | tf_op jit(solution)/shard_map/all_to_all | solution.py:114
  344.4 4.1 %all-to-all-start.10 = ((f32[1,2,8,1,64,128]{5,4,1,3,0,2:T(8,128)}), f32[1,2,8,1,64,128]{5,4,1,3,0,2:T(8,128)}, u32[]{:S(2)}, u32[]{:S(2)}) async-start(f32[1,2,8,1,64,128]{5,4,1,3,0,2:T(8,128)} %bitcast.519), calls=%async_computation.10 | async-start | bytes 1048576 | tf_op jit(solution)/shard_map/all_to_all | solution.py:113
  350.7 7.2 %all-to-all-done.10 = f32[1,2,8,1,64,128]{5,4,1,3,0,2:T(8,128)} async-done(((f32[1,2,8,1,64,128]{5,4,1,3,0,2:T(8,128)}), f32[1,2,8,1,64,128]{5,4,1,3,0,2:T(8,128)}, u32[]{:S(2)}, u32[]{:S(2)}) %all-to-all-start.10) | async-done | bytes 524320 | tf_op jit(solution)/shard_map/all_to_all | solution.py:113
  364.0 4.1 %all-to-all-start.11 = ((f32[1,2,256,256]{3,1,0,2:T(2,128)}), f32[1,2,256,256]{3,1,0,2:T(2,128)}, u32[]{:S(2)}, u32[]{:S(2)}) async-start(f32[1,2,256,256]{3,1,0,2:T(2,128)} %copy.343), calls=%async_computation.11 | async-start | bytes 1048576 | tf_op jit(solution)/shard_map/all_to_all | solution.py:135
  379.0 9.2 %collective-permute-done.2 = bf16[8,64,256]{1,2,0:T(8,128)(2,1)} collective-permute-done((bf16[8,64,256]{1,2,0:T(8,128)(2,1)}, bf16[8,64,256]{1,2,0:T(8,128)(2,1)}, u32[]{:S(2)}, u32[]{:S(2)}) %collective-permute-start.2) | collective-permute-done | bytes 262176 | tf_op jit(solution)/shard_map/ppermute | solution.py:17
  (238 shorter events, 120.4 us)
Async XLA Ops:
  0.6 12.6 %all-to-all-start = ((f32[1,8,64,256]{3,2,0,1:T(8,128)}), f32[1,8,64,256]{3,2,0,1:T(8,128)S(1)}, u32[]{:S(2)}, u32[]{:S(2)}) async-start(f32[1,8,64,256]{3,2,0,1:T(8,128)} %bitcast.516), calls=%async_computation | async-start | bytes 1048576 | tf_op jit(solution)/shard_map/all_to_all | solution.py:63
  9.9 58.7 %copy-start.45 = (f32[128]{0:T(128)}, f32[128]{0:T(128)S(1)}, u32[]{:S(2)}) copy-start(f32[128]{0:T(128)S(1)} %get-tuple-element.84) | copy-start | bytes 1540
  10.0 58.7 %copy-start.47 = (f32[128]{0:T(128)}, f32[128]{0:T(128)S(1)}, u32[]{:S(2)}) copy-start(f32[128]{0:T(128)S(1)} %get-tuple-element.86) | copy-start | bytes 1540
  16.3 32.1 %all-to-all-start.1 = ((f32[1,2,2,4,64,128]{5,3,2,1,0,4:T(4,128)}), f32[1,2,2,4,64,128]{5,3,2,1,0,4:T(4,128)S(1)}, u32[]{:S(2)}, u32[]{:S(2)}) async-start(f32[1,2,2,4,64,128]{5,3,2,1,0,4:T(4,128)} %copy.291), calls=%async_computation.1 | async-start | bytes 1048576 | tf_op jit(solution)/shard_map/all_to_all | solution.py:82
  31.7 30.7 %copy-start.18 = (f32[1,2,64,64]{2,3,0,1:T(8,128)}, f32[1,2,64,64]{2,3,0,1:T(8,128)S(1)}, u32[]{:S(2)}) copy-start(f32[1,2,64,64]{2,3,0,1:T(8,128)S(1)} %get-tuple-element.45) | copy-start | bytes 98308
  31.7 30.7 %copy-start.20 = (f32[1,2,64,64]{2,3,0,1:T(8,128)}, f32[1,2,64,64]{2,3,0,1:T(8,128)S(1)}, u32[]{:S(2)}) copy-start(f32[1,2,64,64]{2,3,0,1:T(8,128)S(1)} %get-tuple-element.46) | copy-start | bytes 98308
  31.8 34.9 %copy-start.30 = (f32[1,1,4,2,8]{4,2,3,0,1:T(4,128)}, f32[1,1,4,2,8]{4,2,3,0,1:T(4,128)S(1)}, u32[]{:S(2)}) copy-start(f32[1,1,4,2,8]{4,2,3,0,1:T(4,128)S(1)} %get-tuple-element.71) | copy-start | bytes 772
  31.8 34.9 %copy-start.32 = (f32[1,1,4,2,8]{4,2,3,0,1:T(4,128)}, f32[1,1,4,2,8]{4,2,3,0,1:T(4,128)S(1)}, u32[]{:S(2)}) copy-start(f32[1,1,4,2,8]{4,2,3,0,1:T(4,128)S(1)} %get-tuple-element.72) | copy-start | bytes 772
  31.8 34.9 %copy-start.34 = (f32[1,1,4,2,8]{4,2,3,0,1:T(4,128)}, f32[1,1,4,2,8]{4,2,3,0,1:T(4,128)S(1)}, u32[]{:S(2)}) copy-start(f32[1,1,4,2,8]{4,2,3,0,1:T(4,128)S(1)} %get-tuple-element.73) | copy-start | bytes 772
  49.5 12.8 %all-to-all-start.2 = ((f32[1,2,128,4,1,128]{5,2,1,4,0,3:T(8,128)}), f32[1,2,128,4,1,128]{5,2,1,4,0,3:T(8,128)S(1)}, u32[]{:S(2)}, u32[]{:S(2)}) async-start(f32[1,2,128,4,1,128]{5,2,1,4,0,3:T(8,128)} %copy.293), calls=%async_computation.2 | async-start | bytes 1048576 | tf_op jit(solution)/shard_map/all_to_all | solution.py:81
  53.2 15.4 %copy-start.43 = (f32[128]{0:T(128)}, f32[128]{0:T(128)S(1)}, u32[]{:S(2)}) copy-start(f32[128]{0:T(128)S(1)} %get-tuple-element.88) | copy-start | bytes 1540
  53.3 15.4 %copy-start.16 = (f32[64,8]{1,0:T(8,128)}, f32[64,8]{1,0:T(8,128)S(1)}, u32[]{:S(2)}) copy-start(f32[64,8]{1,0:T(8,128)S(1)} %copy.299) | copy-start | bytes 6148
  53.4 14.7 %copy-start.22 = (f32[64,8]{1,0:T(8,128)}, f32[64,8]{1,0:T(8,128)S(1)}, u32[]{:S(2)}) copy-start(f32[64,8]{1,0:T(8,128)S(1)} %copy.301) | copy-start | bytes 6148
  130.7 23.1 %all-to-all-start.4 = ((f32[3,2,8,1,64,128]{5,4,1,0,3,2:T(8,128)}), f32[3,2,8,1,64,128]{5,4,1,0,3,2:T(8,128)S(1)}, u32[]{:S(2)}, u32[]{:S(2)}) async-start(f32[3,2,8,1,64,128]{5,4,1,0,3,2:T(8,128)} %bitcast.505), calls=%async_computation.4 | async-start | bytes 3145728 | tf_op jit(solution)/shard_map/all_to_all | solution.py:113
  216.6 54.2 %all-to-all-start.7 = ((f32[3,2,2,4,64,128]{5,3,2,1,0,4:T(4,128)}), f32[3,2,2,4,64,128]{5,3,2,1,0,4:T(4,128)S(1)}, u32[]{:S(2)}, u32[]{:S(2)}) async-start(f32[3,2,2,4,64,128]{5,3,2,1,0,4:T(4,128)} %copy.322), calls=%async_computation.7 | async-start | bytes 3145728 | tf_op jit(solution)/shard_map/all_to_all | solution.py:82
  238.5 87.8 %collective-permute-start = (bf16[8,8,32,32]{3,2,1,0:T(8,128)(2,1)}, bf16[8,8,32,32]{3,2,1,0:T(8,128)(2,1)}, u32[]{:S(2)}, u32[]{:S(2)}) collective-permute-start(bf16[8,8,32,32]{3,2,1,0:T(8,128)(2,1)} %gather_fusion.1), channel_id=1, source_target_pairs={{0,4},{4,8},{8,12},{12,16},{16,20},{20,24},{24,28},{28,32},{32,36}... | collective-permute-start | bytes 393224 | tf_op jit(solution)/shard_map/ppermute | solution.py:17
  243.2 81.5 %collective-permute-start.1 = (bf16[8,8,32,32]{3,2,1,0:T(8,128)(2,1)}, bf16[8,8,32,32]{3,2,1,0:T(8,128)(2,1)}, u32[]{:S(2)}, u32[]{:S(2)}) collective-permute-start(bf16[8,8,32,32]{3,2,1,0:T(8,128)(2,1)} %gather_fusion.2), channel_id=1, source_target_pairs={{0,8},{4,12},{8,16},{12,20},{16,24},{20,28},{24,32},{28,36},{32,40... | collective-permute-start | bytes 393224 | tf_op jit(solution)/shard_map/ppermute | solution.py:17
  272.8 24.4 %all-to-all-start.8 = ((f32[3,2,128,4,1,128]{5,2,1,0,4,3:T(8,128)}), f32[3,2,128,4,1,128]{5,2,1,0,4,3:T(8,128)S(1)}, u32[]{:S(2)}, u32[]{:S(2)}) async-start(f32[3,2,128,4,1,128]{5,2,1,0,4,3:T(8,128)} %copy.324), calls=%async_computation.8 | async-start | bytes 3145728 | tf_op jit(solution)/shard_map/all_to_all | solution.py:81
  277.2 20.1 %copy-start.19 = (f32[1,2,64,64]{2,3,0,1:T(8,128)S(1)}, f32[1,2,64,64]{2,3,0,1:T(8,128)}, u32[]{:S(2)}) copy-start(f32[1,2,64,64]{2,3,0,1:T(8,128)} %copy-done.18) | copy-start | bytes 98308
  277.2 20.1 %copy-start.21 = (f32[1,2,64,64]{2,3,0,1:T(8,128)S(1)}, f32[1,2,64,64]{2,3,0,1:T(8,128)}, u32[]{:S(2)}) copy-start(f32[1,2,64,64]{2,3,0,1:T(8,128)} %copy-done.20) | copy-start | bytes 98308
  319.0 23.4 %all-to-all-start.9 = ((f32[1,2,512,1,1,128]{5,1,4,3,0,2:T(2,128)}), f32[1,2,512,1,1,128]{5,1,4,3,0,2:T(2,128)}, u32[]{:S(2)}, u32[]{:S(2)}) async-start(f32[1,2,512,1,1,128]{5,1,4,3,0,2:T(2,128)} %copy.338), calls=%async_computation.9 | async-start | bytes 1048576 | tf_op jit(solution)/shard_map/all_to_all | solution.py:114
  344.4 13.4 %all-to-all-start.10 = ((f32[1,2,8,1,64,128]{5,4,1,3,0,2:T(8,128)}), f32[1,2,8,1,64,128]{5,4,1,3,0,2:T(8,128)}, u32[]{:S(2)}, u32[]{:S(2)}) async-start(f32[1,2,8,1,64,128]{5,4,1,3,0,2:T(8,128)} %bitcast.519), calls=%async_computation.10 | async-start | bytes 1048576 | tf_op jit(solution)/shard_map/all_to_all | solution.py:113
  364.0 12.5 %all-to-all-start.11 = ((f32[1,2,256,256]{3,1,0,2:T(2,128)}), f32[1,2,256,256]{3,1,0,2:T(2,128)}, u32[]{:S(2)}, u32[]{:S(2)}) async-start(f32[1,2,256,256]{3,1,0,2:T(2,128)} %copy.343), calls=%async_computation.11 | async-start | bytes 1048576 | tf_op jit(solution)/shard_map/all_to_all | solution.py:135
  370.1 18.0 %collective-permute-start.2 = (bf16[8,64,256]{1,2,0:T(8,128)(2,1)}, bf16[8,64,256]{1,2,0:T(8,128)(2,1)}, u32[]{:S(2)}, u32[]{:S(2)}) collective-permute-start(bf16[8,64,256]{1,2,0:T(8,128)(2,1)} %slice.225), channel_id=1, source_target_pairs={{0,1},{1,2},{2,3},{3,0},{4,5},{5,6},{6,7},{7,4},{8,9},{9,10},{10,1... | collective-permute-start | bytes 786440 | tf_op jit(solution)/shard_map/ppermute | solution.py:17
  (43 other events, 223.6 us)
where the time goes:
time: 401 us; the launch traced here: 394 us
  waiting for transfers between devices  106 us (26%)
  blocking collectives  85.3 us (21%)
  matrix products  63 us (16%)
  starting transfers between devices  62.6 us (16%)
  local copies, waits for them, and re-layouts  55.1 us (14%)
  other arithmetic  19.5 us (5%)
    all_to_all x1, blocking collectives, inverse_z(): lax.all_to_all(sectioned, 'gz', split_axis=2, concat_axis=4, tiled=True)  45 us
    all_to_all x2, waiting for transfers between devices, forward_z(): lax.all_to_all(blocks, 'gz', split_axis=4, concat_axis=2, tiled=True)  31.9 us
    all_to_all x2, starting transfers between devices, forward_z(): lax.all_to_all(blocks, 'gz', split_axis=4, concat_axis=2, tiled=True)  28 us
    all_to_all x2, waiting for transfers between devices, forward_z(): lax.all_to_all(lax.all_to_all(blocks, 'gz', split_axis=4, concat_axis=2,...  27.1 us
    all_to_all x2, waiting for transfers between devices, inverse_z(): lax.all_to_all(lax.all_to_all(sectioned, 'gz', split_axis=2, concat_axis=...  24.5 us
    all_to_all x1, blocking collectives, inverse_xy(): return lax.all_to_all(pieces, 'gy', split_axis=2, concat_axis=1, tiled=True)  20.7 us
    all_to_all x1, blocking collectives, forward_xy(): lax.all_to_all(fields, 'gy', split_axis=1, concat_axis=2, tiled=True)  19.6 us
    dot_general x2, matrix products, forward_z(): jnp.einsum('fcjaqm,cdjaq->fdjaqm', sectioned, turns, precision=highest)  11.5 us
  transfers between devices with their start and end apart: 12, of which 9 were waited for; matrix products, arithmetic and copies ran while one was open for 19% of the time, Pallas kernels for 0%

commit v1 on v0

v1 whole, which is shorter than its diff:
```python
import functools
import math

import jax
import jax.numpy as jnp
import ml_dtypes
import numpy as np
from jax import lax
from jax.experimental import pallas as pl
from jax.experimental.pallas import tpu as pltpu
from jax.sharding import PartitionSpec as P

NX = 256
NY = 256
NZ = 512
HALF = 128
ROWS = 64
PEERS_Y = 4
kappa_courant = 0.3
f32 = jnp.float32
bf16 = jnp.bfloat16
f16 = jnp.float16

SPECTRUM_SCALE = 1.0 / 256.0
SLOPE_LINK = 0.25
MIDDLE_LINK = 1.0 / 16.0
DIVERGENCE_LINK = 1.0 / 32.0


def split_table(table):
    high = table.astype(ml_dtypes.bfloat16)
    low = (table - high.astype(np.float64)).astype(ml_dtypes.bfloat16)
    return high, low


def make_tables():
    index = np.arange(256)
    angle = 2.0 * np.pi / 256 * (np.outer(index, index) % 256)
    cos_high, cos_low = split_table(np.cos(angle))
    sin_high, sin_low = split_table(np.sin(angle))
    rows = np.concatenate(
        [
            np.concatenate([cos_high, cos_high, cos_low], axis=1),
            np.concatenate([sin_high, sin_high, sin_low], axis=1),
        ],
        axis=0,
    )
    wave_x = 2.0 * np.pi / NX * np.arange(HALF)
    angle_x = 2.0 * np.pi / NX * (np.outer(index, np.arange(HALF)) % NX)

    def stacked(table):
        high, low = split_table(table)
        return np.concatenate([high, high, low], axis=0)

    def forward_x(factor):
        spectrum = np.exp(-1j * angle_x) * factor[None, :]
        return stacked(np.concatenate([spectrum.real, spectrum.imag], axis=1))

    def inverse_x(factor):
        weight = np.where(np.arange(HALF) == 0, 1.0, 2.0) * factor
        wave = np.exp(1j * angle_x.T) * weight[:, None]
        return stacked(np.concatenate([wave.real, -wave.imag], axis=0))

    ahead = 1j * wave_x * np.exp(0.5j * wave_x)
    behind = 1j * wave_x * np.exp(-0.5j * wave_x)
    plain = np.ones(HALF)
    wave_z = 2.0 * np.pi / NZ * np.where(np.arange(NZ) < NZ // 2, np.arange(NZ), np.arange(NZ) - NZ)
    wave_y = 2.0 * np.pi / NY * np.where(np.arange(NY) < NY // 2, np.arange(NY), np.arange(NY) - NY)

    def lanes(column):
        return np.broadcast_to(column[:, None], (column.shape[0], HALF)).astype(np.float32)

    def derivative(wave):
        return np.stack([lanes(-wave * np.sin(0.5 * wave)), lanes(wave * np.cos(0.5 * wave))])

    turn = np.exp(-2j * np.pi / NZ * index)
    return {
        "rows": rows,
        "x_forward": forward_x(plain),
        "x_forward_behind": forward_x(behind),
        "x_inverse": inverse_x(plain),
        "x_inverse_ahead": inverse_x(ahead),
        "wave_z": derivative(wave_z),
        "wave_y": derivative(wave_y),
        "turn": np.stack([lanes(turn.real), lanes(turn.imag)]),
    }


TABLES = make_tables()


def pieces(x, axis):
    high = x.astype(bf16)
    low = (x - high.astype(f32)).astype(bf16)
    return jnp.concatenate([high, low, high], axis=axis)


def rows_transform(rows_ref, fields):
    stacked = pieces(jnp.concatenate(fields, axis=1), 0)
    both = jnp.dot(rows_ref[...], stacked, preferred_element_type=f32)
    cosine = [both[:256, HALF * i : HALF * (i + 1)] for i in range(len(fields))]
    sine = [both[256:, HALF * i : HALF * (i + 1)] for i in range(len(fields))]
    return cosine, sine


def forward_rows(rows_ref, fields):
    cosine, sine = rows_transform(rows_ref, fields)
    out = []
    for i in range(0, len(fields), 2):
        out += [cosine[i] + sine[i + 1], cosine[i + 1] - sine[i]]
    return out


def inverse_rows(rows_ref, fields):
    cosine, sine = rows_transform(rows_ref, fields)
    out = []
    for i in range(0, len(fields), 2):
        out += [cosine[i] - sine[i + 1], cosine[i + 1] + sine[i]]
    return out


def times(real, imag, factor_real, factor_imag):
    return real * factor_real - imag * factor_imag, real * factor_imag + imag * factor_real


def columns_transform(x, table_ref):
    return jnp.dot(pieces(x, 1), table_ref[...], preferred_element_type=f32)


def kappa_rows(first, ky, signed_start):
    kz = lax.broadcasted_iota(jnp.int32, (256, HALF), 0) + signed_start
    kx = lax.broadcasted_iota(jnp.int32, (256, HALF), 1)
    ky = jnp.where(ky < NY // 2, ky, ky - NY)
    wave_z = kz.astype(f32) * (2.0 * math.pi / NZ)
    wave_x = kx.astype(f32) * (2.0 * math.pi / NX)
    wave_y = ky.astype(f32) * (2.0 * math.pi / NY)
    square = (kappa_courant / 2.0) ** 2 * (wave_x * wave_x + wave_z * wave_z + wave_y * wave_y)
    total = jnp.full((256, HALF), 1.0 / math.factorial(15), f32)
    for order in range(6, -1, -1):
        total = 1.0 / math.factorial(2 * order + 1) - square * total
    return total


def place_rows(scratch, position, blocks):
    for back, block in enumerate(blocks):
        start = pl.multiple_of(((position + PEERS_Y - back) % PEERS_Y) * ROWS, ROWS)
        scratch[..., pl.ds(start, ROWS), :] = block[...].astype(f32)


def forward_plane_kernel(where, b0, b1, b2, b3, rows_ref, x_ref, out, planes):
    place_rows(planes, where[0], (b0, b1, b2, b3))
    spectrum = columns_transform(planes[...].reshape(512, NX), x_ref) * SPECTRUM_SCALE
    fields = []
    for r in range(2):
        part = spectrum[256 * r : 256 * (r + 1)]
        fields += [part[:, :HALF], part[:, HALF:]]
    for i, field in enumerate(forward_rows(rows_ref, fields)):
        out[pl.ds(i, 256, stride=4), :] = field


def forward_z(rows_ref, turn_ref, even, odd):
    out = forward_rows(rows_ref, even + odd)
    count = len(even)
    low, high = [], []
    for i in range(0, count, 2):
        real, imag = times(out[count + i], out[count + i + 1], turn_ref[0], turn_ref[1])
        low += [out[i] + real, out[i + 1] + imag]
        high += [out[i] - real, out[i + 1] - imag]
    return low, high


def inverse_z(rows_ref, turn_ref, low, high):
    even, odd = [], []
    for i in range(0, len(low), 2):
        even += [low[i] + high[i], low[i + 1] + high[i + 1]]
        odd += times(low[i] - high[i], low[i + 1] - high[i + 1], turn_ref[0], -turn_ref[1])
    out = inverse_rows(rows_ref, even + odd)
    return out[: len(low)], out[len(low) :]


def slope_columns_kernel(where, data, rows_ref, turn_ref, wave_ref, out):
    even = [data[pl.ds(i, 256, stride=4), :] for i in (0, 1)]
    odd = [data[pl.ds(i, 256, stride=4), :] for i in (2, 3)]
    spectra = forward_z(rows_ref, turn_ref, even, odd)
    filtered = []
    for half in range(2):
        kappa = kappa_rows(half, where[0], -256 * half) * (SLOPE_LINK / NZ)
        real, imag = spectra[half][0] * kappa, spectra[half][1] * kappa
        span = pl.ds(256 * half, 256)
        filtered.append([real, imag, *times(real, imag, wave_ref[0, span], wave_ref[1, span])])
    even, odd = inverse_z(rows_ref, turn_ref, filtered[0], filtered[1])
    for r, fields in enumerate((even, odd)):
        for i, field in enumerate(fields):
            out[pl.ds(4 * r + i, 256, stride=8), :] = field


def middle_kernel(
    where, data, f0, f1, f2, f3, rows_ref, xi_ref, xia_ref, xf_ref, xfb_ref, wave_ref, slopes, out, planes
):
    place_rows(planes, where[0], (f0, f1, f2, f3))
    for r in range(2):
        q_real, q_imag, g_real, g_imag = [
            data[pl.ds(4 * r + i, 256, stride=8), :] for i in range(4)
        ]
        along = times(q_real, q_imag, wave_ref[0], wave_ref[1])
        mixed = inverse_rows(rows_ref, [q_real, q_imag, *along, g_real, g_imag])
        turned = []
        for d, table in enumerate((xia_ref, xi_ref, xi_ref)):
            pair = jnp.concatenate(mixed[2 * d : 2 * d + 2], axis=1)
            slope = columns_transform(pair, table) * SPECTRUM_SCALE
            slopes[d, r] = slope
            velocity = planes[d, r] - planes[3, r] * (slope * (1.0 / SLOPE_LINK))
            spectrum = columns_transform(velocity, (xfb_ref, xf_ref, xf_ref)[d])
            spectrum = spectrum * (SPECTRUM_SCALE * MIDDLE_LINK)
            turned += [spectrum[:, :HALF], spectrum[:, HALF:]]
        x_real, x_imag, y_real, y_imag, z_real, z_imag = forward_rows(rows_ref, turned)
        y_real, y_imag = times(y_real, y_imag, -wave_ref[0], wave_ref[1])
        fields = (x_real + y_real, x_imag + y_imag, z_real, z_imag)
        for i, field in enumerate(fields):
            out[pl.ds(4 * r + i, 256, stride=8), :] = field


def divergence_columns_kernel(where, data, rows_ref, turn_ref, wave_ref, out):
    even = [data[pl.ds(i, 256, stride=8), :] for i in range(4)]
    odd = [data[pl.ds(4 + i, 256, stride=8), :] for i in range(4)]
    spectra = forward_z(rows_ref, turn_ref, even, odd)
    summed = []
    for half in range(2):
        kappa = kappa_rows(half, where[0], -256 * half) * (DIVERGENCE_LINK / MIDDLE_LINK / NZ)
        span = pl.ds(256 * half, 256)
        a_real, a_imag, z_real, z_imag = spectra[half]
        real, imag = times(z_real, z_imag, -wave_ref[0, span], wave_ref[1, span])
        summed.append([(a_real + real) * kappa, (a_imag + imag) * kappa])
    even, odd = inverse_z(rows_ref, turn_ref, summed[0], summed[1])
    for i, field in enumerate(even + odd):
        out[pl.ds(i, 256, stride=4), :] = field


def inverse_plane_kernel(where, data, rows_ref, x_ref, o0, o1, o2, o3, planes):
    fields = [data[pl.ds(i, 256, stride=4), :] for i in range(4)]
    mixed = inverse_rows(rows_ref, fields)
    for r in range(2):
        pair = jnp.concatenate(mixed[2 * r : 2 * r + 2], axis=1)
        planes[r] = columns_transform(pair, x_ref) * SPECTRUM_SCALE
    for ahead, out in enumerate((o0, o1, o2, o3)):
        start = pl.multiple_of(((where[0] + ahead) % PEERS_Y) * ROWS, ROWS)
        out[...] = planes[:, pl.ds(start, ROWS), :]


VMEM = pl.BlockSpec(memory_space=pltpu.VMEM)
SMEM = pl.BlockSpec(memory_space=pltpu.SMEM)


def call(kernel, where, arrays, shapes, scratch=(), name=None, limit=24, flops=4e8):
    return pl.pallas_call(
        kernel,
        out_shape=[jax.ShapeDtypeStruct(shape, f32) for shape in shapes],
        in_specs=[SMEM] + [VMEM] * len(arrays),
        out_specs=[VMEM] * len(shapes),
        scratch_shapes=[pltpu.VMEM(shape, f32) for shape in scratch],
        compiler_params=pltpu.CompilerParams(vmem_limit_bytes=limit << 20),
        cost_estimate=pl.CostEstimate(flops=int(flops), bytes_accessed=1 << 20, transcendentals=0),
        name=name,
    )(where, *arrays)


def from_behind(x, axis, by):
    peers = lax.axis_size(axis)
    return lax.ppermute(x, axis, [(i, (i + by) % peers) for i in range(peers)])


def to_planes(fields, row_block):
    axis = fields.ndim - 3

    def planes_of(device):
        return lax.dynamic_slice_in_dim(fields, 2 * device, 2, axis).astype(f16)

    blocks = [planes_of(row_block)]
    for ahead in range(1, PEERS_Y):
        blocks.append(from_behind(planes_of((row_block + ahead) % PEERS_Y), "gy", ahead))
    return blocks


def to_rows(blocks, row_block, axis):
    arrived = [blocks[0]] + [
        from_behind(blocks[ahead].astype(f16), "gy", ahead).astype(f32)
        for ahead in range(1, PEERS_Y)
    ]
    ordered = []
    for device in range(PEERS_Y):
        back = (row_block - device) % PEERS_Y
        ordered.append(lax.select_n(back, *arrived))
    return jnp.concatenate(ordered, axis)


def exchange(columns, rows):
    blocks = columns.astype(f16).reshape(256, rows, HALF)
    moved = lax.all_to_all(blocks, ("gz", "gy"), 0, 0, tiled=True)
    return moved.reshape(256 * rows, HALF).astype(f32)


def one_hot_place(extent, start, span):
    target = jnp.arange(extent, dtype=jnp.int32)[None, :, None]
    wanted = start[:, None, None] + jnp.arange(span, dtype=jnp.int32)[None, None, :]
    return (target == wanted).astype(jnp.bfloat16)


def place_tiles(buffer, blocks, plane_start, row_start, column_start):
    planes, rows, columns = buffer.shape
    tile_z, tile_y, tile_x = (blocks.shape[1], blocks.shape[2], blocks.shape[3])
    column_hot = one_hot_place(columns, column_start, tile_x)
    across = jnp.einsum(
        "sabc,sxc->sabx", blocks, column_hot, preferred_element_type=jnp.float32
    ).astype(jnp.bfloat16)
    plane_hot = one_hot_place(planes, plane_start, tile_z)
    lifted = jnp.einsum(
        "sAa,sabx->sAbx", plane_hot, across, preferred_element_type=jnp.float32
    ).astype(jnp.bfloat16)
    row_hot = one_hot_place(rows, row_start, tile_y)
    return buffer + jnp.einsum("sAbx,srb->Arx", lifted, row_hot, preferred_element_type=jnp.float32)


def fold_columns(buffer, grid_x, tile_x):
    return buffer[..., :grid_x].at[..., :tile_x].add(buffer[..., grid_x:])


def source_of(tiles, tile_corner, live_count, slab_index, row_block):
    slabs_z = lax.axis_size("gz")
    rows_y = lax.axis_size("gy")
    slab_planes, row_count, grid_x = NZ // slabs_z, ROWS, NX
    slot_count, tile_z, tile_y, tile_x = tiles.shape
    slab_reach = (slab_planes + tile_z - 2) // slab_planes + 1
    own_device = slab_index * rows_y + row_block
    own_corners = lax.dynamic_slice_in_dim(tile_corner, own_device * slot_count, slot_count, 0)
    live_mask = (jnp.arange(slot_count, dtype=jnp.int32) < live_count[own_device]).astype(
        jnp.bfloat16
    )
    masked = tiles * live_mask[:, None, None, None]
    plane_offset = own_corners[:, 0] - slab_index * slab_planes
    padded = jnp.pad(masked, ((0, 0), (slab_planes, slab_planes), (0, 0), (0, 0)))
    window = jnp.zeros((slab_planes, 2 * row_count, grid_x + tile_x), jnp.float32)
    zero_start = jnp.zeros((slot_count,), jnp.int32)
    for step_index in range(slab_reach):
        first_plane = step_index * slab_planes - plane_offset + slab_planes
        blocks = jax.vmap(
            lambda tile_block, first_index: lax.dynamic_slice_in_dim(
                tile_block, first_index, slab_planes, 0
            )
        )(padded, first_plane)
        corners = own_corners
        if step_index > 0:
            blocks = from_behind(blocks, "gz", step_index)
            sender = (slab_index - step_index) % slabs_z * rows_y + row_block
            corners = lax.dynamic_slice_in_dim(tile_corner, sender * slot_count, slot_count, 0)
        window = place_tiles(
            window, blocks, zero_start, corners[:, 1] - row_block * row_count, corners[:, 2]
        )
    window = fold_columns(window, grid_x, tile_x)
    return window[:, :row_count] + from_behind(
        window[:, row_count:].astype(jnp.bfloat16), "gy", 1
    ).astype(jnp.float32)


def local(pressure, velocity, bulk, buoyancy, tiles, tile_corner, live_count):
    slab_index = lax.axis_index("gz")
    row_block = lax.axis_index("gy")
    here = row_block.reshape(1).astype(jnp.int32)
    device = (slab_index * PEERS_Y + row_block).reshape(1).astype(jnp.int32)
    table = {key: jnp.asarray(value) for key, value in TABLES.items()}
    rows, turn, wave_z, wave_y = (table[key] for key in ("rows", "turn", "wave_z", "wave_y"))

    blocks = to_planes(pressure, row_block)
    (spectrum,) = call(
        forward_plane_kernel,
        here,
        [*blocks_f32(blocks), rows, table["x_forward"]],
        [(1024, HALF)],
        [(2, NY, NX)],
        name="forward_plane",
    )
    velocity, buoyancy_after, spectrum = lax.optimization_barrier((velocity, buoyancy, spectrum))
    fields = jnp.concatenate([velocity, buoyancy_after[None]])
    field_blocks = to_planes(fields, row_block)

    columns = exchange(spectrum, 4)
    (slope_columns,) = call(
        slope_columns_kernel,
        device,
        [columns, rows, turn, wave_z],
        [(2048, HALF)],
        name="slope_columns",
    )
    slope_columns = exchange(slope_columns, 8)
    slopes, middle = call(
        middle_kernel,
        here,
        [
            slope_columns,
            *blocks_f32(field_blocks),
            rows,
            table["x_inverse"],
            table["x_inverse_ahead"],
            table["x_forward"],
            table["x_forward_behind"],
            wave_y,
        ],
        [(3, 2, NY, NX), (2048, HALF)],
        [(4, 2, NY, NX)],
        name="middle",
        limit=40,
    )
    slope_blocks = [
        lax.dynamic_slice_in_dim(slopes, ROWS * ((row_block + ahead) % PEERS_Y), ROWS, 2)
        for ahead in range(PEERS_Y)
    ]
    slopes_here = to_rows(slope_blocks, row_block, 1)
    new_velocity = velocity - buoyancy[None] * (slopes_here * (1.0 / SLOPE_LINK))

    middle = exchange(middle, 8)
    (divergence_columns,) = call(
        divergence_columns_kernel,
        device,
        [middle, rows, turn, wave_z],
        [(1024, HALF)],
        name="divergence_columns",
    )
    divergence_columns = exchange(divergence_columns, 4)
    divergence_blocks = call(
        inverse_plane_kernel,
        here,
        [divergence_columns, rows, table["x_inverse"]],
        [(2, ROWS, NX)] * PEERS_Y,
        [(2, NY, NX)],
        name="inverse_plane",
    )
    source = source_of(tiles, tile_corner, live_count, slab_index, row_block)
    divergence = to_rows(divergence_blocks, row_block, 0)
    new_pressure = pressure - bulk * (divergence * (1.0 / DIVERGENCE_LINK)) + source
    return (new_pressure, new_velocity)


def blocks_f32(blocks):
    return [block.astype(f32) for block in blocks]


def solution(mesh):
    in_specs = (
        P("gz", "gy", None),
        P(None, "gz", "gy", None),
        P("gz", "gy", None),
        P("gz", "gy", None),
        P(("gz", "gy"), None, None, None),
        P(),
        P(),
    )
    out_specs = (P("gz", "gy", None), P(None, "gz", "gy", None))
    return jax.shard_map(local, mesh=mesh, in_specs=in_specs, out_specs=out_specs, check_vma=False)
```

time: 401 us -> 154 us (0.38); the launches traced: 394 us -> 153 us
  blocking collectives: 85.3 us -> 0 us
  waiting for transfers between devices: 106 us -> 31.6 us
  matrix products: 63 us -> 9 us
  local copies, waits for them, and re-layouts: 55.1 us -> 19.2 us
  Pallas kernels: 0 us -> 9.96 us
  other arithmetic: 19.5 us -> 26.5 us
  starting transfers between devices: 62.6 us -> 55.8 us
    all_to_all x3 -> x0, blocking collectives: 85.3 us -> none  [the longest x1 45 us: inverse_z(): lax.all_to_all(sectioned, 'gz', split_axis=2, concat_axis=4, tiled=True)]
    all_to_all x9 -> x4, waiting for transfers between devices: 96.7 us -> 29.7 us  [exchange(): moved = lax.all_to_all(blocks, ('gz', 'gy'), 0, 0, tiled=True)]
    dot_general x20 -> x0, matrix products: 51.7 us -> none  [the longest x2 11.5 us: forward_z(): jnp.einsum('fcjaqm,cdjaq->fdjaqm', sectioned, turns, precision=highest)]
    all_to_all x9 -> x4, starting transfers between devices: 58.1 us -> 33.3 us  [exchange(): moved = lax.all_to_all(blocks, ('gz', 'gy'), 0, 0, tiled=True)]
    ppermute x3 -> x15, starting transfers between devices: 4.41 us -> 22.4 us  [from_behind(): return lax.ppermute(x, axis, [(i, (i + by) % peers) for i in range(peers)])]
    convert_element_type x1 -> x19, other arithmetic: 0.65 us -> 12.6 us  [the longest x6 5.51 us: blocks_f32(): return [block.astype(f32) for block in blocks]]
    all_to_all x15 -> x0, local copies, waits for them, and re-layouts: 11.1 us -> none  [the longest x2 3.63 us: inverse_z(): lax.all_to_all(sectioned, 'gz', split_axis=2, concat_axis=4, tiled=True)]
    pallas_call x0 -> x5, Pallas kernels: none -> 9.96 us  [call(): pl.pallas_call(kernel, out_shape=[jax.ShapeDtypeStruct(shape, f32) for sh...]
  transfers between devices with their start and end apart: 12 -> 19, of which waited for: 9 -> 5; matrix products, arithmetic and copies ran while one was open for 19% -> 27% of each run, Pallas kernels for 0% -> 7%
where the time goes in v1:
time: 154 us; the launch traced here: 153 us
  starting transfers between devices  55.8 us (36%)
  waiting for transfers between devices  31.6 us (21%)
  other arithmetic  26.5 us (17%)
  local copies, waits for them, and re-layouts  19.2 us (12%)
  Pallas kernels  9.96 us (6%)
  matrix products  9 us (6%)
    all_to_all x4, starting transfers between devices, exchange(): moved = lax.all_to_all(blocks, ('gz', 'gy'), 0, 0, tiled=True)  33.3 us
    all_to_all x4, waiting for transfers between devices, exchange(): moved = lax.all_to_all(blocks, ('gz', 'gy'), 0, 0, tiled=True)  29.7 us
    ppermute x15, starting transfers between devices, from_behind(): return lax.ppermute(x, axis, [(i, (i + by) % peers) for i in range(peers)])  22.4 us
    pallas_call x5, Pallas kernels, call(): pl.pallas_call(kernel, out_shape=[jax.ShapeDtypeStruct(shape, f32) for sh...  9.96 us
    convert_element_type x6, other arithmetic, blocks_f32(): return [block.astype(f32) for block in blocks]  5.51 us
    unnamed x58, local copies, waits for them, and re-layouts  5.12 us
    dot_general x3, matrix products, place_tiles(): jnp.einsum('sabc,sxc->sabx', blocks, column_hot, preferred_element_type=j...  3.79 us
    scatter-add x1, local copies, waits for them, and re-layouts, fold_columns(): return buffer[..., :grid_x].at[..., :tile_x].add(buffer[..., grid_x:])  3.51 us
  transfers between devices with their start and end apart: 19, of which 5 were waited for; matrix products, arithmetic and copies ran while one was open for 27% of the time, Pallas kernels for 7%

profile of v1, /device:TPU:1, one launch (start us, length us, event | category | flops | bytes accessed | tf_op | source)
XLA Modules:
  0.0 153.2 jit_solution(15235588339694908971)
XLA Ops:
  7.3 2.6 %collective-permute-start.9 = (bf16[8,8,32,32]{3,2,1,0:T(8,128)(2,1)}, bf16[8,8,32,32]{3,2,1,0:T(8,128)(2,1)}, u32[]{:S(2)}, u32[]{:S(2)}) collective-permute-start(bf16[8,8,32,32]{3,2,1,0:T(8,128)(2,1)} %gather_fusion.1), channel_id=1, source_target_pairs={{0,4},{4,8},{8,12},{12,16},{16,20},{20,24},{24,28},{28,32},{32,36}... | collective-permute-start | bytes 393224 | tf_op jit(solution)/shard_map/ppermute | solution.py:269
  14.6 2.6 %collective-permute-start.1 = (f16[2,64,256]{2,1,0:T(8,128)(2,1)}, f16[2,64,256]{2,1,0:T(8,128)(2,1)}, u32[]{:S(2)}, u32[]{:S(2)}) collective-permute-start(f16[2,64,256]{2,1,0:T(8,128)(2,1)} %get-tuple-element.44), channel_id=1, source_target_pairs={{0,2},{1,3},{2,0},{3,1},{4,6},{5,7},{6,4},{7,5},{8,10},{9,11},{10,... | collective-permute-start | bytes 196616 | tf_op jit(solution)/shard_map/ppermute | solution.py:269
  25.0 12.4 %all-to-all-start = ((f16[256,4,128]{2,1,0:T(4,128)(2,1)}), f16[256,4,128]{2,1,0:T(4,128)(2,1)S(1)}, u32[]{:S(2)}, u32[]{:S(2)}) async-start(f16[256,4,128]{2,1,0:T(4,128)(2,1)} %bitcast.2), calls=%async_computation | async-start | bytes 524288 | tf_op jit(solution)/shard_map/all_to_all | solution.py:298
  38.0 1.8 %fusion.9 = bf16[8,8,32,288]{3,1,2,0:T(8,128)(2,1)} fusion(bf16[8,8,32,288]{3,2,1,0:T(8,128)(2,1)S(1)} %convolution_convert_fusion.2), kind=kOutput, calls=%fused_computation.28 | convolution fusion | flops 9437696 | bytes 2359296 | tf_op jit(solution)/shard_map/sAa,sabx->sAbx/dot_general | solution.py:316
  42.2 2.4 %collective-permute-start.4 = (f16[4,2,64,256]{3,2,1,0:T(8,128)(2,1)}, f16[4,2,64,256]{3,2,1,0:T(8,128)(2,1)}, u32[]{:S(2)}, u32[]{:S(2)}) collective-permute-start(f16[4,2,64,256]{3,2,1,0:T(8,128)(2,1)} %get-tuple-element.39), channel_id=1, source_target_pairs={{0,2},{1,3},{2,0},{3,1},{4,6},{5,7},{6,4},{7,5},{8,10},{9,11},{10,... | collective-permute-start | bytes 786440 | tf_op jit(solution)/shard_map/ppermute | solution.py:269
  45.8 6.8 %all-to-all-done = f16[256,4,128]{2,1,0:T(4,128)(2,1)S(1)} async-done(((f16[256,4,128]{2,1,0:T(4,128)(2,1)}), f16[256,4,128]{2,1,0:T(4,128)(2,1)S(1)}, u32[]{:S(2)}, u32[]{:S(2)}) %all-to-all-start) | async-done | bytes 262176 | tf_op jit(solution)/shard_map/all_to_all | solution.py:298
  52.7 1.8 %slope_columns.1 = f32[2048,128]{1,0:T(8,128)S(1)} custom-call(s32[1]{0:T(128)} %bitcast.1.where, f32[1024,128]{1,0:T(8,128)S(1)} %convert.8.data, bf16[512,768]{1,0:T(8,128)(2,1)S(1)} %copy-done, f32[2,256,128]{2,1,0:T(8,128)S(1)} %copy-done.8, f32[2,512,128]{2,1,0:T(8,128)S(1)} %copy-done.1), custom_call_target="tpu_custom_call" | custom-call | flops 400000000 | bytes 1048576 | tf_op jit(solution)/shard_map/slope_columns/pallas_call | solution.py:255
  55.4 7.2 %all-to-all-start.1 = ((f16[256,8,128]{2,1,0:T(8,128)(2,1)}), f16[256,8,128]{2,1,0:T(8,128)(2,1)}, u32[]{:S(2)}, u32[]{:S(2)}) async-start(f16[256,8,128]{2,1,0:T(8,128)(2,1)} %convert_bitcast_fusion.1), calls=%async_computation.1 | async-start | bytes 1048576 | tf_op jit(solution)/shard_map/all_to_all | solution.py:298
  67.1 1.6 %copy.22 = f32[128,8,288]{2,0,1:T(8,128)} copy(f32[128,8,288]{0,2,1:T(8,128)S(1)} %fusion.13) | data formatting | bytes 2359296 | tf_op jit(solution)/shard_map/add | solution.py:320
  71.7 10.1 %all-to-all-done.1 = f16[256,8,128]{2,1,0:T(8,128)(2,1)} async-done(((f16[256,8,128]{2,1,0:T(8,128)(2,1)}), f16[256,8,128]{2,1,0:T(8,128)(2,1)}, u32[]{:S(2)}, u32[]{:S(2)}) %all-to-all-start.1) | async-done | bytes 524320 | tf_op jit(solution)/shard_map/all_to_all | solution.py:298
  84.2 4.3 %middle.1 = (f32[3,2,256,256]{3,2,1,0:T(8,128)S(1)}, f32[2048,128]{1,0:T(8,128)S(1)}) custom-call(s32[1]{0:T(128)} %bitcast.where, f32[2048,128]{1,0:T(8,128)S(1)} %bitcast_convert_fusion.1.data, f32[4,2,64,256]{3,2,1,0:T(8,128)S(1)} %get-tuple-element.37.f0, f32[4,2,64,256]{3,2,1,0:T(8,128)S(1)} %convert_element_type.173.f1, ...), custom_call_target="tpu_custom_call" | custom-call | flops 400000000 | bytes 1048576 | tf_op jit(solution)/shard_map/middle/pallas_call | solution.py:255
  90.6 7.4 %all-to-all-start.2 = ((f16[256,8,128]{2,1,0:T(8,128)(2,1)}), f16[256,8,128]{2,1,0:T(8,128)(2,1)}, u32[]{:S(2)}, u32[]{:S(2)}) async-start(f16[256,8,128]{2,1,0:T(8,128)(2,1)} %convert_bitcast_fusion), calls=%async_computation.2 | async-start | bytes 1048576 | tf_op jit(solution)/shard_map/all_to_all | solution.py:298
  107.4 1.7 %collective-permute-start.13 = (f16[3,2,64,256]{3,2,1,0:T(8,128)(2,1)}, f16[3,2,64,256]{3,2,1,0:T(8,128)(2,1)}, u32[]{:S(2)}, u32[]{:S(2)}) collective-permute-start(f16[3,2,64,256]{3,2,1,0:T(8,128)(2,1)} %get-tuple-element.40), channel_id=1, source_target_pairs={{0,2},{1,3},{2,0},{3,1},{4,6},{5,7},{6,4},{7,5},{8,10},{9,11},{10,... | collective-permute-start | bytes 589832 | tf_op jit(solution)/shard_map/ppermute | solution.py:269
  109.1 7.9 %all-to-all-done.2 = f16[256,8,128]{2,1,0:T(8,128)(2,1)} async-done(((f16[256,8,128]{2,1,0:T(8,128)(2,1)}), f16[256,8,128]{2,1,0:T(8,128)(2,1)}, u32[]{:S(2)}, u32[]{:S(2)}) %all-to-all-start.2) | async-done | bytes 524320 | tf_op jit(solution)/shard_map/all_to_all | solution.py:298
  118.1 2.0 %divergence_columns.1 = f32[1024,128]{1,0:T(8,128)S(1)} custom-call(s32[1]{0:T(128)} %bitcast.1.where, f32[2048,128]{1,0:T(8,128)S(1)} %bitcast_convert_fusion.data, bf16[512,768]{1,0:T(8,128)(2,1)S(1)} %copy-done, f32[2,256,128]{2,1,0:T(8,128)S(1)} %copy-done.9, f32[2,512,128]{2,1,0:T(8,128)S(1)} %copy-done.1), custom_call_target="tpu_custom_call" | custom-call | flops 400000000 | bytes 1048576 | tf_op jit(solution)/shard_map/divergence_columns/pallas_call | solution.py:255
  120.9 6.4 %all-to-all-start.3 = ((f16[256,4,128]{2,1,0:T(4,128)(2,1)}), f16[256,4,128]{2,1,0:T(4,128)(2,1)S(1)}, u32[]{:S(2)}, u32[]{:S(2)}) async-start(f16[256,4,128]{2,1,0:T(4,128)(2,1)} %bitcast.9), calls=%async_computation.3 | async-start | bytes 524288 | tf_op jit(solution)/shard_map/all_to_all | solution.py:298
  128.6 3.5 %scatter-add.4 = f32[8,128,256]{2,1,0:T(8,128)} dynamic-update-slice(f32[8,128,256]{2,1,0:T(8,128)} %slice.92, f32[8,128,32]{2,1,0:T(8,128)S(1)} %slice_add_fusion.1, s32[]{:T(128)} %constant.142.clone.1, s32[]{:T(128)} %constant.142.clone.1, s32[]{:T(128)} %constant.142.clone.1) | dynamic-update-slice | bytes 262148 | tf_op jit(solution)/shard_map/scatter-add | solution.py:324
  132.1 1.8 %slice.116 = bf16[8,64,256]{2,1,0:T(8,128)(2,1)} slice(f32[8,128,256]{2,1,0:T(8,128)} %scatter-add.4), slice={[0:8], [64:128], [0:256]} | slice | bytes 524288 | tf_op jit(solution)/shard_map/slice | solution.py:360
  135.3 2.4 %fusion.34 = (f32[3,2,64,256]{3,2,1,0:T(8,128)}, f32[3,2,64,256]{3,2,1,0:T(8,128)}, f32[3,2,64,256]{3,2,1,0:T(8,128)}, f32[3,2,64,256]{3,2,1,0:T(8,128)}) fusion(f16[3,2,64,256]{3,2,1,0:T(8,128)(2,1)} %collective-permute-done.12, f16[3,2,64,256]{3,2,1,0:T(8,128)(2,1)} %collective-permute-done.14, f16[3,2,64,256]{3,2,1,0:T(8,128)(2,1)} %collective-permute-done.13, ...), kind=kLoop, calls=%fused_computation.70 | loop fusion | flops 1474560 | bytes 2555920 | tf_op jit(solution)/shard_map/select_n | solution.py:292
  137.8 4.8 %all-to-all-done.3 = f16[256,4,128]{2,1,0:T(4,128)(2,1)S(1)} async-done(((f16[256,4,128]{2,1,0:T(4,128)(2,1)}), f16[256,4,128]{2,1,0:T(4,128)(2,1)S(1)}, u32[]{:S(2)}, u32[]{:S(2)}) %all-to-all-start.3) | async-done | bytes 262176 | tf_op jit(solution)/shard_map/all_to_all | solution.py:298
  143.8 2.6 %collective-permute-start.8 = (f16[2,64,256]{2,1,0:T(8,128)(2,1)S(1)}, f16[2,64,256]{2,1,0:T(8,128)(2,1)S(1)}, u32[]{:S(2)}, u32[]{:S(2)}) collective-permute-start(f16[2,64,256]{2,1,0:T(8,128)(2,1)S(1)} %convert_element_type.188), channel_id=1, source_target_pairs={{0,3},{1,0},{2,1},{3,2},{4,7},{5,4},{6,5},{7,6},{8,11},{9,8},{10,9... | collective-permute-start | bytes 196616 | tf_op jit(solution)/shard_map/ppermute | solution.py:269
  146.6 2.7 %fusion.3 = f32[3,8,64,256]{3,2,1,0:T(8,128)} fusion(f32[3,8,64,256]{3,2,1,0:T(8,128)S(1)} %copy-done.16, f32[3,2,64,256]{3,2,1,0:T(8,128)} %get-tuple-element.35, f32[3,2,64,256]{3,2,1,0:T(8,128)} %get-tuple-element.34, f32[3,2,64,256]{3,2,1,0:T(8,128)S(1)} %copy-done.24, f32[3,2,64,256]{3,2,1,0:T(8,128)S(1)} %copy-done.23, f32[8,64,256]{2,1,0:T(8,128)S(1)} %copy-done.19), kind=kLoop, calls=%fused_computation.21 | loop fusion | flops 1966080 | bytes 5242880 | tf_op jit(solution)/shard_map/sub | solution.py:417
  149.3 1.9 %collective-permute-done.7 = f16[2,64,256]{2,1,0:T(8,128)(2,1)S(1)} collective-permute-done((f16[2,64,256]{2,1,0:T(8,128)(2,1)S(1)}, f16[2,64,256]{2,1,0:T(8,128)(2,1)S(1)}, u32[]{:S(2)}, u32[]{:S(2)}) %collective-permute-start.7) | collective-permute-done | bytes 65568 | tf_op jit(solution)/shard_map/ppermute | solution.py:269
  151.3 1.9 %fusion.31 = f32[8,64,256]{2,1,0:T(8,128)} fusion(f32[8,128,256]{2,1,0:T(8,128)S(1)} %copy-done.18, f32[8,64,256]{2,1,0:T(8,128)S(1)} %copy-done.22, f32[8,64,256]{2,1,0:T(8,128)S(1)} %copy-done.25, f32[2,64,256]{2,1,0:T(8,128)S(1)} %get-tuple-element.48, f32[2,64,256]{2,1,0:T(8,128)S(1)} %get-tuple-element.49, f32[2,64,256]{2,1,0:T(8,128)S(1)} %get-tuple-element.50, ...), kind=kLoop, calls=%fused_computation.61 | loop fusion | flops 1179648 | bytes 2883584 | tf_op jit(solution)/shard_map/add | solution.py:438
  (131 shorter events, 51.2 us)
Async XLA Ops:
  7.3 11.7 %copy-start.20 = (f32[8,64,256]{2,1,0:T(8,128)S(1)}, f32[8,64,256]{2,1,0:T(8,128)}, u32[]{:S(2)}) copy-start(f32[8,64,256]{2,1,0:T(8,128)} %param.20) | copy-start | bytes 1572868
  7.3 55.2 %collective-permute-start.9 = (bf16[8,8,32,32]{3,2,1,0:T(8,128)(2,1)}, bf16[8,8,32,32]{3,2,1,0:T(8,128)(2,1)}, u32[]{:S(2)}, u32[]{:S(2)}) collective-permute-start(bf16[8,8,32,32]{3,2,1,0:T(8,128)(2,1)} %gather_fusion.1), channel_id=1, source_target_pairs={{0,4},{4,8},{8,12},{12,16},{16,20},{20,24},{24,28},{28,32},{32,36}... | collective-permute-start | bytes 393224 | tf_op jit(solution)/shard_map/ppermute | solution.py:269
  11.4 86.5 %collective-permute-start.10 = (bf16[8,8,32,32]{3,2,1,0:T(8,128)(2,1)}, bf16[8,8,32,32]{3,2,1,0:T(8,128)(2,1)}, u32[]{:S(2)}, u32[]{:S(2)}) collective-permute-start(bf16[8,8,32,32]{3,2,1,0:T(8,128)(2,1)} %gather_fusion.2), channel_id=1, source_target_pairs={{0,8},{4,12},{8,16},{12,20},{16,24},{20,28},{24,32},{28,36},{32,40... | collective-permute-start | bytes 393224 | tf_op jit(solution)/shard_map/ppermute | solution.py:269
  13.3 7.4 %collective-permute-start = (f16[2,64,256]{2,1,0:T(8,128)(2,1)}, f16[2,64,256]{2,1,0:T(8,128)(2,1)}, u32[]{:S(2)}, u32[]{:S(2)}) collective-permute-start(f16[2,64,256]{2,1,0:T(8,128)(2,1)} %get-tuple-element.45), channel_id=1, source_target_pairs={{0,1},{1,2},{2,3},{3,0},{4,5},{5,6},{6,7},{7,4},{8,9},{9,10},{10,1... | collective-permute-start | bytes 196616 | tf_op jit(solution)/shard_map/ppermute | solution.py:269
  14.6 7.0 %collective-permute-start.1 = (f16[2,64,256]{2,1,0:T(8,128)(2,1)}, f16[2,64,256]{2,1,0:T(8,128)(2,1)}, u32[]{:S(2)}, u32[]{:S(2)}) collective-permute-start(f16[2,64,256]{2,1,0:T(8,128)(2,1)} %get-tuple-element.44), channel_id=1, source_target_pairs={{0,2},{1,3},{2,0},{3,1},{4,6},{5,7},{6,4},{7,5},{8,10},{9,11},{10,... | collective-permute-start | bytes 196616 | tf_op jit(solution)/shard_map/ppermute | solution.py:269
  17.2 5.2 %collective-permute-start.2 = (f16[2,64,256]{2,1,0:T(8,128)(2,1)}, f16[2,64,256]{2,1,0:T(8,128)(2,1)}, u32[]{:S(2)}, u32[]{:S(2)}) collective-permute-start(f16[2,64,256]{2,1,0:T(8,128)(2,1)} %get-tuple-element.43), channel_id=1, source_target_pairs={{0,3},{1,0},{2,1},{3,2},{4,7},{5,4},{6,5},{7,6},{8,11},{9,8},{10,9... | collective-permute-start | bytes 196616 | tf_op jit(solution)/shard_map/ppermute | solution.py:269
  23.3 14.1 %copy-start.27 = (s32[8]{0:T(128)S(1)}, s32[8]{0:T(128)}, u32[]{:S(2)}) copy-start(s32[8]{0:T(128)} %get-tuple-element.64) | copy-start | bytes 100
  25.0 27.7 %all-to-all-start = ((f16[256,4,128]{2,1,0:T(4,128)(2,1)}), f16[256,4,128]{2,1,0:T(4,128)(2,1)S(1)}, u32[]{:S(2)}, u32[]{:S(2)}) async-start(f16[256,4,128]{2,1,0:T(4,128)(2,1)} %bitcast.2), calls=%async_computation | async-start | bytes 524288 | tf_op jit(solution)/shard_map/all_to_all | solution.py:298
  39.8 12.8 %copy-start.1 = (f32[2,512,128]{2,1,0:T(8,128)S(1)}, f32[2,512,128]{2,1,0:T(8,128)}, u32[]{:S(2)}) copy-start(f32[2,512,128]{2,1,0:T(8,128)} %constant.170.clone.wave_ref) | copy-start | bytes 1572868
  39.8 12.9 %copy-start.8 = (f32[2,256,128]{2,1,0:T(8,128)S(1)}, f32[2,256,128]{2,1,0:T(8,128)}, u32[]{:S(2)}) copy-start(f32[2,256,128]{2,1,0:T(8,128)} %constant.172.clone.turn_ref) | copy-start | bytes 786436
  40.8 27.9 %collective-permute-start.3 = (f16[4,2,64,256]{3,2,1,0:T(8,128)(2,1)}, f16[4,2,64,256]{3,2,1,0:T(8,128)(2,1)}, u32[]{:S(2)}, u32[]{:S(2)}) collective-permute-start(f16[4,2,64,256]{3,2,1,0:T(8,128)(2,1)} %get-tuple-element.38), channel_id=1, source_target_pairs={{0,1},{1,2},{2,3},{3,0},{4,5},{5,6},{6,7},{7,4},{8,9},{9,10},{10,1... | collective-permute-start | bytes 786440 | tf_op jit(solution)/shard_map/ppermute | solution.py:269
  42.2 27.5 %collective-permute-start.4 = (f16[4,2,64,256]{3,2,1,0:T(8,128)(2,1)}, f16[4,2,64,256]{3,2,1,0:T(8,128)(2,1)}, u32[]{:S(2)}, u32[]{:S(2)}) collective-permute-start(f16[4,2,64,256]{3,2,1,0:T(8,128)(2,1)} %get-tuple-element.39), channel_id=1, source_target_pairs={{0,2},{1,3},{2,0},{3,1},{4,6},{5,7},{6,4},{7,5},{8,10},{9,11},{10,... | collective-permute-start | bytes 786440 | tf_op jit(solution)/shard_map/ppermute | solution.py:269
  44.6 26.0 %collective-permute-start.5 = (f16[4,2,64,256]{3,2,1,0:T(8,128)(2,1)S(1)}, f16[4,2,64,256]{3,2,1,0:T(8,128)(2,1)}, u32[]{:S(2)}, u32[]{:S(2)}) collective-permute-start(f16[4,2,64,256]{3,2,1,0:T(8,128)(2,1)S(1)} %get-tuple-element.36), channel_id=1, source_target_pairs={{0,3},{1,0},{2,1},{3,2},{4,7},{5,4},{6,5},{7,6},{8,11},{9,8},{10,9... | collective-permute-start | bytes 786440 | tf_op jit(solution)/shard_map/ppermute | solution.py:269
  55.4 26.4 %all-to-all-start.1 = ((f16[256,8,128]{2,1,0:T(8,128)(2,1)}), f16[256,8,128]{2,1,0:T(8,128)(2,1)}, u32[]{:S(2)}, u32[]{:S(2)}) async-start(f16[256,8,128]{2,1,0:T(8,128)(2,1)} %convert_bitcast_fusion.1), calls=%async_computation.1 | async-start | bytes 1048576 | tf_op jit(solution)/shard_map/all_to_all | solution.py:298
  90.6 26.5 %all-to-all-start.2 = ((f16[256,8,128]{2,1,0:T(8,128)(2,1)}), f16[256,8,128]{2,1,0:T(8,128)(2,1)}, u32[]{:S(2)}, u32[]{:S(2)}) async-start(f16[256,8,128]{2,1,0:T(8,128)(2,1)} %convert_bitcast_fusion), calls=%async_computation.2 | async-start | bytes 1048576 | tf_op jit(solution)/shard_map/all_to_all | solution.py:298
  103.9 14.2 %copy-start.9 = (f32[2,256,128]{2,1,0:T(8,128)S(1)}, f32[2,256,128]{2,1,0:T(8,128)}, u32[]{:S(2)}) copy-start(f32[2,256,128]{2,1,0:T(8,128)} %constant.172.clone.turn_ref) | copy-start | bytes 786436
  104.8 30.6 %collective-permute-start.12 = (f16[3,2,64,256]{3,2,1,0:T(8,128)(2,1)}, f16[3,2,64,256]{3,2,1,0:T(8,128)(2,1)}, u32[]{:S(2)}, u32[]{:S(2)}) collective-permute-start(f16[3,2,64,256]{3,2,1,0:T(8,128)(2,1)} %get-tuple-element.42), channel_id=1, source_target_pairs={{0,1},{1,2},{2,3},{3,0},{4,5},{5,6},{6,7},{7,4},{8,9},{9,10},{10,1... | collective-permute-start | bytes 589832 | tf_op jit(solution)/shard_map/ppermute | solution.py:269
  106.2 29.2 %collective-permute-start.14 = (f16[3,2,64,256]{3,2,1,0:T(8,128)(2,1)}, f16[3,2,64,256]{3,2,1,0:T(8,128)(2,1)}, u32[]{:S(2)}, u32[]{:S(2)}) collective-permute-start(f16[3,2,64,256]{3,2,1,0:T(8,128)(2,1)} %get-tuple-element.41), channel_id=1, source_target_pairs={{0,3},{1,0},{2,1},{3,2},{4,7},{5,4},{6,5},{7,6},{8,11},{9,8},{10,9... | collective-permute-start | bytes 589832 | tf_op jit(solution)/shard_map/ppermute | solution.py:269
  107.4 27.9 %collective-permute-start.13 = (f16[3,2,64,256]{3,2,1,0:T(8,128)(2,1)}, f16[3,2,64,256]{3,2,1,0:T(8,128)(2,1)}, u32[]{:S(2)}, u32[]{:S(2)}) collective-permute-start(f16[3,2,64,256]{3,2,1,0:T(8,128)(2,1)} %get-tuple-element.40), channel_id=1, source_target_pairs={{0,2},{1,3},{2,0},{3,1},{4,6},{5,7},{6,4},{7,5},{8,10},{9,11},{10,... | collective-permute-start | bytes 589832 | tf_op jit(solution)/shard_map/ppermute | solution.py:269
  120.9 21.7 %all-to-all-start.3 = ((f16[256,4,128]{2,1,0:T(4,128)(2,1)}), f16[256,4,128]{2,1,0:T(4,128)(2,1)S(1)}, u32[]{:S(2)}, u32[]{:S(2)}) async-start(f16[256,4,128]{2,1,0:T(4,128)(2,1)} %bitcast.9), calls=%async_computation.3 | async-start | bytes 524288 | tf_op jit(solution)/shard_map/all_to_all | solution.py:298
  133.9 17.3 %collective-permute-start.11 = (bf16[8,64,256]{2,1,0:T(8,128)(2,1)}, bf16[8,64,256]{2,1,0:T(8,128)(2,1)}, u32[]{:S(2)}, u32[]{:S(2)}) collective-permute-start(bf16[8,64,256]{2,1,0:T(8,128)(2,1)} %slice.116), channel_id=1, source_target_pairs={{0,1},{1,2},{2,3},{3,0},{4,5},{5,6},{6,7},{7,4},{8,9},{9,10},{10,1... | collective-permute-start | bytes 786440 | tf_op jit(solution)/shard_map/ppermute | solution.py:269
  143.6 5.7 %collective-permute-start.6 = (f16[2,64,256]{2,1,0:T(8,128)(2,1)S(1)}, f16[2,64,256]{2,1,0:T(8,128)(2,1)S(1)}, u32[]{:S(2)}, u32[]{:S(2)}) collective-permute-start(f16[2,64,256]{2,1,0:T(8,128)(2,1)S(1)} %convert_element_type.184), channel_id=1, source_target_pairs={{0,1},{1,2},{2,3},{3,0},{4,5},{5,6},{6,7},{7,4},{8,9},{9,10},{10,1... | collective-permute-start | bytes 196616 | tf_op jit(solution)/shard_map/ppermute | solution.py:269
  143.8 5.5 %collective-permute-start.8 = (f16[2,64,256]{2,1,0:T(8,128)(2,1)S(1)}, f16[2,64,256]{2,1,0:T(8,128)(2,1)S(1)}, u32[]{:S(2)}, u32[]{:S(2)}) collective-permute-start(f16[2,64,256]{2,1,0:T(8,128)(2,1)S(1)} %convert_element_type.188), channel_id=1, source_target_pairs={{0,3},{1,0},{2,1},{3,2},{4,7},{5,4},{6,5},{7,6},{8,11},{9,8},{10,9... | collective-permute-start | bytes 196616 | tf_op jit(solution)/shard_map/ppermute | solution.py:269
  146.5 4.7 %collective-permute-start.7 = (f16[2,64,256]{2,1,0:T(8,128)(2,1)S(1)}, f16[2,64,256]{2,1,0:T(8,128)(2,1)S(1)}, u32[]{:S(2)}, u32[]{:S(2)}) collective-permute-start(f16[2,64,256]{2,1,0:T(8,128)(2,1)S(1)} %convert_element_type.186), channel_id=1, source_target_pairs={{0,2},{1,3},{2,0},{3,1},{4,6},{5,7},{6,4},{7,5},{8,10},{9,11},{10,... | collective-permute-start | bytes 196616 | tf_op jit(solution)/shard_map/ppermute | solution.py:269
  (24 other events, 77.1 us)

commit v2 on v1

v2 whole, which is shorter than its diff:
```python
import math

import jax
import jax.numpy as jnp
import ml_dtypes
import numpy as np
from jax import lax
from jax.experimental import pallas as pl
from jax.experimental.pallas import tpu as pltpu
from jax.sharding import PartitionSpec as P

NX = 256
NY = 256
NZ = 512
HALF = 128
ROWS = 64
SLAB = 8
SLOTS_HERE = 8
TILE = 32
PEERS_Y = 4
PEERS_Z = 64
kappa_courant = 0.3
f32 = jnp.float32
bf16 = jnp.bfloat16
f16 = jnp.float16

X_SCALE = 1.0 / 16.0
SLOPE_LINK = 0.25
MIDDLE_LINK = 1.0 / 16.0
DIVERGENCE_LINK = 1.0 / 32.0


def split_table(table):
    high = table.astype(ml_dtypes.bfloat16)
    low = (table - high.astype(np.float64)).astype(ml_dtypes.bfloat16)
    return high, low


def left_table(table):
    high, low = split_table(table)
    return np.concatenate([high, high, low], axis=1)


def right_table(table):
    return np.ascontiguousarray(left_table(table.T).T)


def signed_waves(length):
    index = np.arange(length)
    return 2.0 * np.pi / length * np.where(index < length // 2, index, index - length)


def derivative_matrix(length, orientation):
    wave = signed_waves(length)
    kernel = np.fft.ifft(1j * wave * np.exp(orientation * 0.5j * wave)).real
    index = np.arange(length)
    return kernel[(index[:, None] - index[None, :]) % length]


def cas(rows, columns, length):
    angle = 2.0 * np.pi / length * (np.outer(rows, columns) % length)
    return np.cos(angle) + np.sin(angle)


def make_tables():
    index = np.arange(256)
    wave_x = 2.0 * np.pi / NX * np.arange(HALF)
    angle_x = 2.0 * np.pi / NX * (np.outer(np.arange(HALF), index) % NX)

    def forward_x(factor):
        spectrum = np.exp(-1j * angle_x) * factor[:, None]
        return left_table(np.concatenate([spectrum.real, spectrum.imag], axis=0))

    def inverse_x(factor):
        weight = np.where(np.arange(HALF) == 0, 1.0, 2.0) * factor
        wave = np.exp(1j * angle_x) * weight[:, None]
        return np.concatenate([wave.real, -wave.imag], axis=0)

    ahead = 1j * wave_x * np.exp(0.5j * wave_x)
    behind = 1j * wave_x * np.exp(-0.5j * wave_x)
    plain = np.ones(HALF)
    waves = np.arange(NZ)
    pair_order = (2 * np.arange(256)[None, :] + np.arange(2)[:, None]).reshape(-1)
    slab_order = (
        8 * np.arange(64)[None, None, :]
        + 2 * np.arange(4)[None, :, None]
        + np.arange(2)[:, None, None]
    ).reshape(-1)
    natural = cas(waves, waves, NZ)
    ahead_z = derivative_matrix(NZ, 1.0)
    behind_z = derivative_matrix(NZ, -1.0)
    return {
        "x_forward": forward_x(plain),
        "x_forward_behind": forward_x(behind),
        "x_inverse": right_table(inverse_x(plain)),
        "x_inverse_both": right_table(
            np.concatenate([inverse_x(ahead), inverse_x(plain)], axis=1)
        ),
        "y_ahead": left_table(derivative_matrix(NY, 1.0)),
        "y_behind": left_table(derivative_matrix(NY, -1.0)),
        "y_waves": right_table(cas(index, index, NY)),
        "z_from_slabs": left_table(natural[:, slab_order]),
        "z_to_pairs": left_table(
            np.concatenate([natural[pair_order], (ahead_z @ natural)[pair_order]], axis=0)
        ),
        "z_from_pairs": np.concatenate(
            [left_table(natural[:, pair_order]), left_table((natural @ behind_z)[:, pair_order])],
            axis=1,
        ),
        "z_to_slabs": left_table(natural[slab_order]),
    }


TABLES = make_tables()


def pieces(x, axis):
    high = x.astype(bf16)
    low = (x - high.astype(f32)).astype(bf16)
    return jnp.concatenate([high, low, high], axis=axis)


def contract(a, b, a_dim, b_dim):
    return lax.dot_general(a, b, (((a_dim,), (b_dim,)), ((), ())), preferred_element_type=f32)


def left(table_ref, x):
    return contract(table_ref[...], pieces(x, 0), 1, 0)


def right(x, table_ref):
    return contract(pieces(x, 1), table_ref[...], 1, 0)


def to_components(table_ref, lines):
    return contract(table_ref[...], pieces(lines, 1), 1, 1)


def to_lines(components, table_ref):
    return contract(pieces(components, 0), table_ref[...], 0, 0)


def kappa_plane(kx):
    kz = lax.broadcasted_iota(jnp.int32, (NZ, NY), 0)
    ky = lax.broadcasted_iota(jnp.int32, (NZ, NY), 1)
    wave_z = jnp.where(kz < NZ // 2, kz, kz - NZ).astype(f32) * (2.0 * math.pi / NZ)
    wave_y = jnp.where(ky < NY // 2, ky, ky - NY).astype(f32) * (2.0 * math.pi / NY)
    wave_x = jnp.full((NZ, NY), kx, jnp.int32).astype(f32) * (2.0 * math.pi / NX)
    square = (kappa_courant / 2.0) ** 2 * (wave_x * wave_x + wave_z * wave_z + wave_y * wave_y)
    total = jnp.full((NZ, NY), 1.0 / math.factorial(15), f32)
    for order in range(6, -1, -1):
        total = 1.0 / math.factorial(2 * order + 1) - square * total
    return total


def first_half():
    return lax.broadcasted_iota(jnp.int32, (64, HALF), 1) < ROWS


def forward_lines_kernel(pressure, x_ref, out):
    components = to_components(x_ref, pressure[...].reshape(512, NX)) * X_SCALE
    for i in range(4):
        out[pl.ds(i, 256, stride=4), :] = components[:, HALF * i : HALF * (i + 1)]


def filter_out_kernel(where, data, y_ref, z_from_ref, z_to_ref, out, plane):
    early = first_half()
    for pair in range(4):
        for side in range(2):
            a = data[pl.ds(8 * side + pair, 64, stride=16), :]
            b = data[pl.ds(8 * side + 4 + pair, 64, stride=16), :]
            span = pl.ds(HALF * side, HALF)
            plane[pl.ds(64 * pair, 64), span] = jnp.where(early, a, pltpu.roll(b, ROWS, 1))
            plane[pl.ds(256 + 64 * pair, 64), span] = jnp.where(early, pltpu.roll(a, ROWS, 1), b)
    waves = left(z_from_ref, right(plane[...], y_ref))
    waves = waves * (kappa_plane(where[0] % HALF) * (SLOPE_LINK / (NZ * NY)))
    planes = left(z_to_ref, right(waves, y_ref))
    for field in range(2):
        for r in range(2):
            for side in range(2):
                start = 512 * field + 256 * r
                out[pl.ds(4 * r + 2 * field + side, 256, stride=8), :] = planes[
                    start : start + 256, HALF * side : HALF * (side + 1)
                ]


def middle_kernel(
    where, data, f0, f1, f2, f3, xi_ref, xib_ref, xf_ref, xfb_ref, ya_ref, yb_ref, slopes, out, fields
):
    for back, block in enumerate((f0, f1, f2, f3)):
        start = pl.multiple_of(((where[0] + PEERS_Y - back) % PEERS_Y) * ROWS, ROWS)
        fields[:, :, pl.ds(start, ROWS), :] = block[...].astype(f32)
    for r in range(2):
        q, g = [
            jnp.concatenate(
                [data[pl.ds(4 * r + 2 * field + side, 256, stride=8), :] for side in range(2)], axis=1
            )
            for field in range(2)
        ]
        both = to_lines(q, xib_ref) * X_SCALE
        along = (both[:, :NX], left(ya_ref, both[:, NX:]), to_lines(g, xi_ref) * X_SCALE)
        moved = []
        for d, slope in enumerate(along):
            slopes[d, r] = slope
            moved.append(fields[d, r] - fields[3, r] * (slope * (1.0 / SLOPE_LINK)))
        scale = X_SCALE * MIDDLE_LINK
        summed = to_components(xfb_ref, moved[0]) + to_components(xf_ref, left(yb_ref, moved[1]))
        for field, components in enumerate((summed * scale, to_components(xf_ref, moved[2]) * scale)):
            for side in range(2):
                out[pl.ds(4 * r + 2 * field + side, 256, stride=8), :] = components[
                    :, HALF * side : HALF * (side + 1)
                ]


def filter_back_kernel(where, data, y_ref, z_from_ref, z_to_ref, out):
    arrived = []
    for field in range(2):
        whole = jnp.concatenate(
            [
                jnp.concatenate(
                    [data[pl.ds(4 * r + 2 * field + side, 256, stride=8), :] for side in range(2)],
                    axis=1,
                )
                for r in range(2)
            ],
            axis=0,
        )
        arrived.append(pieces(whole, 0))
    waves = contract(z_from_ref[...], jnp.concatenate(arrived, axis=0), 1, 0)
    scale = DIVERGENCE_LINK / MIDDLE_LINK / (NZ * NY)
    waves = right(waves, y_ref) * (kappa_plane(where[0] % HALF) * scale)
    plane = left(z_to_ref, right(waves, y_ref))
    early = first_half()
    for pair in range(4):
        for side in range(2):
            span = slice(HALF * side, HALF * (side + 1))
            even = plane[64 * pair : 64 * (pair + 1), span]
            odd = plane[256 + 64 * pair : 256 + 64 * (pair + 1), span]
            out[pl.ds(8 * side + pair, 64, stride=16), :] = jnp.where(
                early, even, pltpu.roll(odd, ROWS, 1)
            )
            out[pl.ds(8 * side + 4 + pair, 64, stride=16), :] = jnp.where(
                early, pltpu.roll(even, ROWS, 1), odd
            )


def new_pressure_kernel(data, x_ref, pressure, bulk, own, passed, out):
    components = jnp.concatenate([data[pl.ds(i, 256, stride=4), :] for i in range(4)], axis=1)
    lines = to_lines(components, x_ref) * (X_SCALE / DIVERGENCE_LINK)
    out[...] = pressure[...] - bulk[...] * lines.reshape(SLAB, ROWS, NX) + own[...]
    out[:, :TILE, :] += passed[...].astype(f32)


def source_kernel(offset, column, starts, t0, t1, t2, own, passed, l0, l1, l2):
    blank = jnp.zeros((SLAB, 256, NX), bf16)
    l0[:SLAB] = blank
    l2[SLAB:] = blank

    def place(slot, carry):
        rows = pl.ds(pl.multiple_of(slot * TILE, TILE), TILE)
        lane = lax.broadcasted_iota(jnp.int32, (TILE, NX), 1)
        line = lax.broadcasted_iota(jnp.int32, (TILE, NX), 0)
        for reach, (tiles, placed) in enumerate(((t0, l0), (t1, l1), (t2, l2))):
            hot = ((lane - line - column[reach, slot]) & (NX - 1)) == 0
            hot = jnp.where(hot, 1.0, 0.0).astype(bf16)
            first = SLAB - offset[reach, slot] if reach == 1 else 0
            to = 0 if reach == 1 else offset[reach, slot]
            block = tiles[slot, pl.ds(first, SLAB)].reshape(SLAB * TILE, TILE)
            across = jnp.dot(block, hot, preferred_element_type=f32).astype(bf16)
            placed[pl.ds(to, SLAB), rows, :] = across.reshape(SLAB, TILE, NX)
        return carry

    lax.fori_loop(0, SLOTS_HERE, place, 0)
    line = lax.broadcasted_iota(jnp.int32, (ROWS + TILE, 256), 0)
    hots = [
        jnp.where(line == starts[0:1, 256 * reach : 256 * (reach + 1)], 1.0, 0.0).astype(bf16)
        for reach in range(3)
    ]
    for z in range(SLAB):
        window = jnp.dot(hots[0], l0[z], preferred_element_type=f32)
        window += jnp.dot(hots[1], l1[z], preferred_element_type=f32)
        window += jnp.dot(hots[2], l2[SLAB + z], preferred_element_type=f32)
        own[z] = window[:ROWS]
        passed[z] = window[ROWS:].astype(bf16)


VMEM = pl.BlockSpec(memory_space=pltpu.VMEM)
SMEM = pl.BlockSpec(memory_space=pltpu.SMEM)


def call(kernel, scalars, arrays, shapes, scratch=(), name=None, limit=24, flops=4e8):
    return pl.pallas_call(
        kernel,
        out_shape=[jax.ShapeDtypeStruct(shape, kind) for shape, kind in shapes],
        in_specs=[SMEM] * len(scalars) + [VMEM] * len(arrays),
        out_specs=[VMEM] * len(shapes),
        scratch_shapes=[pltpu.VMEM(shape, kind) for shape, kind in scratch],
        compiler_params=pltpu.CompilerParams(vmem_limit_bytes=limit << 20),
        cost_estimate=pl.CostEstimate(flops=int(flops), bytes_accessed=1 << 20, transcendentals=0),
        name=name,
    )(*scalars, *arrays)


def from_behind(x, axis, by):
    peers = lax.axis_size(axis)
    return lax.ppermute(x, axis, [(i, (i + by) % peers) for i in range(peers)])


def to_planes(fields, row_block):
    axis = fields.ndim - 3

    def planes_of(device):
        return lax.dynamic_slice_in_dim(fields, 2 * device, 2, axis).astype(f16)

    blocks = [planes_of(row_block)]
    for ahead in range(1, PEERS_Y):
        blocks.append(from_behind(planes_of((row_block + ahead) % PEERS_Y), "gy", ahead))
    return [block.astype(f32) for block in blocks]


def to_rows(blocks, row_block, axis):
    arrived = [blocks[0]] + [
        from_behind(blocks[ahead].astype(f16), "gy", ahead).astype(f32)
        for ahead in range(1, PEERS_Y)
    ]
    ordered = []
    for device in range(PEERS_Y):
        back = (row_block - device) % PEERS_Y
        ordered.append(lax.select_n(back, *arrived))
    return jnp.concatenate(ordered, axis)


def exchange(columns, rows):
    blocks = columns.astype(f16).reshape(256, rows, HALF)
    moved = lax.all_to_all(blocks, ("gz", "gy"), 0, 0, tiled=True)
    return moved.reshape(256 * rows, HALF).astype(f32)


def source_of(tiles, tile_corner, live_count, slab_index, row_block):
    corners, lives = [], []
    for reach in range(3):
        sender = (slab_index - reach) % PEERS_Z * PEERS_Y + row_block
        corners.append(lax.dynamic_slice_in_dim(tile_corner, sender * SLOTS_HERE, SLOTS_HERE, 0))
        lives.append(live_count[sender])
    corners = jnp.stack(corners)
    live = jnp.arange(SLOTS_HERE, dtype=jnp.int32)[None, :] < jnp.stack(lives)[:, None]
    offset = corners[:, :, 0] % SLAB
    first_row = jnp.where(live, corners[:, :, 1] - row_block * ROWS, -2 * TILE)
    starts = first_row[:, :, None] + jnp.arange(TILE, dtype=jnp.int32)[None, None, :]
    packed = tiles.reshape(SLOTS_HERE, 2 * SLAB, 8, HALF)
    before = from_behind(packed, "gz", 1).reshape(SLOTS_HERE, 2 * SLAB, TILE, TILE)
    second = from_behind(packed[:, SLAB:], "gz", 2).reshape(SLOTS_HERE, SLAB, TILE, TILE)
    own, passed = call(
        source_kernel,
        [offset, corners[:, :, 2]],
        [starts.reshape(1, 3 * 256), tiles, before, second],
        [((SLAB, ROWS, NX), f32), ((SLAB, TILE, NX), bf16)],
        [((2 * SLAB, 256, NX), bf16), ((SLAB, 256, NX), bf16), ((2 * SLAB, 256, NX), bf16)],
        name="source",
    )
    return own, from_behind(passed, "gy", 1)


def local(pressure, velocity, bulk, buoyancy, tiles, tile_corner, live_count):
    slab_index = lax.axis_index("gz")
    row_block = lax.axis_index("gy")
    here = row_block.reshape(1).astype(jnp.int32)
    device = (slab_index * PEERS_Y + row_block).reshape(1).astype(jnp.int32)
    table = {key: jnp.asarray(value) for key, value in TABLES.items()}

    (components,) = call(
        forward_lines_kernel,
        [],
        [pressure, table["x_forward"]],
        [((1024, HALF), f32)],
        name="forward_lines",
    )
    velocity, buoyancy, tiles, tile_corner, components = lax.optimization_barrier(
        (velocity, buoyancy, tiles, tile_corner, components)
    )
    field_blocks = to_planes(jnp.concatenate([velocity, buoyancy[None]]), row_block)
    (filtered,) = call(
        filter_out_kernel,
        [device],
        [exchange(components, 4), table["y_waves"], table["z_from_slabs"], table["z_to_pairs"]],
        [((2048, HALF), f32)],
        [((NZ, NY), f32)],
        name="filter_out",
    )
    slopes, middle = call(
        middle_kernel,
        [here],
        [
            exchange(filtered, 8),
            *field_blocks,
            table["x_inverse"],
            table["x_inverse_both"],
            table["x_forward"],
            table["x_forward_behind"],
            table["y_ahead"],
            table["y_behind"],
        ],
        [((3, 2, NY, NX), f32), ((2048, HALF), f32)],
        [((4, 2, NY, NX), f32)],
        name="middle",
        limit=32,
    )
    slope_blocks = [
        lax.dynamic_slice_in_dim(slopes, ROWS * ((row_block + ahead) % PEERS_Y), ROWS, 2)
        for ahead in range(PEERS_Y)
    ]
    slopes_here = to_rows(slope_blocks, row_block, 1)
    new_velocity = velocity - buoyancy[None] * (slopes_here * (1.0 / SLOPE_LINK))
    (filtered_back,) = call(
        filter_back_kernel,
        [device],
        [exchange(middle, 8), table["y_waves"], table["z_from_pairs"], table["z_to_slabs"]],
        [((1024, HALF), f32)],
        name="filter_back",
    )
    own, passed = source_of(tiles, tile_corner, live_count, slab_index, row_block)
    divergence = exchange(filtered_back, 4)
    divergence, new_velocity = lax.optimization_barrier((divergence, new_velocity))
    (new_pressure,) = call(
        new_pressure_kernel,
        [],
        [divergence, table["x_inverse"], pressure, bulk, own, passed],
        [((SLAB, ROWS, NX), f32)],
        name="new_pressure",
    )
    return (new_pressure, new_velocity)


def solution(mesh):
    in_specs = (
        P("gz", "gy", None),
        P(None, "gz", "gy", None),
        P("gz", "gy", None),
        P("gz", "gy", None),
        P(("gz", "gy"), None, None, None),
        P(),
        P(),
    )
    out_specs = (P("gz", "gy", None), P(None, "gz", "gy", None))
    return jax.shard_map(local, mesh=mesh, in_specs=in_specs, out_specs=out_specs, check_vma=False)
```

time: 154 us -> 148 us (0.961)
  matrix products: 9 us -> 0 us
  other arithmetic: 26.5 us -> 18.8 us
  Pallas kernels: 9.96 us -> 16.4 us
  starting transfers between devices: 55.8 us -> 60.1 us
  waiting for transfers between devices: 31.6 us -> 33.7 us
  local copies, waits for them, and re-layouts: 19.2 us -> 17.5 us
    all_to_all x4, starting transfers between devices: 33.3 us -> 46.2 us  [exchange(): moved = lax.all_to_all(blocks, ('gz', 'gy'), 0, 0, tiled=True)]
    dot_general x9 -> x0, matrix products: 9 us -> none  [the longest x3 3.79 us: place_tiles(): jnp.einsum('sabc,sxc->sabx', blocks, column_hot, preferred_element_type=j...]
    ppermute x15 -> x9, starting transfers between devices: 22.4 us -> 13.9 us  [from_behind(): return lax.ppermute(x, axis, [(i, (i + by) % peers) for i in range(peers)])]
    pallas_call x5 -> x6, Pallas kernels: 9.96 us -> 16.4 us  [call(): pl.pallas_call(kernel, out_shape=[jax.ShapeDtypeStruct(shape, kind) for s...]
    unnamed x58 -> x52, local copies, waits for them, and re-layouts: 5.12 us -> 10.3 us
    convert_element_type x7 -> x3, other arithmetic: 6.16 us -> 1.07 us  [to_planes(): return [block.astype(f32) for block in blocks]]
    add x7 -> x1, other arithmetic: 4.13 us -> 0.07 us  [source_of(): first_row[:, :, None] + jnp.arange(TILE, dtype=jnp.int32)[None, None, :]]
    reshape x0 -> x3, local copies, waits for them, and re-layouts: none -> 4.05 us  [the longest x1 1.67 us: source_of(): from_behind(packed, 'gz', 1).reshape(SLOTS_HERE, 2 * SLAB, TILE, TILE)]
  transfers between devices with their start and end apart: 19 -> 13, of which waited for: 5 -> 4; matrix products, arithmetic and copies ran while one was open for 27% -> 16% of each run, Pallas kernels for 7% -> 7%
where the time goes in v2:
time: 148 us
  starting transfers between devices  60.1 us (41%)
  waiting for transfers between devices  33.7 us (23%)
  other arithmetic  18.8 us (13%)
  local copies, waits for them, and re-layouts  17.5 us (12%)
  Pallas kernels  16.4 us (11%)
    all_to_all x4, starting transfers between devices, exchange(): moved = lax.all_to_all(blocks, ('gz', 'gy'), 0, 0, tiled=True)  46.2 us
    all_to_all x4, waiting for transfers between devices, exchange(): moved = lax.all_to_all(blocks, ('gz', 'gy'), 0, 0, tiled=True)  28.6 us
    pallas_call x6, Pallas kernels, call(): pl.pallas_call(kernel, out_shape=[jax.ShapeDtypeStruct(shape, kind) for s...  16.4 us
    ppermute x9, starting transfers between devices, from_behind(): return lax.ppermute(x, axis, [(i, (i + by) % peers) for i in range(peers)])  13.9 us
    unnamed x52, local copies, waits for them, and re-layouts  10.3 us
    ppermute x9, waiting for transfers between devices, from_behind(): return lax.ppermute(x, axis, [(i, (i + by) % peers) for i in range(peers)])  5.13 us
    convert_element_type x4, other arithmetic, exchange(): return moved.reshape(256 * rows, HALF).astype(f32)  4.31 us
  transfers between devices with their start and end apart: 13, of which 4 were waited for; matrix products, arithmetic and copies ran while one was open for 16% of the time, Pallas kernels for 7%

profile of v2, /device:TPU:1, one launch (start us, length us, event | category | flops | bytes accessed | tf_op | source)
XLA Modules:
  0.0 147.7 jit_solution(921522473903863626)
XLA Ops:
  4.0 16.7 %all-to-all-start = ((f16[256,4,128]{2,1,0:T(4,128)(2,1)}), f16[256,4,128]{2,1,0:T(4,128)(2,1)}, u32[]{:S(2)}, u32[]{:S(2)}) async-start(f16[256,4,128]{2,1,0:T(4,128)(2,1)} %bitcast.43), calls=%async_computation | async-start | bytes 524288 | tf_op jit(solution)/shard_map/all_to_all | solution.py:335
  20.7 14.3 %all-to-all-done = f16[256,4,128]{2,1,0:T(4,128)(2,1)} async-done(((f16[256,4,128]{2,1,0:T(4,128)(2,1)}), f16[256,4,128]{2,1,0:T(4,128)(2,1)}, u32[]{:S(2)}, u32[]{:S(2)}) %all-to-all-start) | async-done | bytes 262176 | tf_op jit(solution)/shard_map/all_to_all | solution.py:335
  37.4 3.0 %filter_out.1 = f32[2048,128]{1,0:T(8,128)S(1)} custom-call(s32[1]{0:T(128)} %bitcast.where, f32[1024,128]{1,0:T(8,128)S(1)} %convert.4.data, bf16[768,256]{1,0:T(8,128)(2,1)S(1)} %copy-done.8, bf16[512,1536]{1,0:T(8,128)(2,1)S(1)} %copy-done.7, bf16[1024,1536]{1,0:T(8,128)(2,1)S(1)} %copy-done.2), custom_call_target="tpu_custom_call" | custom-call | flops 400000000 | bytes 1048576 | tf_op jit(solution)/shard_map/filter_out/pallas_call | solution.py:292
  41.3 7.0 %all-to-all-start.1 = ((f16[256,8,128]{2,1,0:T(8,128)(2,1)}), f16[256,8,128]{2,1,0:T(8,128)(2,1)}, u32[]{:S(2)}, u32[]{:S(2)}) async-start(f16[256,8,128]{2,1,0:T(8,128)(2,1)} %convert_bitcast_fusion.1), calls=%async_computation.1 | async-start | bytes 1048576 | tf_op jit(solution)/shard_map/all_to_all | solution.py:335
  48.4 2.2 %fusion.2 = (f16[4,2,64,256]{3,2,1,0:T(8,128)(2,1)}, f32[4,2,64,256]{3,2,1,0:T(8,128)S(1)}, f16[4,2,64,256]{3,2,1,0:T(8,128)(2,1)S(1)}, f16[4,2,64,256]{3,2,1,0:T(8,128)(2,1)}) fusion(s32[]{:T(128)S(6)} %select_n.218, f32[3,8,64,256]{3,2,1,0:T(8,128)S(1)} %copy-done.21, f32[1,8,64,256]{3,2,1,0:T(8,128)} %bitcast.42, s32[]{:T(128)S(6)} %select_n.212, ...), kind=kLoop, calls=%fused_computation.19 | loop fusion | flops 1179648 | bytes 3407888 | tf_op jit(solution)/shard_map/convert_element_type | solution.py:313
  50.5 1.4 collective-permute-start
  52.0 2.5 %collective-permute-start.1 = (f16[4,2,64,256]{3,2,1,0:T(8,128)(2,1)}, f16[4,2,64,256]{3,2,1,0:T(8,128)(2,1)S(1)}, u32[]{:S(2)}, u32[]{:S(2)}) collective-permute-start(f16[4,2,64,256]{3,2,1,0:T(8,128)(2,1)} %get-tuple-element.31), channel_id=1, source_target_pairs={{0,2},{1,3},{2,0},{3,1},{4,6},{5,7},{6,4},{7,5},{8,10},{9,11},{10,... | collective-permute-start | bytes 786440 | tf_op jit(solution)/shard_map/ppermute | solution.py:306
  56.9 2.3 %collective-permute-start.6 = (bf16[8,16,8,128]{3,2,1,0:T(8,128)(2,1)}, bf16[8,16,8,128]{3,2,1,0:T(8,128)(2,1)}, u32[]{:S(2)}, u32[]{:S(2)}) collective-permute-start(bf16[8,16,8,128]{3,2,1,0:T(8,128)(2,1)} %reshape.104), channel_id=1, source_target_pairs={{0,4},{4,8},{8,12},{12,16},{16,20},{20,24},{24,28},{28,32},{32,36}... | collective-permute-start | bytes 786440 | tf_op jit(solution)/shard_map/ppermute | solution.py:306
  59.2 1.6 %slice.16 = bf16[8,8,8,128]{3,2,1,0:T(8,128)(2,1)} slice(bf16[8,16,8,128]{3,2,1,0:T(8,128)(2,1)} %reshape.104), slice={[0:8], [8:16], [0:8], [0:128]} | slice | bytes 262144 | tf_op jit(solution)/shard_map/slice | solution.py:352
  62.6 2.1 %pad_add_fusion.4 = s32[3]{0:T(128)S(1)} fusion(s32[1]{0:T(128)} %get-tuple-element.41, s32[1]{0:T(128)} %get-tuple-element.42, s32[1]{0:T(128)} %get-tuple-element.40), kind=kLoop, calls=%fused_computation.58 | loop fusion | flops 6 | bytes 24 | tf_op jit(solution)/shard_map/stack | solution.py:346
  65.6 5.1 %collective-permute-done.1 = f16[4,2,64,256]{3,2,1,0:T(8,128)(2,1)S(1)} collective-permute-done((f16[4,2,64,256]{3,2,1,0:T(8,128)(2,1)}, f16[4,2,64,256]{3,2,1,0:T(8,128)(2,1)S(1)}, u32[]{:S(2)}, u32[]{:S(2)}) %collective-permute-start.1) | collective-permute-done | bytes 262176 | tf_op jit(solution)/shard_map/ppermute | solution.py:306
  75.3 3.2 %middle.1 = (f32[3,2,256,256]{3,2,1,0:T(8,128)S(1)}, f32[2048,128]{1,0:T(8,128)S(1)}) custom-call(s32[1]{0:T(128)} %bitcast.1.where, f32[2048,128]{1,0:T(8,128)S(1)} %bitcast_convert_fusion.1.data, f32[4,2,64,256]{3,2,1,0:T(8,128)S(1)} %get-tuple-element.29.f0, f32[4,2,64,256]{3,2,1,0:T(8,128)S(1)} %convert_element_type.84.f1, ...), custom_call_target="tpu_custom_call" | custom-call | flops 400000000 | bytes 1048576 | tf_op jit(solution)/shard_map/middle/pallas_call | solution.py:292
  80.5 12.1 %all-to-all-start.2 = ((f16[256,8,128]{2,1,0:T(8,128)(2,1)}), f16[256,8,128]{2,1,0:T(8,128)(2,1)}, u32[]{:S(2)}, u32[]{:S(2)}) async-start(f16[256,8,128]{2,1,0:T(8,128)(2,1)} %convert_bitcast_fusion), calls=%async_computation.2 | async-start | bytes 1048576 | tf_op jit(solution)/shard_map/all_to_all | solution.py:335
  94.9 1.7 %reshape.105.t1 = bf16[8,16,32,32]{3,2,1,0:T(8,128)(2,1)S(1)} reshape(bf16[8,16,8,128]{3,2,1,0:T(8,128)(2,1)} %collective-permute-done.6) | data formatting | bytes 524288 | tf_op jit(solution)/shard_map/reshape | solution.py:351
  96.6 3.9 %source.1 = (f32[8,64,256]{2,1,0:T(8,128)S(1)}, bf16[8,32,256]{2,1,0:T(8,128)(2,1)}) custom-call(s32[3,8]{1,0:T(4,128)S(1)} %add_select_fusion.offset, s32[3,8]{1,0:T(4,128)S(1)} %bitcast.41, s32[1,768]{1,0:T(1,128)S(1)} %add.173.starts, bf16[8,16,32,32]{3,2,1,0:T(8,128)(2,1)S(1)} %copy-done, bf16[8,16,32,32]{3,2,1,0:T(8,128)(2,1)S(1)} %reshape.105.t1, ...), custom_call_target="tpu_custom_call" | custom-call | flops 400000000 | bytes 1048576 | tf_op jit(solution)/shard_map/source/pallas_call | solution.py:292
  104.8 1.5 %collective-permute-start.5 = (f16[3,2,64,256]{3,2,1,0:T(8,128)(2,1)}, f16[3,2,64,256]{3,2,1,0:T(8,128)(2,1)}, u32[]{:S(2)}, u32[]{:S(2)}) collective-permute-start(f16[3,2,64,256]{3,2,1,0:T(8,128)(2,1)} %get-tuple-element.33), channel_id=1, source_target_pairs={{0,3},{1,0},{2,1},{3,2},{4,7},{5,4},{6,5},{7,6},{8,11},{9,8},{10,9... | collective-permute-start | bytes 589832 | tf_op jit(solution)/shard_map/ppermute | solution.py:306
  107.5 4.2 %all-to-all-done.2 = f16[256,8,128]{2,1,0:T(8,128)(2,1)} async-done(((f16[256,8,128]{2,1,0:T(8,128)(2,1)}), f16[256,8,128]{2,1,0:T(8,128)(2,1)}, u32[]{:S(2)}, u32[]{:S(2)}) %all-to-all-start.2) | async-done | bytes 524320 | tf_op jit(solution)/shard_map/all_to_all | solution.py:335
  112.8 1.4 copy-done.6
  115.2 3.8 %filter_back.1 = f32[1024,128]{1,0:T(8,128)S(1)} custom-call(s32[1]{0:T(128)} %bitcast.where, f32[2048,128]{1,0:T(8,128)S(1)} %bitcast_convert_fusion.data, bf16[768,256]{1,0:T(8,128)(2,1)S(1)} %copy-done.9, bf16[512,3072]{1,0:T(8,128)(2,1)S(1)} %copy-done.1, bf16[512,1536]{1,0:T(8,128)(2,1)S(1)} %copy-done.6), custom_call_target="tpu_custom_call" | custom-call | flops 400000000 | bytes 1048576 | tf_op jit(solution)/shard_map/filter_back/pallas_call | solution.py:292
  119.8 10.4 %all-to-all-start.3 = ((f16[256,4,128]{2,1,0:T(4,128)(2,1)}), f16[256,4,128]{2,1,0:T(4,128)(2,1)}, u32[]{:S(2)}, u32[]{:S(2)}) async-start(f16[256,4,128]{2,1,0:T(4,128)(2,1)} %bitcast.9), calls=%async_computation.3 | async-start | bytes 524288 | tf_op jit(solution)/shard_map/all_to_all | solution.py:335
  130.2 1.5 %fusion.9 = (f32[3,2,64,256]{3,2,1,0:T(8,128)S(1)}, f32[3,2,64,256]{3,2,1,0:T(8,128)S(1)}, f32[3,2,64,256]{3,2,1,0:T(8,128)S(1)}, f32[3,2,64,256]{3,2,1,0:T(8,128)S(1)}) fusion(f16[3,2,64,256]{3,2,1,0:T(8,128)(2,1)} %collective-permute-done.3, f16[3,2,64,256]{3,2,1,0:T(8,128)(2,1)} %collective-permute-done.5, ...), kind=kLoop, calls=%fused_computation.30 | loop fusion | flops 1474560 | bytes 2555920 | tf_op jit(solution)/shard_map/select_n | solution.py:329
  131.8 2.6 %fusion = f32[3,8,64,256]{3,2,1,0:T(8,128)} fusion(f32[3,8,64,256]{3,2,1,0:T(8,128)S(1)} %copy-done.22, f32[3,2,64,256]{3,2,1,0:T(8,128)S(1)} %get-tuple-element.27, f32[3,2,64,256]{3,2,1,0:T(8,128)S(1)} %get-tuple-element.26, f32[3,2,64,256]{3,2,1,0:T(8,128)S(1)} %get-tuple-element.25, f32[3,2,64,256]{3,2,1,0:T(8,128)S(1)} %get-tuple-element.24, ...), kind=kLoop, calls=%fused_computation.9 | loop fusion | flops 1966080 | bytes 5242880 | tf_op jit(solution)/shard_map/sub | solution.py:413
  134.4 10.1 %all-to-all-done.3 = f16[256,4,128]{2,1,0:T(4,128)(2,1)} async-done(((f16[256,4,128]{2,1,0:T(4,128)(2,1)}), f16[256,4,128]{2,1,0:T(4,128)(2,1)}, u32[]{:S(2)}, u32[]{:S(2)}) %all-to-all-start.3) | async-done | bytes 262176 | tf_op jit(solution)/shard_map/all_to_all | solution.py:335
  145.5 2.1 %new_pressure.1 = f32[8,64,256]{2,1,0:T(8,128)} custom-call(f32[1024,128]{1,0:T(8,128)S(1)} %convert.7.data, bf16[768,256]{1,0:T(8,128)(2,1)S(1)} %copy-done.3, f32[8,64,256]{2,1,0:T(8,128)S(1)} %copy-done.12, f32[8,64,256]{2,1,0:T(8,128)S(1)} %copy-done.13, f32[8,64,256]{2,1,0:T(8,128)S(1)} %copy-done.15, bf16[8,32,256]{2,1,0:T(8,128)(2,1)} %collective-permute-done.8.passed), custom_call_target="tpu_custom_call" | custom-call | flops 400000000 | bytes 1048576 | tf_op jit(solution)/shard_map/new_pressure/pallas_call | solution.py:292
  (88 shorter events, 29.8 us)
Async XLA Ops:
  0.6 35.3 %copy-start.2 = (bf16[1024,1536]{1,0:T(8,128)(2,1)S(1)}, bf16[1024,1536]{1,0:T(8,128)(2,1)}, u32[]{:S(2)}) copy-start(bf16[1024,1536]{1,0:T(8,128)(2,1)} %constant.138.clone.z_to_ref) | copy-start | bytes 9437188
  0.6 35.3 %copy-start.8 = (bf16[768,256]{1,0:T(8,128)(2,1)S(1)}, bf16[768,256]{1,0:T(8,128)(2,1)}, u32[]{:S(2)}) copy-start(bf16[768,256]{1,0:T(8,128)(2,1)} %constant.136.clone.y_ref) | copy-start | bytes 1179652
  4.0 31.0 %all-to-all-start = ((f16[256,4,128]{2,1,0:T(4,128)(2,1)}), f16[256,4,128]{2,1,0:T(4,128)(2,1)}, u32[]{:S(2)}, u32[]{:S(2)}) async-start(f16[256,4,128]{2,1,0:T(4,128)(2,1)} %bitcast.43), calls=%async_computation | async-start | bytes 524288 | tf_op jit(solution)/shard_map/all_to_all | solution.py:335
  40.4 7.9 %copy-start.21 = (f32[3,8,64,256]{3,2,1,0:T(8,128)S(1)}, f32[3,8,64,256]{3,2,1,0:T(8,128)}, u32[]{:S(2)}) copy-start(f32[3,8,64,256]{3,2,1,0:T(8,128)} %param.19) | copy-start | bytes 4718596
  41.3 30.5 %all-to-all-start.1 = ((f16[256,8,128]{2,1,0:T(8,128)(2,1)}), f16[256,8,128]{2,1,0:T(8,128)(2,1)}, u32[]{:S(2)}, u32[]{:S(2)}) async-start(f16[256,8,128]{2,1,0:T(8,128)(2,1)} %convert_bitcast_fusion.1), calls=%async_computation.1 | async-start | bytes 1048576 | tf_op jit(solution)/shard_map/all_to_all | solution.py:335
  50.5 11.4 %copy-start.24 = (s32[256]{0:T(256)S(1)}, s32[256]{0:T(256)}, u32[]{:S(2)}) copy-start(s32[256]{0:T(256)} %param.24) | copy-start | bytes 3076
  50.5 15.0 %collective-permute-start = (f16[4,2,64,256]{3,2,1,0:T(8,128)(2,1)S(1)}, f16[4,2,64,256]{3,2,1,0:T(8,128)(2,1)S(1)}, u32[]{:S(2)}, u32[]{:S(2)}) collective-permute-start(f16[4,2,64,256]{3,2,1,0:T(8,128)(2,1)S(1)} %get-tuple-element.30), channel_id=1, source_target_pairs={{0,1},{1,2},{2,3},{3,0},{4,5},{5,6},{6,7},{7,4},{8,9},{9,10},{10,1... | collective-permute-start | bytes 786440 | tf_op jit(solution)/shard_map/ppermute | solution.py:306
  52.0 18.8 %collective-permute-start.1 = (f16[4,2,64,256]{3,2,1,0:T(8,128)(2,1)}, f16[4,2,64,256]{3,2,1,0:T(8,128)(2,1)S(1)}, u32[]{:S(2)}, u32[]{:S(2)}) collective-permute-start(f16[4,2,64,256]{3,2,1,0:T(8,128)(2,1)} %get-tuple-element.31), channel_id=1, source_target_pairs={{0,2},{1,3},{2,0},{3,1},{4,6},{5,7},{6,4},{7,5},{8,10},{9,11},{10,... | collective-permute-start | bytes 786440 | tf_op jit(solution)/shard_map/ppermute | solution.py:306
  54.5 16.3 %collective-permute-start.2 = (f16[4,2,64,256]{3,2,1,0:T(8,128)(2,1)}, f16[4,2,64,256]{3,2,1,0:T(8,128)(2,1)}, u32[]{:S(2)}, u32[]{:S(2)}) collective-permute-start(f16[4,2,64,256]{3,2,1,0:T(8,128)(2,1)} %get-tuple-element.28), channel_id=1, source_target_pairs={{0,3},{1,0},{2,1},{3,2},{4,7},{5,4},{6,5},{7,6},{8,11},{9,8},{10,9... | collective-permute-start | bytes 786440 | tf_op jit(solution)/shard_map/ppermute | solution.py:306
  56.9 38.0 %collective-permute-start.6 = (bf16[8,16,8,128]{3,2,1,0:T(8,128)(2,1)}, bf16[8,16,8,128]{3,2,1,0:T(8,128)(2,1)}, u32[]{:S(2)}, u32[]{:S(2)}) collective-permute-start(bf16[8,16,8,128]{3,2,1,0:T(8,128)(2,1)} %reshape.104), channel_id=1, source_target_pairs={{0,4},{4,8},{8,12},{12,16},{16,20},{20,24},{24,28},{28,32},{32,36}... | collective-permute-start | bytes 786440 | tf_op jit(solution)/shard_map/ppermute | solution.py:306
  60.7 33.0 %collective-permute-start.7 = (bf16[8,8,8,128]{3,2,1,0:T(8,128)(2,1)}, bf16[8,8,8,128]{3,2,1,0:T(8,128)(2,1)}, u32[]{:S(2)}, u32[]{:S(2)}) collective-permute-start(bf16[8,8,8,128]{3,2,1,0:T(8,128)(2,1)} %slice.16), channel_id=1, source_target_pairs={{0,8},{4,12},{8,16},{12,20},{16,24},{20,28},{24,32},{28,36},{32,40... | collective-permute-start | bytes 393224 | tf_op jit(solution)/shard_map/ppermute | solution.py:306
  65.6 7.5 %copy-start.3 = (bf16[768,256]{1,0:T(8,128)(2,1)S(1)}, bf16[768,256]{1,0:T(8,128)(2,1)}, u32[]{:S(2)}) copy-start(bf16[768,256]{1,0:T(8,128)(2,1)} %constant.132.clone.xi_ref.x_ref) | copy-start | bytes 1179652
  79.6 13.2 %copy-start.23 = (f32[8,64,256]{2,1,0:T(8,128)S(1)}, f32[8,64,256]{2,1,0:T(8,128)}, u32[]{:S(2)}) copy-start(f32[8,64,256]{2,1,0:T(8,128)} %param.21) | copy-start | bytes 1572868
  80.5 31.2 %all-to-all-start.2 = ((f16[256,8,128]{2,1,0:T(8,128)(2,1)}), f16[256,8,128]{2,1,0:T(8,128)(2,1)}, u32[]{:S(2)}, u32[]{:S(2)}) async-start(f16[256,8,128]{2,1,0:T(8,128)(2,1)} %convert_bitcast_fusion), calls=%async_computation.2 | async-start | bytes 1048576 | tf_op jit(solution)/shard_map/all_to_all | solution.py:335
  101.4 44.1 %collective-permute-start.8 = (bf16[8,32,256]{2,1,0:T(8,128)(2,1)}, bf16[8,32,256]{2,1,0:T(8,128)(2,1)}, u32[]{:S(2)}, u32[]{:S(2)}) collective-permute-start(bf16[8,32,256]{2,1,0:T(8,128)(2,1)} %get-tuple-element.22), channel_id=1, source_target_pairs={{0,1},{1,2},{2,3},{3,0},{4,5},{5,6},{6,7},{7,4},{8,9},{9,10},{10,1... | collective-permute-start | bytes 393224 | tf_op jit(solution)/shard_map/ppermute | solution.py:306
  102.8 10.1 %copy-start.1 = (bf16[512,3072]{1,0:T(8,128)(2,1)S(1)}, bf16[512,3072]{1,0:T(8,128)(2,1)}, u32[]{:S(2)}) copy-start(bf16[512,3072]{1,0:T(8,128)(2,1)} %constant.139.clone.z_from_ref) | copy-start | bytes 9437188
  103.6 26.6 %collective-permute-start.3 = (f16[3,2,64,256]{3,2,1,0:T(8,128)(2,1)}, f16[3,2,64,256]{3,2,1,0:T(8,128)(2,1)}, u32[]{:S(2)}, u32[]{:S(2)}) collective-permute-start(f16[3,2,64,256]{3,2,1,0:T(8,128)(2,1)} %get-tuple-element.34), channel_id=1, source_target_pairs={{0,1},{1,2},{2,3},{3,0},{4,5},{5,6},{6,7},{7,4},{8,9},{9,10},{10,1... | collective-permute-start | bytes 589832 | tf_op jit(solution)/shard_map/ppermute | solution.py:306
  104.8 25.5 %collective-permute-start.5 = (f16[3,2,64,256]{3,2,1,0:T(8,128)(2,1)}, f16[3,2,64,256]{3,2,1,0:T(8,128)(2,1)}, u32[]{:S(2)}, u32[]{:S(2)}) collective-permute-start(f16[3,2,64,256]{3,2,1,0:T(8,128)(2,1)} %get-tuple-element.33), channel_id=1, source_target_pairs={{0,3},{1,0},{2,1},{3,2},{4,7},{5,4},{6,5},{7,6},{8,11},{9,8},{10,9... | collective-permute-start | bytes 589832 | tf_op jit(solution)/shard_map/ppermute | solution.py:306
  106.3 23.9 %collective-permute-start.4 = (f16[3,2,64,256]{3,2,1,0:T(8,128)(2,1)}, f16[3,2,64,256]{3,2,1,0:T(8,128)(2,1)}, u32[]{:S(2)}, u32[]{:S(2)}) collective-permute-start(f16[3,2,64,256]{3,2,1,0:T(8,128)(2,1)} %get-tuple-element.32), channel_id=1, source_target_pairs={{0,2},{1,3},{2,0},{3,1},{4,6},{5,7},{6,4},{7,5},{8,10},{9,11},{10,... | collective-permute-start | bytes 589832 | tf_op jit(solution)/shard_map/ppermute | solution.py:306
  119.8 12.0 %copy-start.22 = (f32[3,8,64,256]{3,2,1,0:T(8,128)S(1)}, f32[3,8,64,256]{3,2,1,0:T(8,128)}, u32[]{:S(2)}) copy-start(f32[3,8,64,256]{3,2,1,0:T(8,128)} %param.19) | copy-start | bytes 4718596
  119.8 24.7 %all-to-all-start.3 = ((f16[256,4,128]{2,1,0:T(4,128)(2,1)}), f16[256,4,128]{2,1,0:T(4,128)(2,1)}, u32[]{:S(2)}, u32[]{:S(2)}) async-start(f16[256,4,128]{2,1,0:T(4,128)(2,1)} %bitcast.9), calls=%async_computation.3 | async-start | bytes 524288 | tf_op jit(solution)/shard_map/all_to_all | solution.py:335
  131.8 13.7 %copy-start.12 = (f32[8,64,256]{2,1,0:T(8,128)S(1)}, f32[8,64,256]{2,1,0:T(8,128)}, u32[]{:S(2)}) copy-start(f32[8,64,256]{2,1,0:T(8,128)} %pressure.3) | copy-start | bytes 1572868
  131.8 13.7 %copy-start.13 = (f32[8,64,256]{2,1,0:T(8,128)S(1)}, f32[8,64,256]{2,1,0:T(8,128)}, u32[]{:S(2)}) copy-start(f32[8,64,256]{2,1,0:T(8,128)} %bulk.1) | copy-start | bytes 1572868
  131.8 13.7 %copy-start.15 = (f32[8,64,256]{2,1,0:T(8,128)S(1)}, f32[8,64,256]{2,1,0:T(8,128)}, u32[]{:S(2)}) copy-start(f32[8,64,256]{2,1,0:T(8,128)} %copy-done.14) | copy-start | bytes 1572868
  (14 other events, 27.6 us)

commit v3 on v2

v3 whole, which is shorter than its diff:
```python
import math

import jax
import jax.numpy as jnp
import ml_dtypes
import numpy as np
from jax import lax
from jax.experimental import pallas as pl
from jax.experimental.pallas import tpu as pltpu
from jax.sharding import PartitionSpec as P

NX = 256
NY = 256
NZ = 512
HALF = 128
ROWS = 64
SLAB = 8
SLOTS_HERE = 8
TILE = 32
PEERS_Y = 4
PEERS_Z = 64
kappa_courant = 0.3
f32 = jnp.float32
bf16 = jnp.bfloat16
f16 = jnp.float16

X_SCALE = 1.0 / 16.0
SLOPE_LINK = 0.25
MIDDLE_LINK = 1.0 / 16.0
DIVERGENCE_LINK = 1.0 / 32.0


def split_table(table):
    high = table.astype(ml_dtypes.bfloat16)
    low = (table - high.astype(np.float64)).astype(ml_dtypes.bfloat16)
    return high, low


def left_table(table):
    high, low = split_table(table)
    return np.concatenate([high, high, low], axis=1)


def right_table(table):
    return np.ascontiguousarray(left_table(table.T).T)


def signed_waves(length):
    index = np.arange(length)
    return 2.0 * np.pi / length * np.where(index < length // 2, index, index - length)


def derivative_matrix(length, orientation):
    wave = signed_waves(length)
    kernel = np.fft.ifft(1j * wave * np.exp(orientation * 0.5j * wave)).real
    index = np.arange(length)
    return kernel[(index[:, None] - index[None, :]) % length]


def make_tables():
    index = np.arange(256)
    angle = 2.0 * np.pi / 256 * (np.outer(index, index) % 256)
    wave_x = 2.0 * np.pi / NX * np.arange(HALF)

    def forward_x(factor):
        spectrum = np.exp(-1j * angle[:HALF]) * factor[:, None]
        return left_table(np.concatenate([spectrum.real, spectrum.imag], axis=0))

    def inverse_x(factor):
        weight = np.where(np.arange(HALF) == 0, 1.0, 2.0) * factor
        wave = np.exp(1j * angle[:HALF]) * weight[:, None]
        return np.concatenate([wave.real, -wave.imag], axis=0)

    ahead = 1j * wave_x * np.exp(0.5j * wave_x)
    behind = 1j * wave_x * np.exp(-0.5j * wave_x)
    plain = np.ones(HALF)
    forward_z = np.concatenate([np.cos(angle[:HALF]), -np.sin(angle[:HALF])], axis=0)
    forward_z[HALF] = np.cos(angle[HALF])
    inverse_z = 2.0 * forward_z.T
    inverse_z[:, 0] = forward_z[0]
    inverse_z[:, HALF] = forward_z[HALF]
    slab_order = (4 * np.arange(64)[None, :] + np.arange(4)[:, None]).reshape(-1)
    low = np.arange(HALF)
    high = low - 256
    coefficients = np.zeros((HALF, HALF), np.float32)
    coefficients[:, 0] = np.cos(2.0 * np.pi / NZ * low)
    coefficients[:, 1] = np.sin(2.0 * np.pi / NZ * low)

    def derivative(number, orientation):
        wave = 2.0 * np.pi / NZ * number
        return -orientation * wave * np.sin(0.5 * wave), wave * np.cos(0.5 * wave)

    for first, orientation in ((2, 1.0), (9, -1.0)):
        middle_real, middle_imag = derivative(128, orientation)
        for at, number in ((first, low), (first + 3, high)):
            real, imag = derivative(number, orientation)
            coefficients[:, at] = real
            coefficients[:, at + 1] = np.where((low == 0), 0.0, imag)
            coefficients[:, at + 2] = np.where((low == 0), middle_real, real)
        coefficients[:, first + 6] = np.where((low == 0), middle_imag, 0.0)
    return {
        "x_forward": forward_x(plain),
        "x_forward_behind": forward_x(behind),
        "x_inverse": right_table(inverse_x(plain)),
        "x_inverse_both": right_table(
            np.concatenate([inverse_x(ahead), inverse_x(plain)], axis=1)
        ),
        "y_ahead": left_table(derivative_matrix(NY, 1.0)),
        "y_behind": left_table(derivative_matrix(NY, -1.0)),
        "y_waves": right_table(np.cos(angle) + np.sin(angle)),
        "z_from_slabs": left_table(forward_z[:, slab_order]),
        "z_to_pairs": left_table(inverse_z),
        "z_from_pairs": left_table(forward_z),
        "z_to_slabs": left_table(inverse_z[slab_order]),
        "z_coefficients": coefficients,
    }


TABLES = make_tables()


def pieces(x, axis):
    high = x.astype(bf16)
    low = (x - high.astype(f32)).astype(bf16)
    return jnp.concatenate([high, low, high], axis=axis)


def contract(a, b, a_dim, b_dim):
    return lax.dot_general(a, b, (((a_dim,), (b_dim,)), ((), ())), preferred_element_type=f32)


def left(table_ref, x):
    return contract(table_ref[...], pieces(x, 0), 1, 0)


def right(x, table_ref):
    return contract(pieces(x, 1), table_ref[...], 1, 0)


def to_components(table_ref, lines):
    return contract(table_ref[...], pieces(lines, 1), 1, 1)


def to_lines(components, table_ref):
    return right(components.T, table_ref)


class Fetch:
    def __init__(self, sources, targets, semaphores):
        self.targets = targets
        self.copies = [
            pltpu.make_async_copy(source, target, semaphores.at[i])
            for i, (source, target) in enumerate(zip(sources, targets))
        ]
        for copy in self.copies:
            copy.start()

    def __getitem__(self, i):
        if self.copies[i] is not None:
            self.copies[i].wait()
            self.copies[i] = None
        return self.targets[i]


def kappa_rows(kx, part):
    kz = lax.broadcasted_iota(jnp.int32, (HALF, NY), 0)
    ky = lax.broadcasted_iota(jnp.int32, (HALF, NY), 1)
    number = kz - 256 * (part // 2)
    if part % 2:
        number = jnp.where(kz == 0, 128, number)
    wave_z = number.astype(f32) * (2.0 * math.pi / NZ)
    wave_y = jnp.where(ky < NY // 2, ky, ky - NY).astype(f32) * (2.0 * math.pi / NY)
    wave_x = jnp.full((HALF, NY), kx, jnp.int32).astype(f32) * (2.0 * math.pi / NX)
    square = (kappa_courant / 2.0) ** 2 * (wave_x * wave_x + wave_z * wave_z + wave_y * wave_y)
    total = jnp.full((HALF, NY), 1.0 / math.factorial(15), f32)
    for order in range(6, -1, -1):
        total = 1.0 / math.factorial(2 * order + 1) - square * total
    return total


def forward_z(table_ref, coefficient, fields):
    sides = [side for field in fields for side in (field[:256], field[256:])]
    sums = left(table_ref, jnp.concatenate(sides, axis=1))
    cosine, sine = coefficient(0), coefficient(1)
    spectra = []
    for i in range(0, len(sides), 2):
        even = sums[:, NY * i : NY * (i + 1)]
        odd = sums[:, NY * (i + 1) : NY * (i + 2)]
        real = cosine * odd[:HALF] + sine * odd[HALF:]
        imag = cosine * odd[HALF:] - sine * odd[:HALF]
        spectra.append(
            [even[:HALF] + real, even[HALF:] + imag, even[:HALF] - real, even[HALF:] - imag]
        )
    return spectra


def inverse_z(table_ref, coefficient, spectra):
    cosine, sine = coefficient(0), coefficient(1)
    sides = []
    for a, b, c, d in spectra:
        real, imag = a - c, b - d
        sides.append(jnp.concatenate([a + c, b + d], axis=0))
        sides.append(jnp.concatenate([cosine * real - sine * imag, cosine * imag + sine * real], axis=0))
    return left(table_ref, jnp.concatenate(sides, axis=1))


def derivative_z(coefficient, first, spectrum):
    a, b, c, d = spectrum
    mixed = coefficient(first + 6)
    return [
        coefficient(first) * a - coefficient(first + 1) * b,
        coefficient(first + 2) * b + coefficient(first + 1) * a - mixed * d,
        coefficient(first + 3) * c - coefficient(first + 4) * d,
        coefficient(first + 5) * d + coefficient(first + 4) * c + mixed * b,
    ]


def blocks_of(x):
    return [x[HALF * i : HALF * (i + 1)] for i in range(4)]


def first_half():
    return lax.broadcasted_iota(jnp.int32, (64, HALF), 1) < ROWS


def forward_lines_kernel(pressure, x_table, out, *scratch):
    *targets, semaphores = scratch
    sources = [x_table] + [pressure.at[pl.ds(2 * i, 2)] for i in range(4)]
    fetch = Fetch(sources, targets, semaphores)
    x_ref = fetch[0]
    for i in range(4):
        lines = fetch[i + 1][...].reshape(HALF, NX)
        out[pl.ds(i, 256, stride=4), :] = to_components(x_ref, lines) * X_SCALE


def filter_out_kernel(where, data, y, z_from, z_to, z_numbers, out, plane, *scratch):
    *targets, semaphores = scratch
    fetch = Fetch((y, z_from, z_numbers, z_to), targets, semaphores)
    early = first_half()
    for pair in range(4):
        for side in range(2):
            a = data[pl.ds(8 * side + pair, 64, stride=16), :]
            b = data[pl.ds(8 * side + 4 + pair, 64, stride=16), :]
            span = pl.ds(HALF * side, HALF)
            plane[pl.ds(64 * pair, 64), span] = jnp.where(early, a, pltpu.roll(b, ROWS, 1))
            plane[pl.ds(256 + 64 * pair, 64), span] = jnp.where(early, pltpu.roll(a, ROWS, 1), b)
    mixed = right(plane[...], fetch[0])
    z_from_ref, numbers = fetch[1], fetch[2]

    def coefficient(i):
        return numbers[:, i : i + 1]

    (spectrum,) = forward_z(z_from_ref, coefficient, [mixed])
    scale = SLOPE_LINK / (NZ * NY)
    waves = [x * (kappa_rows(where[0] % HALF, part) * scale) for part, x in enumerate(spectrum)]
    waves = blocks_of(right(jnp.concatenate(waves, axis=0), fetch[0]))
    planes = inverse_z(fetch[3], coefficient, [waves, derivative_z(coefficient, 2, waves)])
    for field in range(2):
        for r in range(2):
            for side in range(2):
                start = NY * (2 * field + r) + HALF * side
                out[pl.ds(4 * r + 2 * field + side, 256, stride=8), :] = planes[
                    :, start : start + HALF
                ]


def middle_kernel(
    where, data, f0, f1, f2, f3, xib, xi, ya, yb, xfb, xf, slopes, out, fields, held, *scratch
):
    *targets, semaphores = scratch
    fetch = Fetch((xib, xi, ya, yb, xfb, xf), targets, semaphores)
    for back, block in enumerate((f0, f1, f2, f3)):
        start = pl.multiple_of(((where[0] + PEERS_Y - back) % PEERS_Y) * ROWS, ROWS)
        fields[:, :, pl.ds(start, ROWS), :] = block[...]
    returned = []
    for r in range(2):
        q, g = [
            jnp.concatenate(
                [data[pl.ds(4 * r + 2 * field + side, 256, stride=8), :] for side in range(2)], axis=1
            )
            for field in range(2)
        ]
        both = to_lines(q, fetch[0]) * X_SCALE
        along = (both[:, :NX], left(fetch[2], both[:, NX:]), to_lines(g, fetch[1]) * X_SCALE)
        moved = []
        for d, slope in enumerate(along):
            held[r, d] = slope
            moved.append(fields[d, r] - fields[3, r] * (slope * (1.0 / SLOPE_LINK)))
        returned.append(pltpu.make_async_copy(held.at[r], slopes.at[r], semaphores.at[6 + r]))
        returned[r].start()
        scale = X_SCALE * MIDDLE_LINK
        along_y = left(fetch[3], moved[1])
        summed = to_components(fetch[4], moved[0]) + to_components(fetch[5], along_y)
        for field, components in enumerate(
            (summed * scale, to_components(fetch[5], moved[2]) * scale)
        ):
            for side in range(2):
                out[pl.ds(4 * r + 2 * field + side, 256, stride=8), :] = components[
                    :, HALF * side : HALF * (side + 1)
                ]
    for copy in returned:
        copy.wait()


def filter_back_kernel(where, data, y, z_from, z_to, z_numbers, out, *scratch):
    *targets, semaphores = scratch
    fetch = Fetch((z_from, z_numbers, y, z_to), targets, semaphores)
    arrived = [
        jnp.concatenate(
            [
                jnp.concatenate(
                    [data[pl.ds(4 * r + 2 * field + side, 256, stride=8), :] for side in range(2)],
                    axis=1,
                )
                for r in range(2)
            ],
            axis=0,
        )
        for field in range(2)
    ]
    z_from_ref, numbers = fetch[0], fetch[1]

    def coefficient(i):
        return numbers[:, i : i + 1]

    across, along = forward_z(z_from_ref, coefficient, arrived)
    waves = [x + z for x, z in zip(across, derivative_z(coefficient, 9, along))]
    waves = blocks_of(right(jnp.concatenate(waves, axis=0), fetch[2]))
    scale = DIVERGENCE_LINK / MIDDLE_LINK / (NZ * NY)
    waves = [x * (kappa_rows(where[0] % HALF, part) * scale) for part, x in enumerate(waves)]
    waves = blocks_of(right(jnp.concatenate(waves, axis=0), fetch[2]))
    plane = inverse_z(fetch[3], coefficient, [waves])
    early = first_half()
    for pair in range(4):
        for side in range(2):
            rows = slice(64 * pair, 64 * (pair + 1))
            even = plane[rows, HALF * side : HALF * (side + 1)]
            odd = plane[rows, NY + HALF * side : NY + HALF * (side + 1)]
            out[pl.ds(8 * side + pair, 64, stride=16), :] = jnp.where(
                early, even, pltpu.roll(odd, ROWS, 1)
            )
            out[pl.ds(8 * side + 4 + pair, 64, stride=16), :] = jnp.where(
                early, pltpu.roll(even, ROWS, 1), odd
            )


def new_pressure_kernel(data, x_table, pressure, bulk, own, passed, out, held, x_ref, semaphores):
    fetch = Fetch((x_table,), (x_ref,), semaphores)
    sent = []
    for i in range(4):
        planes = pl.ds(2 * i, 2)
        components = data[pl.ds(i, 256, stride=4), :]
        lines = to_lines(components, fetch[0]) * (X_SCALE / DIVERGENCE_LINK)
        held[planes] = pressure[planes] - bulk[planes] * lines.reshape(2, ROWS, NX) + own[planes]
        held[planes, :TILE, :] += passed[planes].astype(f32)
        sent.append(pltpu.make_async_copy(held.at[planes], out.at[planes], semaphores.at[1 + i]))
        sent[i].start()
    for copy in sent:
        copy.wait()


def source_kernel(where, lives, c0, c1, c2, t0, t1, t2, own, passed, l0, l1, l2):
    blank = jnp.zeros((SLAB, 256, NX), bf16)
    l0[:SLAB] = blank
    l2[SLAB:] = blank
    corners = (c0, c1, c2)

    def place(slot, carry):
        rows = pl.ds(pl.multiple_of(slot * TILE, TILE), TILE)
        lane = lax.broadcasted_iota(jnp.int32, (TILE, NX), 1)
        line = lax.broadcasted_iota(jnp.int32, (TILE, NX), 0)
        for reach, (tiles, placed) in enumerate(((t0, l0), (t1, l1), (t2, l2))):
            offset = corners[reach][slot, 0] & (SLAB - 1)
            hot = ((lane - line - corners[reach][slot, 2]) & (NX - 1)) == 0
            hot = jnp.where(hot, 1.0, 0.0).astype(bf16)
            first = SLAB - offset if reach == 1 else 0
            to = 0 if reach == 1 else offset
            block = tiles[slot, pl.ds(first, SLAB)].reshape(SLAB * TILE, TILE)
            across = jnp.dot(block, hot, preferred_element_type=f32).astype(bf16)
            placed[pl.ds(to, SLAB), rows, :] = across.reshape(SLAB, TILE, NX)
        return carry

    lax.fori_loop(0, SLOTS_HERE, place, 0)
    line = lax.broadcasted_iota(jnp.int32, (ROWS + TILE, 256), 0)
    lane = lax.broadcasted_iota(jnp.int32, (ROWS + TILE, 256), 1)
    hots = []
    for reach in range(3):
        sender = ((where[0] + PEERS_Z - reach) % PEERS_Z) * PEERS_Y + where[1]
        start = jnp.full((ROWS + TILE, 256), -2 * TILE, jnp.int32)
        for slot in range(SLOTS_HERE):
            row = corners[reach][slot, 1] - where[1] * ROWS - slot * TILE
            row = jnp.where(slot < lives[sender], row, -NX)
            start = jnp.where(lane // TILE == slot, lane + row, start)
        hots.append(jnp.where(line == start, 1.0, 0.0).astype(bf16))
    for z in range(SLAB):
        window = jnp.dot(hots[0], l0[z], preferred_element_type=f32)
        window += jnp.dot(hots[1], l1[z], preferred_element_type=f32)
        window += jnp.dot(hots[2], l2[SLAB + z], preferred_element_type=f32)
        own[z] = window[:ROWS]
        passed[z] = window[ROWS:].astype(bf16)


VMEM = pl.BlockSpec(memory_space=pltpu.VMEM)
SMEM = pl.BlockSpec(memory_space=pltpu.SMEM)
ANY = pl.BlockSpec(memory_space=pl.ANY)


def call(
    kernel, name, scalars, arrays, far, shapes, scratch=(), far_out=0, targets=None, extra=0, limit=16
):
    if targets is None:
        targets = [(x.shape, x.dtype) for x in far]
    scratch = [pltpu.VMEM(shape, kind) for shape, kind in (*scratch, *targets)]
    if far:
        scratch.append(pltpu.SemaphoreType.DMA((len(targets) + extra,)))
    return pl.pallas_call(
        kernel,
        out_shape=[jax.ShapeDtypeStruct(shape, kind) for shape, kind in shapes],
        in_specs=[SMEM] * len(scalars) + [VMEM] * len(arrays) + [ANY] * len(far),
        out_specs=[ANY] * far_out + [VMEM] * (len(shapes) - far_out),
        scratch_shapes=scratch,
        compiler_params=pltpu.CompilerParams(vmem_limit_bytes=limit << 20),
        cost_estimate=pl.CostEstimate(flops=int(4e8), bytes_accessed=1 << 20, transcendentals=0),
        name=name,
    )(*scalars, *arrays, *far)


def from_behind(x, axis, by):
    peers = lax.axis_size(axis)
    return lax.ppermute(x, axis, [(i, (i + by) % peers) for i in range(peers)])


def to_planes(fields, row_block):
    axis = fields.ndim - 3

    def planes_of(device):
        return lax.dynamic_slice_in_dim(fields, 2 * device, 2, axis)

    blocks = [planes_of(row_block)]
    for ahead in range(1, PEERS_Y):
        sent = planes_of((row_block + ahead) % PEERS_Y).astype(f16)
        blocks.append(from_behind(sent, "gy", ahead))
    return blocks


def to_rows(blocks, row_block, axis):
    arrived = [blocks[0]] + [
        from_behind(blocks[ahead].astype(f16), "gy", ahead).astype(f32)
        for ahead in range(1, PEERS_Y)
    ]
    ordered = []
    for device in range(PEERS_Y):
        back = (row_block - device) % PEERS_Y
        ordered.append(lax.select_n(back, *arrived))
    return jnp.concatenate(ordered, axis)


def exchange(columns, rows):
    blocks = columns.astype(f16).reshape(256, rows, HALF)
    return lax.all_to_all(blocks, ("gz", "gy"), 0, 0, tiled=True)


def arrived(moved):
    return moved.reshape(-1, HALF).astype(f32)


def local(pressure, velocity, bulk, buoyancy, tiles, tile_corner, live_count):
    slab_index = lax.axis_index("gz")
    row_block = lax.axis_index("gy")
    here = row_block.reshape(1).astype(jnp.int32)
    device = (slab_index * PEERS_Y + row_block).reshape(1).astype(jnp.int32)
    place = jnp.stack([slab_index, row_block]).astype(jnp.int32)
    table = {key: jnp.asarray(value) for key, value in TABLES.items()}

    (components,) = call(
        forward_lines_kernel,
        "forward_lines",
        [],
        [],
        [pressure, table["x_forward"]],
        [((1024, HALF), f32)],
        targets=[((256, 768), bf16)] + [((2, ROWS, NX), f32)] * 4,
    )
    velocity, buoyancy, tiles, tile_corner, components = lax.optimization_barrier(
        (velocity, buoyancy, tiles, tile_corner, components)
    )
    field_blocks = to_planes(jnp.concatenate([velocity, buoyancy[None]]), row_block)
    packed = tiles.reshape(SLOTS_HERE, 2 * SLAB, 8, HALF)
    tiles_before = from_behind(packed, "gz", 1)
    tiles_second = from_behind(packed[:, SLAB:], "gz", 2)
    moved, *field_blocks = lax.optimization_barrier((exchange(components, 4), *field_blocks))
    (filtered,) = call(
        filter_out_kernel,
        "filter_out",
        [device],
        [arrived(moved)],
        [table["y_waves"], table["z_from_slabs"], table["z_to_pairs"], table["z_coefficients"]],
        [((2048, HALF), f32)],
        [((NZ, NY), f32)],
        targets=[((768, 256), bf16), ((256, 768), bf16), ((HALF, HALF), f32), ((256, 768), bf16)],
    )
    moved, tiles_before, tiles_second = lax.optimization_barrier(
        (exchange(filtered, 8), tiles_before, tiles_second)
    )
    slopes, middle = call(
        middle_kernel,
        "middle",
        [here],
        [arrived(moved), *[block.astype(f32) for block in field_blocks]],
        [
            table[key]
            for key in (
                "x_inverse_both", "x_inverse", "y_ahead", "y_behind", "x_forward_behind", "x_forward"
            )
        ],
        [((2, 3, NY, NX), f32), ((2048, HALF), f32)],
        [((4, 2, NY, NX), f32), ((2, 3, NY, NX), f32)],
        far_out=1,
        extra=2,
        limit=24,
    )
    slope_blocks = [
        lax.dynamic_slice_in_dim(slopes, ROWS * ((row_block + ahead) % PEERS_Y), ROWS, 2)
        for ahead in range(PEERS_Y)
    ]
    slopes_here = jnp.swapaxes(to_rows(slope_blocks, row_block, 0), 0, 1)
    new_velocity = velocity - buoyancy[None] * (slopes_here * (1.0 / SLOPE_LINK))

    corners = [
        lax.dynamic_slice_in_dim(
            tile_corner,
            ((slab_index - reach) % PEERS_Z * PEERS_Y + row_block) * SLOTS_HERE,
            SLOTS_HERE,
            0,
        )
        for reach in range(3)
    ]
    own, passed = call(
        source_kernel,
        "source",
        [place, live_count, *corners],
        [
            tiles,
            tiles_before.reshape(SLOTS_HERE, 2 * SLAB, TILE, TILE),
            tiles_second.reshape(SLOTS_HERE, SLAB, TILE, TILE),
        ],
        [],
        [((SLAB, ROWS, NX), f32), ((SLAB, TILE, NX), bf16)],
        [((2 * SLAB, 256, NX), bf16), ((SLAB, 256, NX), bf16), ((2 * SLAB, 256, NX), bf16)],
    )
    moved, own, passed = lax.optimization_barrier((exchange(middle, 8), own, passed))
    passed = from_behind(passed, "gy", 1)
    (filtered_back,) = call(
        filter_back_kernel,
        "filter_back",
        [device],
        [arrived(moved)],
        [table["y_waves"], table["z_from_pairs"], table["z_to_slabs"], table["z_coefficients"]],
        [((1024, HALF), f32)],
        targets=[((256, 768), bf16), ((HALF, HALF), f32), ((768, 256), bf16), ((256, 768), bf16)],
    )
    moved, new_velocity, passed = lax.optimization_barrier(
        (exchange(filtered_back, 4), new_velocity, passed)
    )
    (new_pressure,) = pl.pallas_call(
        new_pressure_kernel,
        out_shape=[jax.ShapeDtypeStruct((SLAB, ROWS, NX), f32)],
        in_specs=[VMEM, ANY, VMEM, VMEM, VMEM, VMEM],
        out_specs=[ANY],
        scratch_shapes=[
            pltpu.VMEM((SLAB, ROWS, NX), f32),
            pltpu.VMEM((768, 256), bf16),
            pltpu.SemaphoreType.DMA((5,)),
        ],
        compiler_params=pltpu.CompilerParams(vmem_limit_bytes=16 << 20),
        name="new_pressure",
    )(arrived(moved), table["x_inverse"], pressure, bulk, own, passed)
    return (new_pressure, new_velocity)


def solution(mesh):
    in_specs = (
        P("gz", "gy", None),
        P(None, "gz", "gy", None),
        P("gz", "gy", None),
        P("gz", "gy", None),
        P(("gz", "gy"), None, None, None),
        P(),
        P(),
    )
    out_specs = (P("gz", "gy", None), P(None, "gz", "gy", None))
    return jax.shard_map(local, mesh=mesh, in_specs=in_specs, out_specs=out_specs, check_vma=False)
```

time: 148 us -> 156 us (1.054)
  waiting for transfers between devices: 33.7 us -> 40.4 us
  other arithmetic: 18.8 us -> 14.9 us
  Pallas kernels: 16.4 us -> 19.1 us
  starting transfers between devices: 60.1 us -> 62.5 us
    ppermute x9, waiting for transfers between devices: 5.13 us -> 32.5 us  [from_behind(): return lax.ppermute(x, axis, [(i, (i + by) % peers) for i in range(peers)])]
    all_to_all x4, waiting for transfers between devices: 28.6 us -> 7.88 us  [exchange(): return lax.all_to_all(blocks, ('gz', 'gy'), 0, 0, tiled=True)]
    another operation x1, other arithmetic: 2.12 us -> 0.07 us  [local(): place = jnp.stack([slab_index, row_block]).astype(jnp.int32)]
    all_to_all x4, starting transfers between devices: 46.2 us -> 48 us  [exchange(): return lax.all_to_all(blocks, ('gz', 'gy'), 0, 0, tiled=True)]
    convert_element_type x8, other arithmetic: 7.55 us -> 5.91 us  [the longest x4 3.36 us: arrived(): return moved.reshape(-1, HALF).astype(f32)]
    pallas_call x6 -> x5, Pallas kernels: 16.4 us -> 17.7 us  [call(): pl.pallas_call(kernel, out_shape=[jax.ShapeDtypeStruct(shape, kind) for s...]
    unnamed x52 -> x65, local copies, waits for them, and re-layouts: 10.3 us -> 9.65 us
  transfers between devices with their start and end apart: 13 -> 13, of which waited for: 4 -> 6; matrix products, arithmetic and copies ran while one was open for 16% -> 11% of each run, Pallas kernels for 7% -> 4%
where the time goes in v3:
time: 156 us; the launch traced here: 155 us
  starting transfers between devices  62.5 us (40%)
  waiting for transfers between devices  40.4 us (26%)
  Pallas kernels  19.1 us (12%)
  local copies, waits for them, and re-layouts  16.7 us (11%)
  other arithmetic  14.9 us (10%)
    all_to_all x4, starting transfers between devices, exchange(): return lax.all_to_all(blocks, ('gz', 'gy'), 0, 0, tiled=True)  48 us
    ppermute x9, waiting for transfers between devices, from_behind(): return lax.ppermute(x, axis, [(i, (i + by) % peers) for i in range(peers)])  32.5 us
    pallas_call x5, Pallas kernels, call(): pl.pallas_call(kernel, out_shape=[jax.ShapeDtypeStruct(shape, kind) for s...  17.7 us
    ppermute x9, starting transfers between devices, from_behind(): return lax.ppermute(x, axis, [(i, (i + by) % peers) for i in range(peers)])  14.5 us
    unnamed x65, local copies, waits for them, and re-layouts  9.65 us
    all_to_all x4, waiting for transfers between devices, exchange(): return lax.all_to_all(blocks, ('gz', 'gy'), 0, 0, tiled=True)  7.88 us
    convert_element_type x4, other arithmetic, arrived(): return moved.reshape(-1, HALF).astype(f32)  3.36 us
  transfers between devices with their start and end apart: 13, of which 6 were waited for; matrix products, arithmetic and copies ran while one was open for 11% of the time, Pallas kernels for 4%

profile of v3, /device:TPU:1, one launch (start us, length us, event | category | flops | bytes accessed | tf_op | source)
XLA Modules:
  0.0 154.9 jit_solution(14615609784148225538)
XLA Ops:
  2.7 2.3 %forward_lines.1 = f32[1024,128]{1,0:T(8,128)S(1)} custom-call(f32[8,64,256]{2,1,0:T(8,128)S(1)} %copy-done.7, bf16[256,768]{1,0:T(8,128)(2,1)S(1)} %copy-done.14), custom_call_target="tpu_custom_call" | custom-call | flops 400000000 | bytes 1048576 | tf_op jit(solution)/shard_map/forward_lines/pallas_call | solution.py:416
  5.7 15.7 %all-to-all-start = ((f16[256,4,128]{2,1,0:T(4,128)(2,1)}), f16[256,4,128]{2,1,0:T(4,128)(2,1)S(1)}, u32[]{:S(2)}, u32[]{:S(2)}) async-start(f16[256,4,128]{2,1,0:T(4,128)(2,1)} %bitcast.2), calls=%async_computation | async-start | bytes 524288 | tf_op jit(solution)/shard_map/all_to_all | solution.py:460
  21.5 2.4 %fusion.3 = (f16[4,2,64,256]{3,2,1,0:T(8,128)(2,1)S(1)}, f32[4,2,64,256]{3,2,1,0:T(8,128)S(1)}, f16[4,2,64,256]{3,2,1,0:T(8,128)(2,1)}, f16[4,2,64,256]{3,2,1,0:T(8,128)(2,1)}) fusion(s32[]{:T(128)S(6)} %select_n.198, f32[3,8,64,256]{3,2,1,0:T(8,128)} %param.20, f32[1,8,64,256]{3,2,1,0:T(8,128)S(1)} %bitcast.30, s32[]{:T(128)S(6)} %select_n.192, ...), kind=kLoop, calls=%fused_computation.20 | loop fusion | flops 917504 | bytes 3407888 | tf_op jit(solution)/shard_map/convert_element_type | solution.py:441
  25.3 2.4 %collective-permute-start.1 = (f16[4,2,64,256]{3,2,1,0:T(8,128)(2,1)}, f16[4,2,64,256]{3,2,1,0:T(8,128)(2,1)S(1)}, u32[]{:S(2)}, u32[]{:S(2)}) collective-permute-start(f16[4,2,64,256]{3,2,1,0:T(8,128)(2,1)} %get-tuple-element.57), channel_id=1, source_target_pairs={{0,2},{1,3},{2,0},{3,1},{4,6},{5,7},{6,4},{7,5},{8,10},{9,11},{10,... | collective-permute-start | bytes 786440 | tf_op jit(solution)/shard_map/ppermute | solution.py:430
  28.9 4.5 %collective-permute-done = f16[4,2,64,256]{3,2,1,0:T(8,128)(2,1)S(1)} collective-permute-done((f16[4,2,64,256]{3,2,1,0:T(8,128)(2,1)}, f16[4,2,64,256]{3,2,1,0:T(8,128)(2,1)S(1)}, u32[]{:S(2)}, u32[]{:S(2)}) %collective-permute-start) | collective-permute-done | bytes 262176 | tf_op jit(solution)/shard_map/ppermute | solution.py:430
  33.4 8.5 %collective-permute-done.1 = f16[4,2,64,256]{3,2,1,0:T(8,128)(2,1)S(1)} collective-permute-done((f16[4,2,64,256]{3,2,1,0:T(8,128)(2,1)}, f16[4,2,64,256]{3,2,1,0:T(8,128)(2,1)S(1)}, u32[]{:S(2)}, u32[]{:S(2)}) %collective-permute-start.1) | collective-permute-done | bytes 262176 | tf_op jit(solution)/shard_map/ppermute | solution.py:430
  42.0 3.5 %filter_out.1 = f32[2048,128]{1,0:T(8,128)S(1)} custom-call(s32[1]{0:T(128)} %bitcast.where, f32[1024,128]{1,0:T(8,128)S(1)} %convert.4.data, bf16[768,256]{1,0:T(8,128)(2,1)S(1)} %copy-done.2, bf16[256,768]{1,0:T(8,128)(2,1)S(1)} %copy-done.19, bf16[256,768]{1,0:T(8,128)(2,1)S(1)} %copy-done.20, f32[128,128]{1,0:T(8,128)S(1)} %copy-done.21), custom_call_target="tpu_custom_call" | custom-call | flops 400000000 | bytes 1048576 | tf_op jit(solution)/shard_map/filter_out/pallas_call | solution.py:416
  46.4 12.8 %all-to-all-start.1 = ((f16[256,8,128]{2,1,0:T(8,128)(2,1)}), f16[256,8,128]{2,1,0:T(8,128)(2,1)}, u32[]{:S(2)}, u32[]{:S(2)}) async-start(f16[256,8,128]{2,1,0:T(8,128)(2,1)} %convert_bitcast_fusion.1), calls=%async_computation.1 | async-start | bytes 1048576 | tf_op jit(solution)/shard_map/all_to_all | solution.py:460
  60.4 1.6 %collective-permute-start.3 = (bf16[8,16,8,128]{3,2,1,0:T(8,128)(2,1)}, bf16[8,16,8,128]{3,2,1,0:T(8,128)(2,1)}, u32[]{:S(2)}, u32[]{:S(2)}) collective-permute-start(bf16[8,16,8,128]{3,2,1,0:T(8,128)(2,1)} %reshape.48), channel_id=1, source_target_pairs={{0,4},{4,8},{8,12},{12,16},{16,20},{20,24},{24,28},{28,32},{32,36}... | collective-permute-start | bytes 786440 | tf_op jit(solution)/shard_map/ppermute | solution.py:430
  63.0 1.4 collective-permute-start.4
  64.6 16.4 %collective-permute-done.4 = bf16[8,8,8,128]{3,2,1,0:T(8,128)(2,1)} collective-permute-done((bf16[8,8,8,128]{3,2,1,0:T(8,128)(2,1)S(1)}, bf16[8,8,8,128]{3,2,1,0:T(8,128)(2,1)}, u32[]{:S(2)}, u32[]{:S(2)}) %collective-permute-start.4) | collective-permute-done | bytes 131104 | tf_op jit(solution)/shard_map/ppermute | solution.py:430
  84.5 5.2 %middle.1 = (f32[2,3,256,256]{3,2,1,0:T(8,128)S(1)}, f32[2048,128]{1,0:T(8,128)S(1)}) custom-call(s32[1]{0:T(128)} %bitcast.1.where, f32[2048,128]{1,0:T(8,128)S(1)} %bitcast_convert_fusion.1.data, f32[4,2,64,256]{3,2,1,0:T(8,128)S(1)} %get-tuple-element.31.f0, f32[4,2,64,256]{3,2,1,0:T(8,128)S(1)} %convert_element_type.77.f1, ...), custom_call_target="tpu_custom_call" | custom-call | flops 400000000 | bytes 1048576 | tf_op jit(solution)/shard_map/middle/pallas_call | solution.py:416
  91.7 7.7 %all-to-all-start.2 = ((f16[256,8,128]{2,1,0:T(8,128)(2,1)}), f16[256,8,128]{2,1,0:T(8,128)(2,1)}, u32[]{:S(2)}, u32[]{:S(2)}) async-start(f16[256,8,128]{2,1,0:T(8,128)(2,1)} %convert_bitcast_fusion), calls=%async_computation.2 | async-start | bytes 1048576 | tf_op jit(solution)/shard_map/all_to_all | solution.py:460
  101.7 1.9 %broadcast_multiply_fusion = f32[8,64,256]{2,1,0:T(8,128)} fusion(f32[8,64,256]{2,1,0:T(8,128)} %param.22), kind=kLoop, calls=%fused_computation.37 | loop fusion | flops 131072 | bytes 1048576 | tf_op jit(solution)/shard_map/mul | solution.py:527
  105.9 2.4 %collective-permute-start.6 = (f16[2,3,64,256]{3,2,1,0:T(8,128)(2,1)}, f16[2,3,64,256]{3,2,1,0:T(8,128)(2,1)}, u32[]{:S(2)}, u32[]{:S(2)}) collective-permute-start(f16[2,3,64,256]{3,2,1,0:T(8,128)(2,1)} %get-tuple-element.58), channel_id=1, source_target_pairs={{0,2},{1,3},{2,0},{3,1},{4,6},{5,7},{6,4},{7,5},{8,10},{9,11},{10,... | collective-permute-start | bytes 589832 | tf_op jit(solution)/shard_map/ppermute | solution.py:430
  109.5 1.7 %reshape.50.t1 = bf16[8,16,32,32]{3,2,1,0:T(8,128)(2,1)S(1)} reshape(bf16[8,16,8,128]{3,2,1,0:T(8,128)(2,1)} %collective-permute-done.3) | data formatting | bytes 524288 | tf_op jit(solution)/shard_map/reshape | solution.py:544
  112.3 3.4 %source.1 = (f32[8,64,256]{2,1,0:T(8,128)S(1)}, bf16[8,32,256]{2,1,0:T(8,128)(2,1)S(1)}) custom-call(s32[2]{0:T(128)S(1)} %pad_add_fusion.where, s32[256]{0:T(256)S(1)} %copy-done.23, s32[8,3]{1,0:T(8,128)S(1)} %get-tuple-element.63.c0, s32[8,3]{1,0:T(8,128)S(1)} %get-tuple-element.62.c1, s32[8,3]{1,0:T(8,128)S(1)} %get-tuple-element.61.c2, ...), custom_call_target="tpu_custom_call" | custom-call | flops 400000000 | bytes 1048576 | tf_op jit(solution)/shard_map/source/pallas_call | solution.py:416
  119.7 3.2 %filter_back.1 = f32[1024,128]{1,0:T(8,128)S(1)} custom-call(s32[1]{0:T(128)} %bitcast.where, f32[2048,128]{1,0:T(8,128)S(1)} %bitcast_convert_fusion.data, bf16[768,256]{1,0:T(8,128)(2,1)S(1)} %copy-done.3, bf16[256,768]{1,0:T(8,128)(2,1)S(1)} %copy-done.12, bf16[256,768]{1,0:T(8,128)(2,1)S(1)} %copy-done.13, f32[128,128]{1,0:T(8,128)S(1)} %copy-done.22), custom_call_target="tpu_custom_call" | custom-call | flops 400000000 | bytes 1048576 | tf_op jit(solution)/shard_map/filter_back/pallas_call | solution.py:416
  123.6 11.8 %all-to-all-start.3 = ((f16[256,4,128]{2,1,0:T(4,128)(2,1)}), f16[256,4,128]{2,1,0:T(4,128)(2,1)}, u32[]{:S(2)}, u32[]{:S(2)}) async-start(f16[256,4,128]{2,1,0:T(4,128)(2,1)} %bitcast.10), calls=%async_computation.3 | async-start | bytes 524288 | tf_op jit(solution)/shard_map/all_to_all | solution.py:460
  135.5 1.5 fusion.9
  137.0 1.5 collective-permute-start.8
  139.9 3.2 %collective-permute-done.8.passed = bf16[8,32,256]{2,1,0:T(8,128)(2,1)S(1)} collective-permute-done((bf16[8,32,256]{2,1,0:T(8,128)(2,1)S(1)}, bf16[8,32,256]{2,1,0:T(8,128)(2,1)S(1)}, u32[]{:S(2)}, u32[]{:S(2)}) %collective-permute-start.8) | collective-permute-done | bytes 131104 | tf_op jit(solution)/shard_map/ppermute | solution.py:430
  143.1 6.6 %all-to-all-done.3 = f16[256,4,128]{2,1,0:T(4,128)(2,1)} async-done(((f16[256,4,128]{2,1,0:T(4,128)(2,1)}), f16[256,4,128]{2,1,0:T(4,128)(2,1)}, u32[]{:S(2)}, u32[]{:S(2)}) %all-to-all-start.3) | async-done | bytes 262176 | tf_op jit(solution)/shard_map/all_to_all | solution.py:460
  149.6 2.7 %copy.25 = f32[3,8,64,256]{3,2,1,0:T(8,128)} copy(f32[3,8,64,256]{3,2,0,1:T(8,128)} %fusion.1) | data formatting | bytes 3145728
  (96 shorter events, 29.1 us)
Async XLA Ops:
  2.7 18.8 %copy-start.28 = (f32[8,64,256]{2,1,0:T(8,128)S(1)}, f32[8,64,256]{2,1,0:T(8,128)}, u32[]{:S(2)}) copy-start(f32[8,64,256]{2,1,0:T(8,128)} %param.22) | copy-start | bytes 1572868
  5.7 36.1 %all-to-all-start = ((f16[256,4,128]{2,1,0:T(4,128)(2,1)}), f16[256,4,128]{2,1,0:T(4,128)(2,1)S(1)}, u32[]{:S(2)}, u32[]{:S(2)}) async-start(f16[256,4,128]{2,1,0:T(4,128)(2,1)} %bitcast.2), calls=%async_computation | async-start | bytes 524288 | tf_op jit(solution)/shard_map/all_to_all | solution.py:460
  21.5 20.5 %copy-start.2 = (bf16[768,256]{1,0:T(8,128)(2,1)S(1)}, bf16[768,256]{1,0:T(8,128)(2,1)}, u32[]{:S(2)}) copy-start(bf16[768,256]{1,0:T(8,128)(2,1)} %constant.124.clone.y) | copy-start | bytes 1179652
  21.5 20.5 %copy-start.19 = (bf16[256,768]{1,0:T(8,128)(2,1)S(1)}, bf16[256,768]{1,0:T(8,128)(2,1)}, u32[]{:S(2)}) copy-start(bf16[256,768]{1,0:T(8,128)(2,1)} %constant.125.clone.z_from) | copy-start | bytes 1179652
  21.5 20.5 %copy-start.20 = (bf16[256,768]{1,0:T(8,128)(2,1)S(1)}, bf16[256,768]{1,0:T(8,128)(2,1)}, u32[]{:S(2)}) copy-start(bf16[256,768]{1,0:T(8,128)(2,1)} %constant.126.clone.z_to) | copy-start | bytes 1179652
  21.5 20.4 %copy-start.21 = (f32[128,128]{1,0:T(8,128)S(1)}, f32[128,128]{1,0:T(8,128)}, u32[]{:S(2)}) copy-start(f32[128,128]{1,0:T(8,128)} %constant.129.clone.z_numbers) | copy-start | bytes 196612
  23.9 9.4 %collective-permute-start = (f16[4,2,64,256]{3,2,1,0:T(8,128)(2,1)}, f16[4,2,64,256]{3,2,1,0:T(8,128)(2,1)S(1)}, u32[]{:S(2)}, u32[]{:S(2)}) collective-permute-start(f16[4,2,64,256]{3,2,1,0:T(8,128)(2,1)} %get-tuple-element.56), channel_id=1, source_target_pairs={{0,1},{1,2},{2,3},{3,0},{4,5},{5,6},{6,7},{7,4},{8,9},{9,10},{10,1... | collective-permute-start | bytes 786440 | tf_op jit(solution)/shard_map/ppermute | solution.py:430
  25.3 16.5 %collective-permute-start.1 = (f16[4,2,64,256]{3,2,1,0:T(8,128)(2,1)}, f16[4,2,64,256]{3,2,1,0:T(8,128)(2,1)S(1)}, u32[]{:S(2)}, u32[]{:S(2)}) collective-permute-start(f16[4,2,64,256]{3,2,1,0:T(8,128)(2,1)} %get-tuple-element.57), channel_id=1, source_target_pairs={{0,2},{1,3},{2,0},{3,1},{4,6},{5,7},{6,4},{7,5},{8,10},{9,11},{10,... | collective-permute-start | bytes 786440 | tf_op jit(solution)/shard_map/ppermute | solution.py:430
  27.8 14.1 %collective-permute-start.2 = (f16[4,2,64,256]{3,2,1,0:T(8,128)(2,1)S(1)}, f16[4,2,64,256]{3,2,1,0:T(8,128)(2,1)S(1)}, u32[]{:S(2)}, u32[]{:S(2)}) collective-permute-start(f16[4,2,64,256]{3,2,1,0:T(8,128)(2,1)S(1)} %get-tuple-element.54), channel_id=1, source_target_pairs={{0,3},{1,0},{2,1},{3,2},{4,7},{5,4},{6,5},{7,6},{8,11},{9,8},{10,9... | collective-permute-start | bytes 786440 | tf_op jit(solution)/shard_map/ppermute | solution.py:430
  45.5 13.6 %copy-start = (bf16[8,16,32,32]{3,2,1,0:T(8,128)(2,1)S(1)}, bf16[8,16,32,32]{3,2,1,0:T(8,128)(2,1)}, u32[]{:S(2)}) copy-start(bf16[8,16,32,32]{3,2,1,0:T(8,128)(2,1)} %t0) | copy-start | bytes 786436
  46.4 34.6 %all-to-all-start.1 = ((f16[256,8,128]{2,1,0:T(8,128)(2,1)}), f16[256,8,128]{2,1,0:T(8,128)(2,1)}, u32[]{:S(2)}, u32[]{:S(2)}) async-start(f16[256,8,128]{2,1,0:T(8,128)(2,1)} %convert_bitcast_fusion.1), calls=%async_computation.1 | async-start | bytes 1048576 | tf_op jit(solution)/shard_map/all_to_all | solution.py:460
  60.4 20.6 %collective-permute-start.3 = (bf16[8,16,8,128]{3,2,1,0:T(8,128)(2,1)}, bf16[8,16,8,128]{3,2,1,0:T(8,128)(2,1)}, u32[]{:S(2)}, u32[]{:S(2)}) collective-permute-start(bf16[8,16,8,128]{3,2,1,0:T(8,128)(2,1)} %reshape.48), channel_id=1, source_target_pairs={{0,4},{4,8},{8,12},{12,16},{16,20},{20,24},{24,28},{28,32},{32,36}... | collective-permute-start | bytes 786440 | tf_op jit(solution)/shard_map/ppermute | solution.py:430
  63.0 18.0 %collective-permute-start.4 = (bf16[8,8,8,128]{3,2,1,0:T(8,128)(2,1)S(1)}, bf16[8,8,8,128]{3,2,1,0:T(8,128)(2,1)}, u32[]{:S(2)}, u32[]{:S(2)}) collective-permute-start(bf16[8,8,8,128]{3,2,1,0:T(8,128)(2,1)S(1)} %slice.4), channel_id=1, source_target_pairs={{0,8},{4,12},{8,16},{12,20},{16,24},{20,28},{24,32},{28,36},{32,40... | collective-permute-start | bytes 393224 | tf_op jit(solution)/shard_map/ppermute | solution.py:430
  64.5 17.8 %copy-start.1 = (bf16[768,256]{1,0:T(8,128)(2,1)S(1)}, bf16[768,256]{1,0:T(8,128)(2,1)}, u32[]{:S(2)}) copy-start(bf16[768,256]{1,0:T(8,128)(2,1)} %constant.120.clone.xi.x_table) | copy-start | bytes 1179652
  91.7 26.8 %all-to-all-start.2 = ((f16[256,8,128]{2,1,0:T(8,128)(2,1)}), f16[256,8,128]{2,1,0:T(8,128)(2,1)}, u32[]{:S(2)}, u32[]{:S(2)}) async-start(f16[256,8,128]{2,1,0:T(8,128)(2,1)} %convert_bitcast_fusion), calls=%async_computation.2 | async-start | bytes 1048576 | tf_op jit(solution)/shard_map/all_to_all | solution.py:460
  104.5 31.0 %collective-permute-start.5 = (f16[2,3,64,256]{3,2,1,0:T(8,128)(2,1)}, f16[2,3,64,256]{3,2,1,0:T(8,128)(2,1)}, u32[]{:S(2)}, u32[]{:S(2)}) collective-permute-start(f16[2,3,64,256]{3,2,1,0:T(8,128)(2,1)} %get-tuple-element.60), channel_id=1, source_target_pairs={{0,1},{1,2},{2,3},{3,0},{4,5},{5,6},{6,7},{7,4},{8,9},{9,10},{10,1... | collective-permute-start | bytes 589832 | tf_op jit(solution)/shard_map/ppermute | solution.py:430
  105.9 29.6 %collective-permute-start.6 = (f16[2,3,64,256]{3,2,1,0:T(8,128)(2,1)}, f16[2,3,64,256]{3,2,1,0:T(8,128)(2,1)}, u32[]{:S(2)}, u32[]{:S(2)}) collective-permute-start(f16[2,3,64,256]{3,2,1,0:T(8,128)(2,1)} %get-tuple-element.58), channel_id=1, source_target_pairs={{0,2},{1,3},{2,0},{3,1},{4,6},{5,7},{6,4},{7,5},{8,10},{9,11},{10,... | collective-permute-start | bytes 589832 | tf_op jit(solution)/shard_map/ppermute | solution.py:430
  108.3 27.1 %collective-permute-start.7 = (f16[2,3,64,256]{3,2,1,0:T(8,128)(2,1)}, f16[2,3,64,256]{3,2,1,0:T(8,128)(2,1)}, u32[]{:S(2)}, u32[]{:S(2)}) collective-permute-start(f16[2,3,64,256]{3,2,1,0:T(8,128)(2,1)} %get-tuple-element.59), channel_id=1, source_target_pairs={{0,3},{1,0},{2,1},{3,2},{4,7},{5,4},{6,5},{7,6},{8,11},{9,8},{10,9... | collective-permute-start | bytes 589832 | tf_op jit(solution)/shard_map/ppermute | solution.py:430
  123.6 14.8 %copy-start.26 = (f32[3,8,64,256]{3,2,1,0:T(8,128)S(1)}, f32[3,8,64,256]{3,2,1,0:T(8,128)}, u32[]{:S(2)}) copy-start(f32[3,8,64,256]{3,2,1,0:T(8,128)} %param.20) | copy-start | bytes 4718596
  123.6 14.8 %copy-start.27 = (f32[8,64,256]{2,1,0:T(8,128)S(1)}, f32[8,64,256]{2,1,0:T(8,128)}, u32[]{:S(2)}) copy-start(f32[8,64,256]{2,1,0:T(8,128)} %broadcast_multiply_fusion) | copy-start | bytes 1572868
  123.6 26.0 %all-to-all-start.3 = ((f16[256,4,128]{2,1,0:T(4,128)(2,1)}), f16[256,4,128]{2,1,0:T(4,128)(2,1)}, u32[]{:S(2)}, u32[]{:S(2)}) async-start(f16[256,4,128]{2,1,0:T(4,128)(2,1)} %bitcast.10), calls=%async_computation.3 | async-start | bytes 524288 | tf_op jit(solution)/shard_map/all_to_all | solution.py:460
  137.0 6.1 %collective-permute-start.8 = (bf16[8,32,256]{2,1,0:T(8,128)(2,1)S(1)}, bf16[8,32,256]{2,1,0:T(8,128)(2,1)S(1)}, u32[]{:S(2)}, u32[]{:S(2)}) collective-permute-start(bf16[8,32,256]{2,1,0:T(8,128)(2,1)S(1)} %copy-done.25), channel_id=1, source_target_pairs={{0,1},{1,2},{2,3},{3,0},{4,5},{5,6},{6,7},{7,4},{8,9},{9,10},{10,1... | collective-permute-start | bytes 393224 | tf_op jit(solution)/shard_map/ppermute | solution.py:430
  139.9 13.5 %copy-start.9 = (f32[8,64,256]{2,1,0:T(8,128)S(1)}, f32[8,64,256]{2,1,0:T(8,128)}, u32[]{:S(2)}) copy-start(f32[8,64,256]{2,1,0:T(8,128)} %bulk.1) | copy-start | bytes 1572868
  139.9 13.5 %copy-start.11 = (f32[8,64,256]{2,1,0:T(8,128)S(1)}, f32[8,64,256]{2,1,0:T(8,128)}, u32[]{:S(2)}) copy-start(f32[8,64,256]{2,1,0:T(8,128)} %copy-done.10) | copy-start | bytes 1572868
  (21 other events, 94.3 us)

commit v4 on v3

--- a/solution.py
+++ b/solution.py
@@ -265,13 +265,24 @@
 
 
 def middle_kernel(
-    where, data, f0, f1, f2, f3, xib, xi, ya, yb, xfb, xf, slopes, out, fields, held, *scratch
+    where, data, xib, xi, ya, yb, xfb, xf, velocity, buoyancy, near, f2, slopes, out, held, *scratch
 ):
-    *targets, semaphores = scratch
+    *targets, fields, semaphores = scratch
+    own = pl.ds(2 * where[0], 2)
+    starts = [
+        pl.ds(pl.multiple_of(((where[0] + PEERS_Y - back) % PEERS_Y) * ROWS, ROWS), ROWS)
+        for back in range(PEERS_Y)
+    ]
+    blocks = Fetch(
+        (velocity.at[:, own], buoyancy.at[own], near.at[0], f2, near.at[1]),
+        (
+            fields.at[pl.ds(0, 3), :, starts[0]],
+            fields.at[3, :, starts[0]],
+            *[fields.at[:, :, starts[back]] for back in (1, 2, 3)],
+        ),
+        semaphores.at[pl.ds(8, 5)],
+    )
     fetch = Fetch((xib, xi, ya, yb, xfb, xf), targets, semaphores)
-    for back, block in enumerate((f0, f1, f2, f3)):
-        start = pl.multiple_of(((where[0] + PEERS_Y - back) % PEERS_Y) * ROWS, ROWS)
-        fields[:, :, pl.ds(start, ROWS), :] = block[...]
     returned = []
     for r in range(2):
         q, g = [
@@ -282,11 +293,14 @@
         ]
         both = to_lines(q, fetch[0]) * X_SCALE
         along = (both[:, :NX], left(fetch[2], both[:, NX:]), to_lines(g, fetch[1]) * X_SCALE)
+        if r == 0:
+            for i in range(5):
+                blocks[i]
         moved = []
         for d, slope in enumerate(along):
             held[r, d] = slope
             moved.append(fields[d, r] - fields[3, r] * (slope * (1.0 / SLOPE_LINK)))
-        returned.append(pltpu.make_async_copy(held.at[r], slopes.at[r], semaphores.at[6 + r]))
+        returned.append(pltpu.make_async_copy(held.at[r], slopes.at[:, r], semaphores.at[6 + r]))
         returned[r].start()
         scale = X_SCALE * MIDDLE_LINK
         along_y = left(fetch[3], moved[1])
@@ -344,85 +358,82 @@
             )
 
 
-def new_pressure_kernel(data, x_table, pressure, bulk, own, passed, out, held, x_ref, semaphores):
-    fetch = Fetch((x_table,), (x_ref,), semaphores)
+def new_pressure_kernel(data, x_table, *rest):
+    out, held, x_ref, semaphores = rest[5:6] + rest[-3:]
+    near = rest[6:11]
+    fetch = Fetch((x_table, *rest[:5]), (x_ref, *near), semaphores.at[pl.ds(4, 6)])
     sent = []
     for i in range(4):
         planes = pl.ds(2 * i, 2)
         components = data[pl.ds(i, 256, stride=4), :]
         lines = to_lines(components, fetch[0]) * (X_SCALE / DIVERGENCE_LINK)
-        held[planes] = pressure[planes] - bulk[planes] * lines.reshape(2, ROWS, NX) + own[planes]
-        held[planes, :TILE, :] += passed[planes].astype(f32)
-        sent.append(pltpu.make_async_copy(held.at[planes], out.at[planes], semaphores.at[1 + i]))
+        pressure, bulk, *source = [fetch[1 + j][planes].astype(f32) for j in range(5)]
+        held[planes] = (
+            pressure - bulk * lines.reshape(2, ROWS, NX) + (source[0] + source[1] + source[2])
+        )
+        sent.append(pltpu.make_async_copy(held.at[planes], out.at[planes], semaphores.at[i]))
         sent[i].start()
     for copy in sent:
         copy.wait()
 
 
-def source_kernel(where, lives, c0, c1, c2, t0, t1, t2, own, passed, l0, l1, l2):
-    blank = jnp.zeros((SLAB, 256, NX), bf16)
-    l0[:SLAB] = blank
-    l2[SLAB:] = blank
-    corners = (c0, c1, c2)
+def source_kernel(where, lives, corner, tiles, own, passed, lifted):
+    lifted[:SLAB] = jnp.zeros((SLAB, 256, NX), bf16)
+    lifted[2 * SLAB :] = jnp.zeros((SLAB, 256, NX), bf16)
 
     def place(slot, carry):
         rows = pl.ds(pl.multiple_of(slot * TILE, TILE), TILE)
         lane = lax.broadcasted_iota(jnp.int32, (TILE, NX), 1)
         line = lax.broadcasted_iota(jnp.int32, (TILE, NX), 0)
-        for reach, (tiles, placed) in enumerate(((t0, l0), (t1, l1), (t2, l2))):
-            offset = corners[reach][slot, 0] & (SLAB - 1)
-            hot = ((lane - line - corners[reach][slot, 2]) & (NX - 1)) == 0
-            hot = jnp.where(hot, 1.0, 0.0).astype(bf16)
-            first = SLAB - offset if reach == 1 else 0
-            to = 0 if reach == 1 else offset
-            block = tiles[slot, pl.ds(first, SLAB)].reshape(SLAB * TILE, TILE)
-            across = jnp.dot(block, hot, preferred_element_type=f32).astype(bf16)
-            placed[pl.ds(to, SLAB), rows, :] = across.reshape(SLAB, TILE, NX)
+        hot = ((lane - line - corner[slot, 2]) & (NX - 1)) == 0
+        hot = jnp.where(hot, 1.0, 0.0).astype(bf16)
+        block = tiles[slot].reshape(2 * SLAB * TILE, TILE)
+        across = jnp.dot(block, hot, preferred_element_type=f32).astype(bf16)
+        planes = pl.ds(corner[slot, 0] & (SLAB - 1), 2 * SLAB)
+        lifted[planes, rows, :] = across.reshape(2 * SLAB, TILE, NX)
         return carry
 
     lax.fori_loop(0, SLOTS_HERE, place, 0)
     line = lax.broadcasted_iota(jnp.int32, (ROWS + TILE, 256), 0)
     lane = lax.broadcasted_iota(jnp.int32, (ROWS + TILE, 256), 1)
-    hots = []
-    for reach in range(3):
-        sender = ((where[0] + PEERS_Z - reach) % PEERS_Z) * PEERS_Y + where[1]
-        start = jnp.full((ROWS + TILE, 256), -2 * TILE, jnp.int32)
-        for slot in range(SLOTS_HERE):
-            row = corners[reach][slot, 1] - where[1] * ROWS - slot * TILE
-            row = jnp.where(slot < lives[sender], row, -NX)
-            start = jnp.where(lane // TILE == slot, lane + row, start)
-        hots.append(jnp.where(line == start, 1.0, 0.0).astype(bf16))
-    for z in range(SLAB):
-        window = jnp.dot(hots[0], l0[z], preferred_element_type=f32)
-        window += jnp.dot(hots[1], l1[z], preferred_element_type=f32)
-        window += jnp.dot(hots[2], l2[SLAB + z], preferred_element_type=f32)
+    start = jnp.full((ROWS + TILE, 256), -2 * TILE, jnp.int32)
+    for slot in range(SLOTS_HERE):
+        row = corner[slot, 1] - where[1] * ROWS - slot * TILE
+        row = jnp.where(slot < lives[where[0] * PEERS_Y + where[1]], row, -2 * NX)
+        start = jnp.where(lane // TILE == slot, lane + row, start)
+    hot = jnp.where(line == start, 1.0, 0.0).astype(bf16)
+    for z in range(3 * SLAB):
+        window = jnp.dot(hot, lifted[z], preferred_element_type=f32)
         own[z] = window[:ROWS]
         passed[z] = window[ROWS:].astype(bf16)
 
 
+def source_rows_kernel(own, passed, here, after, second):
+    for first, out in ((0, here), (SLAB, after), (2 * SLAB, second)):
+        planes = pl.ds(first, SLAB)
+        out[...] = own[planes].astype(out.dtype)
+        out[:, :TILE, :] = (own[planes, :TILE, :] + passed[planes].astype(f32)).astype(out.dtype)
+
+
 VMEM = pl.BlockSpec(memory_space=pltpu.VMEM)
 SMEM = pl.BlockSpec(memory_space=pltpu.SMEM)
-ANY = pl.BlockSpec(memory_space=pl.ANY)
-
-
-def call(
-    kernel, name, scalars, arrays, far, shapes, scratch=(), far_out=0, targets=None, extra=0, limit=16
-):
-    if targets is None:
-        targets = [(x.shape, x.dtype) for x in far]
-    scratch = [pltpu.VMEM(shape, kind) for shape, kind in (*scratch, *targets)]
-    if far:
-        scratch.append(pltpu.SemaphoreType.DMA((len(targets) + extra,)))
+FAR = pl.BlockSpec(memory_space=pltpu.HBM)
+
+
+def call(kernel, name, specs, arrays, shapes, outs, scratch=(), semaphores=0, limit=16):
+    scratch = [pltpu.VMEM(shape, kind) for shape, kind in scratch]
+    if semaphores:
+        scratch.append(pltpu.SemaphoreType.DMA((semaphores,)))
     return pl.pallas_call(
         kernel,
         out_shape=[jax.ShapeDtypeStruct(shape, kind) for shape, kind in shapes],
-        in_specs=[SMEM] * len(scalars) + [VMEM] * len(arrays) + [ANY] * len(far),
-        out_specs=[ANY] * far_out + [VMEM] * (len(shapes) - far_out),
+        in_specs=specs,
+        out_specs=outs,
         scratch_shapes=scratch,
         compiler_params=pltpu.CompilerParams(vmem_limit_bytes=limit << 20),
         cost_estimate=pl.CostEstimate(flops=int(4e8), bytes_accessed=1 << 20, transcendentals=0),
         name=name,
-    )(*scalars, *arrays, *far)
+    )(*arrays)
 
 
 def from_behind(x, axis, by):
@@ -430,29 +441,19 @@
     return lax.ppermute(x, axis, [(i, (i + by) % peers) for i in range(peers)])
 
 
-def to_planes(fields, row_block):
-    axis = fields.ndim - 3
-
-    def planes_of(device):
-        return lax.dynamic_slice_in_dim(fields, 2 * device, 2, axis)
-
-    blocks = [planes_of(row_block)]
-    for ahead in range(1, PEERS_Y):
-        sent = planes_of((row_block + ahead) % PEERS_Y).astype(f16)
-        blocks.append(from_behind(sent, "gy", ahead))
-    return blocks
-
-
-def to_rows(blocks, row_block, axis):
+def to_rows(slopes, row_block):
+    blocks = [
+        lax.dynamic_slice_in_dim(slopes, ROWS * ((row_block + ahead) % PEERS_Y), ROWS, 2)
+        for ahead in range(PEERS_Y)
+    ]
     arrived = [blocks[0]] + [
         from_behind(blocks[ahead].astype(f16), "gy", ahead).astype(f32)
         for ahead in range(1, PEERS_Y)
     ]
-    ordered = []
-    for device in range(PEERS_Y):
-        back = (row_block - device) % PEERS_Y
-        ordered.append(lax.select_n(back, *arrived))
-    return jnp.concatenate(ordered, axis)
+    ordered = [
+        lax.select_n((row_block - device) % PEERS_Y, *arrived) for device in range(PEERS_Y)
+    ]
+    return jnp.concatenate(ordered, 1)
 
 
 def exchange(columns, rows):
@@ -468,113 +469,142 @@
     slab_index = lax.axis_index("gz")
     row_block = lax.axis_index("gy")
     here = row_block.reshape(1).astype(jnp.int32)
-    device = (slab_index * PEERS_Y + row_block).reshape(1).astype(jnp.int32)
+    device = (slab_index * PEERS_Y + row_block).astype(jnp.int32)
     place = jnp.stack([slab_index, row_block]).astype(jnp.int32)
     table = {key: jnp.asarray(value) for key, value in TABLES.items()}
+    wide, tall = ((256, 768), bf16), ((768, 256), bf16)
+    numbers = ((HALF, HALF), f32)
+    planes = ((SLAB, ROWS, NX), f32)
 
     (components,) = call(
         forward_lines_kernel,
         "forward_lines",
-        [],
-        [],
+        [FAR, FAR],
         [pressure, table["x_forward"]],
         [((1024, HALF), f32)],
-        targets=[((256, 768), bf16)] + [((2, ROWS, NX), f32)] * 4,
-    )
-    velocity, buoyancy, tiles, tile_corner, components = lax.optimization_barrier(
+        [VMEM],
+        [wide] + [((2, ROWS, NX), f32)] * 4,
+        5,
+    )
+    velocity_later, buoyancy_later, tiles, tile_corner, components = lax.optimization_barrier(
         (velocity, buoyancy, tiles, tile_corner, components)
     )
-    field_blocks = to_planes(jnp.concatenate([velocity, buoyancy[None]]), row_block)
-    packed = tiles.reshape(SLOTS_HERE, 2 * SLAB, 8, HALF)
-    tiles_before = from_behind(packed, "gz", 1)
-    tiles_second = from_behind(packed[:, SLAB:], "gz", 2)
-    moved, *field_blocks = lax.optimization_barrier((exchange(components, 4), *field_blocks))
+    fields = jnp.concatenate([velocity_later, buoyancy_later[None]])
+    sent = [
+        lax.dynamic_slice_in_dim(fields, 2 * ((row_block + ahead) % PEERS_Y), 2, 1).astype(f16)
+        for ahead in range(1, PEERS_Y)
+    ]
+    first, third = from_behind(sent[0], "gy", 1), from_behind(sent[2], "gy", 3)
+    moved, sent[1] = lax.optimization_barrier((exchange(components, 4), sent[1]))
     (filtered,) = call(
         filter_out_kernel,
         "filter_out",
-        [device],
-        [arrived(moved)],
-        [table["y_waves"], table["z_from_slabs"], table["z_to_pairs"], table["z_coefficients"]],
+        [SMEM, VMEM, FAR, FAR, FAR, FAR],
+        [
+            device.reshape(1),
+            arrived(moved),
+            table["y_waves"],
+            table["z_from_slabs"],
+            table["z_to_pairs"],
+            table["z_coefficients"],
+        ],
         [((2048, HALF), f32)],
-        [((NZ, NY), f32)],
-        targets=[((768, 256), bf16), ((256, 768), bf16), ((HALF, HALF), f32), ((256, 768), bf16)],
-    )
-    moved, tiles_before, tiles_second = lax.optimization_barrier(
-        (exchange(filtered, 8), tiles_before, tiles_second)
+        [VMEM],
+        [((NZ, NY), f32), tall, wide, numbers, wide],
+        4,
+    )
+    filtered, first, third, second, tiles, tile_corner = lax.optimization_barrier(
+        (filtered, first, third, sent[1], tiles, tile_corner)
+    )
+    second = from_behind(second, "gy", 2)
+    corner = lax.dynamic_slice_in_dim(tile_corner, device * SLOTS_HERE, SLOTS_HERE, 0)
+    source, passed = call(
+        source_kernel,
+        "source",
+        [SMEM, SMEM, SMEM, VMEM],
+        [place, live_count, corner, tiles],
+        [((3 * SLAB, ROWS, NX), f32), ((3 * SLAB, TILE, NX), bf16)],
+        [VMEM, VMEM],
+        [((3 * SLAB, 256, NX), bf16)],
+    )
+    passed = from_behind(passed, "gy", 1)
+    moved, source, passed, second = lax.optimization_barrier(
+        (exchange(filtered, 8), source, passed, second)
     )
     slopes, middle = call(
         middle_kernel,
         "middle",
-        [here],
-        [arrived(moved), *[block.astype(f32) for block in field_blocks]],
+        [SMEM, VMEM] + [FAR] * 10,
         [
-            table[key]
-            for key in (
-                "x_inverse_both", "x_inverse", "y_ahead", "y_behind", "x_forward_behind", "x_forward"
-            )
+            here,
+            arrived(moved),
+            table["x_inverse_both"],
+            table["x_inverse"],
+            table["y_ahead"],
+            table["y_behind"],
+            table["x_forward_behind"],
+            table["x_forward"],
+            velocity,
+            buoyancy,
+            jnp.stack([first, third]).astype(f32),
+            second.astype(f32),
         ],
-        [((2, 3, NY, NX), f32), ((2048, HALF), f32)],
-        [((4, 2, NY, NX), f32), ((2, 3, NY, NX), f32)],
-        far_out=1,
-        extra=2,
-        limit=24,
-    )
-    slope_blocks = [
-        lax.dynamic_slice_in_dim(slopes, ROWS * ((row_block + ahead) % PEERS_Y), ROWS, 2)
-        for ahead in range(PEERS_Y)
-    ]
-    slopes_here = jnp.swapaxes(to_rows(slope_blocks, row_block, 0), 0, 1)
-    new_velocity = velocity - buoyancy[None] * (slopes_here * (1.0 / SLOPE_LINK))
-
-    corners = [
-        lax.dynamic_slice_in_dim(
-            tile_corner,
-            ((slab_index - reach) % PEERS_Z * PEERS_Y + row_block) * SLOTS_HERE,
-            SLOTS_HERE,
-            0,
-        )
-        for reach in range(3)
-    ]
-    own, passed = call(
-        source_kernel,
-        "source",
-        [place, live_count, *corners],
+        [((3, 2, NY, NX), f32), ((2048, HALF), f32)],
+        [FAR, VMEM],
         [
-            tiles,
-            tiles_before.reshape(SLOTS_HERE, 2 * SLAB, TILE, TILE),
-            tiles_second.reshape(SLOTS_HERE, SLAB, TILE, TILE),
+            ((2, 3, NY, NX), f32),
+            ((768, 512), bf16),
+            tall,
+            wide,
+            wide,
+            wide,
+            wide,
+            ((4, 2, NY, NX), f32),
         ],
-        [],
-        [((SLAB, ROWS, NX), f32), ((SLAB, TILE, NX), bf16)],
-        [((2 * SLAB, 256, NX), bf16), ((SLAB, 256, NX), bf16), ((2 * SLAB, 256, NX), bf16)],
-    )
-    moved, own, passed = lax.optimization_barrier((exchange(middle, 8), own, passed))
-    passed = from_behind(passed, "gy", 1)
+        13,
+        24,
+    )
+    new_velocity = velocity - buoyancy[None] * (to_rows(slopes, row_block) * (1.0 / SLOPE_LINK))
+    own, after, beyond = call(
+        source_rows_kernel,
+        "source_rows",
+        [VMEM, VMEM],
+        [source, passed],
+        [planes, ((SLAB, ROWS, NX), bf16), ((SLAB, ROWS, NX), bf16)],
+        [VMEM, VMEM, VMEM],
+    )
+    moved, own, after, beyond = lax.optimization_barrier((exchange(middle, 8), own, after, beyond))
+    after, beyond = from_behind(after, "gz", 1), from_behind(beyond, "gz", 2)
     (filtered_back,) = call(
         filter_back_kernel,
         "filter_back",
-        [device],
-        [arrived(moved)],
-        [table["y_waves"], table["z_from_pairs"], table["z_to_slabs"], table["z_coefficients"]],
+        [SMEM, VMEM, FAR, FAR, FAR, FAR],
+        [
+            device.reshape(1),
+            arrived(moved),
+            table["y_waves"],
+            table["z_from_pairs"],
+            table["z_to_slabs"],
+            table["z_coefficients"],
+        ],
         [((1024, HALF), f32)],
-        targets=[((256, 768), bf16), ((HALF, HALF), f32), ((768, 256), bf16), ((256, 768), bf16)],
-    )
-    moved, new_velocity, passed = lax.optimization_barrier(
-        (exchange(filtered_back, 4), new_velocity, passed)
-    )
-    (new_pressure,) = pl.pallas_call(
+        [VMEM],
+        [wide, numbers, tall, wide],
+        4,
+    )
+    moved, new_velocity, after, beyond = lax.optimization_barrier(
+        (exchange(filtered_back, 4), new_velocity, after, beyond)
+    )
+    (new_pressure,) = call(
         new_pressure_kernel,
-        out_shape=[jax.ShapeDtypeStruct((SLAB, ROWS, NX), f32)],
-        in_specs=[VMEM, ANY, VMEM, VMEM, VMEM, VMEM],
-        out_specs=[ANY],
-        scratch_shapes=[
-            pltpu.VMEM((SLAB, ROWS, NX), f32),
-            pltpu.VMEM((768, 256), bf16),
-            pltpu.SemaphoreType.DMA((5,)),
-        ],
-        compiler_params=pltpu.CompilerParams(vmem_limit_bytes=16 << 20),
-        name="new_pressure",
-    )(arrived(moved), table["x_inverse"], pressure, bulk, own, passed)
+        "new_pressure",
+        [VMEM] + [FAR] * 6,
+        [arrived(moved), table["x_inverse"], pressure, bulk, own, after, beyond],
+        [planes],
+        [FAR],
+        [planes, planes, planes, *[((SLAB, ROWS, NX), bf16)] * 2, planes, tall],
+        10,
+    )
     return (new_pressure, new_velocity)
 
 

time: 156 us -> 157 us (level)
  waiting for transfers between devices: 40.4 us -> 47.4 us
  starting transfers between devices: 62.5 us -> 56.4 us
  local copies, waits for them, and re-layouts: 16.7 us -> 13.2 us
  other arithmetic: 14.9 us -> 17.6 us
    all_to_all x4, waiting for transfers between devices: 7.88 us -> 20 us  [exchange(): return lax.all_to_all(blocks, ('gz', 'gy'), 0, 0, tiled=True)]
    all_to_all x4, starting transfers between devices: 48 us -> 41.9 us  [exchange(): return lax.all_to_all(blocks, ('gz', 'gy'), 0, 0, tiled=True)]
    ppermute x9, waiting for transfers between devices: 32.5 us -> 27.4 us  [from_behind(): return lax.ppermute(x, axis, [(i, (i + by) % peers) for i in range(peers)])]
    reshape x3 -> x0, local copies, waits for them, and re-layouts: 4.02 us -> none  [the longest x1 1.67 us: local(): tiles_before.reshape(SLOTS_HERE, 2 * SLAB, TILE, TILE)]
    pallas_call x5 -> x7, Pallas kernels: 17.7 us -> 20.5 us  [call(): pl.pallas_call(kernel, out_shape=[jax.ShapeDtypeStruct(shape, kind) for s...]
    unnamed x65 -> x66, local copies, waits for them, and re-layouts: 9.65 us -> 10.4 us
  transfers between devices with their start and end apart: 13 -> 13, of which waited for: 6 -> 5; matrix products, arithmetic and copies ran while one was open for 11% -> 9% of each run, Pallas kernels for 4% -> 7%
where the time goes in v4:
time: 157 us; the launch traced here: 156 us
  starting transfers between devices  56.4 us (36%)
  waiting for transfers between devices  47.4 us (30%)
  Pallas kernels  20.5 us (13%)
  other arithmetic  17.6 us (11%)
  local copies, waits for them, and re-layouts  13.2 us (8%)
    all_to_all x4, starting transfers between devices, exchange(): return lax.all_to_all(blocks, ('gz', 'gy'), 0, 0, tiled=True)  41.9 us
    ppermute x9, waiting for transfers between devices, from_behind(): return lax.ppermute(x, axis, [(i, (i + by) % peers) for i in range(peers)])  27.4 us
    pallas_call x7, Pallas kernels, call(): pl.pallas_call(kernel, out_shape=[jax.ShapeDtypeStruct(shape, kind) for s...  20.5 us
    all_to_all x4, waiting for transfers between devices, exchange(): return lax.all_to_all(blocks, ('gz', 'gy'), 0, 0, tiled=True)  20 us
    ppermute x9, starting transfers between devices, from_behind(): return lax.ppermute(x, axis, [(i, (i + by) % peers) for i in range(peers)])  14.5 us
    unnamed x66, local copies, waits for them, and re-layouts  10.4 us
    convert_element_type x4, other arithmetic, arrived(): return moved.reshape(-1, HALF).astype(f32)  4.34 us
  transfers between devices with their start and end apart: 13, of which 5 were waited for; matrix products, arithmetic and copies ran while one was open for 9% of the time, Pallas kernels for 7%

profile of v4, /device:TPU:1, one launch (start us, length us, event | category | flops | bytes accessed | tf_op | source)
XLA Modules:
  0.0 156.4 jit_solution(5365061616062701623)
XLA Ops:
  2.8 2.3 %forward_lines.1 = f32[1024,128]{1,0:T(8,128)S(1)} custom-call(f32[8,64,256]{2,1,0:T(8,128)S(1)} %copy-done.9, bf16[256,768]{1,0:T(8,128)(2,1)S(1)} %copy-done.20), custom_call_target="tpu_custom_call" | custom-call | flops 400000000 | bytes 1048576 | tf_op jit(solution)/shard_map/forward_lines/pallas_call | solution.py:427
  5.9 16.7 %all-to-all-start = ((f16[256,4,128]{2,1,0:T(4,128)(2,1)}), f16[256,4,128]{2,1,0:T(4,128)(2,1)}, u32[]{:S(2)}, u32[]{:S(2)}) async-start(f16[256,4,128]{2,1,0:T(4,128)(2,1)} %bitcast.2), calls=%async_computation | async-start | bytes 524288 | tf_op jit(solution)/shard_map/all_to_all | solution.py:461
  23.6 1.4 collective-permute-start
  26.3 10.6 %all-to-all-done = f16[256,4,128]{2,1,0:T(4,128)(2,1)} async-done(((f16[256,4,128]{2,1,0:T(4,128)(2,1)}), f16[256,4,128]{2,1,0:T(4,128)(2,1)}, u32[]{:S(2)}, u32[]{:S(2)}) %all-to-all-start) | async-done | bytes 262176 | tf_op jit(solution)/shard_map/all_to_all | solution.py:461
  37.9 3.5 %filter_out.1 = f32[2048,128]{1,0:T(8,128)S(1)} custom-call(s32[1]{0:T(128)} %bitcast.where, f32[1024,128]{1,0:T(8,128)S(1)} %convert.4.data, bf16[768,256]{1,0:T(8,128)(2,1)S(1)} %copy-done.2, bf16[256,768]{1,0:T(8,128)(2,1)S(1)} %copy-done.16, bf16[256,768]{1,0:T(8,128)(2,1)S(1)} %copy-done.17, f32[128,128]{1,0:T(8,128)S(1)} %copy-done.29), custom_call_target="tpu_custom_call" | custom-call | flops 400000000 | bytes 1048576 | tf_op jit(solution)/shard_map/filter_out/pallas_call | solution.py:427
  42.3 7.0 %all-to-all-start.1 = ((f16[256,8,128]{2,1,0:T(8,128)(2,1)}), f16[256,8,128]{2,1,0:T(8,128)(2,1)}, u32[]{:S(2)}, u32[]{:S(2)}) async-start(f16[256,8,128]{2,1,0:T(8,128)(2,1)} %convert_bitcast_fusion.1), calls=%async_computation.1 | async-start | bytes 1048576 | tf_op jit(solution)/shard_map/all_to_all | solution.py:461
  49.4 2.1 %copy.21 = s32[2048,3]{1,0:T(8,128)} copy(s32[2048,3]{0,1:T(4,128)} %param.24) | data formatting | bytes 49152 | tf_op jit(solution)/shard_map/optimization_barrier | solution.py:516
  52.2 3.1 %source.1 = (f32[24,64,256]{2,1,0:T(8,128)S(1)}, bf16[24,32,256]{2,1,0:T(8,128)(2,1)S(1)}) custom-call(s32[2]{0:T(128)S(1)} %pad_add_fusion.where, s32[256]{0:T(256)S(1)} %copy-done.32, s32[8,3]{1,0:T(8,128)S(1)} %constant_dynamic-slice_fusion.corner, bf16[8,16,32,32]{3,2,1,0:T(8,128)(2,1)S(1)} %copy-done.31), custom_call_target="tpu_custom_call" | custom-call | flops 400000000 | bytes 1048576 | tf_op jit(solution)/shard_map/source/pallas_call | solution.py:427
  57.8 2.6 %collective-permute-start.3 = (f16[4,2,64,256]{3,2,1,0:T(8,128)(2,1)}, f16[4,2,64,256]{3,2,1,0:T(8,128)(2,1)}, u32[]{:S(2)}, u32[]{:S(2)}) collective-permute-start(f16[4,2,64,256]{3,2,1,0:T(8,128)(2,1)} %get-tuple-element.46), channel_id=1, source_target_pairs={{0,2},{1,3},{2,0},{3,1},{4,6},{5,7},{6,4},{7,5},{8,10},{9,11},{10,... | collective-permute-start | bytes 786440 | tf_op jit(solution)/shard_map/ppermute | solution.py:441
  61.6 15.9 %collective-permute-done.3 = f16[4,2,64,256]{3,2,1,0:T(8,128)(2,1)} collective-permute-done((f16[4,2,64,256]{3,2,1,0:T(8,128)(2,1)}, f16[4,2,64,256]{3,2,1,0:T(8,128)(2,1)}, u32[]{:S(2)}, u32[]{:S(2)}) %collective-permute-start.3) | collective-permute-done | bytes 262176 | tf_op jit(solution)/shard_map/ppermute | solution.py:441
  81.6 5.6 %middle.1 = (f32[3,2,256,256]{3,2,1,0:T(8,128)S(1)}, f32[2048,128]{1,0:T(8,128)S(1)}) custom-call(s32[1]{0:T(128)} %bitcast.1.where, f32[2048,128]{1,0:T(8,128)S(1)} %bitcast_convert_fusion.1.data, bf16[768,512]{1,0:T(8,128)(2,1)S(1)} %copy-done.8, bf16[768,256]{1,0:T(8,128)(2,1)S(1)} %copy-done.6, bf16[256,768]{1,0:T(8,128)(2,1)S(1)} %copy-done.23, ...), custom_call_target="tpu_custom_call" | custom-call | flops 400000000 | bytes 1048576 | tf_op jit(solution)/shard_map/middle/pallas_call | solution.py:427
  89.2 10.8 %all-to-all-start.2 = ((f16[256,8,128]{2,1,0:T(8,128)(2,1)}), f16[256,8,128]{2,1,0:T(8,128)(2,1)}, u32[]{:S(2)}, u32[]{:S(2)}) async-start(f16[256,8,128]{2,1,0:T(8,128)(2,1)} %convert_bitcast_fusion), calls=%async_computation.2 | async-start | bytes 1048576 | tf_op jit(solution)/shard_map/all_to_all | solution.py:461
  101.0 2.1 %dynamic-slice_convert_fusion.1 = (f16[3,2,64,256]{3,2,1,0:T(8,128)(2,1)}, f16[3,2,64,256]{3,2,1,0:T(8,128)(2,1)}, f16[3,2,64,256]{3,2,1,0:T(8,128)(2,1)}) fusion(f32[3,2,256,256]{3,2,1,0:T(8,128)} %copy-done.3, s32[]{:T(128)S(6)} %select_n.188, s32[]{:T(128)S(6)} %select_n.189, s32[]{:T(128)S(6)} %select_n.184), kind=kLoop, calls=%fused_computation.32 | loop fusion | flops 294912 | bytes 1769484 | tf_op jit(solution)/shard_map/convert_element_type | solution.py:450
  103.1 1.4 collective-permute-start.4
  104.5 2.4 %collective-permute-start.5 = (f16[3,2,64,256]{3,2,1,0:T(8,128)(2,1)}, f16[3,2,64,256]{3,2,1,0:T(8,128)(2,1)}, u32[]{:S(2)}, u32[]{:S(2)}) collective-permute-start(f16[3,2,64,256]{3,2,1,0:T(8,128)(2,1)} %get-tuple-element.73), channel_id=1, source_target_pairs={{0,2},{1,3},{2,0},{3,1},{4,6},{5,7},{6,4},{7,5},{8,10},{9,11},{10,... | collective-permute-start | bytes 589832 | tf_op jit(solution)/shard_map/ppermute | solution.py:441
  109.8 9.4 %all-to-all-done.2 = f16[256,8,128]{2,1,0:T(8,128)(2,1)} async-done(((f16[256,8,128]{2,1,0:T(8,128)(2,1)}), f16[256,8,128]{2,1,0:T(8,128)(2,1)}, u32[]{:S(2)}, u32[]{:S(2)}) %all-to-all-start.2) | async-done | bytes 524320 | tf_op jit(solution)/shard_map/all_to_all | solution.py:461
  120.3 3.2 %filter_back.1 = f32[1024,128]{1,0:T(8,128)S(1)} custom-call(s32[1]{0:T(128)} %bitcast.where, f32[2048,128]{1,0:T(8,128)S(1)} %bitcast_convert_fusion.data, bf16[768,256]{1,0:T(8,128)(2,1)S(1)} %copy-done.2, bf16[256,768]{1,0:T(8,128)(2,1)S(1)} %copy-done.14, bf16[256,768]{1,0:T(8,128)(2,1)S(1)} %copy-done.15, f32[128,128]{1,0:T(8,128)S(1)} %copy-done.30), custom_call_target="tpu_custom_call" | custom-call | flops 400000000 | bytes 1048576 | tf_op jit(solution)/shard_map/filter_back/pallas_call | solution.py:427
  124.3 7.4 %all-to-all-start.3 = ((f16[256,4,128]{2,1,0:T(4,128)(2,1)}), f16[256,4,128]{2,1,0:T(4,128)(2,1)}, u32[]{:S(2)}, u32[]{:S(2)}) async-start(f16[256,4,128]{2,1,0:T(4,128)(2,1)} %bitcast.12), calls=%async_computation.3 | async-start | bytes 524288 | tf_op jit(solution)/shard_map/all_to_all | solution.py:461
  131.7 1.4 fusion.7
  133.1 1.7 %collective-permute-start.7 = (bf16[8,64,256]{2,1,0:T(8,128)(2,1)}, bf16[8,64,256]{2,1,0:T(8,128)(2,1)S(1)}, u32[]{:S(2)}, u32[]{:S(2)}) collective-permute-start(bf16[8,64,256]{2,1,0:T(8,128)(2,1)} %get-tuple-element.59), channel_id=1, source_target_pairs={{0,4},{4,8},{8,12},{12,16},{16,20},{20,24},{24,28},{28,32},{32,36}... | collective-permute-start | bytes 786440 | tf_op jit(solution)/shard_map/ppermute | solution.py:441
  136.0 2.6 %fusion = f32[3,8,64,256]{3,2,1,0:T(8,128)} fusion(f32[3,8,64,256]{3,2,1,0:T(8,128)S(1)} %copy-done, f32[3,2,64,256]{3,2,1,0:T(8,128)S(1)} %get-tuple-element.69, f32[3,2,64,256]{3,2,1,0:T(8,128)S(1)} %get-tuple-element.68, f32[3,2,64,256]{3,2,1,0:T(8,128)S(1)} %get-tuple-element.67, f32[3,2,64,256]{3,2,1,0:T(8,128)S(1)} %get-tuple-element.66, ...), kind=kLoop, calls=%fused_computation.7 | loop fusion | flops 1966080 | bytes 5242880 | tf_op jit(solution)/shard_map/sub | solution.py:567
  138.6 3.6 %collective-permute-done.7.rest_3_ = bf16[8,64,256]{2,1,0:T(8,128)(2,1)S(1)} collective-permute-done((bf16[8,64,256]{2,1,0:T(8,128)(2,1)}, bf16[8,64,256]{2,1,0:T(8,128)(2,1)S(1)}, u32[]{:S(2)}, u32[]{:S(2)}) %collective-permute-start.7) | collective-permute-done | bytes 262176 | tf_op jit(solution)/shard_map/ppermute | solution.py:441
  142.9 7.9 %collective-permute-done.8.rest_4_ = bf16[8,64,256]{2,1,0:T(8,128)(2,1)S(1)} collective-permute-done((bf16[8,64,256]{2,1,0:T(8,128)(2,1)}, bf16[8,64,256]{2,1,0:T(8,128)(2,1)S(1)}, u32[]{:S(2)}, u32[]{:S(2)}) %collective-permute-start.8) | collective-permute-done | bytes 262176 | tf_op jit(solution)/shard_map/ppermute | solution.py:441
  154.4 1.8 %new_pressure.1 = f32[8,64,256]{2,1,0:T(8,128)} custom-call(f32[1024,128]{1,0:T(8,128)S(1)} %convert.7.data, bf16[768,256]{1,0:T(8,128)(2,1)S(1)} %copy-done.7, f32[8,64,256]{2,1,0:T(8,128)S(1)} %copy-done.10, f32[8,64,256]{2,1,0:T(8,128)S(1)} %copy-done.11, f32[8,64,256]{2,1,0:T(8,128)S(1)} %copy-done.13, bf16[8,64,256]{2,1,0:T(8,128)(2,1)S(1)} %copy-done.26, ...), custom_call_target="tpu_custom_call" | custom-call | flops 400000000 | bytes 1048576 | tf_op jit(solution)/shard_map/new_pressure/pallas_call | solution.py:427
  (93 shorter events, 28.5 us)
Async XLA Ops:
  0.6 22.0 %copy-start = (f32[3,8,64,256]{3,2,1,0:T(8,128)S(1)}, f32[3,8,64,256]{3,2,1,0:T(8,128)}, u32[]{:S(2)}) copy-start(f32[3,8,64,256]{3,2,1,0:T(8,128)} %velocity.1) | copy-start | bytes 4718596
  0.6 22.0 %copy-start.1 = (f32[8,64,256]{2,1,0:T(8,128)S(1)}, f32[8,64,256]{2,1,0:T(8,128)}, u32[]{:S(2)}) copy-start(f32[8,64,256]{2,1,0:T(8,128)} %buoyancy.1) | copy-start | bytes 1572868
  5.9 31.0 %all-to-all-start = ((f16[256,4,128]{2,1,0:T(4,128)(2,1)}), f16[256,4,128]{2,1,0:T(4,128)(2,1)}, u32[]{:S(2)}, u32[]{:S(2)}) async-start(f16[256,4,128]{2,1,0:T(4,128)(2,1)} %bitcast.2), calls=%async_computation | async-start | bytes 524288 | tf_op jit(solution)/shard_map/all_to_all | solution.py:461
  22.6 15.2 %copy-start.2 = (bf16[768,256]{1,0:T(8,128)(2,1)S(1)}, bf16[768,256]{1,0:T(8,128)(2,1)}, u32[]{:S(2)}) copy-start(bf16[768,256]{1,0:T(8,128)(2,1)} %constant.106.clone.y) | copy-start | bytes 1179652
  22.6 15.2 %copy-start.16 = (bf16[256,768]{1,0:T(8,128)(2,1)S(1)}, bf16[256,768]{1,0:T(8,128)(2,1)}, u32[]{:S(2)}) copy-start(bf16[256,768]{1,0:T(8,128)(2,1)} %constant.107.clone.z_from) | copy-start | bytes 1179652
  22.7 15.2 %copy-start.17 = (bf16[256,768]{1,0:T(8,128)(2,1)S(1)}, bf16[256,768]{1,0:T(8,128)(2,1)}, u32[]{:S(2)}) copy-start(bf16[256,768]{1,0:T(8,128)(2,1)} %constant.108.clone.z_to) | copy-start | bytes 1179652
  22.7 15.2 %copy-start.29 = (f32[128,128]{1,0:T(8,128)S(1)}, f32[128,128]{1,0:T(8,128)}, u32[]{:S(2)}) copy-start(f32[128,128]{1,0:T(8,128)} %constant.111.clone.z_numbers) | copy-start | bytes 196612
  23.6 17.9 %collective-permute-start = (f16[4,2,64,256]{3,2,1,0:T(8,128)(2,1)}, f16[4,2,64,256]{3,2,1,0:T(8,128)(2,1)}, u32[]{:S(2)}, u32[]{:S(2)}) collective-permute-start(f16[4,2,64,256]{3,2,1,0:T(8,128)(2,1)} %get-tuple-element.72), channel_id=1, source_target_pairs={{0,1},{1,2},{2,3},{3,0},{4,5},{5,6},{6,7},{7,4},{8,9},{9,10},{10,1... | collective-permute-start | bytes 786440 | tf_op jit(solution)/shard_map/ppermute | solution.py:441
  25.0 16.5 %collective-permute-start.1 = (f16[4,2,64,256]{3,2,1,0:T(8,128)(2,1)}, f16[4,2,64,256]{3,2,1,0:T(8,128)(2,1)}, u32[]{:S(2)}, u32[]{:S(2)}) collective-permute-start(f16[4,2,64,256]{3,2,1,0:T(8,128)(2,1)} %get-tuple-element.70), channel_id=1, source_target_pairs={{0,3},{1,0},{2,1},{3,2},{4,7},{5,4},{6,5},{7,6},{8,11},{9,8},{10,9... | collective-permute-start | bytes 786440 | tf_op jit(solution)/shard_map/ppermute | solution.py:441
  42.3 35.9 %all-to-all-start.1 = ((f16[256,8,128]{2,1,0:T(8,128)(2,1)}), f16[256,8,128]{2,1,0:T(8,128)(2,1)}, u32[]{:S(2)}, u32[]{:S(2)}) async-start(f16[256,8,128]{2,1,0:T(8,128)(2,1)} %convert_bitcast_fusion.1), calls=%async_computation.1 | async-start | bytes 1048576 | tf_op jit(solution)/shard_map/all_to_all | solution.py:461
  56.5 21.0 %collective-permute-start.2 = (bf16[24,32,256]{2,1,0:T(8,128)(2,1)S(1)}, bf16[24,32,256]{2,1,0:T(8,128)(2,1)S(1)}, u32[]{:S(2)}, u32[]{:S(2)}) collective-permute-start(bf16[24,32,256]{2,1,0:T(8,128)(2,1)S(1)} %get-tuple-element.45), channel_id=1, source_target_pairs={{0,1},{1,2},{2,3},{3,0},{4,5},{5,6},{6,7},{7,4},{8,9},{9,10},{10,1... | collective-permute-start | bytes 1179656 | tf_op jit(solution)/shard_map/ppermute | solution.py:441
  57.8 19.6 %collective-permute-start.3 = (f16[4,2,64,256]{3,2,1,0:T(8,128)(2,1)}, f16[4,2,64,256]{3,2,1,0:T(8,128)(2,1)}, u32[]{:S(2)}, u32[]{:S(2)}) collective-permute-start(f16[4,2,64,256]{3,2,1,0:T(8,128)(2,1)} %get-tuple-element.46), channel_id=1, source_target_pairs={{0,2},{1,3},{2,0},{3,1},{4,6},{5,7},{6,4},{7,5},{8,10},{9,11},{10,... | collective-permute-start | bytes 786440 | tf_op jit(solution)/shard_map/ppermute | solution.py:441
  89.2 29.9 %all-to-all-start.2 = ((f16[256,8,128]{2,1,0:T(8,128)(2,1)}), f16[256,8,128]{2,1,0:T(8,128)(2,1)}, u32[]{:S(2)}, u32[]{:S(2)}) async-start(f16[256,8,128]{2,1,0:T(8,128)(2,1)} %convert_bitcast_fusion), calls=%async_computation.2 | async-start | bytes 1048576 | tf_op jit(solution)/shard_map/all_to_all | solution.py:461
  103.1 28.6 %collective-permute-start.4 = (f16[3,2,64,256]{3,2,1,0:T(8,128)(2,1)}, f16[3,2,64,256]{3,2,1,0:T(8,128)(2,1)S(1)}, u32[]{:S(2)}, u32[]{:S(2)}) collective-permute-start(f16[3,2,64,256]{3,2,1,0:T(8,128)(2,1)} %get-tuple-element.75), channel_id=1, source_target_pairs={{0,1},{1,2},{2,3},{3,0},{4,5},{5,6},{6,7},{7,4},{8,9},{9,10},{10,1... | collective-permute-start | bytes 589832 | tf_op jit(solution)/shard_map/ppermute | solution.py:441
  104.5 27.2 %collective-permute-start.5 = (f16[3,2,64,256]{3,2,1,0:T(8,128)(2,1)}, f16[3,2,64,256]{3,2,1,0:T(8,128)(2,1)}, u32[]{:S(2)}, u32[]{:S(2)}) collective-permute-start(f16[3,2,64,256]{3,2,1,0:T(8,128)(2,1)} %get-tuple-element.73), channel_id=1, source_target_pairs={{0,2},{1,3},{2,0},{3,1},{4,6},{5,7},{6,4},{7,5},{8,10},{9,11},{10,... | collective-permute-start | bytes 589832 | tf_op jit(solution)/shard_map/ppermute | solution.py:441
  106.9 13.4 %copy-start.30 = (f32[128,128]{1,0:T(8,128)S(1)}, f32[128,128]{1,0:T(8,128)}, u32[]{:S(2)}) copy-start(f32[128,128]{1,0:T(8,128)} %constant.111.clone.z_numbers) | copy-start | bytes 196612
  106.9 24.8 %collective-permute-start.6 = (f16[3,2,64,256]{3,2,1,0:T(8,128)(2,1)}, f16[3,2,64,256]{3,2,1,0:T(8,128)(2,1)}, u32[]{:S(2)}, u32[]{:S(2)}) collective-permute-start(f16[3,2,64,256]{3,2,1,0:T(8,128)(2,1)} %get-tuple-element.74), channel_id=1, source_target_pairs={{0,3},{1,0},{2,1},{3,2},{4,7},{5,4},{6,5},{7,6},{8,11},{9,8},{10,9... | collective-permute-start | bytes 589832 | tf_op jit(solution)/shard_map/ppermute | solution.py:441
  124.3 27.2 %all-to-all-start.3 = ((f16[256,4,128]{2,1,0:T(4,128)(2,1)}), f16[256,4,128]{2,1,0:T(4,128)(2,1)}, u32[]{:S(2)}, u32[]{:S(2)}) async-start(f16[256,4,128]{2,1,0:T(4,128)(2,1)} %bitcast.12), calls=%async_computation.3 | async-start | bytes 524288 | tf_op jit(solution)/shard_map/all_to_all | solution.py:461
  133.1 9.1 %collective-permute-start.7 = (bf16[8,64,256]{2,1,0:T(8,128)(2,1)}, bf16[8,64,256]{2,1,0:T(8,128)(2,1)S(1)}, u32[]{:S(2)}, u32[]{:S(2)}) collective-permute-start(bf16[8,64,256]{2,1,0:T(8,128)(2,1)} %get-tuple-element.59), channel_id=1, source_target_pairs={{0,4},{4,8},{8,12},{12,16},{16,20},{20,24},{24,28},{28,32},{32,36}... | collective-permute-start | bytes 786440 | tf_op jit(solution)/shard_map/ppermute | solution.py:441
  134.8 15.9 %collective-permute-start.8 = (bf16[8,64,256]{2,1,0:T(8,128)(2,1)}, bf16[8,64,256]{2,1,0:T(8,128)(2,1)S(1)}, u32[]{:S(2)}, u32[]{:S(2)}) collective-permute-start(bf16[8,64,256]{2,1,0:T(8,128)(2,1)} %get-tuple-element.60), channel_id=1, source_target_pairs={{0,8},{4,12},{8,16},{12,20},{16,24},{20,28},{24,32},{28,36},{32,40... | collective-permute-start | bytes 786440 | tf_op jit(solution)/shard_map/ppermute | solution.py:441
  136.0 16.5 %copy-start.7 = (bf16[768,256]{1,0:T(8,128)(2,1)S(1)}, bf16[768,256]{1,0:T(8,128)(2,1)}, u32[]{:S(2)}) copy-start(bf16[768,256]{1,0:T(8,128)(2,1)} %constant.102.clone.xi.x_table) | copy-start | bytes 1179652
  136.0 16.5 %copy-start.10 = (f32[8,64,256]{2,1,0:T(8,128)S(1)}, f32[8,64,256]{2,1,0:T(8,128)}, u32[]{:S(2)}) copy-start(f32[8,64,256]{2,1,0:T(8,128)} %rest_0_.1) | copy-start | bytes 1572868
  136.0 16.5 %copy-start.11 = (f32[8,64,256]{2,1,0:T(8,128)S(1)}, f32[8,64,256]{2,1,0:T(8,128)}, u32[]{:S(2)}) copy-start(f32[8,64,256]{2,1,0:T(8,128)} %rest_1_.1) | copy-start | bytes 1572868
  136.0 16.5 %copy-start.13 = (f32[8,64,256]{2,1,0:T(8,128)S(1)}, f32[8,64,256]{2,1,0:T(8,128)}, u32[]{:S(2)}) copy-start(f32[8,64,256]{2,1,0:T(8,128)} %copy-done.12) | copy-start | bytes 1572868
  (22 other events, 86.1 us)

commit v5 on v4

v5 whole, which is shorter than its diff:
```python
import math

import jax
import jax.numpy as jnp
import ml_dtypes
import numpy as np
from jax import lax
from jax.experimental import pallas as pl
from jax.experimental.pallas import tpu as pltpu
from jax.sharding import PartitionSpec as P

NX = 256
NY = 256
NZ = 512
HALF = 128
ROWS = 64
SLAB = 8
SLOTS_HERE = 8
TILE = 32
PEERS_Y = 4
PEERS_Z = 64
kappa_courant = 0.3
f32 = jnp.float32
bf16 = jnp.bfloat16
f16 = jnp.float16

X_SCALE = 1.0 / 16.0
SLOPE_LINK = 0.25
MIDDLE_LINK = 1.0 / 16.0
DIVERGENCE_LINK = 1.0 / 32.0


def split_table(table):
    high = table.astype(ml_dtypes.bfloat16)
    low = (table - high.astype(np.float64)).astype(ml_dtypes.bfloat16)
    return high, low


def packed_table(table):
    return np.concatenate(split_table(table), axis=1)


def signed_waves(length):
    index = np.arange(length)
    return 2.0 * np.pi / length * np.where(index < length // 2, index, index - length)


def derivative_matrix(length, orientation):
    wave = signed_waves(length)
    kernel = np.fft.ifft(1j * wave * np.exp(orientation * 0.5j * wave)).real
    index = np.arange(length)
    return kernel[(index[:, None] - index[None, :]) % length]


def make_tables():
    index = np.arange(256)
    angle = 2.0 * np.pi / 256 * (np.outer(index, index) % 256)
    wave_x = 2.0 * np.pi / NX * np.arange(HALF)

    spectrum = np.exp(-1j * angle[:HALF])
    weight = np.where(np.arange(HALF) == 0, 1.0, 2.0)
    ahead = 1j * wave_x * np.exp(0.5j * wave_x)
    behind = 1j * wave_x * np.exp(-0.5j * wave_x)
    x_rows = np.zeros((8, HALF), np.float32)
    x_rows[0], x_rows[1], x_rows[2] = weight, (weight * ahead).real, (weight * ahead).imag
    forward_z = np.concatenate([np.cos(angle[:HALF]), -np.sin(angle[:HALF])], axis=0)
    forward_z[HALF] = np.cos(angle[HALF])
    inverse_z = 2.0 * forward_z.T
    inverse_z[:, 0] = forward_z[0]
    inverse_z[:, HALF] = forward_z[HALF]
    slab_order = (4 * np.arange(64)[None, :] + np.arange(4)[:, None]).reshape(-1)
    low = np.arange(HALF)
    high = low - 256
    coefficients = np.zeros((HALF, HALF), np.float32)
    coefficients[:, 0] = np.cos(2.0 * np.pi / NZ * low)
    coefficients[:, 1] = np.sin(2.0 * np.pi / NZ * low)

    def derivative(number, orientation):
        wave = 2.0 * np.pi / NZ * number
        return -orientation * wave * np.sin(0.5 * wave), wave * np.cos(0.5 * wave)

    coefficients[:, 16], coefficients[:, 17] = behind.real, behind.imag
    for first, orientation in ((2, 1.0), (9, -1.0)):
        middle_real, middle_imag = derivative(128, orientation)
        for at, number in ((first, low), (first + 3, high)):
            real, imag = derivative(number, orientation)
            coefficients[:, at] = real
            coefficients[:, at + 1] = np.where((low == 0), 0.0, imag)
            coefficients[:, at + 2] = np.where((low == 0), middle_real, real)
        coefficients[:, first + 6] = np.where((low == 0), middle_imag, 0.0)
    return {
        "x_waves": packed_table(np.concatenate([spectrum.real, spectrum.imag], axis=0)),
        "x_rows": x_rows,
        "y_ahead": packed_table(derivative_matrix(NY, 1.0)),
        "y_behind": packed_table(derivative_matrix(NY, -1.0)),
        "y_waves": packed_table(np.cos(angle) + np.sin(angle)),
        "z_from_slabs": packed_table(forward_z[:, slab_order]),
        "z_to_pairs": packed_table(inverse_z),
        "z_from_pairs": packed_table(forward_z),
        "z_to_slabs": packed_table(inverse_z[slab_order]),
        "columns": coefficients,
    }


TABLES = make_tables()


def pieces(x, axis):
    high = x.astype(bf16)
    low = (x - high.astype(f32)).astype(bf16)
    return jnp.concatenate([high, low, high], axis=axis)


def contract(a, b, a_dim, b_dim):
    return lax.dot_general(a, b, (((a_dim,), (b_dim,)), ((), ())), preferred_element_type=f32)


def wide(table_ref):
    table = table_ref[...]
    return jnp.concatenate([table[:, :256], table], axis=1)


def tall(table_ref):
    table = table_ref[...]
    return jnp.concatenate([table[:, :256], table[:, :256], table[:, 256:]], axis=0)


def left(table_ref, x):
    return contract(wide(table_ref), pieces(x, 0), 1, 0)


def right(x, table_ref):
    return contract(pieces(x, 1), tall(table_ref), 1, 0)


def to_components(table_ref, lines):
    return contract(wide(table_ref), pieces(lines, 1), 1, 1)


class Fetch:
    def __init__(self, sources, targets, semaphores):
        self.targets = targets
        self.copies = [
            pltpu.make_async_copy(source, target, semaphores.at[i])
            for i, (source, target) in enumerate(zip(sources, targets))
        ]
        for copy in self.copies:
            copy.start()

    def __getitem__(self, i):
        if self.copies[i] is not None:
            self.copies[i].wait()
            self.copies[i] = None
        return self.targets[i]


def times(real, imag, factor_real, factor_imag):
    return real * factor_real - imag * factor_imag, real * factor_imag + imag * factor_real


def kappa_rows(kx, part):
    kz = lax.broadcasted_iota(jnp.int32, (HALF, NY), 0)
    ky = lax.broadcasted_iota(jnp.int32, (HALF, NY), 1)
    number = kz - 256 * (part // 2)
    if part % 2:
        number = jnp.where(kz == 0, 128, number)
    wave_z = number.astype(f32) * (2.0 * math.pi / NZ)
    wave_y = jnp.where(ky < NY // 2, ky, ky - NY).astype(f32) * (2.0 * math.pi / NY)
    wave_x = jnp.full((HALF, NY), kx, jnp.int32).astype(f32) * (2.0 * math.pi / NX)
    square = (kappa_courant / 2.0) ** 2 * (wave_x * wave_x + wave_z * wave_z + wave_y * wave_y)
    total = jnp.full((HALF, NY), 1.0 / math.factorial(15), f32)
    for order in range(6, -1, -1):
        total = 1.0 / math.factorial(2 * order + 1) - square * total
    return total


def forward_z(table_ref, coefficient, fields):
    sides = [side for field in fields for side in (field[:256], field[256:])]
    sums = left(table_ref, jnp.concatenate(sides, axis=1))
    cosine, sine = coefficient(0), coefficient(1)
    spectra = []
    for i in range(0, len(sides), 2):
        even = sums[:, NY * i : NY * (i + 1)]
        odd = sums[:, NY * (i + 1) : NY * (i + 2)]
        real = cosine * odd[:HALF] + sine * odd[HALF:]
        imag = cosine * odd[HALF:] - sine * odd[:HALF]
        spectra.append(
            [even[:HALF] + real, even[HALF:] + imag, even[:HALF] - real, even[HALF:] - imag]
        )
    return spectra


def inverse_z(table_ref, coefficient, spectra):
    cosine, sine = coefficient(0), coefficient(1)
    sides = []
    for a, b, c, d in spectra:
        real, imag = a - c, b - d
        sides.append(jnp.concatenate([a + c, b + d], axis=0))
        sides.append(jnp.concatenate([cosine * real - sine * imag, cosine * imag + sine * real], axis=0))
    return left(table_ref, jnp.concatenate(sides, axis=1))


def derivative_z(coefficient, first, spectrum):
    a, b, c, d = spectrum
    mixed = coefficient(first + 6)
    return [
        coefficient(first) * a - coefficient(first + 1) * b,
        coefficient(first + 2) * b + coefficient(first + 1) * a - mixed * d,
        coefficient(first + 3) * c - coefficient(first + 4) * d,
        coefficient(first + 5) * d + coefficient(first + 4) * c + mixed * b,
    ]


def blocks_of(x):
    return [x[HALF * i : HALF * (i + 1)] for i in range(4)]


def first_half():
    return lax.broadcasted_iota(jnp.int32, (64, HALF), 1) < ROWS


def forward_lines_kernel(pressure, x_ref, out):
    components = to_components(x_ref, pressure[...].reshape(512, NX)) * X_SCALE
    for i in range(4):
        out[pl.ds(i, 256, stride=4), :] = components[:, HALF * i : HALF * (i + 1)]


def filter_out_kernel(where, data, y_ref, z_from_ref, z_to_ref, numbers, out, plane):
    early = first_half()
    for pair in range(4):
        for side in range(2):
            a = data[pl.ds(8 * side + pair, 64, stride=16), :]
            b = data[pl.ds(8 * side + 4 + pair, 64, stride=16), :]
            span = pl.ds(HALF * side, HALF)
            plane[pl.ds(64 * pair, 64), span] = jnp.where(early, a, pltpu.roll(b, ROWS, 1))
            plane[pl.ds(256 + 64 * pair, 64), span] = jnp.where(early, pltpu.roll(a, ROWS, 1), b)
    mixed = right(plane[...], y_ref)

    def coefficient(i):
        return numbers[:, i : i + 1]

    (spectrum,) = forward_z(z_from_ref, coefficient, [mixed])
    scale = SLOPE_LINK / (NZ * NY)
    waves = [x * (kappa_rows(where[0] % HALF, part) * scale) for part, x in enumerate(spectrum)]
    waves = blocks_of(right(jnp.concatenate(waves, axis=0), y_ref))
    planes = inverse_z(z_to_ref, coefficient, [waves, derivative_z(coefficient, 2, waves)])
    for field in range(2):
        for r in range(2):
            for side in range(2):
                start = NY * (2 * field + r) + HALF * side
                out[pl.ds(4 * r + 2 * field + side, 256, stride=8), :] = planes[
                    :, start : start + HALF
                ]


def middle_kernel(
    where, data, x_ref, rows, ya_ref, yb_ref, columns, velocity, buoyancy, *rest
):
    blocks, (slopes, out, held, fields, semaphores) = rest[:3], rest[3:]
    own = pl.ds(2 * where[0], 2)
    starts = [
        pl.ds(pl.multiple_of(((where[0] + PEERS_Y - back) % PEERS_Y) * ROWS, ROWS), ROWS)
        for back in range(PEERS_Y)
    ]
    fetch = Fetch(
        (velocity.at[:, own], buoyancy.at[own], *blocks),
        (
            fields.at[pl.ds(0, 3), :, starts[0]],
            fields.at[3, :, starts[0]],
            *[fields.at[:, :, start] for start in starts[1:]],
        ),
        semaphores,
    )
    weight, ahead_real, ahead_imag = rows[0:1, :], rows[1:2, :], rows[2:3, :]
    behind = columns[:, 16:17], columns[:, 17:18]
    returned = []
    for r in range(2):
        q, g = [
            jnp.concatenate(
                [data[pl.ds(4 * r + 2 * field + side, 256, stride=8), :] for side in range(2)], axis=1
            )
            for field in range(2)
        ]
        lines = []
        for x, slope in ((q, True), (q, False), (g, False)):
            x = x.T
            real, imag = x[:, :HALF], x[:, HALF:]
            if slope:
                real, imag = (
                    ahead_real * real - ahead_imag * imag,
                    ahead_real * imag + ahead_imag * real,
                )
            else:
                real, imag = weight * real, weight * imag
            lines.append(jnp.concatenate([real, imag], axis=1))
        lines = right(jnp.concatenate(lines, axis=0), x_ref) * X_SCALE
        along = (lines[:NY], left(ya_ref, lines[NY : 2 * NY]), lines[2 * NY :])
        if r == 0:
            for i in range(5):
                fetch[i]
        moved = []
        for d, slope in enumerate(along):
            held[r, d] = slope
            moved.append(fields[d, r] - fields[3, r] * (slope * (1.0 / SLOPE_LINK)))
        returned.append(pltpu.make_async_copy(held.at[r], slopes.at[:, r], semaphores.at[5 + r]))
        returned[r].start()
        lines = jnp.concatenate([moved[0], left(yb_ref, moved[1]), moved[2]], axis=0)
        components = to_components(x_ref, lines) * (X_SCALE * MIDDLE_LINK)
        real, imag = components[:HALF, :NY], components[HALF:, :NY]
        across = jnp.concatenate(
            times(real, imag, behind[0], behind[1]), axis=0
        ) + components[:, NY : 2 * NY]
        for field, components in enumerate((across, components[:, 2 * NY :])):
            for side in range(2):
                out[pl.ds(4 * r + 2 * field + side, 256, stride=8), :] = components[
                    :, HALF * side : HALF * (side + 1)
                ]
    for copy in returned:
        copy.wait()


def filter_back_kernel(where, data, y_ref, z_from_ref, z_to_ref, numbers, out):
    arrived = [
        jnp.concatenate(
            [
                jnp.concatenate(
                    [data[pl.ds(4 * r + 2 * field + side, 256, stride=8), :] for side in range(2)],
                    axis=1,
                )
                for r in range(2)
            ],
            axis=0,
        )
        for field in range(2)
    ]
    def coefficient(i):
        return numbers[:, i : i + 1]

    across, along = forward_z(z_from_ref, coefficient, arrived)
    waves = [x + z for x, z in zip(across, derivative_z(coefficient, 9, along))]
    waves = blocks_of(right(jnp.concatenate(waves, axis=0), y_ref))
    scale = DIVERGENCE_LINK / MIDDLE_LINK / (NZ * NY)
    waves = [x * (kappa_rows(where[0] % HALF, part) * scale) for part, x in enumerate(waves)]
    waves = blocks_of(right(jnp.concatenate(waves, axis=0), y_ref))
    plane = inverse_z(z_to_ref, coefficient, [waves])
    early = first_half()
    for pair in range(4):
        for side in range(2):
            rows = slice(64 * pair, 64 * (pair + 1))
            even = plane[rows, HALF * side : HALF * (side + 1)]
            odd = plane[rows, NY + HALF * side : NY + HALF * (side + 1)]
            out[pl.ds(8 * side + pair, 64, stride=16), :] = jnp.where(
                early, even, pltpu.roll(odd, ROWS, 1)
            )
            out[pl.ds(8 * side + 4 + pair, 64, stride=16), :] = jnp.where(
                early, pltpu.roll(even, ROWS, 1), odd
            )


def new_pressure_kernel(data, x_ref, pressure, bulk, own, passed, out, held, semaphores):
    row = lax.broadcasted_iota(jnp.int32, (256, HALF), 0)
    weight = jnp.where((row & (HALF - 1)) == 0, 1.0, 2.0) * (X_SCALE / DIVERGENCE_LINK)
    components = [(data[pl.ds(i, 256, stride=4), :] * weight).T for i in range(4)]
    lines = right(jnp.concatenate(components, axis=0), x_ref).reshape(SLAB, ROWS, NX)
    sent = []
    for i in range(4):
        planes = pl.ds(2 * i, 2)
        source = own[planes].astype(f32)
        held[planes] = pressure[planes] - bulk[planes] * lines[2 * i : 2 * i + 2] + source
        held[planes, :TILE] += passed[planes].astype(f32)
        sent.append(pltpu.make_async_copy(held.at[planes], out.at[planes], semaphores.at[i]))
        sent[i].start()
    for copy in sent:
        copy.wait()


def source_kernel(where, lives, corner, tiles, here, after, beyond, lifted):
    lifted[:SLAB] = jnp.zeros((SLAB, 256, NX), bf16)
    lifted[2 * SLAB :] = jnp.zeros((SLAB, 256, NX), bf16)

    def place(slot, carry):
        rows = pl.ds(pl.multiple_of(slot * TILE, TILE), TILE)
        lane = lax.broadcasted_iota(jnp.int32, (TILE, NX), 1)
        line = lax.broadcasted_iota(jnp.int32, (TILE, NX), 0)
        hot = ((lane - line - corner[slot, 2]) & (NX - 1)) == 0
        hot = jnp.where(hot, 1.0, 0.0).astype(bf16)
        block = tiles[slot].reshape(2 * SLAB * TILE, TILE)
        across = jnp.dot(block, hot, preferred_element_type=f32).astype(bf16)
        planes = pl.ds(corner[slot, 0] & (SLAB - 1), 2 * SLAB)
        lifted[planes, rows, :] = across.reshape(2 * SLAB, TILE, NX)
        return carry

    lax.fori_loop(0, SLOTS_HERE, place, 0)
    line = lax.broadcasted_iota(jnp.int32, (ROWS + TILE, 256), 0)
    lane = lax.broadcasted_iota(jnp.int32, (ROWS + TILE, 256), 1)
    start = jnp.full((ROWS + TILE, 256), -2 * TILE, jnp.int32)
    for slot in range(SLOTS_HERE):
        row = corner[slot, 1] - where[1] * ROWS - slot * TILE
        row = jnp.where(slot < lives[where[0] * PEERS_Y + where[1]], row, -2 * NX)
        start = jnp.where(lane // TILE == slot, lane + row, start)
    hot = jnp.where(line == start, 1.0, 0.0).astype(bf16)
    for group, out in enumerate((here, after, beyond)):
        for z in range(SLAB):
            window = jnp.dot(hot, lifted[SLAB * group + z], preferred_element_type=f32)
            out[z] = window.astype(bf16)


def source_sum_kernel(here, after, beyond, own, passed):
    total = here[...].astype(f32) + after[...].astype(f32) + beyond[...].astype(f32)
    own[...] = total[:, :ROWS].astype(bf16)
    passed[...] = total[:, ROWS:].astype(bf16)


VMEM = pl.BlockSpec(memory_space=pltpu.VMEM)
SMEM = pl.BlockSpec(memory_space=pltpu.SMEM)
FAR = pl.BlockSpec(memory_space=pltpu.HBM)


def call(kernel, name, specs, arrays, shapes, outs, scratch=(), semaphores=0, limit=20):
    scratch = [pltpu.VMEM(shape, kind) for shape, kind in scratch]
    if semaphores:
        scratch.append(pltpu.SemaphoreType.DMA((semaphores,)))
    return pl.pallas_call(
        kernel,
        out_shape=[jax.ShapeDtypeStruct(shape, kind) for shape, kind in shapes],
        in_specs=specs,
        out_specs=outs,
        scratch_shapes=scratch,
        compiler_params=pltpu.CompilerParams(vmem_limit_bytes=limit << 20),
        cost_estimate=pl.CostEstimate(flops=int(4e8), bytes_accessed=1 << 20, transcendentals=0),
        name=name,
    )(*arrays)


def from_behind(x, axis, by):
    peers = lax.axis_size(axis)
    return lax.ppermute(x, axis, [(i, (i + by) % peers) for i in range(peers)])


def to_rows(slopes, row_block):
    blocks = [
        lax.dynamic_slice_in_dim(slopes, ROWS * ((row_block + ahead) % PEERS_Y), ROWS, 2)
        for ahead in range(PEERS_Y)
    ]
    arrived = [blocks[0]] + [from_behind(blocks[ahead], "gy", ahead) for ahead in range(1, PEERS_Y)]
    ordered = [
        lax.select_n((row_block - device) % PEERS_Y, *arrived) for device in range(PEERS_Y)
    ]
    return jnp.concatenate(ordered, 1).astype(f32)


def exchange(columns, rows):
    blocks = columns.astype(f16).reshape(256, rows, HALF)
    return lax.all_to_all(blocks, ("gz", "gy"), 0, 0, tiled=True)


def arrived(moved):
    return moved.reshape(-1, HALF).astype(f32)


def local(pressure, velocity, bulk, buoyancy, tiles, tile_corner, live_count):
    slab_index = lax.axis_index("gz")
    row_block = lax.axis_index("gy")
    here = row_block.reshape(1).astype(jnp.int32)
    device = (slab_index * PEERS_Y + row_block).astype(jnp.int32)
    place = jnp.stack([slab_index, row_block]).astype(jnp.int32)
    table = {key: jnp.asarray(value) for key, value in TABLES.items()}

    (components,) = call(
        forward_lines_kernel,
        "forward_lines",
        [VMEM, VMEM],
        [pressure, table["x_waves"]],
        [((1024, HALF), f32)],
        [VMEM],
    )
    velocity_later, buoyancy_later, tiles, device_later, components = lax.optimization_barrier(
        (velocity, buoyancy, tiles, device, components)
    )
    fields = jnp.concatenate([velocity_later, buoyancy_later[None]])
    sent = [
        lax.dynamic_slice_in_dim(fields, 2 * ((row_block + ahead) % PEERS_Y), 2, 1).astype(f16)
        for ahead in range(1, PEERS_Y)
    ]
    first, third = from_behind(sent[0], "gy", 1), from_behind(sent[2], "gy", 3)
    moved, second = lax.optimization_barrier((exchange(components, 4), sent[1]))
    (filtered,) = call(
        filter_out_kernel,
        "filter_out",
        [SMEM] + [VMEM] * 5,
        [
            device.reshape(1),
            arrived(moved),
            table["y_waves"],
            table["z_from_slabs"],
            table["z_to_pairs"],
            table["columns"],
        ],
        [((2048, HALF), f32)],
        [VMEM],
        [((NZ, NY), f32)],
    )
    filtered, tiles, device_later, first, second, third = lax.optimization_barrier(
        (filtered, tiles, device_later, first, second, third)
    )
    second = from_behind(second, "gy", 2)
    corner = lax.dynamic_slice_in_dim(tile_corner, device_later * SLOTS_HERE, SLOTS_HERE, 0)
    window = ((SLAB, ROWS + TILE, NX), bf16)
    source, after, beyond = call(
        source_kernel,
        "source",
        [SMEM, SMEM, SMEM, VMEM],
        [place, live_count, corner, tiles],
        [window] * 3,
        [VMEM] * 3,
        [((3 * SLAB, 256, NX), bf16)],
    )
    after, beyond = from_behind(after, "gz", 1), from_behind(beyond, "gz", 2)
    moved, source = lax.optimization_barrier((exchange(filtered, 8), source))
    slopes, middle = call(
        middle_kernel,
        "middle",
        [SMEM] + [VMEM] * 6 + [FAR] * 5,
        [
            here,
            arrived(moved),
            table["x_waves"],
            table["x_rows"],
            table["y_ahead"],
            table["y_behind"],
            table["columns"],
            velocity,
            buoyancy,
            *[block.astype(f32) for block in (first, second, third)],
        ],
        [((3, 2, NY, NX), f32), ((2048, HALF), f32)],
        [FAR, VMEM],
        [((2, 3, NY, NX), f32), ((4, 2, NY, NX), f32)],
        7,
    )
    middle, slopes = lax.optimization_barrier((middle, slopes.astype(f16)))
    slopes = to_rows(slopes, row_block)
    new_velocity = velocity - buoyancy[None] * (slopes * (1.0 / SLOPE_LINK))
    (filtered_back,) = call(
        filter_back_kernel,
        "filter_back",
        [SMEM] + [VMEM] * 5,
        [
            device.reshape(1),
            arrived(exchange(middle, 8)),
            table["y_waves"],
            table["z_from_pairs"],
            table["z_to_slabs"],
            table["columns"],
        ],
        [((1024, HALF), f32)],
        [VMEM],
    )
    filtered_back, source, after, beyond = lax.optimization_barrier(
        (filtered_back, source, after, beyond)
    )
    own, passed = call(
        source_sum_kernel,
        "source_sum",
        [VMEM] * 3,
        [source, after, beyond],
        [((SLAB, ROWS, NX), bf16), ((SLAB, TILE, NX), bf16)],
        [VMEM] * 2,
    )
    passed = from_behind(passed, "gy", 1)
    moved, new_velocity = lax.optimization_barrier((exchange(filtered_back, 4), new_velocity))
    (new_pressure,) = call(
        new_pressure_kernel,
        "new_pressure",
        [VMEM] * 6,
        [arrived(moved), table["x_waves"], pressure, bulk, own, passed],
        [((SLAB, ROWS, NX), f32)],
        [FAR],
        [((SLAB, ROWS, NX), f32)],
        4,
    )
    return (new_pressure, new_velocity)


def solution(mesh):
    in_specs = (
        P("gz", "gy", None),
        P(None, "gz", "gy", None),
        P("gz", "gy", None),
        P("gz", "gy", None),
        P(("gz", "gy"), None, None, None),
        P(),
        P(),
    )
    out_specs = (P("gz", "gy", None), P(None, "gz", "gy", None))
    return jax.shard_map(local, mesh=mesh, in_specs=in_specs, out_specs=out_specs, check_vma=False)
```

time: 157 us -> 138 us (0.88)
  waiting for transfers between devices: 47.4 us -> 41.2 us
  Pallas kernels: 20.5 us -> 15 us
  local copies, waits for them, and re-layouts: 13.2 us -> 7.95 us
  other arithmetic: 17.6 us -> 15.3 us
    ppermute x9, waiting for transfers between devices: 27.4 us -> 7.19 us  [from_behind(): return lax.ppermute(x, axis, [(i, (i + by) % peers) for i in range(peers)])]
    all_to_all x4, waiting for transfers between devices: 20 us -> 34 us  [exchange(): return lax.all_to_all(blocks, ('gz', 'gy'), 0, 0, tiled=True)]
    pallas_call x7, Pallas kernels: 20.5 us -> 15 us  [call(): pl.pallas_call(kernel, out_shape=[jax.ShapeDtypeStruct(shape, kind) for s...]
    unnamed x66 -> x57, local copies, waits for them, and re-layouts: 10.4 us -> 5.9 us
    optimization_barrier x1 -> x0, local copies, waits for them, and re-layouts: 2.1 us -> none  [local(): lax.optimization_barrier((filtered, first, third, sent[1], tiles, tile_co...]
    convert_element_type x3 -> x4, other arithmetic: 4.19 us -> 3.84 us  [the longest x3 2.82 us: local(): block.astype(f32)]
  transfers between devices with their start and end apart: 13 -> 13, of which waited for: 5 -> 6; matrix products, arithmetic and copies ran while one was open for 9% -> 9% of each run, Pallas kernels for 7% -> 7%
where the time goes in v5:
time: 138 us; the launch traced here: 137 us
  starting transfers between devices  56.2 us (41%)
  waiting for transfers between devices  41.2 us (30%)
  other arithmetic  15.3 us (11%)
  Pallas kernels  15 us (11%)
  local copies, waits for them, and re-layouts  7.95 us (6%)
    all_to_all x4, starting transfers between devices, exchange(): return lax.all_to_all(blocks, ('gz', 'gy'), 0, 0, tiled=True)  41.4 us
    all_to_all x4, waiting for transfers between devices, exchange(): return lax.all_to_all(blocks, ('gz', 'gy'), 0, 0, tiled=True)  34 us
    pallas_call x7, Pallas kernels, call(): pl.pallas_call(kernel, out_shape=[jax.ShapeDtypeStruct(shape, kind) for s...  15 us
    ppermute x9, starting transfers between devices, from_behind(): return lax.ppermute(x, axis, [(i, (i + by) % peers) for i in range(peers)])  14.8 us
    ppermute x9, waiting for transfers between devices, from_behind(): return lax.ppermute(x, axis, [(i, (i + by) % peers) for i in range(peers)])  7.19 us
    unnamed x57, local copies, waits for them, and re-layouts  5.9 us
    convert_element_type x4, other arithmetic, arrived(): return moved.reshape(-1, HALF).astype(f32)  3.33 us
    convert_element_type x3, other arithmetic, local(): block.astype(f32)  2.82 us
  transfers between devices with their start and end apart: 13, of which 6 were waited for; matrix products, arithmetic and copies ran while one was open for 9% of the time, Pallas kernels for 7%

profile of v5, /device:TPU:1, one launch (start us, length us, event | category | flops | bytes accessed | tf_op | source)
XLA Modules:
  0.0 136.9 jit_solution(1019543779801738488)
XLA Ops:
  4.0 15.7 %all-to-all-start = ((f16[256,4,128]{2,1,0:T(4,128)(2,1)}), f16[256,4,128]{2,1,0:T(4,128)(2,1)S(1)}, u32[]{:S(2)}, u32[]{:S(2)}) async-start(f16[256,4,128]{2,1,0:T(4,128)(2,1)} %bitcast.2), calls=%async_computation | async-start | bytes 524288 | tf_op jit(solution)/shard_map/all_to_all | solution.py:454
  20.7 1.4 %collective-permute-start = (f16[4,2,64,256]{3,2,1,0:T(8,128)(2,1)}, f16[4,2,64,256]{3,2,1,0:T(8,128)(2,1)S(1)}, u32[]{:S(2)}, u32[]{:S(2)}) collective-permute-start(f16[4,2,64,256]{3,2,1,0:T(8,128)(2,1)} %get-tuple-element.64), channel_id=1, source_target_pairs={{0,1},{1,2},{2,3},{3,0},{4,5},{5,6},{6,7},{7,4},{8,9},{9,10},{10,1... | collective-permute-start | bytes 786440 | tf_op jit(solution)/shard_map/ppermute | solution.py:437
  22.1 1.3 collective-permute-start.1
  23.4 11.5 %all-to-all-done = f16[256,4,128]{2,1,0:T(4,128)(2,1)S(1)} async-done(((f16[256,4,128]{2,1,0:T(4,128)(2,1)}), f16[256,4,128]{2,1,0:T(4,128)(2,1)S(1)}, u32[]{:S(2)}, u32[]{:S(2)}) %all-to-all-start) | async-done | bytes 262176 | tf_op jit(solution)/shard_map/all_to_all | solution.py:454
  35.0 2.6 %filter_out.1 = f32[2048,128]{1,0:T(8,128)S(1)} custom-call(s32[1]{0:T(128)} %bitcast.where, f32[1024,128]{1,0:T(8,128)S(1)} %convert.4.data, bf16[256,512]{1,0:T(8,128)(2,1)S(1)} %copy-done.6, bf16[256,512]{1,0:T(8,128)(2,1)S(1)} %copy-done.16, bf16[256,512]{1,0:T(8,128)(2,1)S(1)} %copy-done.17, f32[128,128]{1,0:T(8,128)S(1)} %copy-done.8), custom_call_target="tpu_custom_call" | custom-call | flops 400000000 | bytes 1048576 | tf_op jit(solution)/shard_map/filter_out/pallas_call | solution.py:423
  38.5 7.9 %all-to-all-start.1 = ((f16[256,8,128]{2,1,0:T(8,128)(2,1)}), f16[256,8,128]{2,1,0:T(8,128)(2,1)}, u32[]{:S(2)}, u32[]{:S(2)}) async-start(f16[256,8,128]{2,1,0:T(8,128)(2,1)} %convert_bitcast_fusion.1), calls=%async_computation.1 | async-start | bytes 1048576 | tf_op jit(solution)/shard_map/all_to_all | solution.py:454
  46.4 3.0 %collective-permute-start.2 = (f16[4,2,64,256]{3,2,1,0:T(8,128)(2,1)}, f16[4,2,64,256]{3,2,1,0:T(8,128)(2,1)}, u32[]{:S(2)}, u32[]{:S(2)}) collective-permute-start(f16[4,2,64,256]{3,2,1,0:T(8,128)(2,1)} %get-tuple-element.45), channel_id=1, source_target_pairs={{0,2},{1,3},{2,0},{3,1},{4,6},{5,7},{6,4},{7,5},{8,10},{9,11},{10,... | collective-permute-start | bytes 786440 | tf_op jit(solution)/shard_map/ppermute | solution.py:437
  51.9 3.1 %source.1 = (bf16[8,96,256]{2,1,0:T(8,128)(2,1)S(1)}, bf16[8,96,256]{2,1,0:T(8,128)(2,1)S(1)}, bf16[8,96,256]{2,1,0:T(8,128)(2,1)S(1)}) custom-call(s32[2]{0:T(128)S(1)} %pad_add_fusion.where, s32[256]{0:T(256)S(1)} %copy-done.24, s32[8,3]{1,0:T(8,128)S(1)} %copy.20.corner, bf16[8,16,32,32]{3,2,1,0:T(8,128)(2,1)S(1)} %copy-done.19), custom_call_target="tpu_custom_call" | custom-call | flops 400000000 | bytes 1048576 | tf_op jit(solution)/shard_map/source/pallas_call | solution.py:423
  57.2 1.5 %collective-permute-done.2 = f16[4,2,64,256]{3,2,1,0:T(8,128)(2,1)} collective-permute-done((f16[4,2,64,256]{3,2,1,0:T(8,128)(2,1)}, f16[4,2,64,256]{3,2,1,0:T(8,128)(2,1)}, u32[]{:S(2)}, u32[]{:S(2)}) %collective-permute-start.2) | collective-permute-done | bytes 262176 | tf_op jit(solution)/shard_map/ppermute | solution.py:437
  58.7 1.8 %convert_element_type.66.rest_1_ = f32[4,2,64,256]{3,2,1,0:T(8,128)} convert(f16[4,2,64,256]{3,2,1,0:T(8,128)(2,1)} %collective-permute-done.2) | non-fusion elementwise | flops 131072 | bytes 786432 | tf_op jit(solution)/shard_map/convert_element_type | solution.py:534
  60.5 5.0 %all-to-all-done.1 = f16[256,8,128]{2,1,0:T(8,128)(2,1)} async-done(((f16[256,8,128]{2,1,0:T(8,128)(2,1)}), f16[256,8,128]{2,1,0:T(8,128)(2,1)}, u32[]{:S(2)}, u32[]{:S(2)}) %all-to-all-start.1) | async-done | bytes 524320 | tf_op jit(solution)/shard_map/all_to_all | solution.py:454
  66.8 4.2 %middle.1 = (f32[3,2,256,256]{3,2,1,0:T(8,128)S(1)}, f32[2048,128]{1,0:T(8,128)S(1)}) custom-call(s32[1]{0:T(128)} %bitcast.1.where, f32[2048,128]{1,0:T(8,128)S(1)} %bitcast_convert_fusion.1.data, bf16[256,512]{1,0:T(8,128)(2,1)S(1)} %copy-done.5, f32[8,128]{1,0:T(8,128)S(1)} %copy-done.18, bf16[256,512]{1,0:T(8,128)(2,1)S(1)} %copy-done.12, ...), custom_call_target="tpu_custom_call" | custom-call | flops 400000000 | bytes 1048576 | tf_op jit(solution)/shard_map/middle/pallas_call | solution.py:423
  72.9 10.1 %all-to-all-start.2 = ((f16[256,8,128]{2,1,0:T(8,128)(2,1)}), f16[256,8,128]{2,1,0:T(8,128)(2,1)}, u32[]{:S(2)}, u32[]{:S(2)}) async-start(f16[256,8,128]{2,1,0:T(8,128)(2,1)} %convert_bitcast_fusion), calls=%async_computation.2 | async-start | bytes 1048576 | tf_op jit(solution)/shard_map/all_to_all | solution.py:454
  84.0 1.7 %collective-permute-start.3 = (bf16[8,96,256]{2,1,0:T(8,128)(2,1)S(1)}, bf16[8,96,256]{2,1,0:T(8,128)(2,1)}, u32[]{:S(2)}, u32[]{:S(2)}) collective-permute-start(bf16[8,96,256]{2,1,0:T(8,128)(2,1)S(1)} %copy-done.23), channel_id=1, source_target_pairs={{0,4},{4,8},{8,12},{12,16},{16,20},{20,24},{24,28},{28,32},{32,36}... | collective-permute-start | bytes 1179656 | tf_op jit(solution)/shard_map/ppermute | solution.py:437
  86.9 2.0 %constant_dynamic-slice_fusion.2 = (f16[3,2,64,256]{3,2,1,0:T(8,128)(2,1)}, f16[3,2,64,256]{3,2,1,0:T(8,128)(2,1)}, f16[3,2,64,256]{3,2,1,0:T(8,128)(2,1)}) fusion(f16[3,2,256,256]{3,2,1,0:T(8,128)(2,1)} %convert_element_type.68, s32[]{:T(128)S(6)} %select_n.184, s32[]{:T(128)S(6)} %select_n.189, s32[]{:T(128)S(6)} %select_n.188), kind=kLoop, calls=%fused_computation.24 | loop fusion | bytes 1179660 | tf_op jit(solution)/shard_map/dynamic_slice | solution.py:442
  90.0 2.5 %collective-permute-start.6 = (f16[3,2,64,256]{3,2,1,0:T(8,128)(2,1)}, f16[3,2,64,256]{3,2,1,0:T(8,128)(2,1)}, u32[]{:S(2)}, u32[]{:S(2)}) collective-permute-start(f16[3,2,64,256]{3,2,1,0:T(8,128)(2,1)} %get-tuple-element.71), channel_id=1, source_target_pairs={{0,2},{1,3},{2,0},{3,1},{4,6},{5,7},{6,4},{7,5},{8,10},{9,11},{10,... | collective-permute-start | bytes 589832 | tf_op jit(solution)/shard_map/ppermute | solution.py:437
  93.6 9.0 %all-to-all-done.2 = f16[256,8,128]{2,1,0:T(8,128)(2,1)} async-done(((f16[256,8,128]{2,1,0:T(8,128)(2,1)}), f16[256,8,128]{2,1,0:T(8,128)(2,1)}, u32[]{:S(2)}, u32[]{:S(2)}) %all-to-all-start.2) | async-done | bytes 524320 | tf_op jit(solution)/shard_map/all_to_all | solution.py:454
  103.8 2.3 %filter_back.1 = f32[1024,128]{1,0:T(8,128)S(1)} custom-call(s32[1]{0:T(128)} %bitcast.where, f32[2048,128]{1,0:T(8,128)S(1)} %bitcast_convert_fusion.data, bf16[256,512]{1,0:T(8,128)(2,1)S(1)} %copy-done.7, bf16[256,512]{1,0:T(8,128)(2,1)S(1)} %copy-done.14, bf16[256,512]{1,0:T(8,128)(2,1)S(1)} %copy-done.15, f32[128,128]{1,0:T(8,128)S(1)} %copy-done.8), custom_call_target="tpu_custom_call" | custom-call | flops 400000000 | bytes 1048576 | tf_op jit(solution)/shard_map/filter_back/pallas_call | solution.py:423
  106.1 5.7 %collective-permute-done.4.beyond = bf16[8,96,256]{2,1,0:T(8,128)(2,1)} collective-permute-done((bf16[8,96,256]{2,1,0:T(8,128)(2,1)S(1)}, bf16[8,96,256]{2,1,0:T(8,128)(2,1)}, u32[]{:S(2)}, u32[]{:S(2)}) %collective-permute-start.4) | collective-permute-done | bytes 393248 | tf_op jit(solution)/shard_map/ppermute | solution.py:437
  112.6 7.7 %all-to-all-start.3 = ((f16[256,4,128]{2,1,0:T(4,128)(2,1)}), f16[256,4,128]{2,1,0:T(4,128)(2,1)}, u32[]{:S(2)}, u32[]{:S(2)}) async-start(f16[256,4,128]{2,1,0:T(4,128)(2,1)} %bitcast.10), calls=%async_computation.3 | async-start | bytes 524288 | tf_op jit(solution)/shard_map/all_to_all | solution.py:454
  120.3 1.6 %select_select_fusion.3 = (f16[3,2,64,256]{3,2,1,0:T(8,128)(2,1)S(1)}, f16[3,2,64,256]{3,2,1,0:T(8,128)(2,1)S(1)}, f16[3,2,64,256]{3,2,1,0:T(8,128)(2,1)S(1)}, f16[3,2,64,256]{3,2,1,0:T(8,128)(2,1)S(1)}) fusion(f16[3,2,64,256]{3,2,1,0:T(8,128)(2,1)} %collective-permute-done.6, f16[3,2,64,256]{3,2,1,0:T(8,128)(2,1)} %collective-permute-done.7, ...), kind=kLoop, calls=%fused_computation.21 | loop fusion | flops 1179648 | bytes 1572880 | tf_op jit(solution)/shard_map/select_n | solution.py:447
  123.2 1.5 %collective-permute-start.8 = (bf16[8,32,256]{2,1,0:T(8,128)(2,1)S(1)}, bf16[8,32,256]{2,1,0:T(8,128)(2,1)S(1)}, u32[]{:S(2)}, u32[]{:S(2)}) collective-permute-start(bf16[8,32,256]{2,1,0:T(8,128)(2,1)S(1)} %get-tuple-element.60), channel_id=1, source_target_pairs={{0,1},{1,2},{2,3},{3,0},{4,5},{5,6},{6,7},{7,4},{8,9},{9,10},{10,1... | collective-permute-start | bytes 393224 | tf_op jit(solution)/shard_map/ppermute | solution.py:437
  124.6 1.5 %multiply_subtract_fusion = f32[3,8,64,256]{3,2,1,0:T(8,128)} fusion(f32[3,8,64,256]{3,2,1,0:T(8,128)S(1)} %copy-done.1, f16[3,2,64,256]{3,2,1,0:T(8,128)(2,1)S(1)} %get-tuple-element.66, f16[3,2,64,256]{3,2,1,0:T(8,128)(2,1)S(1)} %get-tuple-element.67, f16[3,2,64,256]{3,2,1,0:T(8,128)(2,1)S(1)} %get-tuple-element.68, ...), kind=kLoop, calls=%fused_computation.6 | loop fusion | flops 2359296 | bytes 4456448 | tf_op jit(solution)/shard_map/sub | solution.py:543
  126.2 8.5 %all-to-all-done.3 = f16[256,4,128]{2,1,0:T(4,128)(2,1)} async-done(((f16[256,4,128]{2,1,0:T(4,128)(2,1)}), f16[256,4,128]{2,1,0:T(4,128)(2,1)}, u32[]{:S(2)}, u32[]{:S(2)}) %all-to-all-start.3) | async-done | bytes 262176 | tf_op jit(solution)/shard_map/all_to_all | solution.py:454
  (85 shorter events, 22.7 us)
Async XLA Ops:
  0.6 48.8 %copy-start = (s32[2048,3]{0,1:T(4,128)S(1)}, s32[2048,3]{0,1:T(4,128)}, u32[]{:S(2)}) copy-start(s32[2048,3]{0,1:T(4,128)} %param.22) | copy-start | bytes 73732
  0.6 19.0 %copy-start.1 = (f32[3,8,64,256]{3,2,1,0:T(8,128)S(1)}, f32[3,8,64,256]{3,2,1,0:T(8,128)}, u32[]{:S(2)}) copy-start(f32[3,8,64,256]{3,2,1,0:T(8,128)} %velocity.1) | copy-start | bytes 4718596
  0.7 19.0 %copy-start.2 = (f32[8,64,256]{2,1,0:T(8,128)S(1)}, f32[8,64,256]{2,1,0:T(8,128)}, u32[]{:S(2)}) copy-start(f32[8,64,256]{2,1,0:T(8,128)} %buoyancy.1) | copy-start | bytes 1572868
  4.0 30.9 %all-to-all-start = ((f16[256,4,128]{2,1,0:T(4,128)(2,1)}), f16[256,4,128]{2,1,0:T(4,128)(2,1)S(1)}, u32[]{:S(2)}, u32[]{:S(2)}) async-start(f16[256,4,128]{2,1,0:T(4,128)(2,1)} %bitcast.2), calls=%async_computation | async-start | bytes 524288 | tf_op jit(solution)/shard_map/all_to_all | solution.py:454
  19.7 15.3 %copy-start.6 = (bf16[256,512]{1,0:T(8,128)(2,1)S(1)}, bf16[256,512]{1,0:T(8,128)(2,1)}, u32[]{:S(2)}) copy-start(bf16[256,512]{1,0:T(8,128)(2,1)} %constant.100.clone.y_ref) | copy-start | bytes 786436
  19.7 15.3 %copy-start.8 = (f32[128,128]{1,0:T(8,128)S(1)}, f32[128,128]{1,0:T(8,128)}, u32[]{:S(2)}) copy-start(f32[128,128]{1,0:T(8,128)} %constant.105.clone.numbers.columns) | copy-start | bytes 196612
  19.7 15.2 %copy-start.16 = (bf16[256,512]{1,0:T(8,128)(2,1)S(1)}, bf16[256,512]{1,0:T(8,128)(2,1)}, u32[]{:S(2)}) copy-start(bf16[256,512]{1,0:T(8,128)(2,1)} %constant.101.clone.z_from_ref) | copy-start | bytes 786436
  19.7 15.2 %copy-start.17 = (bf16[256,512]{1,0:T(8,128)(2,1)S(1)}, bf16[256,512]{1,0:T(8,128)(2,1)}, u32[]{:S(2)}) copy-start(bf16[256,512]{1,0:T(8,128)(2,1)} %constant.102.clone.z_to_ref) | copy-start | bytes 786436
  20.7 16.9 %collective-permute-start = (f16[4,2,64,256]{3,2,1,0:T(8,128)(2,1)}, f16[4,2,64,256]{3,2,1,0:T(8,128)(2,1)S(1)}, u32[]{:S(2)}, u32[]{:S(2)}) collective-permute-start(f16[4,2,64,256]{3,2,1,0:T(8,128)(2,1)} %get-tuple-element.64), channel_id=1, source_target_pairs={{0,1},{1,2},{2,3},{3,0},{4,5},{5,6},{6,7},{7,4},{8,9},{9,10},{10,1... | collective-permute-start | bytes 786440 | tf_op jit(solution)/shard_map/ppermute | solution.py:437
  22.1 15.5 %collective-permute-start.1 = (f16[4,2,64,256]{3,2,1,0:T(8,128)(2,1)}, f16[4,2,64,256]{3,2,1,0:T(8,128)(2,1)}, u32[]{:S(2)}, u32[]{:S(2)}) collective-permute-start(f16[4,2,64,256]{3,2,1,0:T(8,128)(2,1)} %get-tuple-element.62), channel_id=1, source_target_pairs={{0,3},{1,0},{2,1},{3,2},{4,7},{5,4},{6,5},{7,6},{8,11},{9,8},{10,9... | collective-permute-start | bytes 786440 | tf_op jit(solution)/shard_map/ppermute | solution.py:437
  38.5 27.0 %all-to-all-start.1 = ((f16[256,8,128]{2,1,0:T(8,128)(2,1)}), f16[256,8,128]{2,1,0:T(8,128)(2,1)}, u32[]{:S(2)}, u32[]{:S(2)}) async-start(f16[256,8,128]{2,1,0:T(8,128)(2,1)} %convert_bitcast_fusion.1), calls=%async_computation.1 | async-start | bytes 1048576 | tf_op jit(solution)/shard_map/all_to_all | solution.py:454
  46.4 12.3 %collective-permute-start.2 = (f16[4,2,64,256]{3,2,1,0:T(8,128)(2,1)}, f16[4,2,64,256]{3,2,1,0:T(8,128)(2,1)}, u32[]{:S(2)}, u32[]{:S(2)}) collective-permute-start(f16[4,2,64,256]{3,2,1,0:T(8,128)(2,1)} %get-tuple-element.45), channel_id=1, source_target_pairs={{0,2},{1,3},{2,0},{3,1},{4,6},{5,7},{6,4},{7,5},{8,10},{9,11},{10,... | collective-permute-start | bytes 786440 | tf_op jit(solution)/shard_map/ppermute | solution.py:437
  72.9 29.8 %all-to-all-start.2 = ((f16[256,8,128]{2,1,0:T(8,128)(2,1)}), f16[256,8,128]{2,1,0:T(8,128)(2,1)}, u32[]{:S(2)}, u32[]{:S(2)}) async-start(f16[256,8,128]{2,1,0:T(8,128)(2,1)} %convert_bitcast_fusion), calls=%async_computation.2 | async-start | bytes 1048576 | tf_op jit(solution)/shard_map/all_to_all | solution.py:454
  84.0 19.8 %copy-start.7 = (bf16[256,512]{1,0:T(8,128)(2,1)S(1)}, bf16[256,512]{1,0:T(8,128)(2,1)}, u32[]{:S(2)}) copy-start(bf16[256,512]{1,0:T(8,128)(2,1)} %constant.100.clone.y_ref) | copy-start | bytes 786436
  84.0 19.8 %copy-start.14 = (bf16[256,512]{1,0:T(8,128)(2,1)S(1)}, bf16[256,512]{1,0:T(8,128)(2,1)}, u32[]{:S(2)}) copy-start(bf16[256,512]{1,0:T(8,128)(2,1)} %constant.103.clone.z_from_ref) | copy-start | bytes 786436
  84.0 19.8 %copy-start.15 = (bf16[256,512]{1,0:T(8,128)(2,1)S(1)}, bf16[256,512]{1,0:T(8,128)(2,1)}, u32[]{:S(2)}) copy-start(bf16[256,512]{1,0:T(8,128)(2,1)} %constant.104.clone.z_to_ref) | copy-start | bytes 786436
  84.0 22.2 %collective-permute-start.3 = (bf16[8,96,256]{2,1,0:T(8,128)(2,1)S(1)}, bf16[8,96,256]{2,1,0:T(8,128)(2,1)}, u32[]{:S(2)}, u32[]{:S(2)}) collective-permute-start(bf16[8,96,256]{2,1,0:T(8,128)(2,1)S(1)} %copy-done.23), channel_id=1, source_target_pairs={{0,4},{4,8},{8,12},{12,16},{16,20},{20,24},{24,28},{28,32},{32,36}... | collective-permute-start | bytes 1179656 | tf_op jit(solution)/shard_map/ppermute | solution.py:437
  85.7 26.1 %collective-permute-start.4 = (bf16[8,96,256]{2,1,0:T(8,128)(2,1)S(1)}, bf16[8,96,256]{2,1,0:T(8,128)(2,1)}, u32[]{:S(2)}, u32[]{:S(2)}) collective-permute-start(bf16[8,96,256]{2,1,0:T(8,128)(2,1)S(1)} %copy-done.21), channel_id=1, source_target_pairs={{0,8},{4,12},{8,16},{12,20},{16,24},{20,28},{24,32},{28,36},{32,40... | collective-permute-start | bytes 1179656 | tf_op jit(solution)/shard_map/ppermute | solution.py:437
  88.9 31.5 %collective-permute-start.5 = (f16[3,2,64,256]{3,2,1,0:T(8,128)(2,1)}, f16[3,2,64,256]{3,2,1,0:T(8,128)(2,1)}, u32[]{:S(2)}, u32[]{:S(2)}) collective-permute-start(f16[3,2,64,256]{3,2,1,0:T(8,128)(2,1)} %get-tuple-element.69), channel_id=1, source_target_pairs={{0,1},{1,2},{2,3},{3,0},{4,5},{5,6},{6,7},{7,4},{8,9},{9,10},{10,1... | collective-permute-start | bytes 589832 | tf_op jit(solution)/shard_map/ppermute | solution.py:437
  90.0 30.3 %collective-permute-start.6 = (f16[3,2,64,256]{3,2,1,0:T(8,128)(2,1)}, f16[3,2,64,256]{3,2,1,0:T(8,128)(2,1)}, u32[]{:S(2)}, u32[]{:S(2)}) collective-permute-start(f16[3,2,64,256]{3,2,1,0:T(8,128)(2,1)} %get-tuple-element.71), channel_id=1, source_target_pairs={{0,2},{1,3},{2,0},{3,1},{4,6},{5,7},{6,4},{7,5},{8,10},{9,11},{10,... | collective-permute-start | bytes 589832 | tf_op jit(solution)/shard_map/ppermute | solution.py:437
  92.5 27.8 %collective-permute-start.7 = (f16[3,2,64,256]{3,2,1,0:T(8,128)(2,1)}, f16[3,2,64,256]{3,2,1,0:T(8,128)(2,1)}, u32[]{:S(2)}, u32[]{:S(2)}) collective-permute-start(f16[3,2,64,256]{3,2,1,0:T(8,128)(2,1)} %get-tuple-element.70), channel_id=1, source_target_pairs={{0,3},{1,0},{2,1},{3,2},{4,7},{5,4},{6,5},{7,6},{8,11},{9,8},{10,9... | collective-permute-start | bytes 589832 | tf_op jit(solution)/shard_map/ppermute | solution.py:437
  106.1 15.8 %copy-start.26 = (bf16[8,96,256]{2,1,0:T(8,128)(2,1)S(1)}, bf16[8,96,256]{2,1,0:T(8,128)(2,1)}, u32[]{:S(2)}) copy-start(bf16[8,96,256]{2,1,0:T(8,128)(2,1)} %copy-done.25) | copy-start | bytes 1179652
  112.6 22.0 %all-to-all-start.3 = ((f16[256,4,128]{2,1,0:T(4,128)(2,1)}), f16[256,4,128]{2,1,0:T(4,128)(2,1)}, u32[]{:S(2)}, u32[]{:S(2)}) async-start(f16[256,4,128]{2,1,0:T(4,128)(2,1)} %bitcast.10), calls=%async_computation.3 | async-start | bytes 524288 | tf_op jit(solution)/shard_map/all_to_all | solution.py:454
  123.2 12.4 %collective-permute-start.8 = (bf16[8,32,256]{2,1,0:T(8,128)(2,1)S(1)}, bf16[8,32,256]{2,1,0:T(8,128)(2,1)S(1)}, u32[]{:S(2)}, u32[]{:S(2)}) collective-permute-start(bf16[8,32,256]{2,1,0:T(8,128)(2,1)S(1)} %get-tuple-element.60), channel_id=1, source_target_pairs={{0,1},{1,2},{2,3},{3,0},{4,5},{5,6},{6,7},{7,4},{8,9},{9,10},{10,1... | collective-permute-start | bytes 393224 | tf_op jit(solution)/shard_map/ppermute | solution.py:437
  (17 other events, 103.1 us)

commit v6 on v5

--- a/solution.py
+++ b/solution.py
@@ -25,9 +25,12 @@
 f16 = jnp.float16
 
 X_SCALE = 1.0 / 16.0
-SLOPE_LINK = 0.25
-MIDDLE_LINK = 1.0 / 16.0
-DIVERGENCE_LINK = 1.0 / 32.0
+FIELD_LINK = 4096.0
+COMPONENT_LINK = 256.0
+SLOPE_LINK = 128.0
+RETURN_LINK = 1024.0
+MIDDLE_LINK = 16.0
+DIVERGENCE_LINK = 8.0
 
 
 def split_table(table):
@@ -88,17 +91,25 @@
             coefficients[:, at + 1] = np.where((low == 0), 0.0, imag)
             coefficients[:, at + 2] = np.where((low == 0), middle_real, real)
         coefficients[:, first + 6] = np.where((low == 0), middle_imag, 0.0)
+    x_waves = packed_table(np.concatenate([spectrum.real, spectrum.imag], axis=0))
+    y_waves = packed_table(np.cos(angle) + np.sin(angle))
     return {
-        "x_waves": packed_table(np.concatenate([spectrum.real, spectrum.imag], axis=0)),
-        "x_rows": x_rows,
-        "y_ahead": packed_table(derivative_matrix(NY, 1.0)),
-        "y_behind": packed_table(derivative_matrix(NY, -1.0)),
-        "y_waves": packed_table(np.cos(angle) + np.sin(angle)),
-        "z_from_slabs": packed_table(forward_z[:, slab_order]),
-        "z_to_pairs": packed_table(inverse_z),
-        "z_from_pairs": packed_table(forward_z),
-        "z_to_slabs": packed_table(inverse_z[slab_order]),
-        "columns": coefficients,
+        "x_waves": x_waves,
+        "middle": np.concatenate(
+            [
+                x_waves,
+                packed_table(derivative_matrix(NY, 1.0)),
+                packed_table(derivative_matrix(NY, -1.0)),
+            ],
+            axis=1,
+        ),
+        "filter_out": np.concatenate(
+            [y_waves, packed_table(forward_z[:, slab_order]), packed_table(inverse_z)], axis=1
+        ),
+        "filter_back": np.concatenate(
+            [y_waves, packed_table(forward_z), packed_table(inverse_z[slab_order])], axis=1
+        ),
+        "numbers": np.concatenate([coefficients, x_rows], axis=0),
     }
 
 
@@ -115,14 +126,12 @@
     return lax.dot_general(a, b, (((a_dim,), (b_dim,)), ((), ())), preferred_element_type=f32)
 
 
-def wide(table_ref):
-    table = table_ref[...]
-    return jnp.concatenate([table[:, :256], table], axis=1)
-
-
-def tall(table_ref):
-    table = table_ref[...]
-    return jnp.concatenate([table[:, :256], table[:, :256], table[:, 256:]], axis=0)
+def wide(table):
+    return jnp.concatenate([table[:, :256], table[:, :512]], axis=1)
+
+
+def tall(table):
+    return jnp.concatenate([table[:, :256], table[:, :256], table[:, 256:512]], axis=0)
 
 
 def left(table_ref, x):
@@ -220,12 +229,13 @@
 
 
 def forward_lines_kernel(pressure, x_ref, out):
-    components = to_components(x_ref, pressure[...].reshape(512, NX)) * X_SCALE
+    components = to_components(x_ref, pressure[...].reshape(512, NX)) * (X_SCALE * COMPONENT_LINK)
     for i in range(4):
         out[pl.ds(i, 256, stride=4), :] = components[:, HALF * i : HALF * (i + 1)]
 
 
-def filter_out_kernel(where, data, y_ref, z_from_ref, z_to_ref, numbers, out, plane):
+def filter_out_kernel(where, data, tables, numbers, out, plane):
+    y_ref, z_from_ref, z_to_ref = (tables[:, 512 * i : 512 * (i + 1)] for i in range(3))
     early = first_half()
     for pair in range(4):
         for side in range(2):
@@ -237,10 +247,10 @@
     mixed = right(plane[...], y_ref)
 
     def coefficient(i):
-        return numbers[:, i : i + 1]
+        return numbers[:HALF, i : i + 1]
 
     (spectrum,) = forward_z(z_from_ref, coefficient, [mixed])
-    scale = SLOPE_LINK / (NZ * NY)
+    scale = SLOPE_LINK / COMPONENT_LINK / (NZ * NY)
     waves = [x * (kappa_rows(where[0] % HALF, part) * scale) for part, x in enumerate(spectrum)]
     waves = blocks_of(right(jnp.concatenate(waves, axis=0), y_ref))
     planes = inverse_z(z_to_ref, coefficient, [waves, derivative_z(coefficient, 2, waves)])
@@ -254,7 +264,7 @@
 
 
 def middle_kernel(
-    where, data, x_ref, rows, ya_ref, yb_ref, columns, velocity, buoyancy, *rest
+    where, data, tables, numbers, velocity, buoyancy, *rest
 ):
     blocks, (slopes, out, held, fields, semaphores) = rest[:3], rest[3:]
     own = pl.ds(2 * where[0], 2)
@@ -271,8 +281,9 @@
         ),
         semaphores,
     )
-    weight, ahead_real, ahead_imag = rows[0:1, :], rows[1:2, :], rows[2:3, :]
-    behind = columns[:, 16:17], columns[:, 17:18]
+    x_ref, ya_ref, yb_ref = (tables[:, 512 * i : 512 * (i + 1)] for i in range(3))
+    weight, ahead_real, ahead_imag = (numbers[HALF + i : HALF + i + 1, :] for i in range(3))
+    behind = numbers[:HALF, 16:17], numbers[:HALF, 17:18]
     returned = []
     for r in range(2):
         q, g = [
@@ -293,15 +304,15 @@
             else:
                 real, imag = weight * real, weight * imag
             lines.append(jnp.concatenate([real, imag], axis=1))
-        lines = right(jnp.concatenate(lines, axis=0), x_ref) * X_SCALE
+        lines = right(jnp.concatenate(lines, axis=0), x_ref) * (X_SCALE / SLOPE_LINK)
         along = (lines[:NY], left(ya_ref, lines[NY : 2 * NY]), lines[2 * NY :])
         if r == 0:
             for i in range(5):
                 fetch[i]
         moved = []
         for d, slope in enumerate(along):
-            held[r, d] = slope
-            moved.append(fields[d, r] - fields[3, r] * (slope * (1.0 / SLOPE_LINK)))
+            held[r, d] = slope * RETURN_LINK
+            moved.append(fields[d, r] - fields[3, r] * slope)
         returned.append(pltpu.make_async_copy(held.at[r], slopes.at[:, r], semaphores.at[5 + r]))
         returned[r].start()
         lines = jnp.concatenate([moved[0], left(yb_ref, moved[1]), moved[2]], axis=0)
@@ -319,7 +330,8 @@
         copy.wait()
 
 
-def filter_back_kernel(where, data, y_ref, z_from_ref, z_to_ref, numbers, out):
+def filter_back_kernel(where, data, tables, numbers, out):
+    y_ref, z_from_ref, z_to_ref = (tables[:, 512 * i : 512 * (i + 1)] for i in range(3))
     arrived = [
         jnp.concatenate(
             [
@@ -334,7 +346,7 @@
         for field in range(2)
     ]
     def coefficient(i):
-        return numbers[:, i : i + 1]
+        return numbers[:HALF, i : i + 1]
 
     across, along = forward_z(z_from_ref, coefficient, arrived)
     waves = [x + z for x, z in zip(across, derivative_z(coefficient, 9, along))]
@@ -357,7 +369,7 @@
             )
 
 
-def new_pressure_kernel(data, x_ref, pressure, bulk, own, passed, out, held, semaphores):
+def new_pressure_kernel(data, x_ref, bulk, own, passed, out, held, semaphores):
     row = lax.broadcasted_iota(jnp.int32, (256, HALF), 0)
     weight = jnp.where((row & (HALF - 1)) == 0, 1.0, 2.0) * (X_SCALE / DIVERGENCE_LINK)
     components = [(data[pl.ds(i, 256, stride=4), :] * weight).T for i in range(4)]
@@ -365,8 +377,7 @@
     sent = []
     for i in range(4):
         planes = pl.ds(2 * i, 2)
-        source = own[planes].astype(f32)
-        held[planes] = pressure[planes] - bulk[planes] * lines[2 * i : 2 * i + 2] + source
+        held[planes] = own[planes] - bulk[planes] * lines[2 * i : 2 * i + 2]
         held[planes, :TILE] += passed[planes].astype(f32)
         sent.append(pltpu.make_async_copy(held.at[planes], out.at[planes], semaphores.at[i]))
         sent[i].start()
@@ -374,41 +385,49 @@
         copy.wait()
 
 
-def source_kernel(where, lives, corner, tiles, here, after, beyond, lifted):
-    lifted[:SLAB] = jnp.zeros((SLAB, 256, NX), bf16)
-    lifted[2 * SLAB :] = jnp.zeros((SLAB, 256, NX), bf16)
+def source_kernel(where, lives, c0, c1, c2, t0, t1, t2, pressure, own, passed, l0, l1, l2):
+    blank = jnp.zeros((SLAB, 256, NX), bf16)
+    l0[:SLAB] = blank
+    l2[SLAB:] = blank
+    corners = (c0, c1, c2)
 
     def place(slot, carry):
         rows = pl.ds(pl.multiple_of(slot * TILE, TILE), TILE)
-        lane = lax.broadcasted_iota(jnp.int32, (TILE, NX), 1)
-        line = lax.broadcasted_iota(jnp.int32, (TILE, NX), 0)
-        hot = ((lane - line - corner[slot, 2]) & (NX - 1)) == 0
-        hot = jnp.where(hot, 1.0, 0.0).astype(bf16)
-        block = tiles[slot].reshape(2 * SLAB * TILE, TILE)
-        across = jnp.dot(block, hot, preferred_element_type=f32).astype(bf16)
-        planes = pl.ds(corner[slot, 0] & (SLAB - 1), 2 * SLAB)
-        lifted[planes, rows, :] = across.reshape(2 * SLAB, TILE, NX)
+        lane = lax.broadcasted_iota(jnp.int32, (HALF, NX), 1)
+        line = lax.broadcasted_iota(jnp.int32, (HALF, NX), 0) & (TILE - 1)
+        quarter = lax.broadcasted_iota(jnp.int32, (SLAB, 8, HALF), 2) // TILE
+        for reach, (tiles, placed) in enumerate(((t0, l0), (t1, l1), (t2, l2))):
+            offset = corners[reach][slot, 0] & (SLAB - 1)
+            hot = ((lane - line - corners[reach][slot, 2]) & (NX - 1)) == 0
+            hot = jnp.where(hot, 1.0, 0.0).astype(bf16)
+            first = SLAB - offset if reach == 1 else 0
+            to = 0 if reach == 1 else offset
+            block = tiles[slot, pl.ds(first, SLAB)].astype(f32)
+            block = jnp.stack([jnp.where(quarter == i, block, 0.0) for i in range(4)], axis=1)
+            block = block.reshape(SLAB * TILE, HALF).astype(bf16)
+            across = jnp.dot(block, hot, preferred_element_type=f32).astype(bf16)
+            placed[pl.ds(to, SLAB), rows, :] = across.reshape(SLAB, TILE, NX)
         return carry
 
     lax.fori_loop(0, SLOTS_HERE, place, 0)
     line = lax.broadcasted_iota(jnp.int32, (ROWS + TILE, 256), 0)
     lane = lax.broadcasted_iota(jnp.int32, (ROWS + TILE, 256), 1)
-    start = jnp.full((ROWS + TILE, 256), -2 * TILE, jnp.int32)
-    for slot in range(SLOTS_HERE):
-        row = corner[slot, 1] - where[1] * ROWS - slot * TILE
-        row = jnp.where(slot < lives[where[0] * PEERS_Y + where[1]], row, -2 * NX)
-        start = jnp.where(lane // TILE == slot, lane + row, start)
-    hot = jnp.where(line == start, 1.0, 0.0).astype(bf16)
-    for group, out in enumerate((here, after, beyond)):
-        for z in range(SLAB):
-            window = jnp.dot(hot, lifted[SLAB * group + z], preferred_element_type=f32)
-            out[z] = window.astype(bf16)
-
-
-def source_sum_kernel(here, after, beyond, own, passed):
-    total = here[...].astype(f32) + after[...].astype(f32) + beyond[...].astype(f32)
-    own[...] = total[:, :ROWS].astype(bf16)
-    passed[...] = total[:, ROWS:].astype(bf16)
+    hots = []
+    for reach in range(3):
+        sender = ((where[0] + PEERS_Z - reach) % PEERS_Z) * PEERS_Y + where[1]
+        start = jnp.full((ROWS + TILE, 256), -2 * TILE, jnp.int32)
+        for slot in range(SLOTS_HERE):
+            row = corners[reach][slot, 1] - where[1] * ROWS
+            row = jnp.where(slot < lives[sender], row, -2 * NX)
+            within = 4 * (lane & 7) + ((lane // 8) & 3)
+            start = jnp.where(lane // TILE == slot, within + row, start)
+        hots.append(jnp.where(line == start, 1.0, 0.0).astype(bf16))
+    for z in range(SLAB):
+        window = jnp.dot(hots[0], l0[z], preferred_element_type=f32)
+        window += jnp.dot(hots[1], l1[z], preferred_element_type=f32)
+        window += jnp.dot(hots[2], l2[SLAB + z], preferred_element_type=f32)
+        own[z] = pressure[z] + window[:ROWS]
+        passed[z] = window[ROWS:].astype(bf16)
 
 
 VMEM = pl.BlockSpec(memory_space=pltpu.VMEM)
@@ -474,106 +493,111 @@
         [((1024, HALF), f32)],
         [VMEM],
     )
-    velocity_later, buoyancy_later, tiles, device_later, components = lax.optimization_barrier(
-        (velocity, buoyancy, tiles, device, components)
+    velocity_later, buoyancy_later, tiles, slab_later, components = lax.optimization_barrier(
+        (velocity, buoyancy, tiles, slab_index, components)
     )
     fields = jnp.concatenate([velocity_later, buoyancy_later[None]])
     sent = [
-        lax.dynamic_slice_in_dim(fields, 2 * ((row_block + ahead) % PEERS_Y), 2, 1).astype(f16)
+        (
+            lax.dynamic_slice_in_dim(fields, 2 * ((row_block + ahead) % PEERS_Y), 2, 1) * FIELD_LINK
+        ).astype(f16)
         for ahead in range(1, PEERS_Y)
     ]
     first, third = from_behind(sent[0], "gy", 1), from_behind(sent[2], "gy", 3)
-    moved, second = lax.optimization_barrier((exchange(components, 4), sent[1]))
+    packed = tiles.reshape(SLOTS_HERE, 2 * SLAB, 8, HALF)
+    moved, second, packed, packed_end = lax.optimization_barrier(
+        (exchange(components, 4), sent[1], packed, packed[:, SLAB:])
+    )
     (filtered,) = call(
         filter_out_kernel,
         "filter_out",
-        [SMEM] + [VMEM] * 5,
+        [SMEM] + [VMEM] * 3,
         [
             device.reshape(1),
             arrived(moved),
-            table["y_waves"],
-            table["z_from_slabs"],
-            table["z_to_pairs"],
-            table["columns"],
+            table["filter_out"],
+            table["numbers"],
         ],
         [((2048, HALF), f32)],
         [VMEM],
         [((NZ, NY), f32)],
     )
-    filtered, tiles, device_later, first, second, third = lax.optimization_barrier(
-        (filtered, tiles, device_later, first, second, third)
+    filtered, first, second, third, packed, packed_end = lax.optimization_barrier(
+        (filtered, first, second, third, packed, packed_end)
     )
     second = from_behind(second, "gy", 2)
-    corner = lax.dynamic_slice_in_dim(tile_corner, device_later * SLOTS_HERE, SLOTS_HERE, 0)
-    window = ((SLAB, ROWS + TILE, NX), bf16)
-    source, after, beyond = call(
-        source_kernel,
-        "source",
-        [SMEM, SMEM, SMEM, VMEM],
-        [place, live_count, corner, tiles],
-        [window] * 3,
-        [VMEM] * 3,
-        [((3 * SLAB, 256, NX), bf16)],
-    )
-    after, beyond = from_behind(after, "gz", 1), from_behind(beyond, "gz", 2)
-    moved, source = lax.optimization_barrier((exchange(filtered, 8), source))
+    tiles_before, tiles_second = from_behind(packed, "gz", 1), from_behind(packed_end, "gz", 2)
+    moved = exchange(filtered, 8)
     slopes, middle = call(
         middle_kernel,
         "middle",
-        [SMEM] + [VMEM] * 6 + [FAR] * 5,
+        [SMEM] + [VMEM] * 3 + [FAR] * 5,
         [
             here,
             arrived(moved),
-            table["x_waves"],
-            table["x_rows"],
-            table["y_ahead"],
-            table["y_behind"],
-            table["columns"],
+            table["middle"],
+            table["numbers"],
             velocity,
             buoyancy,
-            *[block.astype(f32) for block in (first, second, third)],
+            *[block.astype(f32) * (1.0 / FIELD_LINK) for block in (first, second, third)],
         ],
         [((3, 2, NY, NX), f32), ((2048, HALF), f32)],
         [FAR, VMEM],
         [((2, 3, NY, NX), f32), ((4, 2, NY, NX), f32)],
         7,
     )
-    middle, slopes = lax.optimization_barrier((middle, slopes.astype(f16)))
+    middle, slopes, tiles_before, tiles_second = lax.optimization_barrier(
+        (middle, slopes.astype(f16), tiles_before, tiles_second)
+    )
     slopes = to_rows(slopes, row_block)
-    new_velocity = velocity - buoyancy[None] * (slopes * (1.0 / SLOPE_LINK))
+    new_velocity = velocity - buoyancy[None] * (slopes * (1.0 / RETURN_LINK))
+    corners = [
+        lax.dynamic_slice_in_dim(
+            tile_corner,
+            ((slab_later - reach) % PEERS_Z * PEERS_Y + row_block) * SLOTS_HERE,
+            SLOTS_HERE,
+            0,
+        )
+        for reach in range(3)
+    ]
+    own, passed = call(
+        source_kernel,
+        "source",
+        [SMEM] * 5 + [VMEM] * 4,
+        [
+            place,
+            live_count,
+            *corners,
+            packed,
+            tiles_before,
+            tiles_second,
+            pressure,
+        ],
+        [((SLAB, ROWS, NX), f32), ((SLAB, TILE, NX), bf16)],
+        [VMEM] * 2,
+        [((2 * SLAB, 256, NX), bf16), ((SLAB, 256, NX), bf16), ((2 * SLAB, 256, NX), bf16)],
+    )
     (filtered_back,) = call(
         filter_back_kernel,
         "filter_back",
-        [SMEM] + [VMEM] * 5,
+        [SMEM] + [VMEM] * 3,
         [
             device.reshape(1),
             arrived(exchange(middle, 8)),
-            table["y_waves"],
-            table["z_from_pairs"],
-            table["z_to_slabs"],
-            table["columns"],
+            table["filter_back"],
+            table["numbers"],
         ],
         [((1024, HALF), f32)],
         [VMEM],
     )
-    filtered_back, source, after, beyond = lax.optimization_barrier(
-        (filtered_back, source, after, beyond)
-    )
-    own, passed = call(
-        source_sum_kernel,
-        "source_sum",
-        [VMEM] * 3,
-        [source, after, beyond],
-        [((SLAB, ROWS, NX), bf16), ((SLAB, TILE, NX), bf16)],
-        [VMEM] * 2,
-    )
+    filtered_back, own, passed = lax.optimization_barrier((filtered_back, own, passed))
     passed = from_behind(passed, "gy", 1)
     moved, new_velocity = lax.optimization_barrier((exchange(filtered_back, 4), new_velocity))
     (new_pressure,) = call(
         new_pressure_kernel,
         "new_pressure",
-        [VMEM] * 6,
-        [arrived(moved), table["x_waves"], pressure, bulk, own, passed],
+        [VMEM] * 5,
+        [arrived(moved), table["x_waves"], bulk, own, passed],
         [((SLAB, ROWS, NX), f32)],
         [FAR],
         [((SLAB, ROWS, NX), f32)],

time: 138 us -> 129 us (0.935)
  waiting for transfers between devices: 41.2 us -> 35.6 us
  starting transfers between devices: 56.2 us -> 54.4 us
    all_to_all x4, waiting for transfers between devices: 34 us -> 30.3 us  [exchange(): return lax.all_to_all(blocks, ('gz', 'gy'), 0, 0, tiled=True)]
    convert_element_type x5 -> x2, other arithmetic: 4.77 us -> 1.11 us  [the longest x1 0.96 us: local(): sent = [(lax.dynamic_slice_in_dim(fields, 2 * ((row_block + ahead) % PEER...]
    unnamed x57 -> x31, local copies, waits for them, and re-layouts: 5.9 us -> 3.68 us
    all_to_all x4, starting transfers between devices: 41.4 us -> 39.4 us  [exchange(): return lax.all_to_all(blocks, ('gz', 'gy'), 0, 0, tiled=True)]
    mul x1 -> x3, other arithmetic: 0.85 us -> 2.82 us  [the longest x2 1.98 us: local(): block.astype(f32) * (1.0 / FIELD_LINK)]
    reshape x0 -> x1, local copies, waits for them, and re-layouts: none -> 1.93 us  [local(): packed = tiles.reshape(SLOTS_HERE, 2 * SLAB, 8, HALF)]
    ppermute x9, waiting for transfers between devices: 7.19 us -> 5.32 us  [from_behind(): return lax.ppermute(x, axis, [(i, (i + by) % peers) for i in range(peers)])]
    pallas_call x7 -> x6, Pallas kernels: 15 us -> 14.5 us  [call(): pl.pallas_call(kernel, out_shape=[jax.ShapeDtypeStruct(shape, kind) for s...]
  transfers between devices with their start and end apart: 13 -> 13, of which waited for: 6 -> 5; matrix products, arithmetic and copies ran while one was open for 9% -> 13% of each run, Pallas kernels for 7% -> 10%
where the time goes in v6:
time: 129 us
  starting transfers between devices  54.4 us (42%)
  waiting for transfers between devices  35.6 us (28%)
  other arithmetic  14.8 us (11%)
  Pallas kernels  14.5 us (11%)
  local copies, waits for them, and re-layouts  7.96 us (6%)
  between operations  1.3 us (1%)
    all_to_all x4, starting transfers between devices, exchange(): return lax.all_to_all(blocks, ('gz', 'gy'), 0, 0, tiled=True)  39.4 us
    all_to_all x4, waiting for transfers between devices, exchange(): return lax.all_to_all(blocks, ('gz', 'gy'), 0, 0, tiled=True)  30.3 us
    ppermute x9, starting transfers between devices, from_behind(): return lax.ppermute(x, axis, [(i, (i + by) % peers) for i in range(peers)])  15 us
    pallas_call x6, Pallas kernels, call(): pl.pallas_call(kernel, out_shape=[jax.ShapeDtypeStruct(shape, kind) for s...  14.5 us
    ppermute x9, waiting for transfers between devices, from_behind(): return lax.ppermute(x, axis, [(i, (i + by) % peers) for i in range(peers)])  5.32 us
    unnamed x31, local copies, waits for them, and re-layouts  3.68 us
    convert_element_type x4, other arithmetic, arrived(): return moved.reshape(-1, HALF).astype(f32)  3.35 us
    sub x1, other arithmetic, local(): new_velocity = velocity - buoyancy[None] * (slopes * (1.0 / RETURN_LINK))  2.59 us
  transfers between devices with their start and end apart: 13, of which 5 were waited for; matrix products, arithmetic and copies ran while one was open for 13% of the time, Pallas kernels for 10%

profile of v6, /device:TPU:1, one launch (start us, length us, event | category | flops | bytes accessed | tf_op | source)
XLA Modules:
  0.0 128.6 jit_solution(16216753342965998553)
XLA Ops:
  3.9 15.7 %all-to-all-start = ((f16[256,4,128]{2,1,0:T(4,128)(2,1)}), f16[256,4,128]{2,1,0:T(4,128)(2,1)S(1)}, u32[]{:S(2)}, u32[]{:S(2)}) async-start(f16[256,4,128]{2,1,0:T(4,128)(2,1)} %bitcast.2), calls=%async_computation | async-start | bytes 524288 | tf_op jit(solution)/shard_map/all_to_all | solution.py:473
  20.6 1.4 %collective-permute-start = (f16[4,2,64,256]{3,2,1,0:T(8,128)(2,1)}, f16[4,2,64,256]{3,2,1,0:T(8,128)(2,1)}, u32[]{:S(2)}, u32[]{:S(2)}) collective-permute-start(f16[4,2,64,256]{3,2,1,0:T(8,128)(2,1)} %get-tuple-element.60), channel_id=1, source_target_pairs={{0,1},{1,2},{2,3},{3,0},{4,5},{5,6},{6,7},{7,4},{8,9},{9,10},{10,1... | collective-permute-start | bytes 786440 | tf_op jit(solution)/shard_map/ppermute | solution.py:456
  22.0 1.3 %collective-permute-start.1 = (f16[4,2,64,256]{3,2,1,0:T(8,128)(2,1)}, f16[4,2,64,256]{3,2,1,0:T(8,128)(2,1)}, u32[]{:S(2)}, u32[]{:S(2)}) collective-permute-start(f16[4,2,64,256]{3,2,1,0:T(8,128)(2,1)} %get-tuple-element.58), channel_id=1, source_target_pairs={{0,3},{1,0},{2,1},{3,2},{4,7},{5,4},{6,5},{7,6},{8,11},{9,8},{10,9... | collective-permute-start | bytes 786440 | tf_op jit(solution)/shard_map/ppermute | solution.py:456
  23.4 1.9 %reshape.42.t0 = bf16[8,16,8,128]{3,2,1,0:T(8,128)(2,1)S(1)} reshape(bf16[8,16,32,32]{3,2,1,0:T(8,128)(2,1)} %param.16) | data formatting | bytes 524288 | tf_op jit(solution)/shard_map/reshape | solution.py:507
  26.0 8.9 %all-to-all-done = f16[256,4,128]{2,1,0:T(4,128)(2,1)S(1)} async-done(((f16[256,4,128]{2,1,0:T(4,128)(2,1)}), f16[256,4,128]{2,1,0:T(4,128)(2,1)S(1)}, u32[]{:S(2)}, u32[]{:S(2)}) %all-to-all-start) | async-done | bytes 262176 | tf_op jit(solution)/shard_map/all_to_all | solution.py:473
  34.9 2.6 %filter_out.1 = f32[2048,128]{1,0:T(8,128)S(1)} custom-call(s32[1]{0:T(128)} %bitcast.where, f32[1024,128]{1,0:T(8,128)S(1)} %convert.4.data, bf16[256,1536]{1,0:T(8,128)(2,1)S(1)} %copy-done.5, f32[136,128]{1,0:T(8,128)S(1)} %copy-done.6), custom_call_target="tpu_custom_call" | custom-call | flops 400000000 | bytes 1048576 | tf_op jit(solution)/shard_map/filter_out/pallas_call | solution.py:442
  38.5 7.9 %all-to-all-start.1 = ((f16[256,8,128]{2,1,0:T(8,128)(2,1)}), f16[256,8,128]{2,1,0:T(8,128)(2,1)}, u32[]{:S(2)}, u32[]{:S(2)}) async-start(f16[256,8,128]{2,1,0:T(8,128)(2,1)} %convert_bitcast_fusion.1), calls=%async_computation.1 | async-start | bytes 1048576 | tf_op jit(solution)/shard_map/all_to_all | solution.py:473
  46.3 3.0 %collective-permute-start.2 = (f16[4,2,64,256]{3,2,1,0:T(8,128)(2,1)}, f16[4,2,64,256]{3,2,1,0:T(8,128)(2,1)S(1)}, u32[]{:S(2)}, u32[]{:S(2)}) collective-permute-start(f16[4,2,64,256]{3,2,1,0:T(8,128)(2,1)} %get-tuple-element.40), channel_id=1, source_target_pairs={{0,2},{1,3},{2,0},{3,1},{4,6},{5,7},{6,4},{7,5},{8,10},{9,11},{10,... | collective-permute-start | bytes 786440 | tf_op jit(solution)/shard_map/ppermute | solution.py:456
  49.3 1.7 %collective-permute-start.3 = (bf16[8,16,8,128]{3,2,1,0:T(8,128)(2,1)S(1)}, bf16[8,16,8,128]{3,2,1,0:T(8,128)(2,1)}, u32[]{:S(2)}, u32[]{:S(2)}) collective-permute-start(bf16[8,16,8,128]{3,2,1,0:T(8,128)(2,1)S(1)} %reshape.42.t0), channel_id=1, source_target_pairs={{0,4},{4,8},{8,12},{12,16},{16,20},{20,24},{24,28},{28,32},{32,36}... | collective-permute-start | bytes 786440 | tf_op jit(solution)/shard_map/ppermute | solution.py:456
  53.4 5.3 %collective-permute-done.2 = f16[4,2,64,256]{3,2,1,0:T(8,128)(2,1)S(1)} collective-permute-done((f16[4,2,64,256]{3,2,1,0:T(8,128)(2,1)}, f16[4,2,64,256]{3,2,1,0:T(8,128)(2,1)S(1)}, u32[]{:S(2)}, u32[]{:S(2)}) %collective-permute-start.2) | collective-permute-done | bytes 262176 | tf_op jit(solution)/shard_map/ppermute | solution.py:456
  59.5 6.5 %all-to-all-done.1 = f16[256,8,128]{2,1,0:T(8,128)(2,1)} async-done(((f16[256,8,128]{2,1,0:T(8,128)(2,1)}), f16[256,8,128]{2,1,0:T(8,128)(2,1)}, u32[]{:S(2)}, u32[]{:S(2)}) %all-to-all-start.1) | async-done | bytes 524320 | tf_op jit(solution)/shard_map/all_to_all | solution.py:473
  66.0 1.2 bitcast_convert_fusion.1.data
  67.4 4.2 %middle.1 = (f32[3,2,256,256]{3,2,1,0:T(8,128)S(1)}, f32[2048,128]{1,0:T(8,128)S(1)}) custom-call(s32[1]{0:T(128)} %bitcast.1.where, f32[2048,128]{1,0:T(8,128)S(1)} %bitcast_convert_fusion.1.data, bf16[256,1536]{1,0:T(8,128)(2,1)S(1)} %copy-done.3, f32[136,128]{1,0:T(8,128)S(1)} %copy-done.6, f32[3,8,64,256]{3,2,1,0:T(8,128)S(1)} %copy-done, ...), custom_call_target="tpu_custom_call" | custom-call | flops 400000000 | bytes 1048576 | tf_op jit(solution)/shard_map/middle/pallas_call | solution.py:442
  72.8 8.5 %all-to-all-start.2 = ((f16[256,8,128]{2,1,0:T(8,128)(2,1)}), f16[256,8,128]{2,1,0:T(8,128)(2,1)}, u32[]{:S(2)}, u32[]{:S(2)}) async-start(f16[256,8,128]{2,1,0:T(8,128)(2,1)} %convert_bitcast_fusion), calls=%async_computation.2 | async-start | bytes 1048576 | tf_op jit(solution)/shard_map/all_to_all | solution.py:473
  84.3 1.4 %collective-permute-start.5 = (f16[3,2,64,256]{3,2,1,0:T(8,128)(2,1)}, f16[3,2,64,256]{3,2,1,0:T(8,128)(2,1)}, u32[]{:S(2)}, u32[]{:S(2)}) collective-permute-start(f16[3,2,64,256]{3,2,1,0:T(8,128)(2,1)} %get-tuple-element.65), channel_id=1, source_target_pairs={{0,1},{1,2},{2,3},{3,0},{4,5},{5,6},{6,7},{7,4},{8,9},{9,10},{10,1... | collective-permute-start | bytes 589832 | tf_op jit(solution)/shard_map/ppermute | solution.py:456
  85.7 2.4 %collective-permute-start.6 = (f16[3,2,64,256]{3,2,1,0:T(8,128)(2,1)}, f16[3,2,64,256]{3,2,1,0:T(8,128)(2,1)}, u32[]{:S(2)}, u32[]{:S(2)}) collective-permute-start(f16[3,2,64,256]{3,2,1,0:T(8,128)(2,1)} %get-tuple-element.67), channel_id=1, source_target_pairs={{0,2},{1,3},{2,0},{3,1},{4,6},{5,7},{6,4},{7,5},{8,10},{9,11},{10,... | collective-permute-start | bytes 589832 | tf_op jit(solution)/shard_map/ppermute | solution.py:456
  90.3 3.8 %source.1 = (f32[8,64,256]{2,1,0:T(8,128)S(1)}, bf16[8,32,256]{2,1,0:T(8,128)(2,1)S(1)}) custom-call(s32[2]{0:T(128)S(1)} %pad_add_fusion.where, s32[256]{0:T(256)S(1)} %copy-done.12, s32[8,3]{1,0:T(8,128)S(1)} %copy.17.c0, s32[8,3]{1,0:T(8,128)S(1)} %copy.18.c1, s32[8,3]{1,0:T(8,128)S(1)} %copy.19.c2, bf16[8,16,8,128]{3,2,1,0:T(8,128)(2,1)S(1)} %reshape.42.t0, ...), custom_call_target="tpu_custom_call" | custom-call | flops 400000000 | bytes 1048576 | tf_op jit(solution)/shard_map/source/pallas_call | solution.py:442
  94.2 6.2 %all-to-all-done.2 = f16[256,8,128]{2,1,0:T(8,128)(2,1)} async-done(((f16[256,8,128]{2,1,0:T(8,128)(2,1)}), f16[256,8,128]{2,1,0:T(8,128)(2,1)}, u32[]{:S(2)}, u32[]{:S(2)}) %all-to-all-start.2) | async-done | bytes 524320 | tf_op jit(solution)/shard_map/all_to_all | solution.py:473
  101.5 2.3 %filter_back.1 = f32[1024,128]{1,0:T(8,128)S(1)} custom-call(s32[1]{0:T(128)} %bitcast.where, f32[2048,128]{1,0:T(8,128)S(1)} %bitcast_convert_fusion.data, bf16[256,1536]{1,0:T(8,128)(2,1)S(1)} %copy-done.4, f32[136,128]{1,0:T(8,128)S(1)} %copy-done.6), custom_call_target="tpu_custom_call" | custom-call | flops 400000000 | bytes 1048576 | tf_op jit(solution)/shard_map/filter_back/pallas_call | solution.py:442
  104.6 7.4 %all-to-all-start.3 = ((f16[256,4,128]{2,1,0:T(4,128)(2,1)}), f16[256,4,128]{2,1,0:T(4,128)(2,1)}, u32[]{:S(2)}, u32[]{:S(2)}) async-start(f16[256,4,128]{2,1,0:T(4,128)(2,1)} %bitcast.10), calls=%async_computation.3 | async-start | bytes 524288 | tf_op jit(solution)/shard_map/all_to_all | solution.py:473
  112.0 1.5 %select_select_fusion.3 = (f16[3,2,64,256]{3,2,1,0:T(8,128)(2,1)S(1)}, f16[3,2,64,256]{3,2,1,0:T(8,128)(2,1)S(1)}, f16[3,2,64,256]{3,2,1,0:T(8,128)(2,1)S(1)}, f16[3,2,64,256]{3,2,1,0:T(8,128)(2,1)S(1)}) fusion(f16[3,2,64,256]{3,2,1,0:T(8,128)(2,1)} %collective-permute-done.6, f16[3,2,64,256]{3,2,1,0:T(8,128)(2,1)} %collective-permute-done.7, ...), kind=kLoop, calls=%fused_computation.27 | loop fusion | flops 1179648 | bytes 1572880 | tf_op jit(solution)/shard_map/select_n | solution.py:466
  113.6 1.5 %collective-permute-start.8 = (bf16[8,32,256]{2,1,0:T(8,128)(2,1)S(1)}, bf16[8,32,256]{2,1,0:T(8,128)(2,1)S(1)}, u32[]{:S(2)}, u32[]{:S(2)}) collective-permute-start(bf16[8,32,256]{2,1,0:T(8,128)(2,1)S(1)} %get-tuple-element.56), channel_id=1, source_target_pairs={{0,1},{1,2},{2,3},{3,0},{4,5},{5,6},{6,7},{7,4},{8,9},{9,10},{10,1... | collective-permute-start | bytes 393224 | tf_op jit(solution)/shard_map/ppermute | solution.py:456
  115.0 2.6 %multiply_subtract_fusion = f32[3,8,64,256]{3,2,1,0:T(8,128)} fusion(f32[3,8,64,256]{3,2,1,0:T(8,128)S(1)} %copy-done, f16[3,2,64,256]{3,2,1,0:T(8,128)(2,1)S(1)} %get-tuple-element.62, f16[3,2,64,256]{3,2,1,0:T(8,128)(2,1)S(1)} %get-tuple-element.63, f16[3,2,64,256]{3,2,1,0:T(8,128)(2,1)S(1)} %get-tuple-element.64, ...), kind=kLoop, calls=%fused_computation.6 | loop fusion | flops 2359296 | bytes 4456448 | tf_op jit(solution)/shard_map/sub | solution.py:553
  117.6 8.7 %all-to-all-done.3 = f16[256,4,128]{2,1,0:T(4,128)(2,1)} async-done(((f16[256,4,128]{2,1,0:T(4,128)(2,1)}), f16[256,4,128]{2,1,0:T(4,128)(2,1)}, u32[]{:S(2)}, u32[]{:S(2)}) %all-to-all-start.3) | async-done | bytes 262176 | tf_op jit(solution)/shard_map/all_to_all | solution.py:473
  (59 shorter events, 19.4 us)
Async XLA Ops:
  0.6 19.0 %copy-start = (f32[3,8,64,256]{3,2,1,0:T(8,128)S(1)}, f32[3,8,64,256]{3,2,1,0:T(8,128)}, u32[]{:S(2)}) copy-start(f32[3,8,64,256]{3,2,1,0:T(8,128)} %velocity.1) | copy-start | bytes 4718596
  0.6 19.0 %copy-start.1 = (f32[8,64,256]{2,1,0:T(8,128)S(1)}, f32[8,64,256]{2,1,0:T(8,128)}, u32[]{:S(2)}) copy-start(f32[8,64,256]{2,1,0:T(8,128)} %buoyancy.1) | copy-start | bytes 1572868
  3.9 30.9 %all-to-all-start = ((f16[256,4,128]{2,1,0:T(4,128)(2,1)}), f16[256,4,128]{2,1,0:T(4,128)(2,1)S(1)}, u32[]{:S(2)}, u32[]{:S(2)}) async-start(f16[256,4,128]{2,1,0:T(4,128)(2,1)} %bitcast.2), calls=%async_computation | async-start | bytes 524288 | tf_op jit(solution)/shard_map/all_to_all | solution.py:473
  20.6 14.3 %copy-start.5 = (bf16[256,1536]{1,0:T(8,128)(2,1)S(1)}, bf16[256,1536]{1,0:T(8,128)(2,1)}, u32[]{:S(2)}) copy-start(bf16[256,1536]{1,0:T(8,128)(2,1)} %constant.110.clone.tables) | copy-start | bytes 2359300
  20.6 14.3 %copy-start.6 = (f32[136,128]{1,0:T(8,128)S(1)}, f32[136,128]{1,0:T(8,128)}, u32[]{:S(2)}) copy-start(f32[136,128]{1,0:T(8,128)} %constant.112.clone.numbers) | copy-start | bytes 208900
  20.6 16.9 %collective-permute-start = (f16[4,2,64,256]{3,2,1,0:T(8,128)(2,1)}, f16[4,2,64,256]{3,2,1,0:T(8,128)(2,1)}, u32[]{:S(2)}, u32[]{:S(2)}) collective-permute-start(f16[4,2,64,256]{3,2,1,0:T(8,128)(2,1)} %get-tuple-element.60), channel_id=1, source_target_pairs={{0,1},{1,2},{2,3},{3,0},{4,5},{5,6},{6,7},{7,4},{8,9},{9,10},{10,1... | collective-permute-start | bytes 786440 | tf_op jit(solution)/shard_map/ppermute | solution.py:456
  22.0 15.6 %collective-permute-start.1 = (f16[4,2,64,256]{3,2,1,0:T(8,128)(2,1)}, f16[4,2,64,256]{3,2,1,0:T(8,128)(2,1)}, u32[]{:S(2)}, u32[]{:S(2)}) collective-permute-start(f16[4,2,64,256]{3,2,1,0:T(8,128)(2,1)} %get-tuple-element.58), channel_id=1, source_target_pairs={{0,3},{1,0},{2,1},{3,2},{4,7},{5,4},{6,5},{7,6},{8,11},{9,8},{10,9... | collective-permute-start | bytes 786440 | tf_op jit(solution)/shard_map/ppermute | solution.py:456
  38.5 27.5 %all-to-all-start.1 = ((f16[256,8,128]{2,1,0:T(8,128)(2,1)}), f16[256,8,128]{2,1,0:T(8,128)(2,1)}, u32[]{:S(2)}, u32[]{:S(2)}) async-start(f16[256,8,128]{2,1,0:T(8,128)(2,1)} %convert_bitcast_fusion.1), calls=%async_computation.1 | async-start | bytes 1048576 | tf_op jit(solution)/shard_map/all_to_all | solution.py:473
  46.3 12.3 %collective-permute-start.2 = (f16[4,2,64,256]{3,2,1,0:T(8,128)(2,1)}, f16[4,2,64,256]{3,2,1,0:T(8,128)(2,1)S(1)}, u32[]{:S(2)}, u32[]{:S(2)}) collective-permute-start(f16[4,2,64,256]{3,2,1,0:T(8,128)(2,1)} %get-tuple-element.40), channel_id=1, source_target_pairs={{0,2},{1,3},{2,0},{3,1},{4,6},{5,7},{6,4},{7,5},{8,10},{9,11},{10,... | collective-permute-start | bytes 786440 | tf_op jit(solution)/shard_map/ppermute | solution.py:456
  49.3 22.5 %collective-permute-start.3 = (bf16[8,16,8,128]{3,2,1,0:T(8,128)(2,1)S(1)}, bf16[8,16,8,128]{3,2,1,0:T(8,128)(2,1)}, u32[]{:S(2)}, u32[]{:S(2)}) collective-permute-start(bf16[8,16,8,128]{3,2,1,0:T(8,128)(2,1)S(1)} %reshape.42.t0), channel_id=1, source_target_pairs={{0,4},{4,8},{8,12},{12,16},{16,20},{20,24},{24,28},{28,32},{32,36}... | collective-permute-start | bytes 786440 | tf_op jit(solution)/shard_map/ppermute | solution.py:456
  51.0 20.8 %collective-permute-start.4 = (bf16[8,8,8,128]{3,2,1,0:T(8,128)(2,1)}, bf16[8,8,8,128]{3,2,1,0:T(8,128)(2,1)}, u32[]{:S(2)}, u32[]{:S(2)}) collective-permute-start(bf16[8,8,8,128]{3,2,1,0:T(8,128)(2,1)} %slice.4), channel_id=1, source_target_pairs={{0,8},{4,12},{8,16},{12,20},{16,24},{20,28},{24,32},{28,36},{32,40... | collective-permute-start | bytes 393224 | tf_op jit(solution)/shard_map/ppermute | solution.py:456
  66.0 1.2 copy-start.2
  66.0 1.4 %copy-start.3 = (bf16[256,1536]{1,0:T(8,128)(2,1)S(1)}, bf16[256,1536]{1,0:T(8,128)(2,1)}, u32[]{:S(2)}) copy-start(bf16[256,1536]{1,0:T(8,128)(2,1)} %constant.109.clone.tables) | copy-start | bytes 2359300
  71.8 11.7 %copy-start.13 = (f16[3,2,256,256]{3,2,1,0:T(8,128)(2,1)}, f16[3,2,256,256]{3,2,1,0:T(8,128)(2,1)S(1)}, u32[]{:S(2)}) copy-start(f16[3,2,256,256]{3,2,1,0:T(8,128)(2,1)S(1)} %convert_element_type.68) | copy-start | bytes 2359300
  72.8 16.5 %copy-start.12 = (s32[256]{0:T(256)S(1)}, s32[256]{0:T(256)}, u32[]{:S(2)}) copy-start(s32[256]{0:T(256)} %lives.1) | copy-start | bytes 3076
  72.8 27.6 %all-to-all-start.2 = ((f16[256,8,128]{2,1,0:T(8,128)(2,1)}), f16[256,8,128]{2,1,0:T(8,128)(2,1)}, u32[]{:S(2)}, u32[]{:S(2)}) async-start(f16[256,8,128]{2,1,0:T(8,128)(2,1)} %convert_bitcast_fusion), calls=%async_computation.2 | async-start | bytes 1048576 | tf_op jit(solution)/shard_map/all_to_all | solution.py:473
  84.3 17.2 %copy-start.4 = (bf16[256,1536]{1,0:T(8,128)(2,1)S(1)}, bf16[256,1536]{1,0:T(8,128)(2,1)}, u32[]{:S(2)}) copy-start(bf16[256,1536]{1,0:T(8,128)(2,1)} %constant.111.clone.tables) | copy-start | bytes 2359300
  84.3 27.7 %collective-permute-start.5 = (f16[3,2,64,256]{3,2,1,0:T(8,128)(2,1)}, f16[3,2,64,256]{3,2,1,0:T(8,128)(2,1)}, u32[]{:S(2)}, u32[]{:S(2)}) collective-permute-start(f16[3,2,64,256]{3,2,1,0:T(8,128)(2,1)} %get-tuple-element.65), channel_id=1, source_target_pairs={{0,1},{1,2},{2,3},{3,0},{4,5},{5,6},{6,7},{7,4},{8,9},{9,10},{10,1... | collective-permute-start | bytes 589832 | tf_op jit(solution)/shard_map/ppermute | solution.py:456
  85.7 26.3 %collective-permute-start.6 = (f16[3,2,64,256]{3,2,1,0:T(8,128)(2,1)}, f16[3,2,64,256]{3,2,1,0:T(8,128)(2,1)}, u32[]{:S(2)}, u32[]{:S(2)}) collective-permute-start(f16[3,2,64,256]{3,2,1,0:T(8,128)(2,1)} %get-tuple-element.67), channel_id=1, source_target_pairs={{0,2},{1,3},{2,0},{3,1},{4,6},{5,7},{6,4},{7,5},{8,10},{9,11},{10,... | collective-permute-start | bytes 589832 | tf_op jit(solution)/shard_map/ppermute | solution.py:456
  88.2 23.9 %collective-permute-start.7 = (f16[3,2,64,256]{3,2,1,0:T(8,128)(2,1)}, f16[3,2,64,256]{3,2,1,0:T(8,128)(2,1)}, u32[]{:S(2)}, u32[]{:S(2)}) collective-permute-start(f16[3,2,64,256]{3,2,1,0:T(8,128)(2,1)} %get-tuple-element.66), channel_id=1, source_target_pairs={{0,3},{1,0},{2,1},{3,2},{4,7},{5,4},{6,5},{7,6},{8,11},{9,8},{10,9... | collective-permute-start | bytes 589832 | tf_op jit(solution)/shard_map/ppermute | solution.py:456
  104.6 21.7 %all-to-all-start.3 = ((f16[256,4,128]{2,1,0:T(4,128)(2,1)}), f16[256,4,128]{2,1,0:T(4,128)(2,1)}, u32[]{:S(2)}, u32[]{:S(2)}) async-start(f16[256,4,128]{2,1,0:T(4,128)(2,1)} %bitcast.10), calls=%async_computation.3 | async-start | bytes 524288 | tf_op jit(solution)/shard_map/all_to_all | solution.py:473
  113.6 13.7 %collective-permute-start.8 = (bf16[8,32,256]{2,1,0:T(8,128)(2,1)S(1)}, bf16[8,32,256]{2,1,0:T(8,128)(2,1)S(1)}, u32[]{:S(2)}, u32[]{:S(2)}) collective-permute-start(bf16[8,32,256]{2,1,0:T(8,128)(2,1)S(1)} %get-tuple-element.56), channel_id=1, source_target_pairs={{0,1},{1,2},{2,3},{3,0},{4,5},{5,6},{6,7},{7,4},{8,9},{9,10},{10,1... | collective-permute-start | bytes 393224 | tf_op jit(solution)/shard_map/ppermute | solution.py:456
  115.0 12.3 %copy-start.7 = (f32[8,64,256]{2,1,0:T(8,128)S(1)}, f32[8,64,256]{2,1,0:T(8,128)}, u32[]{:S(2)}) copy-start(f32[8,64,256]{2,1,0:T(8,128)} %bulk.1) | copy-start | bytes 1572868
  115.0 12.3 %copy-start.9 = (bf16[256,512]{1,0:T(8,128)(2,1)S(1)}, bf16[256,512]{1,0:T(8,128)(2,1)}, u32[]{:S(2)}) copy-start(bf16[256,512]{1,0:T(8,128)(2,1)} %constant.108.clone.x_ref) | copy-start | bytes 786436
  (3 other events, 3.2 us)

commit v7 on v6

--- a/solution.py
+++ b/solution.py
@@ -95,6 +95,9 @@
     y_waves = packed_table(np.cos(angle) + np.sin(angle))
     return {
         "x_waves": x_waves,
+        "x_lines": (
+            np.concatenate([spectrum.real, spectrum.imag], axis=0) * (X_SCALE * COMPONENT_LINK)
+        ).astype(np.float32),
         "middle": np.concatenate(
             [
                 x_waves,
@@ -264,21 +267,15 @@
 
 
 def middle_kernel(
-    where, data, tables, numbers, velocity, buoyancy, *rest
+    where, data, tables, numbers, near, second, slopes, out, held, fields, semaphores
 ):
-    blocks, (slopes, out, held, fields, semaphores) = rest[:3], rest[3:]
-    own = pl.ds(2 * where[0], 2)
     starts = [
         pl.ds(pl.multiple_of(((where[0] + PEERS_Y - back) % PEERS_Y) * ROWS, ROWS), ROWS)
         for back in range(PEERS_Y)
     ]
     fetch = Fetch(
-        (velocity.at[:, own], buoyancy.at[own], *blocks),
-        (
-            fields.at[pl.ds(0, 3), :, starts[0]],
-            fields.at[3, :, starts[0]],
-            *[fields.at[:, :, start] for start in starts[1:]],
-        ),
+        (near.at[0], near.at[1], second, near.at[2]),
+        [fields.at[:, :, start] for start in starts],
         semaphores,
     )
     x_ref, ya_ref, yb_ref = (tables[:, 512 * i : 512 * (i + 1)] for i in range(3))
@@ -307,13 +304,13 @@
         lines = right(jnp.concatenate(lines, axis=0), x_ref) * (X_SCALE / SLOPE_LINK)
         along = (lines[:NY], left(ya_ref, lines[NY : 2 * NY]), lines[2 * NY :])
         if r == 0:
-            for i in range(5):
+            for i in range(4):
                 fetch[i]
         moved = []
         for d, slope in enumerate(along):
             held[r, d] = slope * RETURN_LINK
             moved.append(fields[d, r] - fields[3, r] * slope)
-        returned.append(pltpu.make_async_copy(held.at[r], slopes.at[:, r], semaphores.at[5 + r]))
+        returned.append(pltpu.make_async_copy(held.at[r], slopes.at[:, r], semaphores.at[4 + r]))
         returned[r].start()
         lines = jnp.concatenate([moved[0], left(yb_ref, moved[1]), moved[2]], axis=0)
         components = to_components(x_ref, lines) * (X_SCALE * MIDDLE_LINK)
@@ -485,13 +482,11 @@
     place = jnp.stack([slab_index, row_block]).astype(jnp.int32)
     table = {key: jnp.asarray(value) for key, value in TABLES.items()}
 
-    (components,) = call(
-        forward_lines_kernel,
-        "forward_lines",
-        [VMEM, VMEM],
-        [pressure, table["x_waves"]],
-        [((1024, HALF), f32)],
-        [VMEM],
+    components = jnp.einsum(
+        "cx,abx->cab",
+        table["x_lines"],
+        pressure.reshape(4, HALF, NX),
+        precision=lax.Precision.HIGHEST,
     )
     velocity_later, buoyancy_later, tiles, slab_later, components = lax.optimization_barrier(
         (velocity, buoyancy, tiles, slab_index, components)
@@ -503,10 +498,11 @@
         ).astype(f16)
         for ahead in range(1, PEERS_Y)
     ]
-    first, third = from_behind(sent[0], "gy", 1), from_behind(sent[2], "gy", 3)
+    own = lax.dynamic_slice_in_dim(fields, 2 * row_block, 2, 1) * FIELD_LINK
+    second = from_behind(sent[1], "gy", 2)
     packed = tiles.reshape(SLOTS_HERE, 2 * SLAB, 8, HALF)
-    moved, second, packed, packed_end = lax.optimization_barrier(
-        (exchange(components, 4), sent[1], packed, packed[:, SLAB:])
+    moved, first, third, packed, packed_end = lax.optimization_barrier(
+        (exchange(components, 4), sent[0], sent[2], packed, packed[:, SLAB:])
     )
     (filtered,) = call(
         filter_out_kernel,
@@ -522,29 +518,28 @@
         [VMEM],
         [((NZ, NY), f32)],
     )
-    filtered, first, second, third, packed, packed_end = lax.optimization_barrier(
-        (filtered, first, second, third, packed, packed_end)
-    )
-    second = from_behind(second, "gy", 2)
+    filtered, own, first, second, third, packed, packed_end = lax.optimization_barrier(
+        (filtered, own, first, second, third, packed, packed_end)
+    )
+    first, third = from_behind(first, "gy", 1), from_behind(third, "gy", 3)
     tiles_before, tiles_second = from_behind(packed, "gz", 1), from_behind(packed_end, "gz", 2)
     moved = exchange(filtered, 8)
     slopes, middle = call(
         middle_kernel,
         "middle",
-        [SMEM] + [VMEM] * 3 + [FAR] * 5,
+        [SMEM] + [VMEM] * 3 + [FAR] * 2,
         [
             here,
             arrived(moved),
             table["middle"],
             table["numbers"],
-            velocity,
-            buoyancy,
-            *[block.astype(f32) * (1.0 / FIELD_LINK) for block in (first, second, third)],
+            jnp.stack([own, first.astype(f32), third.astype(f32)]) * (1.0 / FIELD_LINK),
+            second.astype(f32) * (1.0 / FIELD_LINK),
         ],
         [((3, 2, NY, NX), f32), ((2048, HALF), f32)],
         [FAR, VMEM],
         [((2, 3, NY, NX), f32), ((4, 2, NY, NX), f32)],
-        7,
+        6,
     )
     middle, slopes, tiles_before, tiles_second = lax.optimization_barrier(
         (middle, slopes.astype(f16), tiles_before, tiles_second)

time: 129 us -> 126 us (0.977)
  other arithmetic: 14.8 us -> 11.2 us
  waiting for transfers between devices: 35.6 us -> 39.1 us
  local copies, waits for them, and re-layouts: 7.96 us -> 5.56 us
  matrix products: 0 us -> 1.89 us
  starting transfers between devices: 54.4 us -> 52.7 us
    ppermute x9, waiting for transfers between devices: 5.32 us -> 9 us  [from_behind(): return lax.ppermute(x, axis, [(i, (i + by) % peers) for i in range(peers)])]
    unnamed x31, local copies, waits for them, and re-layouts: 3.68 us -> 0.31 us
    dot_general x0 -> x1, matrix products: none -> 1.89 us  [local(): jnp.einsum('cx,abx->cab', table['x_lines'], pressure.reshape(4, HALF, NX)...]
    all_to_all x4, starting transfers between devices: 39.4 us -> 37.6 us  [exchange(): return lax.all_to_all(blocks, ('gz', 'gy'), 0, 0, tiled=True)]
    mul x2, other arithmetic: 1.98 us -> 0.2 us  [the longest x1 0.15 us: local(): jnp.stack([own, first.astype(f32), third.astype(f32)]) * (1.0 / FIELD_LINK)]
    pallas_call x6 -> x5, Pallas kernels: 14.5 us -> 14 us  [call(): pl.pallas_call(kernel, out_shape=[jax.ShapeDtypeStruct(shape, kind) for s...]
  transfers between devices with their start and end apart: 13 -> 13, of which waited for: 5 -> 6; matrix products, arithmetic and copies ran while one was open for 13% -> 11% of each run, Pallas kernels for 10% -> 10%
where the time goes in v7:
time: 126 us
  starting transfers between devices  52.7 us (42%)
  waiting for transfers between devices  39.1 us (31%)
  Pallas kernels  14 us (11%)
  other arithmetic  11.2 us (9%)
  local copies, waits for them, and re-layouts  5.56 us (4%)
  matrix products  1.89 us (2%)
  between operations  1.35 us (1%)
    all_to_all x4, starting transfers between devices, exchange(): return lax.all_to_all(blocks, ('gz', 'gy'), 0, 0, tiled=True)  37.6 us
    all_to_all x4, waiting for transfers between devices, exchange(): return lax.all_to_all(blocks, ('gz', 'gy'), 0, 0, tiled=True)  30.1 us
    ppermute x9, starting transfers between devices, from_behind(): return lax.ppermute(x, axis, [(i, (i + by) % peers) for i in range(peers)])  15.1 us
    pallas_call x5, Pallas kernels, call(): pl.pallas_call(kernel, out_shape=[jax.ShapeDtypeStruct(shape, kind) for s...  14 us
    ppermute x9, waiting for transfers between devices, from_behind(): return lax.ppermute(x, axis, [(i, (i + by) % peers) for i in range(peers)])  9 us
    sub x1, other arithmetic, local(): new_velocity = velocity - buoyancy[None] * (slopes * (1.0 / RETURN_LINK))  2.6 us
  transfers between devices with their start and end apart: 13, of which 6 were waited for; matrix products, arithmetic and copies ran while one was open for 11% of the time, Pallas kernels for 10%

profile of v7, /device:TPU:1, one launch (start us, length us, event | category | flops | bytes accessed | tf_op | source)
XLA Modules:
  0.0 125.8 jit_solution(3565217746163437678)
XLA Ops:
  0.7 1.9 %fusion.11 = f32[256,4,128]{2,0,1:T(8,128)S(1)} fusion(f32[256,256,1]{1,0,2:T(8,128)} %constant.122, f32[4,128,256]{2,1,0:T(8,128)} %bitcast.32), kind=kOutput, calls=%fused_computation.40 | convolution fusion | flops 402653184 | bytes 1310720 | tf_op jit(solution)/shard_map/cx,abx->cab/dot_general | solution.py:485
  3.5 15.7 %all-to-all-start = ((f16[256,4,128]{2,1,0:T(4,128)(2,1)}), f16[256,4,128]{2,1,0:T(4,128)(2,1)S(1)}, u32[]{:S(2)}, u32[]{:S(2)}) async-start(f16[256,4,128]{2,1,0:T(4,128)(2,1)} %copy.19), calls=%async_computation | async-start | bytes 524288 | tf_op jit(solution)/shard_map/all_to_all | solution.py:470
  20.3 2.9 %collective-permute-start = (f16[4,2,64,256]{3,2,1,0:T(8,128)(2,1)}, f16[4,2,64,256]{3,2,1,0:T(8,128)(2,1)S(1)}, u32[]{:S(2)}, u32[]{:S(2)}) collective-permute-start(f16[4,2,64,256]{3,2,1,0:T(8,128)(2,1)} %get-tuple-element.62), channel_id=1, source_target_pairs={{0,2},{1,3},{2,0},{3,1},{4,6},{5,7},{6,4},{7,5},{8,10},{9,11},{10,... | collective-permute-start | bytes 786440 | tf_op jit(solution)/shard_map/ppermute | solution.py:453
  23.2 1.9 %reshape.42.t0 = bf16[8,16,8,128]{3,2,1,0:T(8,128)(2,1)S(1)} reshape(bf16[8,16,32,32]{3,2,1,0:T(8,128)(2,1)} %param.17) | data formatting | bytes 524288 | tf_op jit(solution)/shard_map/reshape | solution.py:503
  25.8 8.7 %all-to-all-done = f16[256,4,128]{2,1,0:T(4,128)(2,1)S(1)} async-done(((f16[256,4,128]{2,1,0:T(4,128)(2,1)}), f16[256,4,128]{2,1,0:T(4,128)(2,1)S(1)}, u32[]{:S(2)}, u32[]{:S(2)}) %all-to-all-start) | async-done | bytes 262176 | tf_op jit(solution)/shard_map/all_to_all | solution.py:470
  34.5 2.6 %filter_out.1 = f32[2048,128]{1,0:T(8,128)S(1)} custom-call(s32[1]{0:T(128)} %bitcast.where, f32[1024,128]{1,0:T(8,128)S(1)} %convert.6.data, bf16[256,1536]{1,0:T(8,128)(2,1)S(1)} %copy-done.2, f32[136,128]{1,0:T(8,128)S(1)} %copy-done.3), custom_call_target="tpu_custom_call" | custom-call | flops 400000000 | bytes 1048576 | tf_op jit(solution)/shard_map/filter_out/pallas_call | solution.py:439
  38.0 8.0 %all-to-all-start.1 = ((f16[256,8,128]{2,1,0:T(8,128)(2,1)}), f16[256,8,128]{2,1,0:T(8,128)(2,1)}, u32[]{:S(2)}, u32[]{:S(2)}) async-start(f16[256,8,128]{2,1,0:T(8,128)(2,1)} %convert_bitcast_fusion.1), calls=%async_computation.1 | async-start | bytes 1048576 | tf_op jit(solution)/shard_map/all_to_all | solution.py:470
  46.0 2.7 %collective-permute-start.2 = (f16[4,2,64,256]{3,2,1,0:T(8,128)(2,1)S(1)}, f16[4,2,64,256]{3,2,1,0:T(8,128)(2,1)S(1)}, u32[]{:S(2)}, u32[]{:S(2)}) collective-permute-start(f16[4,2,64,256]{3,2,1,0:T(8,128)(2,1)S(1)} %copy-done.13), channel_id=1, source_target_pairs={{0,3},{1,0},{2,1},{3,2},{4,7},{5,4},{6,5},{7,6},{8,11},{9,8},{10,9... | collective-permute-start | bytes 786440 | tf_op jit(solution)/shard_map/ppermute | solution.py:453
  48.8 1.8 %collective-permute-start.3 = (bf16[8,16,8,128]{3,2,1,0:T(8,128)(2,1)S(1)}, bf16[8,16,8,128]{3,2,1,0:T(8,128)(2,1)S(1)}, u32[]{:S(2)}, u32[]{:S(2)}) collective-permute-start(bf16[8,16,8,128]{3,2,1,0:T(8,128)(2,1)S(1)} %reshape.42.t0), channel_id=1, source_target_pairs={{0,4},{4,8},{8,12},{12,16},{16,20},{20,24},{24,28},{28,32},{32,36}... | collective-permute-start | bytes 786440 | tf_op jit(solution)/shard_map/ppermute | solution.py:453
  51.8 5.8 %collective-permute-done.2 = f16[4,2,64,256]{3,2,1,0:T(8,128)(2,1)S(1)} collective-permute-done((f16[4,2,64,256]{3,2,1,0:T(8,128)(2,1)S(1)}, f16[4,2,64,256]{3,2,1,0:T(8,128)(2,1)S(1)}, u32[]{:S(2)}, u32[]{:S(2)}) %collective-permute-start.2) | collective-permute-done | bytes 262176 | tf_op jit(solution)/shard_map/ppermute | solution.py:453
  57.7 3.2 %collective-permute-done.1 = f16[4,2,64,256]{3,2,1,0:T(8,128)(2,1)S(1)} collective-permute-done((f16[4,2,64,256]{3,2,1,0:T(8,128)(2,1)S(1)}, f16[4,2,64,256]{3,2,1,0:T(8,128)(2,1)S(1)}, u32[]{:S(2)}, u32[]{:S(2)}) %collective-permute-start.1) | collective-permute-done | bytes 262176 | tf_op jit(solution)/shard_map/ppermute | solution.py:453
  61.1 4.6 %all-to-all-done.1 = f16[256,8,128]{2,1,0:T(8,128)(2,1)} async-done(((f16[256,8,128]{2,1,0:T(8,128)(2,1)}), f16[256,8,128]{2,1,0:T(8,128)(2,1)}, u32[]{:S(2)}, u32[]{:S(2)}) %all-to-all-start.1) | async-done | bytes 524320 | tf_op jit(solution)/shard_map/all_to_all | solution.py:470
  66.8 4.1 %middle.1 = (f32[3,2,256,256]{3,2,1,0:T(8,128)S(1)}, f32[2048,128]{1,0:T(8,128)S(1)}) custom-call(s32[1]{0:T(128)} %bitcast.1.where, f32[2048,128]{1,0:T(8,128)S(1)} %bitcast_convert_fusion.1.data, bf16[256,1536]{1,0:T(8,128)(2,1)S(1)} %copy-done, f32[136,128]{1,0:T(8,128)S(1)} %copy-done.3, f32[3,4,2,64,256]{4,3,2,1,0:T(8,128)S(1)} %maximum_multiply_fusion.near, ...), custom_call_target="tpu_custom_call" | custom-call | flops 400000000 | bytes 1048576 | tf_op jit(solution)/shard_map/middle/pallas_call | solution.py:439
  72.0 6.6 %all-to-all-start.2 = ((f16[256,8,128]{2,1,0:T(8,128)(2,1)}), f16[256,8,128]{2,1,0:T(8,128)(2,1)S(1)}, u32[]{:S(2)}, u32[]{:S(2)}) async-start(f16[256,8,128]{2,1,0:T(8,128)(2,1)} %convert_bitcast_fusion), calls=%async_computation.2 | async-start | bytes 1048576 | tf_op jit(solution)/shard_map/all_to_all | solution.py:470
  81.7 1.4 %collective-permute-start.5 = (f16[3,2,64,256]{3,2,1,0:T(8,128)(2,1)}, f16[3,2,64,256]{3,2,1,0:T(8,128)(2,1)}, u32[]{:S(2)}, u32[]{:S(2)}) collective-permute-start(f16[3,2,64,256]{3,2,1,0:T(8,128)(2,1)} %get-tuple-element.70), channel_id=1, source_target_pairs={{0,1},{1,2},{2,3},{3,0},{4,5},{5,6},{6,7},{7,4},{8,9},{9,10},{10,1... | collective-permute-start | bytes 589832 | tf_op jit(solution)/shard_map/ppermute | solution.py:453
  83.0 2.4 %collective-permute-start.6 = (f16[3,2,64,256]{3,2,1,0:T(8,128)(2,1)}, f16[3,2,64,256]{3,2,1,0:T(8,128)(2,1)}, u32[]{:S(2)}, u32[]{:S(2)}) collective-permute-start(f16[3,2,64,256]{3,2,1,0:T(8,128)(2,1)} %get-tuple-element.72), channel_id=1, source_target_pairs={{0,2},{1,3},{2,0},{3,1},{4,6},{5,7},{6,4},{7,5},{8,10},{9,11},{10,... | collective-permute-start | bytes 589832 | tf_op jit(solution)/shard_map/ppermute | solution.py:453
  86.6 3.8 %source.1 = (f32[8,64,256]{2,1,0:T(8,128)S(1)}, bf16[8,32,256]{2,1,0:T(8,128)(2,1)S(1)}) custom-call(s32[2]{0:T(128)S(1)} %pad_add_fusion.where, s32[256]{0:T(256)S(1)} %copy-done.7, s32[8,3]{1,0:T(8,128)S(1)} %copy.23.c0, s32[8,3]{1,0:T(8,128)S(1)} %copy.24.c1, s32[8,3]{1,0:T(8,128)S(1)} %copy.25.c2, bf16[8,16,8,128]{3,2,1,0:T(8,128)(2,1)S(1)} %reshape.42.t0, ...), custom_call_target="tpu_custom_call" | custom-call | flops 400000000 | bytes 1048576 | tf_op jit(solution)/shard_map/source/pallas_call | solution.py:439
  90.4 8.2 %all-to-all-done.2 = f16[256,8,128]{2,1,0:T(8,128)(2,1)S(1)} async-done(((f16[256,8,128]{2,1,0:T(8,128)(2,1)}), f16[256,8,128]{2,1,0:T(8,128)(2,1)S(1)}, u32[]{:S(2)}, u32[]{:S(2)}) %all-to-all-start.2) | async-done | bytes 524320 | tf_op jit(solution)/shard_map/all_to_all | solution.py:470
  98.7 2.3 %filter_back.1 = f32[1024,128]{1,0:T(8,128)S(1)} custom-call(s32[1]{0:T(128)} %bitcast.where, f32[2048,128]{1,0:T(8,128)S(1)} %bitcast_convert_fusion.data, bf16[256,1536]{1,0:T(8,128)(2,1)S(1)} %copy-done.1, f32[136,128]{1,0:T(8,128)S(1)} %copy-done.3), custom_call_target="tpu_custom_call" | custom-call | flops 400000000 | bytes 1048576 | tf_op jit(solution)/shard_map/filter_back/pallas_call | solution.py:439
  101.7 7.4 %all-to-all-start.3 = ((f16[256,4,128]{2,1,0:T(4,128)(2,1)}), f16[256,4,128]{2,1,0:T(4,128)(2,1)}, u32[]{:S(2)}, u32[]{:S(2)}) async-start(f16[256,4,128]{2,1,0:T(4,128)(2,1)} %bitcast.14), calls=%async_computation.3 | async-start | bytes 524288 | tf_op jit(solution)/shard_map/all_to_all | solution.py:470
  109.2 1.5 %select_select_fusion.3 = (f16[3,2,64,256]{3,2,1,0:T(8,128)(2,1)S(1)}, f16[3,2,64,256]{3,2,1,0:T(8,128)(2,1)S(1)}, f16[3,2,64,256]{3,2,1,0:T(8,128)(2,1)S(1)}, f16[3,2,64,256]{3,2,1,0:T(8,128)(2,1)S(1)}) fusion(f16[3,2,64,256]{3,2,1,0:T(8,128)(2,1)} %collective-permute-done.6, f16[3,2,64,256]{3,2,1,0:T(8,128)(2,1)} %collective-permute-done.7, ...), kind=kLoop, calls=%fused_computation.32 | loop fusion | flops 1179648 | bytes 1572880 | tf_op jit(solution)/shard_map/select_n | solution.py:463
  110.7 1.5 %collective-permute-start.8 = (bf16[8,32,256]{2,1,0:T(8,128)(2,1)S(1)}, bf16[8,32,256]{2,1,0:T(8,128)(2,1)S(1)}, u32[]{:S(2)}, u32[]{:S(2)}) collective-permute-start(bf16[8,32,256]{2,1,0:T(8,128)(2,1)S(1)} %get-tuple-element.60), channel_id=1, source_target_pairs={{0,1},{1,2},{2,3},{3,0},{4,5},{5,6},{6,7},{7,4},{8,9},{9,10},{10,1... | collective-permute-start | bytes 393224 | tf_op jit(solution)/shard_map/ppermute | solution.py:453
  112.2 2.6 %multiply_subtract_fusion = f32[3,8,64,256]{3,2,1,0:T(8,128)} fusion(f32[3,8,64,256]{3,2,1,0:T(8,128)S(1)} %copy-done.9, f16[3,2,64,256]{3,2,1,0:T(8,128)(2,1)S(1)} %get-tuple-element.67, f16[3,2,64,256]{3,2,1,0:T(8,128)(2,1)S(1)} %get-tuple-element.68, f16[3,2,64,256]{3,2,1,0:T(8,128)(2,1)S(1)} %get-tuple-element.69, ...), kind=kLoop, calls=%fused_computation.9 | loop fusion | flops 2359296 | bytes 4456448 | tf_op jit(solution)/shard_map/sub | solution.py:548
  114.8 8.7 %all-to-all-done.3 = f16[256,4,128]{2,1,0:T(4,128)(2,1)} async-done(((f16[256,4,128]{2,1,0:T(4,128)(2,1)}), f16[256,4,128]{2,1,0:T(4,128)(2,1)}, u32[]{:S(2)}, u32[]{:S(2)}) %all-to-all-start.3) | async-done | bytes 262176 | tf_op jit(solution)/shard_map/all_to_all | solution.py:470
  (62 shorter events, 14.2 us)
Async XLA Ops:
  0.6 18.6 %copy-start.8 = (f32[3,8,64,256]{3,2,1,0:T(8,128)S(1)}, f32[3,8,64,256]{3,2,1,0:T(8,128)}, u32[]{:S(2)}) copy-start(f32[3,8,64,256]{3,2,1,0:T(8,128)} %param.14) | copy-start | bytes 4718596
  0.6 18.6 %copy-start.11 = (f32[8,64,256]{2,1,0:T(8,128)S(1)}, f32[8,64,256]{2,1,0:T(8,128)}, u32[]{:S(2)}) copy-start(f32[8,64,256]{2,1,0:T(8,128)} %param.16) | copy-start | bytes 1572868
  3.5 30.9 %all-to-all-start = ((f16[256,4,128]{2,1,0:T(4,128)(2,1)}), f16[256,4,128]{2,1,0:T(4,128)(2,1)S(1)}, u32[]{:S(2)}, u32[]{:S(2)}) async-start(f16[256,4,128]{2,1,0:T(4,128)(2,1)} %copy.19), calls=%async_computation | async-start | bytes 524288 | tf_op jit(solution)/shard_map/all_to_all | solution.py:470
  20.3 14.2 %copy-start.2 = (bf16[256,1536]{1,0:T(8,128)(2,1)S(1)}, bf16[256,1536]{1,0:T(8,128)(2,1)}, u32[]{:S(2)}) copy-start(bf16[256,1536]{1,0:T(8,128)(2,1)} %constant.114.clone.tables) | copy-start | bytes 2359300
  20.3 14.2 %copy-start.3 = (f32[136,128]{1,0:T(8,128)S(1)}, f32[136,128]{1,0:T(8,128)}, u32[]{:S(2)}) copy-start(f32[136,128]{1,0:T(8,128)} %constant.116.clone.numbers) | copy-start | bytes 208900
  20.3 16.9 %collective-permute-start = (f16[4,2,64,256]{3,2,1,0:T(8,128)(2,1)}, f16[4,2,64,256]{3,2,1,0:T(8,128)(2,1)S(1)}, u32[]{:S(2)}, u32[]{:S(2)}) collective-permute-start(f16[4,2,64,256]{3,2,1,0:T(8,128)(2,1)} %get-tuple-element.62), channel_id=1, source_target_pairs={{0,2},{1,3},{2,0},{3,1},{4,6},{5,7},{6,4},{7,5},{8,10},{9,11},{10,... | collective-permute-start | bytes 786440 | tf_op jit(solution)/shard_map/ppermute | solution.py:453
  38.0 27.6 %all-to-all-start.1 = ((f16[256,8,128]{2,1,0:T(8,128)(2,1)}), f16[256,8,128]{2,1,0:T(8,128)(2,1)}, u32[]{:S(2)}, u32[]{:S(2)}) async-start(f16[256,8,128]{2,1,0:T(8,128)(2,1)} %convert_bitcast_fusion.1), calls=%async_computation.1 | async-start | bytes 1048576 | tf_op jit(solution)/shard_map/all_to_all | solution.py:470
  46.0 11.6 %collective-permute-start.2 = (f16[4,2,64,256]{3,2,1,0:T(8,128)(2,1)S(1)}, f16[4,2,64,256]{3,2,1,0:T(8,128)(2,1)S(1)}, u32[]{:S(2)}, u32[]{:S(2)}) collective-permute-start(f16[4,2,64,256]{3,2,1,0:T(8,128)(2,1)S(1)} %copy-done.13), channel_id=1, source_target_pairs={{0,3},{1,0},{2,1},{3,2},{4,7},{5,4},{6,5},{7,6},{8,11},{9,8},{10,9... | collective-permute-start | bytes 786440 | tf_op jit(solution)/shard_map/ppermute | solution.py:453
  48.8 12.1 %collective-permute-start.1 = (f16[4,2,64,256]{3,2,1,0:T(8,128)(2,1)S(1)}, f16[4,2,64,256]{3,2,1,0:T(8,128)(2,1)S(1)}, u32[]{:S(2)}, u32[]{:S(2)}) collective-permute-start(f16[4,2,64,256]{3,2,1,0:T(8,128)(2,1)S(1)} %get-tuple-element.43), channel_id=1, source_target_pairs={{0,1},{1,2},{2,3},{3,0},{4,5},{5,6},{6,7},{7,4},{8,9},{9,10},{10,1... | collective-permute-start | bytes 786440 | tf_op jit(solution)/shard_map/ppermute | solution.py:453
  48.8 22.3 %collective-permute-start.3 = (bf16[8,16,8,128]{3,2,1,0:T(8,128)(2,1)S(1)}, bf16[8,16,8,128]{3,2,1,0:T(8,128)(2,1)S(1)}, u32[]{:S(2)}, u32[]{:S(2)}) collective-permute-start(bf16[8,16,8,128]{3,2,1,0:T(8,128)(2,1)S(1)} %reshape.42.t0), channel_id=1, source_target_pairs={{0,4},{4,8},{8,12},{12,16},{16,20},{20,24},{24,28},{28,32},{32,36}... | collective-permute-start | bytes 786440 | tf_op jit(solution)/shard_map/ppermute | solution.py:453
  50.6 20.5 %collective-permute-start.4 = (bf16[8,8,8,128]{3,2,1,0:T(8,128)(2,1)}, bf16[8,8,8,128]{3,2,1,0:T(8,128)(2,1)}, u32[]{:S(2)}, u32[]{:S(2)}) collective-permute-start(bf16[8,8,8,128]{3,2,1,0:T(8,128)(2,1)} %slice.4), channel_id=1, source_target_pairs={{0,8},{4,12},{8,16},{12,20},{16,24},{20,28},{24,32},{28,36},{32,40... | collective-permute-start | bytes 393224 | tf_op jit(solution)/shard_map/ppermute | solution.py:453
  71.0 9.7 %copy-start.10 = (f16[3,2,256,256]{3,2,1,0:T(8,128)(2,1)}, f16[3,2,256,256]{3,2,1,0:T(8,128)(2,1)S(1)}, u32[]{:S(2)}) copy-start(f16[3,2,256,256]{3,2,1,0:T(8,128)(2,1)S(1)} %convert_element_type.62) | copy-start | bytes 2359300
  72.0 14.7 %copy-start.5 = (f32[8,64,256]{2,1,0:T(8,128)S(1)}, f32[8,64,256]{2,1,0:T(8,128)}, u32[]{:S(2)}) copy-start(f32[8,64,256]{2,1,0:T(8,128)} %pressure.1) | copy-start | bytes 1572868
  72.0 14.7 %copy-start.7 = (s32[256]{0:T(256)S(1)}, s32[256]{0:T(256)}, u32[]{:S(2)}) copy-start(s32[256]{0:T(256)} %lives.1) | copy-start | bytes 3076
  72.0 26.6 %all-to-all-start.2 = ((f16[256,8,128]{2,1,0:T(8,128)(2,1)}), f16[256,8,128]{2,1,0:T(8,128)(2,1)S(1)}, u32[]{:S(2)}, u32[]{:S(2)}) async-start(f16[256,8,128]{2,1,0:T(8,128)(2,1)} %convert_bitcast_fusion), calls=%async_computation.2 | async-start | bytes 1048576 | tf_op jit(solution)/shard_map/all_to_all | solution.py:470
  81.7 17.0 %copy-start.1 = (bf16[256,1536]{1,0:T(8,128)(2,1)S(1)}, bf16[256,1536]{1,0:T(8,128)(2,1)}, u32[]{:S(2)}) copy-start(bf16[256,1536]{1,0:T(8,128)(2,1)} %constant.115.clone.tables) | copy-start | bytes 2359300
  81.7 27.5 %collective-permute-start.5 = (f16[3,2,64,256]{3,2,1,0:T(8,128)(2,1)}, f16[3,2,64,256]{3,2,1,0:T(8,128)(2,1)}, u32[]{:S(2)}, u32[]{:S(2)}) collective-permute-start(f16[3,2,64,256]{3,2,1,0:T(8,128)(2,1)} %get-tuple-element.70), channel_id=1, source_target_pairs={{0,1},{1,2},{2,3},{3,0},{4,5},{5,6},{6,7},{7,4},{8,9},{9,10},{10,1... | collective-permute-start | bytes 589832 | tf_op jit(solution)/shard_map/ppermute | solution.py:453
  83.0 26.1 %collective-permute-start.6 = (f16[3,2,64,256]{3,2,1,0:T(8,128)(2,1)}, f16[3,2,64,256]{3,2,1,0:T(8,128)(2,1)}, u32[]{:S(2)}, u32[]{:S(2)}) collective-permute-start(f16[3,2,64,256]{3,2,1,0:T(8,128)(2,1)} %get-tuple-element.72), channel_id=1, source_target_pairs={{0,2},{1,3},{2,0},{3,1},{4,6},{5,7},{6,4},{7,5},{8,10},{9,11},{10,... | collective-permute-start | bytes 589832 | tf_op jit(solution)/shard_map/ppermute | solution.py:453
  85.5 23.7 %collective-permute-start.7 = (f16[3,2,64,256]{3,2,1,0:T(8,128)(2,1)S(1)}, f16[3,2,64,256]{3,2,1,0:T(8,128)(2,1)}, u32[]{:S(2)}, u32[]{:S(2)}) collective-permute-start(f16[3,2,64,256]{3,2,1,0:T(8,128)(2,1)S(1)} %get-tuple-element.71), channel_id=1, source_target_pairs={{0,3},{1,0},{2,1},{3,2},{4,7},{5,4},{6,5},{7,6},{8,11},{9,8},{10,9... | collective-permute-start | bytes 589832 | tf_op jit(solution)/shard_map/ppermute | solution.py:453
  101.0 11.2 %copy-start.9 = (f32[3,8,64,256]{3,2,1,0:T(8,128)S(1)}, f32[3,8,64,256]{3,2,1,0:T(8,128)}, u32[]{:S(2)}) copy-start(f32[3,8,64,256]{3,2,1,0:T(8,128)} %param.14) | copy-start | bytes 4718596
  101.7 21.7 %all-to-all-start.3 = ((f16[256,4,128]{2,1,0:T(4,128)(2,1)}), f16[256,4,128]{2,1,0:T(4,128)(2,1)}, u32[]{:S(2)}, u32[]{:S(2)}) async-start(f16[256,4,128]{2,1,0:T(4,128)(2,1)} %bitcast.14), calls=%async_computation.3 | async-start | bytes 524288 | tf_op jit(solution)/shard_map/all_to_all | solution.py:470
  110.7 13.7 %collective-permute-start.8 = (bf16[8,32,256]{2,1,0:T(8,128)(2,1)S(1)}, bf16[8,32,256]{2,1,0:T(8,128)(2,1)S(1)}, u32[]{:S(2)}, u32[]{:S(2)}) collective-permute-start(bf16[8,32,256]{2,1,0:T(8,128)(2,1)S(1)} %get-tuple-element.60), channel_id=1, source_target_pairs={{0,1},{1,2},{2,3},{3,0},{4,5},{5,6},{6,7},{7,4},{8,9},{9,10},{10,1... | collective-permute-start | bytes 393224 | tf_op jit(solution)/shard_map/ppermute | solution.py:453
  112.2 12.3 %copy-start.4 = (f32[8,64,256]{2,1,0:T(8,128)S(1)}, f32[8,64,256]{2,1,0:T(8,128)}, u32[]{:S(2)}) copy-start(f32[8,64,256]{2,1,0:T(8,128)} %bulk.1) | copy-start | bytes 1572868
  112.2 12.3 %copy-start.6 = (bf16[256,512]{1,0:T(8,128)(2,1)S(1)}, bf16[256,512]{1,0:T(8,128)(2,1)}, u32[]{:S(2)}) copy-start(bf16[256,512]{1,0:T(8,128)(2,1)} %constant.111.clone.x_ref) | copy-start | bytes 786436
  (3 other events, 23.4 us)

commit v8 on v7

--- a/solution.py
+++ b/solution.py
@@ -227,6 +227,14 @@
     return [x[HALF * i : HALF * (i + 1)] for i in range(4)]
 
 
+def filtered_rows(blocks, y_ref, kx, scale):
+    out = []
+    for part, block in enumerate(blocks):
+        waves = right(block, y_ref) * (kappa_rows(kx, part) * scale)
+        out.append(right(waves, y_ref))
+    return out
+
+
 def first_half():
     return lax.broadcasted_iota(jnp.int32, (64, HALF), 1) < ROWS
 
@@ -247,15 +255,11 @@
             span = pl.ds(HALF * side, HALF)
             plane[pl.ds(64 * pair, 64), span] = jnp.where(early, a, pltpu.roll(b, ROWS, 1))
             plane[pl.ds(256 + 64 * pair, 64), span] = jnp.where(early, pltpu.roll(a, ROWS, 1), b)
-    mixed = right(plane[...], y_ref)
-
     def coefficient(i):
         return numbers[:HALF, i : i + 1]
 
-    (spectrum,) = forward_z(z_from_ref, coefficient, [mixed])
-    scale = SLOPE_LINK / COMPONENT_LINK / (NZ * NY)
-    waves = [x * (kappa_rows(where[0] % HALF, part) * scale) for part, x in enumerate(spectrum)]
-    waves = blocks_of(right(jnp.concatenate(waves, axis=0), y_ref))
+    (waves,) = forward_z(z_from_ref, coefficient, [plane[...]])
+    waves = filtered_rows(waves, y_ref, where[0] % HALF, SLOPE_LINK / COMPONENT_LINK / (NZ * NY))
     planes = inverse_z(z_to_ref, coefficient, [waves, derivative_z(coefficient, 2, waves)])
     for field in range(2):
         for r in range(2):
@@ -281,50 +285,57 @@
     x_ref, ya_ref, yb_ref = (tables[:, 512 * i : 512 * (i + 1)] for i in range(3))
     weight, ahead_real, ahead_imag = (numbers[HALF + i : HALF + i + 1, :] for i in range(3))
     behind = numbers[:HALF, 16:17], numbers[:HALF, 17:18]
-    returned = []
-    for r in range(2):
-        q, g = [
-            jnp.concatenate(
-                [data[pl.ds(4 * r + 2 * field + side, 256, stride=8), :] for side in range(2)], axis=1
-            )
-            for field in range(2)
-        ]
-        lines = []
-        for x, slope in ((q, True), (q, False), (g, False)):
-            x = x.T
-            real, imag = x[:, :HALF], x[:, HALF:]
-            if slope:
-                real, imag = (
-                    ahead_real * real - ahead_imag * imag,
-                    ahead_real * imag + ahead_imag * real,
-                )
-            else:
-                real, imag = weight * real, weight * imag
-            lines.append(jnp.concatenate([real, imag], axis=1))
-        lines = right(jnp.concatenate(lines, axis=0), x_ref) * (X_SCALE / SLOPE_LINK)
-        along = (lines[:NY], left(ya_ref, lines[NY : 2 * NY]), lines[2 * NY :])
-        if r == 0:
-            for i in range(4):
-                fetch[i]
-        moved = []
-        for d, slope in enumerate(along):
-            held[r, d] = slope * RETURN_LINK
-            moved.append(fields[d, r] - fields[3, r] * slope)
-        returned.append(pltpu.make_async_copy(held.at[r], slopes.at[:, r], semaphores.at[4 + r]))
-        returned[r].start()
-        lines = jnp.concatenate([moved[0], left(yb_ref, moved[1]), moved[2]], axis=0)
-        components = to_components(x_ref, lines) * (X_SCALE * MIDDLE_LINK)
-        real, imag = components[:HALF, :NY], components[HALF:, :NY]
-        across = jnp.concatenate(
-            times(real, imag, behind[0], behind[1]), axis=0
-        ) + components[:, NY : 2 * NY]
-        for field, components in enumerate((across, components[:, 2 * NY :])):
+    q, g = [
+        jnp.concatenate(
+            [
+                data[pl.ds(4 * r + 2 * field + side, 256, stride=8), :]
+                for r in range(2)
+                for side in range(2)
+            ],
+            axis=1,
+        ).T
+        for field in range(2)
+    ]
+    real, imag = q[:, :HALF], q[:, HALF:]
+    lines = jnp.concatenate(
+        [
+            ahead_real * real - ahead_imag * imag,
+            weight * real,
+            weight * g[:, :HALF],
+            ahead_real * imag + ahead_imag * real,
+            weight * imag,
+            weight * g[:, HALF:],
+        ],
+        axis=0,
+    )
+    lines = jnp.concatenate([lines[: 3 * 512], lines[3 * 512 :]], axis=1)
+    lines = right(lines, x_ref) * (X_SCALE / SLOPE_LINK)
+    along_y = left(ya_ref, jnp.concatenate([lines[512:768], lines[768:1024]], axis=1))
+    along = (
+        (lines[:256], lines[256:512]),
+        (along_y[:, :NX], along_y[:, NX:]),
+        (lines[1024:1280], lines[1280:]),
+    )
+    for d in range(3):
+        for r in range(2):
+            held[d, r] = along[d][r] * RETURN_LINK
+    returned = pltpu.make_async_copy(held, slopes, semaphores.at[4])
+    returned.start()
+    for i in range(4):
+        fetch[i]
+    moved = [[fields[d, r] - fields[3, r] * along[d][r] for r in range(2)] for d in range(3)]
+    along_y = left(yb_ref, jnp.concatenate(moved[1], axis=1))
+    lines = jnp.concatenate([*moved[0], along_y[:, :NX], along_y[:, NX:], *moved[2]], axis=0)
+    components = to_components(x_ref, lines) * (X_SCALE * MIDDLE_LINK)
+    real, imag = components[:HALF, : 2 * NY], components[HALF:, : 2 * NY]
+    across = jnp.concatenate(times(real, imag, behind[0], behind[1]), axis=0)
+    for field, part in enumerate((across + components[:, 2 * NY : 4 * NY], components[:, 4 * NY :])):
+        for r in range(2):
             for side in range(2):
-                out[pl.ds(4 * r + 2 * field + side, 256, stride=8), :] = components[
-                    :, HALF * side : HALF * (side + 1)
+                out[pl.ds(4 * r + 2 * field + side, 256, stride=8), :] = part[
+                    :, NY * r + HALF * side : NY * r + HALF * (side + 1)
                 ]
-    for copy in returned:
-        copy.wait()
+    returned.wait()
 
 
 def filter_back_kernel(where, data, tables, numbers, out):
@@ -347,10 +358,8 @@
 
     across, along = forward_z(z_from_ref, coefficient, arrived)
     waves = [x + z for x, z in zip(across, derivative_z(coefficient, 9, along))]
-    waves = blocks_of(right(jnp.concatenate(waves, axis=0), y_ref))
     scale = DIVERGENCE_LINK / MIDDLE_LINK / (NZ * NY)
-    waves = [x * (kappa_rows(where[0] % HALF, part) * scale) for part, x in enumerate(waves)]
-    waves = blocks_of(right(jnp.concatenate(waves, axis=0), y_ref))
+    waves = filtered_rows(waves, y_ref, where[0] % HALF, scale)
     plane = inverse_z(z_to_ref, coefficient, [waves])
     early = first_half()
     for pair in range(4):
@@ -499,10 +508,10 @@
         for ahead in range(1, PEERS_Y)
     ]
     own = lax.dynamic_slice_in_dim(fields, 2 * row_block, 2, 1) * FIELD_LINK
-    second = from_behind(sent[1], "gy", 2)
+    first, third = from_behind(sent[0], "gy", 1), from_behind(sent[2], "gy", 3)
     packed = tiles.reshape(SLOTS_HERE, 2 * SLAB, 8, HALF)
-    moved, first, third, packed, packed_end = lax.optimization_barrier(
-        (exchange(components, 4), sent[0], sent[2], packed, packed[:, SLAB:])
+    moved, second, packed, packed_end = lax.optimization_barrier(
+        (exchange(components, 4), sent[1], packed, packed[:, SLAB:])
     )
     (filtered,) = call(
         filter_out_kernel,
@@ -521,7 +530,7 @@
     filtered, own, first, second, third, packed, packed_end = lax.optimization_barrier(
         (filtered, own, first, second, third, packed, packed_end)
     )
-    first, third = from_behind(first, "gy", 1), from_behind(third, "gy", 3)
+    second = from_behind(second, "gy", 2)
     tiles_before, tiles_second = from_behind(packed, "gz", 1), from_behind(packed_end, "gz", 2)
     moved = exchange(filtered, 8)
     slopes, middle = call(
@@ -538,8 +547,8 @@
         ],
         [((3, 2, NY, NX), f32), ((2048, HALF), f32)],
         [FAR, VMEM],
-        [((2, 3, NY, NX), f32), ((4, 2, NY, NX), f32)],
-        6,
+        [((3, 2, NY, NX), f32), ((4, 2, NY, NX), f32)],
+        5,
     )
     middle, slopes, tiles_before, tiles_second = lax.optimization_barrier(
         (middle, slopes.astype(f16), tiles_before, tiles_second)

time: 126 us -> 125 us (level)
  Pallas kernels: 14 us -> 12.5 us
    all_to_all x4, waiting for transfers between devices: 30.1 us -> 33.3 us  [exchange(): return lax.all_to_all(blocks, ('gz', 'gy'), 0, 0, tiled=True)]
    ppermute x9, waiting for transfers between devices: 9 us -> 5.88 us  [from_behind(): return lax.ppermute(x, axis, [(i, (i + by) % peers) for i in range(peers)])]
    pallas_call x5, Pallas kernels: 14 us -> 12.5 us  [call(): pl.pallas_call(kernel, out_shape=[jax.ShapeDtypeStruct(shape, kind) for s...]
  transfers between devices with their start and end apart: 13 -> 13, of which waited for: 6 -> 5; matrix products, arithmetic and copies ran while one was open for 11% -> 11% of each run, Pallas kernels for 10% -> 9%
where the time goes in v8:
time: 125 us
  starting transfers between devices  53.2 us (43%)
  waiting for transfers between devices  39.2 us (31%)
  Pallas kernels  12.5 us (10%)
  other arithmetic  11.2 us (9%)
  local copies, waits for them, and re-layouts  5.55 us (4%)
  matrix products  1.89 us (2%)
  between operations  1.33 us (1%)
    all_to_all x4, starting transfers between devices, exchange(): return lax.all_to_all(blocks, ('gz', 'gy'), 0, 0, tiled=True)  38.1 us
    all_to_all x4, waiting for transfers between devices, exchange(): return lax.all_to_all(blocks, ('gz', 'gy'), 0, 0, tiled=True)  33.3 us
    ppermute x9, starting transfers between devices, from_behind(): return lax.ppermute(x, axis, [(i, (i + by) % peers) for i in range(peers)])  15 us
    pallas_call x5, Pallas kernels, call(): pl.pallas_call(kernel, out_shape=[jax.ShapeDtypeStruct(shape, kind) for s...  12.5 us
    ppermute x9, waiting for transfers between devices, from_behind(): return lax.ppermute(x, axis, [(i, (i + by) % peers) for i in range(peers)])  5.88 us
    sub x1, other arithmetic, local(): new_velocity = velocity - buoyancy[None] * (slopes * (1.0 / RETURN_LINK))  2.6 us
  transfers between devices with their start and end apart: 13, of which 5 were waited for; matrix products, arithmetic and copies ran while one was open for 11% of the time, Pallas kernels for 9%

profile of v8, /device:TPU:1, one launch (start us, length us, event | category | flops | bytes accessed | tf_op | source)
XLA Modules:
  0.0 124.9 jit_solution(2810759742985004182)
XLA Ops:
  0.7 1.9 %fusion.11 = f32[256,4,128]{2,0,1:T(8,128)S(1)} fusion(f32[256,256,1]{1,0,2:T(8,128)} %constant.122, f32[4,128,256]{2,1,0:T(8,128)} %bitcast.32), kind=kOutput, calls=%fused_computation.40 | convolution fusion | flops 402653184 | bytes 1310720 | tf_op jit(solution)/shard_map/cx,abx->cab/dot_general | solution.py:494
  3.5 15.7 %all-to-all-start = ((f16[256,4,128]{2,1,0:T(4,128)(2,1)}), f16[256,4,128]{2,1,0:T(4,128)(2,1)S(1)}, u32[]{:S(2)}, u32[]{:S(2)}) async-start(f16[256,4,128]{2,1,0:T(4,128)(2,1)} %copy.19), calls=%async_computation | async-start | bytes 524288 | tf_op jit(solution)/shard_map/all_to_all | solution.py:479
  20.3 1.4 %collective-permute-start = (f16[4,2,64,256]{3,2,1,0:T(8,128)(2,1)}, f16[4,2,64,256]{3,2,1,0:T(8,128)(2,1)S(1)}, u32[]{:S(2)}, u32[]{:S(2)}) collective-permute-start(f16[4,2,64,256]{3,2,1,0:T(8,128)(2,1)} %get-tuple-element.63), channel_id=1, source_target_pairs={{0,1},{1,2},{2,3},{3,0},{4,5},{5,6},{6,7},{7,4},{8,9},{9,10},{10,1... | collective-permute-start | bytes 786440 | tf_op jit(solution)/shard_map/ppermute | solution.py:462
  21.7 1.3 %collective-permute-start.1 = (f16[4,2,64,256]{3,2,1,0:T(8,128)(2,1)}, f16[4,2,64,256]{3,2,1,0:T(8,128)(2,1)S(1)}, u32[]{:S(2)}, u32[]{:S(2)}) collective-permute-start(f16[4,2,64,256]{3,2,1,0:T(8,128)(2,1)} %get-tuple-element.60), channel_id=1, source_target_pairs={{0,3},{1,0},{2,1},{3,2},{4,7},{5,4},{6,5},{7,6},{8,11},{9,8},{10,9... | collective-permute-start | bytes 786440 | tf_op jit(solution)/shard_map/ppermute | solution.py:462
  23.0 1.9 %reshape.42.t0 = bf16[8,16,8,128]{3,2,1,0:T(8,128)(2,1)S(1)} reshape(bf16[8,16,32,32]{3,2,1,0:T(8,128)(2,1)} %param.17) | data formatting | bytes 524288 | tf_op jit(solution)/shard_map/reshape | solution.py:512
  25.6 8.8 %all-to-all-done = f16[256,4,128]{2,1,0:T(4,128)(2,1)S(1)} async-done(((f16[256,4,128]{2,1,0:T(4,128)(2,1)}), f16[256,4,128]{2,1,0:T(4,128)(2,1)S(1)}, u32[]{:S(2)}, u32[]{:S(2)}) %all-to-all-start) | async-done | bytes 262176 | tf_op jit(solution)/shard_map/all_to_all | solution.py:479
  34.5 2.0 %filter_out.1 = f32[2048,128]{1,0:T(8,128)S(1)} custom-call(s32[1]{0:T(128)} %bitcast.where, f32[1024,128]{1,0:T(8,128)S(1)} %convert.6.data, bf16[256,1536]{1,0:T(8,128)(2,1)S(1)} %copy-done.2, f32[136,128]{1,0:T(8,128)S(1)} %copy-done.3), custom_call_target="tpu_custom_call" | custom-call | flops 400000000 | bytes 1048576 | tf_op jit(solution)/shard_map/filter_out/pallas_call | solution.py:448
  37.4 8.5 %all-to-all-start.1 = ((f16[256,8,128]{2,1,0:T(8,128)(2,1)}), f16[256,8,128]{2,1,0:T(8,128)(2,1)}, u32[]{:S(2)}, u32[]{:S(2)}) async-start(f16[256,8,128]{2,1,0:T(8,128)(2,1)} %convert_bitcast_fusion.1), calls=%async_computation.1 | async-start | bytes 1048576 | tf_op jit(solution)/shard_map/all_to_all | solution.py:479
  45.9 3.0 %collective-permute-start.2 = (f16[4,2,64,256]{3,2,1,0:T(8,128)(2,1)S(1)}, f16[4,2,64,256]{3,2,1,0:T(8,128)(2,1)S(1)}, u32[]{:S(2)}, u32[]{:S(2)}) collective-permute-start(f16[4,2,64,256]{3,2,1,0:T(8,128)(2,1)S(1)} %get-tuple-element.43), channel_id=1, source_target_pairs={{0,2},{1,3},{2,0},{3,1},{4,6},{5,7},{6,4},{7,5},{8,10},{9,11},{10,... | collective-permute-start | bytes 786440 | tf_op jit(solution)/shard_map/ppermute | solution.py:462
  48.9 1.7 %collective-permute-start.3 = (bf16[8,16,8,128]{3,2,1,0:T(8,128)(2,1)S(1)}, bf16[8,16,8,128]{3,2,1,0:T(8,128)(2,1)S(1)}, u32[]{:S(2)}, u32[]{:S(2)}) collective-permute-start(bf16[8,16,8,128]{3,2,1,0:T(8,128)(2,1)S(1)} %reshape.42.t0), channel_id=1, source_target_pairs={{0,4},{4,8},{8,12},{12,16},{16,20},{20,24},{24,28},{28,32},{32,36}... | collective-permute-start | bytes 786440 | tf_op jit(solution)/shard_map/ppermute | solution.py:462
  52.0 5.9 %collective-permute-done.2 = f16[4,2,64,256]{3,2,1,0:T(8,128)(2,1)S(1)} collective-permute-done((f16[4,2,64,256]{3,2,1,0:T(8,128)(2,1)S(1)}, f16[4,2,64,256]{3,2,1,0:T(8,128)(2,1)S(1)}, u32[]{:S(2)}, u32[]{:S(2)}) %collective-permute-start.2) | collective-permute-done | bytes 262176 | tf_op jit(solution)/shard_map/ppermute | solution.py:462
  57.9 7.6 %all-to-all-done.1 = f16[256,8,128]{2,1,0:T(8,128)(2,1)} async-done(((f16[256,8,128]{2,1,0:T(8,128)(2,1)}), f16[256,8,128]{2,1,0:T(8,128)(2,1)}, u32[]{:S(2)}, u32[]{:S(2)}) %all-to-all-start.1) | async-done | bytes 524320 | tf_op jit(solution)/shard_map/all_to_all | solution.py:479
  66.6 3.5 %middle.1 = (f32[3,2,256,256]{3,2,1,0:T(8,128)S(1)}, f32[2048,128]{1,0:T(8,128)S(1)}) custom-call(s32[1]{0:T(128)} %bitcast.1.where, f32[2048,128]{1,0:T(8,128)S(1)} %bitcast_convert_fusion.1.data, bf16[256,1536]{1,0:T(8,128)(2,1)S(1)} %copy-done, f32[136,128]{1,0:T(8,128)S(1)} %copy-done.3, f32[3,4,2,64,256]{4,3,2,1,0:T(8,128)S(1)} %maximum_multiply_fusion.near, ...), custom_call_target="tpu_custom_call" | custom-call | flops 400000000 | bytes 1048576 | tf_op jit(solution)/shard_map/middle/pallas_call | solution.py:448
  71.2 6.6 %all-to-all-start.2 = ((f16[256,8,128]{2,1,0:T(8,128)(2,1)}), f16[256,8,128]{2,1,0:T(8,128)(2,1)S(1)}, u32[]{:S(2)}, u32[]{:S(2)}) async-start(f16[256,8,128]{2,1,0:T(8,128)(2,1)} %convert_bitcast_fusion), calls=%async_computation.2 | async-start | bytes 1048576 | tf_op jit(solution)/shard_map/all_to_all | solution.py:479
  80.9 1.4 %collective-permute-start.5 = (f16[3,2,64,256]{3,2,1,0:T(8,128)(2,1)}, f16[3,2,64,256]{3,2,1,0:T(8,128)(2,1)}, u32[]{:S(2)}, u32[]{:S(2)}) collective-permute-start(f16[3,2,64,256]{3,2,1,0:T(8,128)(2,1)} %get-tuple-element.68), channel_id=1, source_target_pairs={{0,1},{1,2},{2,3},{3,0},{4,5},{5,6},{6,7},{7,4},{8,9},{9,10},{10,1... | collective-permute-start | bytes 589832 | tf_op jit(solution)/shard_map/ppermute | solution.py:462
  82.3 2.4 %collective-permute-start.6 = (f16[3,2,64,256]{3,2,1,0:T(8,128)(2,1)}, f16[3,2,64,256]{3,2,1,0:T(8,128)(2,1)}, u32[]{:S(2)}, u32[]{:S(2)}) collective-permute-start(f16[3,2,64,256]{3,2,1,0:T(8,128)(2,1)} %get-tuple-element.70), channel_id=1, source_target_pairs={{0,2},{1,3},{2,0},{3,1},{4,6},{5,7},{6,4},{7,5},{8,10},{9,11},{10,... | collective-permute-start | bytes 589832 | tf_op jit(solution)/shard_map/ppermute | solution.py:462
  85.9 3.8 %source.1 = (f32[8,64,256]{2,1,0:T(8,128)S(1)}, bf16[8,32,256]{2,1,0:T(8,128)(2,1)S(1)}) custom-call(s32[2]{0:T(128)S(1)} %pad_add_fusion.where, s32[256]{0:T(256)S(1)} %copy-done.7, s32[8,3]{1,0:T(8,128)S(1)} %copy.23.c0, s32[8,3]{1,0:T(8,128)S(1)} %copy.24.c1, s32[8,3]{1,0:T(8,128)S(1)} %copy.25.c2, bf16[8,16,8,128]{3,2,1,0:T(8,128)(2,1)S(1)} %reshape.42.t0, ...), custom_call_target="tpu_custom_call" | custom-call | flops 400000000 | bytes 1048576 | tf_op jit(solution)/shard_map/source/pallas_call | solution.py:448
  89.7 8.2 %all-to-all-done.2 = f16[256,8,128]{2,1,0:T(8,128)(2,1)S(1)} async-done(((f16[256,8,128]{2,1,0:T(8,128)(2,1)}), f16[256,8,128]{2,1,0:T(8,128)(2,1)S(1)}, u32[]{:S(2)}, u32[]{:S(2)}) %all-to-all-start.2) | async-done | bytes 524320 | tf_op jit(solution)/shard_map/all_to_all | solution.py:479
  98.0 2.1 %filter_back.1 = f32[1024,128]{1,0:T(8,128)S(1)} custom-call(s32[1]{0:T(128)} %bitcast.where, f32[2048,128]{1,0:T(8,128)S(1)} %bitcast_convert_fusion.data, bf16[256,1536]{1,0:T(8,128)(2,1)S(1)} %copy-done.1, f32[136,128]{1,0:T(8,128)S(1)} %copy-done.3), custom_call_target="tpu_custom_call" | custom-call | flops 400000000 | bytes 1048576 | tf_op jit(solution)/shard_map/filter_back/pallas_call | solution.py:448
  100.8 7.4 %all-to-all-start.3 = ((f16[256,4,128]{2,1,0:T(4,128)(2,1)}), f16[256,4,128]{2,1,0:T(4,128)(2,1)}, u32[]{:S(2)}, u32[]{:S(2)}) async-start(f16[256,4,128]{2,1,0:T(4,128)(2,1)} %bitcast.14), calls=%async_computation.3 | async-start | bytes 524288 | tf_op jit(solution)/shard_map/all_to_all | solution.py:479
  108.3 1.5 %select_select_fusion.3 = (f16[3,2,64,256]{3,2,1,0:T(8,128)(2,1)S(1)}, f16[3,2,64,256]{3,2,1,0:T(8,128)(2,1)S(1)}, f16[3,2,64,256]{3,2,1,0:T(8,128)(2,1)S(1)}, f16[3,2,64,256]{3,2,1,0:T(8,128)(2,1)S(1)}) fusion(f16[3,2,64,256]{3,2,1,0:T(8,128)(2,1)} %collective-permute-done.6, f16[3,2,64,256]{3,2,1,0:T(8,128)(2,1)} %collective-permute-done.7, ...), kind=kLoop, calls=%fused_computation.32 | loop fusion | flops 1179648 | bytes 1572880 | tf_op jit(solution)/shard_map/select_n | solution.py:472
  109.8 1.5 %collective-permute-start.8 = (bf16[8,32,256]{2,1,0:T(8,128)(2,1)S(1)}, bf16[8,32,256]{2,1,0:T(8,128)(2,1)S(1)}, u32[]{:S(2)}, u32[]{:S(2)}) collective-permute-start(bf16[8,32,256]{2,1,0:T(8,128)(2,1)S(1)} %get-tuple-element.58), channel_id=1, source_target_pairs={{0,1},{1,2},{2,3},{3,0},{4,5},{5,6},{6,7},{7,4},{8,9},{9,10},{10,1... | collective-permute-start | bytes 393224 | tf_op jit(solution)/shard_map/ppermute | solution.py:462
  111.3 2.6 %multiply_subtract_fusion = f32[3,8,64,256]{3,2,1,0:T(8,128)} fusion(f32[3,8,64,256]{3,2,1,0:T(8,128)S(1)} %copy-done.9, f16[3,2,64,256]{3,2,1,0:T(8,128)(2,1)S(1)} %get-tuple-element.65, f16[3,2,64,256]{3,2,1,0:T(8,128)(2,1)S(1)} %get-tuple-element.66, f16[3,2,64,256]{3,2,1,0:T(8,128)(2,1)S(1)} %get-tuple-element.67, ...), kind=kLoop, calls=%fused_computation.9 | loop fusion | flops 2359296 | bytes 4456448 | tf_op jit(solution)/shard_map/sub | solution.py:557
  113.9 8.7 %all-to-all-done.3 = f16[256,4,128]{2,1,0:T(4,128)(2,1)} async-done(((f16[256,4,128]{2,1,0:T(4,128)(2,1)}), f16[256,4,128]{2,1,0:T(4,128)(2,1)}, u32[]{:S(2)}, u32[]{:S(2)}) %all-to-all-start.3) | async-done | bytes 262176 | tf_op jit(solution)/shard_map/all_to_all | solution.py:479
  (59 shorter events, 14.2 us)
Async XLA Ops:
  0.6 18.6 %copy-start.8 = (f32[3,8,64,256]{3,2,1,0:T(8,128)S(1)}, f32[3,8,64,256]{3,2,1,0:T(8,128)}, u32[]{:S(2)}) copy-start(f32[3,8,64,256]{3,2,1,0:T(8,128)} %param.14) | copy-start | bytes 4718596
  0.6 18.6 %copy-start.11 = (f32[8,64,256]{2,1,0:T(8,128)S(1)}, f32[8,64,256]{2,1,0:T(8,128)}, u32[]{:S(2)}) copy-start(f32[8,64,256]{2,1,0:T(8,128)} %param.16) | copy-start | bytes 1572868
  3.5 30.9 %all-to-all-start = ((f16[256,4,128]{2,1,0:T(4,128)(2,1)}), f16[256,4,128]{2,1,0:T(4,128)(2,1)S(1)}, u32[]{:S(2)}, u32[]{:S(2)}) async-start(f16[256,4,128]{2,1,0:T(4,128)(2,1)} %copy.19), calls=%async_computation | async-start | bytes 524288 | tf_op jit(solution)/shard_map/all_to_all | solution.py:479
  20.3 14.2 %copy-start.2 = (bf16[256,1536]{1,0:T(8,128)(2,1)S(1)}, bf16[256,1536]{1,0:T(8,128)(2,1)}, u32[]{:S(2)}) copy-start(bf16[256,1536]{1,0:T(8,128)(2,1)} %constant.114.clone.tables) | copy-start | bytes 2359300
  20.3 14.2 %copy-start.3 = (f32[136,128]{1,0:T(8,128)S(1)}, f32[136,128]{1,0:T(8,128)}, u32[]{:S(2)}) copy-start(f32[136,128]{1,0:T(8,128)} %constant.116.clone.numbers) | copy-start | bytes 208900
  20.3 16.2 %collective-permute-start = (f16[4,2,64,256]{3,2,1,0:T(8,128)(2,1)}, f16[4,2,64,256]{3,2,1,0:T(8,128)(2,1)S(1)}, u32[]{:S(2)}, u32[]{:S(2)}) collective-permute-start(f16[4,2,64,256]{3,2,1,0:T(8,128)(2,1)} %get-tuple-element.63), channel_id=1, source_target_pairs={{0,1},{1,2},{2,3},{3,0},{4,5},{5,6},{6,7},{7,4},{8,9},{9,10},{10,1... | collective-permute-start | bytes 786440 | tf_op jit(solution)/shard_map/ppermute | solution.py:462
  21.7 14.8 %collective-permute-start.1 = (f16[4,2,64,256]{3,2,1,0:T(8,128)(2,1)}, f16[4,2,64,256]{3,2,1,0:T(8,128)(2,1)S(1)}, u32[]{:S(2)}, u32[]{:S(2)}) collective-permute-start(f16[4,2,64,256]{3,2,1,0:T(8,128)(2,1)} %get-tuple-element.60), channel_id=1, source_target_pairs={{0,3},{1,0},{2,1},{3,2},{4,7},{5,4},{6,5},{7,6},{8,11},{9,8},{10,9... | collective-permute-start | bytes 786440 | tf_op jit(solution)/shard_map/ppermute | solution.py:462
  37.4 28.1 %all-to-all-start.1 = ((f16[256,8,128]{2,1,0:T(8,128)(2,1)}), f16[256,8,128]{2,1,0:T(8,128)(2,1)}, u32[]{:S(2)}, u32[]{:S(2)}) async-start(f16[256,8,128]{2,1,0:T(8,128)(2,1)} %convert_bitcast_fusion.1), calls=%async_computation.1 | async-start | bytes 1048576 | tf_op jit(solution)/shard_map/all_to_all | solution.py:479
  45.9 12.0 %collective-permute-start.2 = (f16[4,2,64,256]{3,2,1,0:T(8,128)(2,1)S(1)}, f16[4,2,64,256]{3,2,1,0:T(8,128)(2,1)S(1)}, u32[]{:S(2)}, u32[]{:S(2)}) collective-permute-start(f16[4,2,64,256]{3,2,1,0:T(8,128)(2,1)S(1)} %get-tuple-element.43), channel_id=1, source_target_pairs={{0,2},{1,3},{2,0},{3,1},{4,6},{5,7},{6,4},{7,5},{8,10},{9,11},{10,... | collective-permute-start | bytes 786440 | tf_op jit(solution)/shard_map/ppermute | solution.py:462
  48.9 21.5 %collective-permute-start.3 = (bf16[8,16,8,128]{3,2,1,0:T(8,128)(2,1)S(1)}, bf16[8,16,8,128]{3,2,1,0:T(8,128)(2,1)S(1)}, u32[]{:S(2)}, u32[]{:S(2)}) collective-permute-start(bf16[8,16,8,128]{3,2,1,0:T(8,128)(2,1)S(1)} %reshape.42.t0), channel_id=1, source_target_pairs={{0,4},{4,8},{8,12},{12,16},{16,20},{20,24},{24,28},{28,32},{32,36}... | collective-permute-start | bytes 786440 | tf_op jit(solution)/shard_map/ppermute | solution.py:462
  50.6 19.8 %collective-permute-start.4 = (bf16[8,8,8,128]{3,2,1,0:T(8,128)(2,1)}, bf16[8,8,8,128]{3,2,1,0:T(8,128)(2,1)}, u32[]{:S(2)}, u32[]{:S(2)}) collective-permute-start(bf16[8,8,8,128]{3,2,1,0:T(8,128)(2,1)} %slice.4), channel_id=1, source_target_pairs={{0,8},{4,12},{8,16},{12,20},{16,24},{20,28},{24,32},{28,36},{32,40... | collective-permute-start | bytes 393224 | tf_op jit(solution)/shard_map/ppermute | solution.py:462
  52.0 14.6 %copy-start = (bf16[256,1536]{1,0:T(8,128)(2,1)S(1)}, bf16[256,1536]{1,0:T(8,128)(2,1)}, u32[]{:S(2)}) copy-start(bf16[256,1536]{1,0:T(8,128)(2,1)} %constant.113.clone.tables) | copy-start | bytes 2359300
  71.2 14.7 %copy-start.5 = (f32[8,64,256]{2,1,0:T(8,128)S(1)}, f32[8,64,256]{2,1,0:T(8,128)}, u32[]{:S(2)}) copy-start(f32[8,64,256]{2,1,0:T(8,128)} %pressure.1) | copy-start | bytes 1572868
  71.2 14.7 %copy-start.7 = (s32[256]{0:T(256)S(1)}, s32[256]{0:T(256)}, u32[]{:S(2)}) copy-start(s32[256]{0:T(256)} %lives.1) | copy-start | bytes 3076
  71.2 26.6 %all-to-all-start.2 = ((f16[256,8,128]{2,1,0:T(8,128)(2,1)}), f16[256,8,128]{2,1,0:T(8,128)(2,1)S(1)}, u32[]{:S(2)}, u32[]{:S(2)}) async-start(f16[256,8,128]{2,1,0:T(8,128)(2,1)} %convert_bitcast_fusion), calls=%async_computation.2 | async-start | bytes 1048576 | tf_op jit(solution)/shard_map/all_to_all | solution.py:479
  80.9 17.0 %copy-start.1 = (bf16[256,1536]{1,0:T(8,128)(2,1)S(1)}, bf16[256,1536]{1,0:T(8,128)(2,1)}, u32[]{:S(2)}) copy-start(bf16[256,1536]{1,0:T(8,128)(2,1)} %constant.115.clone.tables) | copy-start | bytes 2359300
  80.9 27.3 %collective-permute-start.5 = (f16[3,2,64,256]{3,2,1,0:T(8,128)(2,1)}, f16[3,2,64,256]{3,2,1,0:T(8,128)(2,1)}, u32[]{:S(2)}, u32[]{:S(2)}) collective-permute-start(f16[3,2,64,256]{3,2,1,0:T(8,128)(2,1)} %get-tuple-element.68), channel_id=1, source_target_pairs={{0,1},{1,2},{2,3},{3,0},{4,5},{5,6},{6,7},{7,4},{8,9},{9,10},{10,1... | collective-permute-start | bytes 589832 | tf_op jit(solution)/shard_map/ppermute | solution.py:462
  82.3 25.9 %collective-permute-start.6 = (f16[3,2,64,256]{3,2,1,0:T(8,128)(2,1)}, f16[3,2,64,256]{3,2,1,0:T(8,128)(2,1)}, u32[]{:S(2)}, u32[]{:S(2)}) collective-permute-start(f16[3,2,64,256]{3,2,1,0:T(8,128)(2,1)} %get-tuple-element.70), channel_id=1, source_target_pairs={{0,2},{1,3},{2,0},{3,1},{4,6},{5,7},{6,4},{7,5},{8,10},{9,11},{10,... | collective-permute-start | bytes 589832 | tf_op jit(solution)/shard_map/ppermute | solution.py:462
  84.8 23.5 %collective-permute-start.7 = (f16[3,2,64,256]{3,2,1,0:T(8,128)(2,1)S(1)}, f16[3,2,64,256]{3,2,1,0:T(8,128)(2,1)}, u32[]{:S(2)}, u32[]{:S(2)}) collective-permute-start(f16[3,2,64,256]{3,2,1,0:T(8,128)(2,1)S(1)} %get-tuple-element.69), channel_id=1, source_target_pairs={{0,3},{1,0},{2,1},{3,2},{4,7},{5,4},{6,5},{7,6},{8,11},{9,8},{10,9... | collective-permute-start | bytes 589832 | tf_op jit(solution)/shard_map/ppermute | solution.py:462
  100.1 11.2 %copy-start.9 = (f32[3,8,64,256]{3,2,1,0:T(8,128)S(1)}, f32[3,8,64,256]{3,2,1,0:T(8,128)}, u32[]{:S(2)}) copy-start(f32[3,8,64,256]{3,2,1,0:T(8,128)} %param.14) | copy-start | bytes 4718596
  100.8 21.7 %all-to-all-start.3 = ((f16[256,4,128]{2,1,0:T(4,128)(2,1)}), f16[256,4,128]{2,1,0:T(4,128)(2,1)}, u32[]{:S(2)}, u32[]{:S(2)}) async-start(f16[256,4,128]{2,1,0:T(4,128)(2,1)} %bitcast.14), calls=%async_computation.3 | async-start | bytes 524288 | tf_op jit(solution)/shard_map/all_to_all | solution.py:479
  109.8 13.7 %collective-permute-start.8 = (bf16[8,32,256]{2,1,0:T(8,128)(2,1)S(1)}, bf16[8,32,256]{2,1,0:T(8,128)(2,1)S(1)}, u32[]{:S(2)}, u32[]{:S(2)}) collective-permute-start(bf16[8,32,256]{2,1,0:T(8,128)(2,1)S(1)} %get-tuple-element.58), channel_id=1, source_target_pairs={{0,1},{1,2},{2,3},{3,0},{4,5},{5,6},{6,7},{7,4},{8,9},{9,10},{10,1... | collective-permute-start | bytes 393224 | tf_op jit(solution)/shard_map/ppermute | solution.py:462
  111.2 12.3 %copy-start.4 = (f32[8,64,256]{2,1,0:T(8,128)S(1)}, f32[8,64,256]{2,1,0:T(8,128)}, u32[]{:S(2)}) copy-start(f32[8,64,256]{2,1,0:T(8,128)} %bulk.1) | copy-start | bytes 1572868
  111.3 12.3 %copy-start.6 = (bf16[256,512]{1,0:T(8,128)(2,1)S(1)}, bf16[256,512]{1,0:T(8,128)(2,1)}, u32[]{:S(2)}) copy-start(bf16[256,512]{1,0:T(8,128)(2,1)} %constant.111.clone.x_ref) | copy-start | bytes 786436
  (2 other events, 18.6 us)

commit v9 on v8

--- a/solution.py
+++ b/solution.py
@@ -297,24 +297,19 @@
         for field in range(2)
     ]
     real, imag = q[:, :HALF], q[:, HALF:]
-    lines = jnp.concatenate(
-        [
-            ahead_real * real - ahead_imag * imag,
-            weight * real,
-            weight * g[:, :HALF],
-            ahead_real * imag + ahead_imag * real,
-            weight * imag,
-            weight * g[:, HALF:],
-        ],
-        axis=0,
-    )
-    lines = jnp.concatenate([lines[: 3 * 512], lines[3 * 512 :]], axis=1)
-    lines = right(lines, x_ref) * (X_SCALE / SLOPE_LINK)
-    along_y = left(ya_ref, jnp.concatenate([lines[512:768], lines[768:1024]], axis=1))
+    scale = X_SCALE / SLOPE_LINK
+    plain = right(jnp.concatenate([weight * real, weight * imag], axis=1), x_ref) * scale
+    steep = jnp.concatenate(
+        [ahead_real * real - ahead_imag * imag, ahead_real * imag + ahead_imag * real], axis=1
+    )
+    steep = right(steep, x_ref) * scale
+    along_y = left(ya_ref, jnp.concatenate([plain[:256], plain[256:]], axis=1))
+    along_z = jnp.concatenate([weight * g[:, :HALF], weight * g[:, HALF:]], axis=1)
+    along_z = right(along_z, x_ref) * scale
     along = (
-        (lines[:256], lines[256:512]),
+        (steep[:256], steep[256:]),
         (along_y[:, :NX], along_y[:, NX:]),
-        (lines[1024:1280], lines[1280:]),
+        (along_z[:256], along_z[256:]),
     )
     for d in range(3):
         for r in range(2):
@@ -325,11 +320,13 @@
         fetch[i]
     moved = [[fields[d, r] - fields[3, r] * along[d][r] for r in range(2)] for d in range(3)]
     along_y = left(yb_ref, jnp.concatenate(moved[1], axis=1))
-    lines = jnp.concatenate([*moved[0], along_y[:, :NX], along_y[:, NX:], *moved[2]], axis=0)
-    components = to_components(x_ref, lines) * (X_SCALE * MIDDLE_LINK)
-    real, imag = components[:HALF, : 2 * NY], components[HALF:, : 2 * NY]
-    across = jnp.concatenate(times(real, imag, behind[0], behind[1]), axis=0)
-    for field, part in enumerate((across + components[:, 2 * NY : 4 * NY], components[:, 4 * NY :])):
+    scale = X_SCALE * MIDDLE_LINK
+    steep, along_z, along_y = [
+        to_components(x_ref, jnp.concatenate(lines, axis=0)) * scale
+        for lines in (moved[0], moved[2], (along_y[:, :NX], along_y[:, NX:]))
+    ]
+    across = jnp.concatenate(times(steep[:HALF], steep[HALF:], behind[0], behind[1]), axis=0)
+    for field, part in enumerate((across + along_y, along_z)):
         for r in range(2):
             for side in range(2):
                 out[pl.ds(4 * r + 2 * field + side, 256, stride=8), :] = part[
@@ -495,7 +492,7 @@
         "cx,abx->cab",
         table["x_lines"],
         pressure.reshape(4, HALF, NX),
-        precision=lax.Precision.HIGHEST,
+        precision=lax.Precision.HIGH,
     )
     velocity_later, buoyancy_later, tiles, slab_later, components = lax.optimization_barrier(
         (velocity, buoyancy, tiles, slab_index, components)
@@ -594,8 +591,8 @@
         [((1024, HALF), f32)],
         [VMEM],
     )
-    filtered_back, own, passed = lax.optimization_barrier((filtered_back, own, passed))
     passed = from_behind(passed, "gy", 1)
+    filtered_back, own = lax.optimization_barrier((filtered_back, own))
     moved, new_velocity = lax.optimization_barrier((exchange(filtered_back, 4), new_velocity))
     (new_pressure,) = call(
         new_pressure_kernel,

time: 125 us -> 125 us (level)
  no operation moved by 1% of the time
where the time goes in v9:
time: 125 us; the launch traced here: 124 us
  starting transfers between devices  52.2 us (42%)
  waiting for transfers between devices  40.2 us (32%)
  Pallas kernels  11.9 us (10%)
  other arithmetic  11.2 us (9%)
  local copies, waits for them, and re-layouts  5.56 us (4%)
  matrix products  1.69 us (1%)
  between operations  1.36 us (1%)
    all_to_all x4, starting transfers between devices, exchange(): return lax.all_to_all(blocks, ('gz', 'gy'), 0, 0, tiled=True)  38.2 us
    all_to_all x4, waiting for transfers between devices, exchange(): return lax.all_to_all(blocks, ('gz', 'gy'), 0, 0, tiled=True)  34.3 us
    ppermute x9, starting transfers between devices, from_behind(): return lax.ppermute(x, axis, [(i, (i + by) % peers) for i in range(peers)])  14 us
    pallas_call x5, Pallas kernels, call(): pl.pallas_call(kernel, out_shape=[jax.ShapeDtypeStruct(shape, kind) for s...  11.9 us
    ppermute x9, waiting for transfers between devices, from_behind(): return lax.ppermute(x, axis, [(i, (i + by) % peers) for i in range(peers)])  5.88 us
    sub x1, other arithmetic, local(): new_velocity = velocity - buoyancy[None] * (slopes * (1.0 / RETURN_LINK))  2.6 us
  transfers between devices with their start and end apart: 13, of which 5 were waited for; matrix products, arithmetic and copies ran while one was open for 11% of the time, Pallas kernels for 9%

profile of v9, /device:TPU:1, one launch (start us, length us, event | category | flops | bytes accessed | tf_op | source)
XLA Modules:
  0.0 124.2 jit_solution(15825518317731070368)
XLA Ops:
  0.7 1.7 %fusion.11 = f32[256,4,128]{2,0,1:T(8,128)S(1)} fusion(f32[256,256,1]{1,0,2:T(8,128)} %constant.122, f32[4,128,256]{2,1,0:T(8,128)} %bitcast.32), kind=kOutput, calls=%fused_computation.40 | convolution fusion | flops 201326592 | bytes 1310720 | tf_op jit(solution)/shard_map/cx,abx->cab/dot_general | solution.py:491
  3.3 15.7 %all-to-all-start = ((f16[256,4,128]{2,1,0:T(4,128)(2,1)}), f16[256,4,128]{2,1,0:T(4,128)(2,1)S(1)}, u32[]{:S(2)}, u32[]{:S(2)}) async-start(f16[256,4,128]{2,1,0:T(4,128)(2,1)} %copy.19), calls=%async_computation | async-start | bytes 524288 | tf_op jit(solution)/shard_map/all_to_all | solution.py:476
  20.1 1.4 %collective-permute-start = (f16[4,2,64,256]{3,2,1,0:T(8,128)(2,1)}, f16[4,2,64,256]{3,2,1,0:T(8,128)(2,1)S(1)}, u32[]{:S(2)}, u32[]{:S(2)}) collective-permute-start(f16[4,2,64,256]{3,2,1,0:T(8,128)(2,1)} %get-tuple-element.61), channel_id=1, source_target_pairs={{0,1},{1,2},{2,3},{3,0},{4,5},{5,6},{6,7},{7,4},{8,9},{9,10},{10,1... | collective-permute-start | bytes 786440 | tf_op jit(solution)/shard_map/ppermute | solution.py:459
  21.5 1.3 %collective-permute-start.1 = (f16[4,2,64,256]{3,2,1,0:T(8,128)(2,1)}, f16[4,2,64,256]{3,2,1,0:T(8,128)(2,1)S(1)}, u32[]{:S(2)}, u32[]{:S(2)}) collective-permute-start(f16[4,2,64,256]{3,2,1,0:T(8,128)(2,1)} %get-tuple-element.58), channel_id=1, source_target_pairs={{0,3},{1,0},{2,1},{3,2},{4,7},{5,4},{6,5},{7,6},{8,11},{9,8},{10,9... | collective-permute-start | bytes 786440 | tf_op jit(solution)/shard_map/ppermute | solution.py:459
  22.8 1.9 %reshape.42.t0 = bf16[8,16,8,128]{3,2,1,0:T(8,128)(2,1)S(1)} reshape(bf16[8,16,32,32]{3,2,1,0:T(8,128)(2,1)} %param.17) | data formatting | bytes 524288 | tf_op jit(solution)/shard_map/reshape | solution.py:509
  25.4 8.8 %all-to-all-done = f16[256,4,128]{2,1,0:T(4,128)(2,1)S(1)} async-done(((f16[256,4,128]{2,1,0:T(4,128)(2,1)}), f16[256,4,128]{2,1,0:T(4,128)(2,1)S(1)}, u32[]{:S(2)}, u32[]{:S(2)}) %all-to-all-start) | async-done | bytes 262176 | tf_op jit(solution)/shard_map/all_to_all | solution.py:476
  34.3 2.0 %filter_out.1 = f32[2048,128]{1,0:T(8,128)S(1)} custom-call(s32[1]{0:T(128)} %bitcast.where, f32[1024,128]{1,0:T(8,128)S(1)} %convert.6.data, bf16[256,1536]{1,0:T(8,128)(2,1)S(1)} %copy-done.2, f32[136,128]{1,0:T(8,128)S(1)} %copy-done.3), custom_call_target="tpu_custom_call" | custom-call | flops 400000000 | bytes 1048576 | tf_op jit(solution)/shard_map/filter_out/pallas_call | solution.py:445
  37.2 8.5 %all-to-all-start.1 = ((f16[256,8,128]{2,1,0:T(8,128)(2,1)}), f16[256,8,128]{2,1,0:T(8,128)(2,1)}, u32[]{:S(2)}, u32[]{:S(2)}) async-start(f16[256,8,128]{2,1,0:T(8,128)(2,1)} %convert_bitcast_fusion.1), calls=%async_computation.1 | async-start | bytes 1048576 | tf_op jit(solution)/shard_map/all_to_all | solution.py:476
  45.7 3.0 %collective-permute-start.2 = (f16[4,2,64,256]{3,2,1,0:T(8,128)(2,1)S(1)}, f16[4,2,64,256]{3,2,1,0:T(8,128)(2,1)S(1)}, u32[]{:S(2)}, u32[]{:S(2)}) collective-permute-start(f16[4,2,64,256]{3,2,1,0:T(8,128)(2,1)S(1)} %get-tuple-element.42), channel_id=1, source_target_pairs={{0,2},{1,3},{2,0},{3,1},{4,6},{5,7},{6,4},{7,5},{8,10},{9,11},{10,... | collective-permute-start | bytes 786440 | tf_op jit(solution)/shard_map/ppermute | solution.py:459
  48.7 1.7 %collective-permute-start.3 = (bf16[8,16,8,128]{3,2,1,0:T(8,128)(2,1)S(1)}, bf16[8,16,8,128]{3,2,1,0:T(8,128)(2,1)S(1)}, u32[]{:S(2)}, u32[]{:S(2)}) collective-permute-start(bf16[8,16,8,128]{3,2,1,0:T(8,128)(2,1)S(1)} %reshape.42.t0), channel_id=1, source_target_pairs={{0,4},{4,8},{8,12},{12,16},{16,20},{20,24},{24,28},{28,32},{32,36}... | collective-permute-start | bytes 786440 | tf_op jit(solution)/shard_map/ppermute | solution.py:459
  50.4 1.2 collective-permute-start.4
  51.8 5.9 %collective-permute-done.2 = f16[4,2,64,256]{3,2,1,0:T(8,128)(2,1)S(1)} collective-permute-done((f16[4,2,64,256]{3,2,1,0:T(8,128)(2,1)S(1)}, f16[4,2,64,256]{3,2,1,0:T(8,128)(2,1)S(1)}, u32[]{:S(2)}, u32[]{:S(2)}) %collective-permute-start.2) | collective-permute-done | bytes 262176 | tf_op jit(solution)/shard_map/ppermute | solution.py:459
  57.7 7.6 %all-to-all-done.1 = f16[256,8,128]{2,1,0:T(8,128)(2,1)} async-done(((f16[256,8,128]{2,1,0:T(8,128)(2,1)}), f16[256,8,128]{2,1,0:T(8,128)(2,1)}, u32[]{:S(2)}, u32[]{:S(2)}) %all-to-all-start.1) | async-done | bytes 524320 | tf_op jit(solution)/shard_map/all_to_all | solution.py:476
  66.4 2.9 %middle.1 = (f32[3,2,256,256]{3,2,1,0:T(8,128)S(1)}, f32[2048,128]{1,0:T(8,128)S(1)}) custom-call(s32[1]{0:T(128)} %bitcast.1.where, f32[2048,128]{1,0:T(8,128)S(1)} %bitcast_convert_fusion.1.data, bf16[256,1536]{1,0:T(8,128)(2,1)S(1)} %copy-done, f32[136,128]{1,0:T(8,128)S(1)} %copy-done.3, f32[3,4,2,64,256]{4,3,2,1,0:T(8,128)S(1)} %maximum_multiply_fusion.near, ...), custom_call_target="tpu_custom_call" | custom-call | flops 400000000 | bytes 1048576 | tf_op jit(solution)/shard_map/middle/pallas_call | solution.py:445
  70.4 6.6 %all-to-all-start.2 = ((f16[256,8,128]{2,1,0:T(8,128)(2,1)}), f16[256,8,128]{2,1,0:T(8,128)(2,1)S(1)}, u32[]{:S(2)}, u32[]{:S(2)}) async-start(f16[256,8,128]{2,1,0:T(8,128)(2,1)} %convert_bitcast_fusion), calls=%async_computation.2 | async-start | bytes 1048576 | tf_op jit(solution)/shard_map/all_to_all | solution.py:476
  80.1 1.4 %collective-permute-start.5 = (f16[3,2,64,256]{3,2,1,0:T(8,128)(2,1)}, f16[3,2,64,256]{3,2,1,0:T(8,128)(2,1)}, u32[]{:S(2)}, u32[]{:S(2)}) collective-permute-start(f16[3,2,64,256]{3,2,1,0:T(8,128)(2,1)} %get-tuple-element.66), channel_id=1, source_target_pairs={{0,1},{1,2},{2,3},{3,0},{4,5},{5,6},{6,7},{7,4},{8,9},{9,10},{10,1... | collective-permute-start | bytes 589832 | tf_op jit(solution)/shard_map/ppermute | solution.py:459
  81.5 2.4 %collective-permute-start.6 = (f16[3,2,64,256]{3,2,1,0:T(8,128)(2,1)}, f16[3,2,64,256]{3,2,1,0:T(8,128)(2,1)}, u32[]{:S(2)}, u32[]{:S(2)}) collective-permute-start(f16[3,2,64,256]{3,2,1,0:T(8,128)(2,1)} %get-tuple-element.68), channel_id=1, source_target_pairs={{0,2},{1,3},{2,0},{3,1},{4,6},{5,7},{6,4},{7,5},{8,10},{9,11},{10,... | collective-permute-start | bytes 589832 | tf_op jit(solution)/shard_map/ppermute | solution.py:459
  85.1 3.8 %source.1 = (f32[8,64,256]{2,1,0:T(8,128)S(1)}, bf16[8,32,256]{2,1,0:T(8,128)(2,1)S(1)}) custom-call(s32[2]{0:T(128)S(1)} %pad_add_fusion.where, s32[256]{0:T(256)S(1)} %copy-done.7, s32[8,3]{1,0:T(8,128)S(1)} %copy.23.c0, s32[8,3]{1,0:T(8,128)S(1)} %copy.24.c1, s32[8,3]{1,0:T(8,128)S(1)} %copy.25.c2, bf16[8,16,8,128]{3,2,1,0:T(8,128)(2,1)S(1)} %reshape.42.t0, ...), custom_call_target="tpu_custom_call" | custom-call | flops 400000000 | bytes 1048576 | tf_op jit(solution)/shard_map/source/pallas_call | solution.py:445
  89.3 7.8 %all-to-all-done.2 = f16[256,8,128]{2,1,0:T(8,128)(2,1)S(1)} async-done(((f16[256,8,128]{2,1,0:T(8,128)(2,1)}), f16[256,8,128]{2,1,0:T(8,128)(2,1)S(1)}, u32[]{:S(2)}, u32[]{:S(2)}) %all-to-all-start.2) | async-done | bytes 524320 | tf_op jit(solution)/shard_map/all_to_all | solution.py:476
  97.2 2.1 %filter_back.1 = f32[1024,128]{1,0:T(8,128)S(1)} custom-call(s32[1]{0:T(128)} %bitcast.where, f32[2048,128]{1,0:T(8,128)S(1)} %bitcast_convert_fusion.data, bf16[256,1536]{1,0:T(8,128)(2,1)S(1)} %copy-done.1, f32[136,128]{1,0:T(8,128)S(1)} %copy-done.3), custom_call_target="tpu_custom_call" | custom-call | flops 400000000 | bytes 1048576 | tf_op jit(solution)/shard_map/filter_back/pallas_call | solution.py:445
  100.0 7.5 %all-to-all-start.3 = ((f16[256,4,128]{2,1,0:T(4,128)(2,1)}), f16[256,4,128]{2,1,0:T(4,128)(2,1)}, u32[]{:S(2)}, u32[]{:S(2)}) async-start(f16[256,4,128]{2,1,0:T(4,128)(2,1)} %bitcast.14), calls=%async_computation.3 | async-start | bytes 524288 | tf_op jit(solution)/shard_map/all_to_all | solution.py:476
  107.6 1.5 %select_select_fusion.3 = (f16[3,2,64,256]{3,2,1,0:T(8,128)(2,1)S(1)}, f16[3,2,64,256]{3,2,1,0:T(8,128)(2,1)S(1)}, f16[3,2,64,256]{3,2,1,0:T(8,128)(2,1)S(1)}, f16[3,2,64,256]{3,2,1,0:T(8,128)(2,1)S(1)}) fusion(f16[3,2,64,256]{3,2,1,0:T(8,128)(2,1)} %collective-permute-done.6, f16[3,2,64,256]{3,2,1,0:T(8,128)(2,1)} %collective-permute-done.7, ...), kind=kLoop, calls=%fused_computation.32 | loop fusion | flops 1179648 | bytes 1572880 | tf_op jit(solution)/shard_map/select_n | solution.py:469
  109.1 2.6 %multiply_subtract_fusion = f32[3,8,64,256]{3,2,1,0:T(8,128)} fusion(f32[3,8,64,256]{3,2,1,0:T(8,128)S(1)} %copy-done.9, f16[3,2,64,256]{3,2,1,0:T(8,128)(2,1)S(1)} %get-tuple-element.63, f16[3,2,64,256]{3,2,1,0:T(8,128)(2,1)S(1)} %get-tuple-element.64, f16[3,2,64,256]{3,2,1,0:T(8,128)(2,1)S(1)} %get-tuple-element.65, ...), kind=kLoop, calls=%fused_computation.9 | loop fusion | flops 2359296 | bytes 4456448 | tf_op jit(solution)/shard_map/sub | solution.py:554
  111.7 10.1 %all-to-all-done.3 = f16[256,4,128]{2,1,0:T(4,128)(2,1)} async-done(((f16[256,4,128]{2,1,0:T(4,128)(2,1)}), f16[256,4,128]{2,1,0:T(4,128)(2,1)}, u32[]{:S(2)}, u32[]{:S(2)}) %all-to-all-start.3) | async-done | bytes 262176 | tf_op jit(solution)/shard_map/all_to_all | solution.py:476
  (59 shorter events, 13.4 us)
Async XLA Ops:
  0.6 18.4 %copy-start.8 = (f32[3,8,64,256]{3,2,1,0:T(8,128)S(1)}, f32[3,8,64,256]{3,2,1,0:T(8,128)}, u32[]{:S(2)}) copy-start(f32[3,8,64,256]{3,2,1,0:T(8,128)} %param.14) | copy-start | bytes 4718596
  0.6 18.4 %copy-start.11 = (f32[8,64,256]{2,1,0:T(8,128)S(1)}, f32[8,64,256]{2,1,0:T(8,128)}, u32[]{:S(2)}) copy-start(f32[8,64,256]{2,1,0:T(8,128)} %param.16) | copy-start | bytes 1572868
  3.3 30.9 %all-to-all-start = ((f16[256,4,128]{2,1,0:T(4,128)(2,1)}), f16[256,4,128]{2,1,0:T(4,128)(2,1)S(1)}, u32[]{:S(2)}, u32[]{:S(2)}) async-start(f16[256,4,128]{2,1,0:T(4,128)(2,1)} %copy.19), calls=%async_computation | async-start | bytes 524288 | tf_op jit(solution)/shard_map/all_to_all | solution.py:476
  20.1 14.2 %copy-start.2 = (bf16[256,1536]{1,0:T(8,128)(2,1)S(1)}, bf16[256,1536]{1,0:T(8,128)(2,1)}, u32[]{:S(2)}) copy-start(bf16[256,1536]{1,0:T(8,128)(2,1)} %constant.114.clone.tables) | copy-start | bytes 2359300
  20.1 14.2 %copy-start.3 = (f32[136,128]{1,0:T(8,128)S(1)}, f32[136,128]{1,0:T(8,128)}, u32[]{:S(2)}) copy-start(f32[136,128]{1,0:T(8,128)} %constant.116.clone.numbers) | copy-start | bytes 208900
  20.1 16.2 %collective-permute-start = (f16[4,2,64,256]{3,2,1,0:T(8,128)(2,1)}, f16[4,2,64,256]{3,2,1,0:T(8,128)(2,1)S(1)}, u32[]{:S(2)}, u32[]{:S(2)}) collective-permute-start(f16[4,2,64,256]{3,2,1,0:T(8,128)(2,1)} %get-tuple-element.61), channel_id=1, source_target_pairs={{0,1},{1,2},{2,3},{3,0},{4,5},{5,6},{6,7},{7,4},{8,9},{9,10},{10,1... | collective-permute-start | bytes 786440 | tf_op jit(solution)/shard_map/ppermute | solution.py:459
  21.5 14.8 %collective-permute-start.1 = (f16[4,2,64,256]{3,2,1,0:T(8,128)(2,1)}, f16[4,2,64,256]{3,2,1,0:T(8,128)(2,1)S(1)}, u32[]{:S(2)}, u32[]{:S(2)}) collective-permute-start(f16[4,2,64,256]{3,2,1,0:T(8,128)(2,1)} %get-tuple-element.58), channel_id=1, source_target_pairs={{0,3},{1,0},{2,1},{3,2},{4,7},{5,4},{6,5},{7,6},{8,11},{9,8},{10,9... | collective-permute-start | bytes 786440 | tf_op jit(solution)/shard_map/ppermute | solution.py:459
  37.2 28.1 %all-to-all-start.1 = ((f16[256,8,128]{2,1,0:T(8,128)(2,1)}), f16[256,8,128]{2,1,0:T(8,128)(2,1)}, u32[]{:S(2)}, u32[]{:S(2)}) async-start(f16[256,8,128]{2,1,0:T(8,128)(2,1)} %convert_bitcast_fusion.1), calls=%async_computation.1 | async-start | bytes 1048576 | tf_op jit(solution)/shard_map/all_to_all | solution.py:476
  45.7 12.0 %collective-permute-start.2 = (f16[4,2,64,256]{3,2,1,0:T(8,128)(2,1)S(1)}, f16[4,2,64,256]{3,2,1,0:T(8,128)(2,1)S(1)}, u32[]{:S(2)}, u32[]{:S(2)}) collective-permute-start(f16[4,2,64,256]{3,2,1,0:T(8,128)(2,1)S(1)} %get-tuple-element.42), channel_id=1, source_target_pairs={{0,2},{1,3},{2,0},{3,1},{4,6},{5,7},{6,4},{7,5},{8,10},{9,11},{10,... | collective-permute-start | bytes 786440 | tf_op jit(solution)/shard_map/ppermute | solution.py:459
  48.7 20.9 %collective-permute-start.3 = (bf16[8,16,8,128]{3,2,1,0:T(8,128)(2,1)S(1)}, bf16[8,16,8,128]{3,2,1,0:T(8,128)(2,1)S(1)}, u32[]{:S(2)}, u32[]{:S(2)}) collective-permute-start(bf16[8,16,8,128]{3,2,1,0:T(8,128)(2,1)S(1)} %reshape.42.t0), channel_id=1, source_target_pairs={{0,4},{4,8},{8,12},{12,16},{16,20},{20,24},{24,28},{28,32},{32,36}... | collective-permute-start | bytes 786440 | tf_op jit(solution)/shard_map/ppermute | solution.py:459
  50.4 19.2 %collective-permute-start.4 = (bf16[8,8,8,128]{3,2,1,0:T(8,128)(2,1)}, bf16[8,8,8,128]{3,2,1,0:T(8,128)(2,1)}, u32[]{:S(2)}, u32[]{:S(2)}) collective-permute-start(bf16[8,8,8,128]{3,2,1,0:T(8,128)(2,1)} %slice.4), channel_id=1, source_target_pairs={{0,8},{4,12},{8,16},{12,20},{16,24},{20,28},{24,32},{28,36},{32,40... | collective-permute-start | bytes 393224 | tf_op jit(solution)/shard_map/ppermute | solution.py:459
  51.8 14.6 %copy-start = (bf16[256,1536]{1,0:T(8,128)(2,1)S(1)}, bf16[256,1536]{1,0:T(8,128)(2,1)}, u32[]{:S(2)}) copy-start(bf16[256,1536]{1,0:T(8,128)(2,1)} %constant.113.clone.tables) | copy-start | bytes 2359300
  70.4 14.7 %copy-start.5 = (f32[8,64,256]{2,1,0:T(8,128)S(1)}, f32[8,64,256]{2,1,0:T(8,128)}, u32[]{:S(2)}) copy-start(f32[8,64,256]{2,1,0:T(8,128)} %pressure.1) | copy-start | bytes 1572868
  70.4 14.7 %copy-start.7 = (s32[256]{0:T(256)S(1)}, s32[256]{0:T(256)}, u32[]{:S(2)}) copy-start(s32[256]{0:T(256)} %lives.1) | copy-start | bytes 3076
  70.4 26.6 %all-to-all-start.2 = ((f16[256,8,128]{2,1,0:T(8,128)(2,1)}), f16[256,8,128]{2,1,0:T(8,128)(2,1)S(1)}, u32[]{:S(2)}, u32[]{:S(2)}) async-start(f16[256,8,128]{2,1,0:T(8,128)(2,1)} %convert_bitcast_fusion), calls=%async_computation.2 | async-start | bytes 1048576 | tf_op jit(solution)/shard_map/all_to_all | solution.py:476
  80.1 17.0 %copy-start.1 = (bf16[256,1536]{1,0:T(8,128)(2,1)S(1)}, bf16[256,1536]{1,0:T(8,128)(2,1)}, u32[]{:S(2)}) copy-start(bf16[256,1536]{1,0:T(8,128)(2,1)} %constant.115.clone.tables) | copy-start | bytes 2359300
  80.1 27.4 %collective-permute-start.5 = (f16[3,2,64,256]{3,2,1,0:T(8,128)(2,1)}, f16[3,2,64,256]{3,2,1,0:T(8,128)(2,1)}, u32[]{:S(2)}, u32[]{:S(2)}) collective-permute-start(f16[3,2,64,256]{3,2,1,0:T(8,128)(2,1)} %get-tuple-element.66), channel_id=1, source_target_pairs={{0,1},{1,2},{2,3},{3,0},{4,5},{5,6},{6,7},{7,4},{8,9},{9,10},{10,1... | collective-permute-start | bytes 589832 | tf_op jit(solution)/shard_map/ppermute | solution.py:459
  81.5 26.0 %collective-permute-start.6 = (f16[3,2,64,256]{3,2,1,0:T(8,128)(2,1)}, f16[3,2,64,256]{3,2,1,0:T(8,128)(2,1)}, u32[]{:S(2)}, u32[]{:S(2)}) collective-permute-start(f16[3,2,64,256]{3,2,1,0:T(8,128)(2,1)} %get-tuple-element.68), channel_id=1, source_target_pairs={{0,2},{1,3},{2,0},{3,1},{4,6},{5,7},{6,4},{7,5},{8,10},{9,11},{10,... | collective-permute-start | bytes 589832 | tf_op jit(solution)/shard_map/ppermute | solution.py:459
  84.0 23.6 %collective-permute-start.7 = (f16[3,2,64,256]{3,2,1,0:T(8,128)(2,1)S(1)}, f16[3,2,64,256]{3,2,1,0:T(8,128)(2,1)}, u32[]{:S(2)}, u32[]{:S(2)}) collective-permute-start(f16[3,2,64,256]{3,2,1,0:T(8,128)(2,1)S(1)} %get-tuple-element.67), channel_id=1, source_target_pairs={{0,3},{1,0},{2,1},{3,2},{4,7},{5,4},{6,5},{7,6},{8,11},{9,8},{10,9... | collective-permute-start | bytes 589832 | tf_op jit(solution)/shard_map/ppermute | solution.py:459
  88.9 34.0 %collective-permute-start.8 = (bf16[8,32,256]{2,1,0:T(8,128)(2,1)S(1)}, bf16[8,32,256]{2,1,0:T(8,128)(2,1)S(1)}, u32[]{:S(2)}, u32[]{:S(2)}) collective-permute-start(bf16[8,32,256]{2,1,0:T(8,128)(2,1)S(1)} %get-tuple-element.56), channel_id=1, source_target_pairs={{0,1},{1,2},{2,3},{3,0},{4,5},{5,6},{6,7},{7,4},{8,9},{9,10},{10,1... | collective-permute-start | bytes 393224 | tf_op jit(solution)/shard_map/ppermute | solution.py:459
  99.3 9.8 %copy-start.9 = (f32[3,8,64,256]{3,2,1,0:T(8,128)S(1)}, f32[3,8,64,256]{3,2,1,0:T(8,128)}, u32[]{:S(2)}) copy-start(f32[3,8,64,256]{3,2,1,0:T(8,128)} %param.14) | copy-start | bytes 4718596
  100.0 21.8 %all-to-all-start.3 = ((f16[256,4,128]{2,1,0:T(4,128)(2,1)}), f16[256,4,128]{2,1,0:T(4,128)(2,1)}, u32[]{:S(2)}, u32[]{:S(2)}) async-start(f16[256,4,128]{2,1,0:T(4,128)(2,1)} %bitcast.14), calls=%async_computation.3 | async-start | bytes 524288 | tf_op jit(solution)/shard_map/all_to_all | solution.py:476
  109.1 13.7 %copy-start.4 = (f32[8,64,256]{2,1,0:T(8,128)S(1)}, f32[8,64,256]{2,1,0:T(8,128)}, u32[]{:S(2)}) copy-start(f32[8,64,256]{2,1,0:T(8,128)} %bulk.1) | copy-start | bytes 1572868
  109.1 13.7 %copy-start.6 = (bf16[256,512]{1,0:T(8,128)(2,1)S(1)}, bf16[256,512]{1,0:T(8,128)(2,1)}, u32[]{:S(2)}) copy-start(bf16[256,512]{1,0:T(8,128)(2,1)} %constant.111.clone.x_ref) | copy-start | bytes 786436
  (2 other events, 18.6 us)

commit v10 on v9

--- a/solution.py
+++ b/solution.py
@@ -551,7 +551,7 @@
         (middle, slopes.astype(f16), tiles_before, tiles_second)
     )
     slopes = to_rows(slopes, row_block)
-    new_velocity = velocity - buoyancy[None] * (slopes * (1.0 / RETURN_LINK))
+    new_velocity = (velocity * RETURN_LINK - buoyancy[None] * slopes) * (1.0 / RETURN_LINK)
     corners = [
         lax.dynamic_slice_in_dim(
             tile_corner,

time: 125 us -> 124 us (level)
    sub x1 -> x0, other arithmetic: 2.6 us -> none  [local(): new_velocity = velocity - buoyancy[None] * (slopes * (1.0 / RETURN_LINK))]
    mul x1, other arithmetic: 0.84 us -> 2.67 us  [local(): (velocity * RETURN_LINK - buoyancy[None] * slopes) * (1.0 / RETURN_LINK)]
where the time goes in v10:
time: 124 us
  starting transfers between devices  51.8 us (42%)
  waiting for transfers between devices  41.1 us (33%)
  Pallas kernels  11.9 us (10%)
  other arithmetic  10.5 us (8%)
  local copies, waits for them, and re-layouts  5.53 us (4%)
  matrix products  1.69 us (1%)
  between operations  1.35 us (1%)
    all_to_all x4, starting transfers between devices, exchange(): return lax.all_to_all(blocks, ('gz', 'gy'), 0, 0, tiled=True)  37.9 us
    all_to_all x4, waiting for transfers between devices, exchange(): return lax.all_to_all(blocks, ('gz', 'gy'), 0, 0, tiled=True)  35.2 us
    ppermute x9, starting transfers between devices, from_behind(): return lax.ppermute(x, axis, [(i, (i + by) % peers) for i in range(peers)])  13.9 us
    pallas_call x5, Pallas kernels, call(): pl.pallas_call(kernel, out_shape=[jax.ShapeDtypeStruct(shape, kind) for s...  11.9 us
    ppermute x9, waiting for transfers between devices, from_behind(): return lax.ppermute(x, axis, [(i, (i + by) % peers) for i in range(peers)])  5.88 us
    mul x1, other arithmetic, local(): (velocity * RETURN_LINK - buoyancy[None] * slopes) * (1.0 / RETURN_LINK)  2.67 us
  transfers between devices with their start and end apart: 13, of which 5 were waited for; matrix products, arithmetic and copies ran while one was open for 11% of the time, Pallas kernels for 9%

profile of v10, /device:TPU:1, one launch (start us, length us, event | category | flops | bytes accessed | tf_op | source)
XLA Modules:
  0.0 123.9 jit_solution(15459438479494503287)
XLA Ops:
  0.7 1.7 %fusion.11 = f32[256,4,128]{2,0,1:T(8,128)S(1)} fusion(f32[256,256,1]{1,0,2:T(8,128)} %constant.124, f32[4,128,256]{2,1,0:T(8,128)} %bitcast.32), kind=kOutput, calls=%fused_computation.39 | convolution fusion | flops 201326592 | bytes 1310720 | tf_op jit(solution)/shard_map/cx,abx->cab/dot_general | solution.py:491
  3.3 15.7 %all-to-all-start = ((f16[256,4,128]{2,1,0:T(4,128)(2,1)}), f16[256,4,128]{2,1,0:T(4,128)(2,1)S(1)}, u32[]{:S(2)}, u32[]{:S(2)}) async-start(f16[256,4,128]{2,1,0:T(4,128)(2,1)} %copy.19), calls=%async_computation | async-start | bytes 524288 | tf_op jit(solution)/shard_map/all_to_all | solution.py:476
  20.0 1.4 %collective-permute-start = (f16[4,2,64,256]{3,2,1,0:T(8,128)(2,1)}, f16[4,2,64,256]{3,2,1,0:T(8,128)(2,1)S(1)}, u32[]{:S(2)}, u32[]{:S(2)}) collective-permute-start(f16[4,2,64,256]{3,2,1,0:T(8,128)(2,1)} %get-tuple-element.61), channel_id=1, source_target_pairs={{0,1},{1,2},{2,3},{3,0},{4,5},{5,6},{6,7},{7,4},{8,9},{9,10},{10,1... | collective-permute-start | bytes 786440 | tf_op jit(solution)/shard_map/ppermute | solution.py:459
  21.4 1.3 %collective-permute-start.1 = (f16[4,2,64,256]{3,2,1,0:T(8,128)(2,1)S(1)}, f16[4,2,64,256]{3,2,1,0:T(8,128)(2,1)S(1)}, u32[]{:S(2)}, u32[]{:S(2)}) collective-permute-start(f16[4,2,64,256]{3,2,1,0:T(8,128)(2,1)S(1)} %get-tuple-element.58), channel_id=1, source_target_pairs={{0,3},{1,0},{2,1},{3,2},{4,7},{5,4},{6,5},{7,6},{8,11},{9,8},{10,9... | collective-permute-start | bytes 786440 | tf_op jit(solution)/shard_map/ppermute | solution.py:459
  22.7 1.9 %reshape.42.t0 = bf16[8,16,8,128]{3,2,1,0:T(8,128)(2,1)S(1)} reshape(bf16[8,16,32,32]{3,2,1,0:T(8,128)(2,1)} %param.17) | data formatting | bytes 524288 | tf_op jit(solution)/shard_map/reshape | solution.py:509
  25.3 9.0 %all-to-all-done = f16[256,4,128]{2,1,0:T(4,128)(2,1)S(1)} async-done(((f16[256,4,128]{2,1,0:T(4,128)(2,1)}), f16[256,4,128]{2,1,0:T(4,128)(2,1)S(1)}, u32[]{:S(2)}, u32[]{:S(2)}) %all-to-all-start) | async-done | bytes 262176 | tf_op jit(solution)/shard_map/all_to_all | solution.py:476
  34.3 2.0 %filter_out.1 = f32[2048,128]{1,0:T(8,128)S(1)} custom-call(s32[1]{0:T(128)} %bitcast.where, f32[1024,128]{1,0:T(8,128)S(1)} %convert.6.data, bf16[256,1536]{1,0:T(8,128)(2,1)S(1)} %copy-done.2, f32[136,128]{1,0:T(8,128)S(1)} %copy-done.3), custom_call_target="tpu_custom_call" | custom-call | flops 400000000 | bytes 1048576 | tf_op jit(solution)/shard_map/filter_out/pallas_call | solution.py:445
  37.2 8.2 %all-to-all-start.1 = ((f16[256,8,128]{2,1,0:T(8,128)(2,1)}), f16[256,8,128]{2,1,0:T(8,128)(2,1)}, u32[]{:S(2)}, u32[]{:S(2)}) async-start(f16[256,8,128]{2,1,0:T(8,128)(2,1)} %convert_bitcast_fusion.1), calls=%async_computation.1 | async-start | bytes 1048576 | tf_op jit(solution)/shard_map/all_to_all | solution.py:476
  45.4 3.0 %collective-permute-start.2 = (f16[4,2,64,256]{3,2,1,0:T(8,128)(2,1)S(1)}, f16[4,2,64,256]{3,2,1,0:T(8,128)(2,1)S(1)}, u32[]{:S(2)}, u32[]{:S(2)}) collective-permute-start(f16[4,2,64,256]{3,2,1,0:T(8,128)(2,1)S(1)} %get-tuple-element.42), channel_id=1, source_target_pairs={{0,2},{1,3},{2,0},{3,1},{4,6},{5,7},{6,4},{7,5},{8,10},{9,11},{10,... | collective-permute-start | bytes 786440 | tf_op jit(solution)/shard_map/ppermute | solution.py:459
  48.4 1.7 %collective-permute-start.3 = (bf16[8,16,8,128]{3,2,1,0:T(8,128)(2,1)S(1)}, bf16[8,16,8,128]{3,2,1,0:T(8,128)(2,1)S(1)}, u32[]{:S(2)}, u32[]{:S(2)}) collective-permute-start(bf16[8,16,8,128]{3,2,1,0:T(8,128)(2,1)S(1)} %reshape.42.t0), channel_id=1, source_target_pairs={{0,4},{4,8},{8,12},{12,16},{16,20},{20,24},{24,28},{28,32},{32,36}... | collective-permute-start | bytes 786440 | tf_op jit(solution)/shard_map/ppermute | solution.py:459
  50.1 1.2 collective-permute-start.4
  51.6 5.9 %collective-permute-done.2 = f16[4,2,64,256]{3,2,1,0:T(8,128)(2,1)S(1)} collective-permute-done((f16[4,2,64,256]{3,2,1,0:T(8,128)(2,1)S(1)}, f16[4,2,64,256]{3,2,1,0:T(8,128)(2,1)S(1)}, u32[]{:S(2)}, u32[]{:S(2)}) %collective-permute-start.2) | collective-permute-done | bytes 262176 | tf_op jit(solution)/shard_map/ppermute | solution.py:459
  57.5 7.6 %all-to-all-done.1 = f16[256,8,128]{2,1,0:T(8,128)(2,1)} async-done(((f16[256,8,128]{2,1,0:T(8,128)(2,1)}), f16[256,8,128]{2,1,0:T(8,128)(2,1)}, u32[]{:S(2)}, u32[]{:S(2)}) %all-to-all-start.1) | async-done | bytes 524320 | tf_op jit(solution)/shard_map/all_to_all | solution.py:476
  66.2 2.9 %middle.1 = (f32[3,2,256,256]{3,2,1,0:T(8,128)S(1)}, f32[2048,128]{1,0:T(8,128)S(1)}) custom-call(s32[1]{0:T(128)} %bitcast.1.where, f32[2048,128]{1,0:T(8,128)S(1)} %bitcast_convert_fusion.1.data, bf16[256,1536]{1,0:T(8,128)(2,1)S(1)} %copy-done, f32[136,128]{1,0:T(8,128)S(1)} %copy-done.3, f32[3,4,2,64,256]{4,3,2,1,0:T(8,128)S(1)} %maximum_multiply_fusion.near, ...), custom_call_target="tpu_custom_call" | custom-call | flops 400000000 | bytes 1048576 | tf_op jit(solution)/shard_map/middle/pallas_call | solution.py:445
  70.3 6.6 %all-to-all-start.2 = ((f16[256,8,128]{2,1,0:T(8,128)(2,1)}), f16[256,8,128]{2,1,0:T(8,128)(2,1)S(1)}, u32[]{:S(2)}, u32[]{:S(2)}) async-start(f16[256,8,128]{2,1,0:T(8,128)(2,1)} %convert_bitcast_fusion), calls=%async_computation.2 | async-start | bytes 1048576 | tf_op jit(solution)/shard_map/all_to_all | solution.py:476
  79.1 1.4 %collective-permute-start.5 = (f16[3,2,64,256]{3,2,1,0:T(8,128)(2,1)}, f16[3,2,64,256]{3,2,1,0:T(8,128)(2,1)}, u32[]{:S(2)}, u32[]{:S(2)}) collective-permute-start(f16[3,2,64,256]{3,2,1,0:T(8,128)(2,1)} %get-tuple-element.66), channel_id=1, source_target_pairs={{0,1},{1,2},{2,3},{3,0},{4,5},{5,6},{6,7},{7,4},{8,9},{9,10},{10,1... | collective-permute-start | bytes 589832 | tf_op jit(solution)/shard_map/ppermute | solution.py:459
  80.5 2.4 %collective-permute-start.6 = (f16[3,2,64,256]{3,2,1,0:T(8,128)(2,1)}, f16[3,2,64,256]{3,2,1,0:T(8,128)(2,1)}, u32[]{:S(2)}, u32[]{:S(2)}) collective-permute-start(f16[3,2,64,256]{3,2,1,0:T(8,128)(2,1)} %get-tuple-element.68), channel_id=1, source_target_pairs={{0,2},{1,3},{2,0},{3,1},{4,6},{5,7},{6,4},{7,5},{8,10},{9,11},{10,... | collective-permute-start | bytes 589832 | tf_op jit(solution)/shard_map/ppermute | solution.py:459
  84.1 3.7 %source.1 = (f32[8,64,256]{2,1,0:T(8,128)S(1)}, bf16[8,32,256]{2,1,0:T(8,128)(2,1)S(1)}) custom-call(s32[2]{0:T(128)S(1)} %pad_add_fusion.where, s32[256]{0:T(256)S(1)} %copy-done.7, s32[8,3]{1,0:T(8,128)S(1)} %copy.23.c0, s32[8,3]{1,0:T(8,128)S(1)} %copy.24.c1, s32[8,3]{1,0:T(8,128)S(1)} %copy.25.c2, bf16[8,16,8,128]{3,2,1,0:T(8,128)(2,1)S(1)} %reshape.42.t0, ...), custom_call_target="tpu_custom_call" | custom-call | flops 400000000 | bytes 1048576 | tf_op jit(solution)/shard_map/source/pallas_call | solution.py:445
  88.3 8.6 %all-to-all-done.2 = f16[256,8,128]{2,1,0:T(8,128)(2,1)S(1)} async-done(((f16[256,8,128]{2,1,0:T(8,128)(2,1)}), f16[256,8,128]{2,1,0:T(8,128)(2,1)S(1)}, u32[]{:S(2)}, u32[]{:S(2)}) %all-to-all-start.2) | async-done | bytes 524320 | tf_op jit(solution)/shard_map/all_to_all | solution.py:476
  97.0 2.1 %filter_back.1 = f32[1024,128]{1,0:T(8,128)S(1)} custom-call(s32[1]{0:T(128)} %bitcast.where, f32[2048,128]{1,0:T(8,128)S(1)} %bitcast_convert_fusion.data, bf16[256,1536]{1,0:T(8,128)(2,1)S(1)} %copy-done.1, f32[136,128]{1,0:T(8,128)S(1)} %copy-done.3), custom_call_target="tpu_custom_call" | custom-call | flops 400000000 | bytes 1048576 | tf_op jit(solution)/shard_map/filter_back/pallas_call | solution.py:445
  99.9 7.4 %all-to-all-start.3 = ((f16[256,4,128]{2,1,0:T(4,128)(2,1)}), f16[256,4,128]{2,1,0:T(4,128)(2,1)}, u32[]{:S(2)}, u32[]{:S(2)}) async-start(f16[256,4,128]{2,1,0:T(4,128)(2,1)} %bitcast.14), calls=%async_computation.3 | async-start | bytes 524288 | tf_op jit(solution)/shard_map/all_to_all | solution.py:476
  107.3 1.5 %select_select_fusion.3 = (f16[3,2,64,256]{3,2,1,0:T(8,128)(2,1)S(1)}, f16[3,2,64,256]{3,2,1,0:T(8,128)(2,1)S(1)}, f16[3,2,64,256]{3,2,1,0:T(8,128)(2,1)S(1)}, f16[3,2,64,256]{3,2,1,0:T(8,128)(2,1)S(1)}) fusion(f16[3,2,64,256]{3,2,1,0:T(8,128)(2,1)} %collective-permute-done.6, f16[3,2,64,256]{3,2,1,0:T(8,128)(2,1)} %collective-permute-done.7, ...), kind=kLoop, calls=%fused_computation.31 | loop fusion | flops 1179648 | bytes 1572880 | tf_op jit(solution)/shard_map/select_n | solution.py:469
  108.9 2.7 %subtract_multiply_fusion = f32[3,8,64,256]{3,2,1,0:T(8,128)} fusion(f32[3,8,64,256]{3,2,1,0:T(8,128)S(1)} %copy-done.9, f16[3,2,64,256]{3,2,1,0:T(8,128)(2,1)S(1)} %get-tuple-element.63, f16[3,2,64,256]{3,2,1,0:T(8,128)(2,1)S(1)} %get-tuple-element.64, f16[3,2,64,256]{3,2,1,0:T(8,128)(2,1)S(1)} %get-tuple-element.65, ...), kind=kLoop, calls=%fused_computation.9 | loop fusion | flops 3145728 | bytes 4456448 | tf_op jit(solution)/shard_map/mul | solution.py:554
  111.5 10.0 %all-to-all-done.3 = f16[256,4,128]{2,1,0:T(4,128)(2,1)} async-done(((f16[256,4,128]{2,1,0:T(4,128)(2,1)}), f16[256,4,128]{2,1,0:T(4,128)(2,1)}, u32[]{:S(2)}, u32[]{:S(2)}) %all-to-all-start.3) | async-done | bytes 262176 | tf_op jit(solution)/shard_map/all_to_all | solution.py:476
  (56 shorter events, 12.6 us)
Async XLA Ops:
  0.6 18.4 %copy-start.8 = (f32[3,8,64,256]{3,2,1,0:T(8,128)S(1)}, f32[3,8,64,256]{3,2,1,0:T(8,128)}, u32[]{:S(2)}) copy-start(f32[3,8,64,256]{3,2,1,0:T(8,128)} %param.14) | copy-start | bytes 4718596
  0.6 18.4 %copy-start.11 = (f32[8,64,256]{2,1,0:T(8,128)S(1)}, f32[8,64,256]{2,1,0:T(8,128)}, u32[]{:S(2)}) copy-start(f32[8,64,256]{2,1,0:T(8,128)} %param.16) | copy-start | bytes 1572868
  3.3 30.9 %all-to-all-start = ((f16[256,4,128]{2,1,0:T(4,128)(2,1)}), f16[256,4,128]{2,1,0:T(4,128)(2,1)S(1)}, u32[]{:S(2)}, u32[]{:S(2)}) async-start(f16[256,4,128]{2,1,0:T(4,128)(2,1)} %copy.19), calls=%async_computation | async-start | bytes 524288 | tf_op jit(solution)/shard_map/all_to_all | solution.py:476
  20.0 14.3 %copy-start.2 = (bf16[256,1536]{1,0:T(8,128)(2,1)S(1)}, bf16[256,1536]{1,0:T(8,128)(2,1)}, u32[]{:S(2)}) copy-start(bf16[256,1536]{1,0:T(8,128)(2,1)} %constant.116.clone.tables) | copy-start | bytes 2359300
  20.0 14.3 %copy-start.3 = (f32[136,128]{1,0:T(8,128)S(1)}, f32[136,128]{1,0:T(8,128)}, u32[]{:S(2)}) copy-start(f32[136,128]{1,0:T(8,128)} %constant.118.clone.numbers) | copy-start | bytes 208900
  20.0 16.3 %collective-permute-start = (f16[4,2,64,256]{3,2,1,0:T(8,128)(2,1)}, f16[4,2,64,256]{3,2,1,0:T(8,128)(2,1)S(1)}, u32[]{:S(2)}, u32[]{:S(2)}) collective-permute-start(f16[4,2,64,256]{3,2,1,0:T(8,128)(2,1)} %get-tuple-element.61), channel_id=1, source_target_pairs={{0,1},{1,2},{2,3},{3,0},{4,5},{5,6},{6,7},{7,4},{8,9},{9,10},{10,1... | collective-permute-start | bytes 786440 | tf_op jit(solution)/shard_map/ppermute | solution.py:459
  21.4 14.9 %collective-permute-start.1 = (f16[4,2,64,256]{3,2,1,0:T(8,128)(2,1)S(1)}, f16[4,2,64,256]{3,2,1,0:T(8,128)(2,1)S(1)}, u32[]{:S(2)}, u32[]{:S(2)}) collective-permute-start(f16[4,2,64,256]{3,2,1,0:T(8,128)(2,1)S(1)} %get-tuple-element.58), channel_id=1, source_target_pairs={{0,3},{1,0},{2,1},{3,2},{4,7},{5,4},{6,5},{7,6},{8,11},{9,8},{10,9... | collective-permute-start | bytes 786440 | tf_op jit(solution)/shard_map/ppermute | solution.py:459
  37.2 27.9 %all-to-all-start.1 = ((f16[256,8,128]{2,1,0:T(8,128)(2,1)}), f16[256,8,128]{2,1,0:T(8,128)(2,1)}, u32[]{:S(2)}, u32[]{:S(2)}) async-start(f16[256,8,128]{2,1,0:T(8,128)(2,1)} %convert_bitcast_fusion.1), calls=%async_computation.1 | async-start | bytes 1048576 | tf_op jit(solution)/shard_map/all_to_all | solution.py:476
  45.4 12.0 %collective-permute-start.2 = (f16[4,2,64,256]{3,2,1,0:T(8,128)(2,1)S(1)}, f16[4,2,64,256]{3,2,1,0:T(8,128)(2,1)S(1)}, u32[]{:S(2)}, u32[]{:S(2)}) collective-permute-start(f16[4,2,64,256]{3,2,1,0:T(8,128)(2,1)S(1)} %get-tuple-element.42), channel_id=1, source_target_pairs={{0,2},{1,3},{2,0},{3,1},{4,6},{5,7},{6,4},{7,5},{8,10},{9,11},{10,... | collective-permute-start | bytes 786440 | tf_op jit(solution)/shard_map/ppermute | solution.py:459
  48.4 20.9 %collective-permute-start.3 = (bf16[8,16,8,128]{3,2,1,0:T(8,128)(2,1)S(1)}, bf16[8,16,8,128]{3,2,1,0:T(8,128)(2,1)S(1)}, u32[]{:S(2)}, u32[]{:S(2)}) collective-permute-start(bf16[8,16,8,128]{3,2,1,0:T(8,128)(2,1)S(1)} %reshape.42.t0), channel_id=1, source_target_pairs={{0,4},{4,8},{8,12},{12,16},{16,20},{20,24},{24,28},{28,32},{32,36}... | collective-permute-start | bytes 786440 | tf_op jit(solution)/shard_map/ppermute | solution.py:459
  50.1 19.2 %collective-permute-start.4 = (bf16[8,8,8,128]{3,2,1,0:T(8,128)(2,1)}, bf16[8,8,8,128]{3,2,1,0:T(8,128)(2,1)}, u32[]{:S(2)}, u32[]{:S(2)}) collective-permute-start(bf16[8,8,8,128]{3,2,1,0:T(8,128)(2,1)} %slice.4), channel_id=1, source_target_pairs={{0,8},{4,12},{8,16},{12,20},{16,24},{20,28},{24,32},{28,36},{32,40... | collective-permute-start | bytes 393224 | tf_op jit(solution)/shard_map/ppermute | solution.py:459
  51.6 14.6 %copy-start = (bf16[256,1536]{1,0:T(8,128)(2,1)S(1)}, bf16[256,1536]{1,0:T(8,128)(2,1)}, u32[]{:S(2)}) copy-start(bf16[256,1536]{1,0:T(8,128)(2,1)} %constant.115.clone.tables) | copy-start | bytes 2359300
  70.3 13.8 %copy-start.5 = (f32[8,64,256]{2,1,0:T(8,128)S(1)}, f32[8,64,256]{2,1,0:T(8,128)}, u32[]{:S(2)}) copy-start(f32[8,64,256]{2,1,0:T(8,128)} %pressure.1) | copy-start | bytes 1572868
  70.3 13.8 %copy-start.7 = (s32[256]{0:T(256)S(1)}, s32[256]{0:T(256)}, u32[]{:S(2)}) copy-start(s32[256]{0:T(256)} %lives.1) | copy-start | bytes 3076
  70.3 26.6 %all-to-all-start.2 = ((f16[256,8,128]{2,1,0:T(8,128)(2,1)}), f16[256,8,128]{2,1,0:T(8,128)(2,1)S(1)}, u32[]{:S(2)}, u32[]{:S(2)}) async-start(f16[256,8,128]{2,1,0:T(8,128)(2,1)} %convert_bitcast_fusion), calls=%async_computation.2 | async-start | bytes 1048576 | tf_op jit(solution)/shard_map/all_to_all | solution.py:476
  79.1 17.8 %copy-start.1 = (bf16[256,1536]{1,0:T(8,128)(2,1)S(1)}, bf16[256,1536]{1,0:T(8,128)(2,1)}, u32[]{:S(2)}) copy-start(bf16[256,1536]{1,0:T(8,128)(2,1)} %constant.117.clone.tables) | copy-start | bytes 2359300
  79.1 28.1 %collective-permute-start.5 = (f16[3,2,64,256]{3,2,1,0:T(8,128)(2,1)}, f16[3,2,64,256]{3,2,1,0:T(8,128)(2,1)}, u32[]{:S(2)}, u32[]{:S(2)}) collective-permute-start(f16[3,2,64,256]{3,2,1,0:T(8,128)(2,1)} %get-tuple-element.66), channel_id=1, source_target_pairs={{0,1},{1,2},{2,3},{3,0},{4,5},{5,6},{6,7},{7,4},{8,9},{9,10},{10,1... | collective-permute-start | bytes 589832 | tf_op jit(solution)/shard_map/ppermute | solution.py:459
  80.5 26.8 %collective-permute-start.6 = (f16[3,2,64,256]{3,2,1,0:T(8,128)(2,1)}, f16[3,2,64,256]{3,2,1,0:T(8,128)(2,1)}, u32[]{:S(2)}, u32[]{:S(2)}) collective-permute-start(f16[3,2,64,256]{3,2,1,0:T(8,128)(2,1)} %get-tuple-element.68), channel_id=1, source_target_pairs={{0,2},{1,3},{2,0},{3,1},{4,6},{5,7},{6,4},{7,5},{8,10},{9,11},{10,... | collective-permute-start | bytes 589832 | tf_op jit(solution)/shard_map/ppermute | solution.py:459
  83.0 24.3 %collective-permute-start.7 = (f16[3,2,64,256]{3,2,1,0:T(8,128)(2,1)S(1)}, f16[3,2,64,256]{3,2,1,0:T(8,128)(2,1)}, u32[]{:S(2)}, u32[]{:S(2)}) collective-permute-start(f16[3,2,64,256]{3,2,1,0:T(8,128)(2,1)S(1)} %get-tuple-element.67), channel_id=1, source_target_pairs={{0,3},{1,0},{2,1},{3,2},{4,7},{5,4},{6,5},{7,6},{8,11},{9,8},{10,9... | collective-permute-start | bytes 589832 | tf_op jit(solution)/shard_map/ppermute | solution.py:459
  87.9 34.7 %collective-permute-start.8 = (bf16[8,32,256]{2,1,0:T(8,128)(2,1)S(1)}, bf16[8,32,256]{2,1,0:T(8,128)(2,1)S(1)}, u32[]{:S(2)}, u32[]{:S(2)}) collective-permute-start(bf16[8,32,256]{2,1,0:T(8,128)(2,1)S(1)} %get-tuple-element.56), channel_id=1, source_target_pairs={{0,1},{1,2},{2,3},{3,0},{4,5},{5,6},{6,7},{7,4},{8,9},{9,10},{10,1... | collective-permute-start | bytes 393224 | tf_op jit(solution)/shard_map/ppermute | solution.py:459
  99.1 9.7 %copy-start.9 = (f32[3,8,64,256]{3,2,1,0:T(8,128)S(1)}, f32[3,8,64,256]{3,2,1,0:T(8,128)}, u32[]{:S(2)}) copy-start(f32[3,8,64,256]{3,2,1,0:T(8,128)} %param.14) | copy-start | bytes 4718596
  99.9 21.7 %all-to-all-start.3 = ((f16[256,4,128]{2,1,0:T(4,128)(2,1)}), f16[256,4,128]{2,1,0:T(4,128)(2,1)}, u32[]{:S(2)}, u32[]{:S(2)}) async-start(f16[256,4,128]{2,1,0:T(4,128)(2,1)} %bitcast.14), calls=%async_computation.3 | async-start | bytes 524288 | tf_op jit(solution)/shard_map/all_to_all | solution.py:476
  108.8 13.7 %copy-start.4 = (f32[8,64,256]{2,1,0:T(8,128)S(1)}, f32[8,64,256]{2,1,0:T(8,128)}, u32[]{:S(2)}) copy-start(f32[8,64,256]{2,1,0:T(8,128)} %bulk.1) | copy-start | bytes 1572868
  108.8 13.7 %copy-start.6 = (bf16[256,512]{1,0:T(8,128)(2,1)S(1)}, bf16[256,512]{1,0:T(8,128)(2,1)}, u32[]{:S(2)}) copy-start(bf16[256,512]{1,0:T(8,128)(2,1)} %constant.113.clone.x_ref) | copy-start | bytes 786436
  (1 other events, 9.0 us)

commit v11 on v10

--- a/solution.py
+++ b/solution.py
@@ -529,7 +529,16 @@
     )
     second = from_behind(second, "gy", 2)
     tiles_before, tiles_second = from_behind(packed, "gz", 1), from_behind(packed_end, "gz", 2)
-    moved = exchange(filtered, 8)
+    corners = [
+        lax.dynamic_slice_in_dim(
+            tile_corner,
+            ((slab_later - reach) % PEERS_Z * PEERS_Y + row_block) * SLOTS_HERE,
+            SLOTS_HERE,
+            0,
+        )
+        for reach in range(3)
+    ]
+    moved, *corners = lax.optimization_barrier((exchange(filtered, 8), *corners))
     slopes, middle = call(
         middle_kernel,
         "middle",
@@ -552,15 +561,6 @@
     )
     slopes = to_rows(slopes, row_block)
     new_velocity = (velocity * RETURN_LINK - buoyancy[None] * slopes) * (1.0 / RETURN_LINK)
-    corners = [
-        lax.dynamic_slice_in_dim(
-            tile_corner,
-            ((slab_later - reach) % PEERS_Z * PEERS_Y + row_block) * SLOTS_HERE,
-            SLOTS_HERE,
-            0,
-        )
-        for reach in range(3)
-    ]
     own, passed = call(
         source_kernel,
         "source",

time: 124 us -> 125 us (level)
  no operation moved by 1% of the time
where the time goes in v11:
time: 125 us
  starting transfers between devices  52.6 us (42%)
  waiting for transfers between devices  41.1 us (33%)
  Pallas kernels  11.9 us (10%)
  other arithmetic  10.5 us (8%)
  local copies, waits for them, and re-layouts  5.53 us (4%)
  matrix products  1.69 us (1%)
  between operations  1.35 us (1%)
    all_to_all x4, starting transfers between devices, exchange(): return lax.all_to_all(blocks, ('gz', 'gy'), 0, 0, tiled=True)  38.7 us
    all_to_all x4, waiting for transfers between devices, exchange(): return lax.all_to_all(blocks, ('gz', 'gy'), 0, 0, tiled=True)  35 us
    ppermute x9, starting transfers between devices, from_behind(): return lax.ppermute(x, axis, [(i, (i + by) % peers) for i in range(peers)])  13.9 us
    pallas_call x5, Pallas kernels, call(): pl.pallas_call(kernel, out_shape=[jax.ShapeDtypeStruct(shape, kind) for s...  11.9 us
    ppermute x9, waiting for transfers between devices, from_behind(): return lax.ppermute(x, axis, [(i, (i + by) % peers) for i in range(peers)])  6.03 us
    mul x1, other arithmetic, local(): (velocity * RETURN_LINK - buoyancy[None] * slopes) * (1.0 / RETURN_LINK)  2.7 us
  transfers between devices with their start and end apart: 13, of which 5 were waited for; matrix products, arithmetic and copies ran while one was open for 11% of the time, Pallas kernels for 9%

profile of v11, /device:TPU:1, one launch (start us, length us, event | category | flops | bytes accessed | tf_op | source)
XLA Modules:
  0.0 124.7 jit_solution(1923249076053294666)
XLA Ops:
  0.7 1.7 %fusion.11 = f32[256,4,128]{2,0,1:T(8,128)S(1)} fusion(f32[256,256,1]{1,0,2:T(8,128)} %constant.124, f32[4,128,256]{2,1,0:T(8,128)} %bitcast.32), kind=kOutput, calls=%fused_computation.39 | convolution fusion | flops 201326592 | bytes 1310720 | tf_op jit(solution)/shard_map/cx,abx->cab/dot_general | solution.py:491
  3.3 15.7 %all-to-all-start = ((f16[256,4,128]{2,1,0:T(4,128)(2,1)}), f16[256,4,128]{2,1,0:T(4,128)(2,1)S(1)}, u32[]{:S(2)}, u32[]{:S(2)}) async-start(f16[256,4,128]{2,1,0:T(4,128)(2,1)} %copy.19), calls=%async_computation | async-start | bytes 524288 | tf_op jit(solution)/shard_map/all_to_all | solution.py:476
  20.1 1.4 %collective-permute-start = (f16[4,2,64,256]{3,2,1,0:T(8,128)(2,1)}, f16[4,2,64,256]{3,2,1,0:T(8,128)(2,1)S(1)}, u32[]{:S(2)}, u32[]{:S(2)}) collective-permute-start(f16[4,2,64,256]{3,2,1,0:T(8,128)(2,1)} %get-tuple-element.69), channel_id=1, source_target_pairs={{0,1},{1,2},{2,3},{3,0},{4,5},{5,6},{6,7},{7,4},{8,9},{9,10},{10,1... | collective-permute-start | bytes 786440 | tf_op jit(solution)/shard_map/ppermute | solution.py:459
  21.5 1.3 %collective-permute-start.1 = (f16[4,2,64,256]{3,2,1,0:T(8,128)(2,1)}, f16[4,2,64,256]{3,2,1,0:T(8,128)(2,1)S(1)}, u32[]{:S(2)}, u32[]{:S(2)}) collective-permute-start(f16[4,2,64,256]{3,2,1,0:T(8,128)(2,1)} %get-tuple-element.66), channel_id=1, source_target_pairs={{0,3},{1,0},{2,1},{3,2},{4,7},{5,4},{6,5},{7,6},{8,11},{9,8},{10,9... | collective-permute-start | bytes 786440 | tf_op jit(solution)/shard_map/ppermute | solution.py:459
  22.8 1.9 %reshape.42.t0 = bf16[8,16,8,128]{3,2,1,0:T(8,128)(2,1)S(1)} reshape(bf16[8,16,32,32]{3,2,1,0:T(8,128)(2,1)} %param.17) | data formatting | bytes 524288 | tf_op jit(solution)/shard_map/reshape | solution.py:509
  25.4 8.8 %all-to-all-done = f16[256,4,128]{2,1,0:T(4,128)(2,1)S(1)} async-done(((f16[256,4,128]{2,1,0:T(4,128)(2,1)}), f16[256,4,128]{2,1,0:T(4,128)(2,1)S(1)}, u32[]{:S(2)}, u32[]{:S(2)}) %all-to-all-start) | async-done | bytes 262176 | tf_op jit(solution)/shard_map/all_to_all | solution.py:476
  34.3 2.0 %filter_out.1 = f32[2048,128]{1,0:T(8,128)S(1)} custom-call(s32[1]{0:T(128)} %bitcast.where, f32[1024,128]{1,0:T(8,128)S(1)} %convert.6.data, bf16[256,1536]{1,0:T(8,128)(2,1)S(1)} %copy-done.2, f32[136,128]{1,0:T(8,128)S(1)} %copy-done.3), custom_call_target="tpu_custom_call" | custom-call | flops 400000000 | bytes 1048576 | tf_op jit(solution)/shard_map/filter_out/pallas_call | solution.py:445
  37.2 8.5 %all-to-all-start.1 = ((f16[256,8,128]{2,1,0:T(8,128)(2,1)}), f16[256,8,128]{2,1,0:T(8,128)(2,1)}, u32[]{:S(2)}, u32[]{:S(2)}) async-start(f16[256,8,128]{2,1,0:T(8,128)(2,1)} %convert_bitcast_fusion.1), calls=%async_computation.1 | async-start | bytes 1048576 | tf_op jit(solution)/shard_map/all_to_all | solution.py:476
  46.8 2.9 %collective-permute-start.2 = (f16[4,2,64,256]{3,2,1,0:T(8,128)(2,1)S(1)}, f16[4,2,64,256]{3,2,1,0:T(8,128)(2,1)S(1)}, u32[]{:S(2)}, u32[]{:S(2)}) collective-permute-start(f16[4,2,64,256]{3,2,1,0:T(8,128)(2,1)S(1)} %get-tuple-element.48), channel_id=1, source_target_pairs={{0,2},{1,3},{2,0},{3,1},{4,6},{5,7},{6,4},{7,5},{8,10},{9,11},{10,... | collective-permute-start | bytes 786440 | tf_op jit(solution)/shard_map/ppermute | solution.py:459
  49.7 1.7 %collective-permute-start.3 = (bf16[8,16,8,128]{3,2,1,0:T(8,128)(2,1)S(1)}, bf16[8,16,8,128]{3,2,1,0:T(8,128)(2,1)S(1)}, u32[]{:S(2)}, u32[]{:S(2)}) collective-permute-start(bf16[8,16,8,128]{3,2,1,0:T(8,128)(2,1)S(1)} %reshape.42.t0), channel_id=1, source_target_pairs={{0,4},{4,8},{8,12},{12,16},{16,20},{20,24},{24,28},{28,32},{32,36}... | collective-permute-start | bytes 786440 | tf_op jit(solution)/shard_map/ppermute | solution.py:459
  51.5 1.2 collective-permute-start.4
  52.8 6.0 %collective-permute-done.2 = f16[4,2,64,256]{3,2,1,0:T(8,128)(2,1)S(1)} collective-permute-done((f16[4,2,64,256]{3,2,1,0:T(8,128)(2,1)S(1)}, f16[4,2,64,256]{3,2,1,0:T(8,128)(2,1)S(1)}, u32[]{:S(2)}, u32[]{:S(2)}) %collective-permute-start.2) | collective-permute-done | bytes 262176 | tf_op jit(solution)/shard_map/ppermute | solution.py:459
  58.9 6.4 %all-to-all-done.1 = f16[256,8,128]{2,1,0:T(8,128)(2,1)} async-done(((f16[256,8,128]{2,1,0:T(8,128)(2,1)}), f16[256,8,128]{2,1,0:T(8,128)(2,1)}, u32[]{:S(2)}, u32[]{:S(2)}) %all-to-all-start.1) | async-done | bytes 524320 | tf_op jit(solution)/shard_map/all_to_all | solution.py:476
  66.4 2.9 %middle.1 = (f32[3,2,256,256]{3,2,1,0:T(8,128)S(1)}, f32[2048,128]{1,0:T(8,128)S(1)}) custom-call(s32[1]{0:T(128)} %bitcast.1.where, f32[2048,128]{1,0:T(8,128)S(1)} %bitcast_convert_fusion.1.data, bf16[256,1536]{1,0:T(8,128)(2,1)S(1)} %copy-done, f32[136,128]{1,0:T(8,128)S(1)} %copy-done.3, f32[3,4,2,64,256]{4,3,2,1,0:T(8,128)S(1)} %maximum_multiply_fusion.near, ...), custom_call_target="tpu_custom_call" | custom-call | flops 400000000 | bytes 1048576 | tf_op jit(solution)/shard_map/middle/pallas_call | solution.py:445
  70.5 7.2 %all-to-all-start.2 = ((f16[256,8,128]{2,1,0:T(8,128)(2,1)}), f16[256,8,128]{2,1,0:T(8,128)(2,1)S(1)}, u32[]{:S(2)}, u32[]{:S(2)}) async-start(f16[256,8,128]{2,1,0:T(8,128)(2,1)} %convert_bitcast_fusion), calls=%async_computation.2 | async-start | bytes 1048576 | tf_op jit(solution)/shard_map/all_to_all | solution.py:476
  78.8 1.4 %collective-permute-start.5 = (f16[3,2,64,256]{3,2,1,0:T(8,128)(2,1)}, f16[3,2,64,256]{3,2,1,0:T(8,128)(2,1)}, u32[]{:S(2)}, u32[]{:S(2)}) collective-permute-start(f16[3,2,64,256]{3,2,1,0:T(8,128)(2,1)} %get-tuple-element.74), channel_id=1, source_target_pairs={{0,1},{1,2},{2,3},{3,0},{4,5},{5,6},{6,7},{7,4},{8,9},{9,10},{10,1... | collective-permute-start | bytes 589832 | tf_op jit(solution)/shard_map/ppermute | solution.py:459
  80.2 2.4 %collective-permute-start.6 = (f16[3,2,64,256]{3,2,1,0:T(8,128)(2,1)}, f16[3,2,64,256]{3,2,1,0:T(8,128)(2,1)}, u32[]{:S(2)}, u32[]{:S(2)}) collective-permute-start(f16[3,2,64,256]{3,2,1,0:T(8,128)(2,1)} %get-tuple-element.76), channel_id=1, source_target_pairs={{0,2},{1,3},{2,0},{3,1},{4,6},{5,7},{6,4},{7,5},{8,10},{9,11},{10,... | collective-permute-start | bytes 589832 | tf_op jit(solution)/shard_map/ppermute | solution.py:459
  83.8 3.7 %source.1 = (f32[8,64,256]{2,1,0:T(8,128)S(1)}, bf16[8,32,256]{2,1,0:T(8,128)(2,1)S(1)}) custom-call(s32[2]{0:T(128)S(1)} %pad_add_fusion.where, s32[256]{0:T(256)S(1)} %copy-done.7, s32[8,3]{1,0:T(8,128)S(1)} %copy.23.c0, s32[8,3]{1,0:T(8,128)S(1)} %copy.24.c1, s32[8,3]{1,0:T(8,128)S(1)} %copy.25.c2, bf16[8,16,8,128]{3,2,1,0:T(8,128)(2,1)S(1)} %reshape.42.t0, ...), custom_call_target="tpu_custom_call" | custom-call | flops 400000000 | bytes 1048576 | tf_op jit(solution)/shard_map/source/pallas_call | solution.py:445
  87.9 9.8 %all-to-all-done.2 = f16[256,8,128]{2,1,0:T(8,128)(2,1)S(1)} async-done(((f16[256,8,128]{2,1,0:T(8,128)(2,1)}), f16[256,8,128]{2,1,0:T(8,128)(2,1)S(1)}, u32[]{:S(2)}, u32[]{:S(2)}) %all-to-all-start.2) | async-done | bytes 524320 | tf_op jit(solution)/shard_map/all_to_all | solution.py:476
  97.8 2.1 %filter_back.1 = f32[1024,128]{1,0:T(8,128)S(1)} custom-call(s32[1]{0:T(128)} %bitcast.where, f32[2048,128]{1,0:T(8,128)S(1)} %bitcast_convert_fusion.data, bf16[256,1536]{1,0:T(8,128)(2,1)S(1)} %copy-done.1, f32[136,128]{1,0:T(8,128)S(1)} %copy-done.3), custom_call_target="tpu_custom_call" | custom-call | flops 400000000 | bytes 1048576 | tf_op jit(solution)/shard_map/filter_back/pallas_call | solution.py:445
  100.6 7.4 %all-to-all-start.3 = ((f16[256,4,128]{2,1,0:T(4,128)(2,1)}), f16[256,4,128]{2,1,0:T(4,128)(2,1)}, u32[]{:S(2)}, u32[]{:S(2)}) async-start(f16[256,4,128]{2,1,0:T(4,128)(2,1)} %bitcast.14), calls=%async_computation.3 | async-start | bytes 524288 | tf_op jit(solution)/shard_map/all_to_all | solution.py:476
  108.1 1.5 %select_select_fusion.3 = (f16[3,2,64,256]{3,2,1,0:T(8,128)(2,1)S(1)}, f16[3,2,64,256]{3,2,1,0:T(8,128)(2,1)S(1)}, f16[3,2,64,256]{3,2,1,0:T(8,128)(2,1)S(1)}, f16[3,2,64,256]{3,2,1,0:T(8,128)(2,1)S(1)}) fusion(f16[3,2,64,256]{3,2,1,0:T(8,128)(2,1)} %collective-permute-done.6, f16[3,2,64,256]{3,2,1,0:T(8,128)(2,1)} %collective-permute-done.7, ...), kind=kLoop, calls=%fused_computation.31 | loop fusion | flops 1179648 | bytes 1572880 | tf_op jit(solution)/shard_map/select_n | solution.py:469
  109.7 2.7 %subtract_multiply_fusion = f32[3,8,64,256]{3,2,1,0:T(8,128)} fusion(f32[3,8,64,256]{3,2,1,0:T(8,128)S(1)} %copy-done.9, f16[3,2,64,256]{3,2,1,0:T(8,128)(2,1)S(1)} %get-tuple-element.71, f16[3,2,64,256]{3,2,1,0:T(8,128)(2,1)S(1)} %get-tuple-element.72, f16[3,2,64,256]{3,2,1,0:T(8,128)(2,1)S(1)} %get-tuple-element.73, ...), kind=kLoop, calls=%fused_computation.9 | loop fusion | flops 3145728 | bytes 4456448 | tf_op jit(solution)/shard_map/mul | solution.py:563
  112.4 10.0 %all-to-all-done.3 = f16[256,4,128]{2,1,0:T(4,128)(2,1)} async-done(((f16[256,4,128]{2,1,0:T(4,128)(2,1)}), f16[256,4,128]{2,1,0:T(4,128)(2,1)}, u32[]{:S(2)}, u32[]{:S(2)}) %all-to-all-start.3) | async-done | bytes 262176 | tf_op jit(solution)/shard_map/all_to_all | solution.py:476
  (56 shorter events, 12.7 us)
Async XLA Ops:
  0.6 18.4 %copy-start.8 = (f32[3,8,64,256]{3,2,1,0:T(8,128)S(1)}, f32[3,8,64,256]{3,2,1,0:T(8,128)}, u32[]{:S(2)}) copy-start(f32[3,8,64,256]{3,2,1,0:T(8,128)} %param.14) | copy-start | bytes 4718596
  0.6 18.4 %copy-start.11 = (f32[8,64,256]{2,1,0:T(8,128)S(1)}, f32[8,64,256]{2,1,0:T(8,128)}, u32[]{:S(2)}) copy-start(f32[8,64,256]{2,1,0:T(8,128)} %param.16) | copy-start | bytes 1572868
  3.3 30.9 %all-to-all-start = ((f16[256,4,128]{2,1,0:T(4,128)(2,1)}), f16[256,4,128]{2,1,0:T(4,128)(2,1)S(1)}, u32[]{:S(2)}, u32[]{:S(2)}) async-start(f16[256,4,128]{2,1,0:T(4,128)(2,1)} %copy.19), calls=%async_computation | async-start | bytes 524288 | tf_op jit(solution)/shard_map/all_to_all | solution.py:476
  20.1 14.2 %copy-start.2 = (bf16[256,1536]{1,0:T(8,128)(2,1)S(1)}, bf16[256,1536]{1,0:T(8,128)(2,1)}, u32[]{:S(2)}) copy-start(bf16[256,1536]{1,0:T(8,128)(2,1)} %constant.116.clone.tables) | copy-start | bytes 2359300
  20.1 14.2 %copy-start.3 = (f32[136,128]{1,0:T(8,128)S(1)}, f32[136,128]{1,0:T(8,128)}, u32[]{:S(2)}) copy-start(f32[136,128]{1,0:T(8,128)} %constant.118.clone.numbers) | copy-start | bytes 208900
  20.1 16.2 %collective-permute-start = (f16[4,2,64,256]{3,2,1,0:T(8,128)(2,1)}, f16[4,2,64,256]{3,2,1,0:T(8,128)(2,1)S(1)}, u32[]{:S(2)}, u32[]{:S(2)}) collective-permute-start(f16[4,2,64,256]{3,2,1,0:T(8,128)(2,1)} %get-tuple-element.69), channel_id=1, source_target_pairs={{0,1},{1,2},{2,3},{3,0},{4,5},{5,6},{6,7},{7,4},{8,9},{9,10},{10,1... | collective-permute-start | bytes 786440 | tf_op jit(solution)/shard_map/ppermute | solution.py:459
  21.5 14.8 %collective-permute-start.1 = (f16[4,2,64,256]{3,2,1,0:T(8,128)(2,1)}, f16[4,2,64,256]{3,2,1,0:T(8,128)(2,1)S(1)}, u32[]{:S(2)}, u32[]{:S(2)}) collective-permute-start(f16[4,2,64,256]{3,2,1,0:T(8,128)(2,1)} %get-tuple-element.66), channel_id=1, source_target_pairs={{0,3},{1,0},{2,1},{3,2},{4,7},{5,4},{6,5},{7,6},{8,11},{9,8},{10,9... | collective-permute-start | bytes 786440 | tf_op jit(solution)/shard_map/ppermute | solution.py:459
  37.2 28.1 %all-to-all-start.1 = ((f16[256,8,128]{2,1,0:T(8,128)(2,1)}), f16[256,8,128]{2,1,0:T(8,128)(2,1)}, u32[]{:S(2)}, u32[]{:S(2)}) async-start(f16[256,8,128]{2,1,0:T(8,128)(2,1)} %convert_bitcast_fusion.1), calls=%async_computation.1 | async-start | bytes 1048576 | tf_op jit(solution)/shard_map/all_to_all | solution.py:476
  46.8 12.0 %collective-permute-start.2 = (f16[4,2,64,256]{3,2,1,0:T(8,128)(2,1)S(1)}, f16[4,2,64,256]{3,2,1,0:T(8,128)(2,1)S(1)}, u32[]{:S(2)}, u32[]{:S(2)}) collective-permute-start(f16[4,2,64,256]{3,2,1,0:T(8,128)(2,1)S(1)} %get-tuple-element.48), channel_id=1, source_target_pairs={{0,2},{1,3},{2,0},{3,1},{4,6},{5,7},{6,4},{7,5},{8,10},{9,11},{10,... | collective-permute-start | bytes 786440 | tf_op jit(solution)/shard_map/ppermute | solution.py:459
  49.7 19.8 %collective-permute-start.3 = (bf16[8,16,8,128]{3,2,1,0:T(8,128)(2,1)S(1)}, bf16[8,16,8,128]{3,2,1,0:T(8,128)(2,1)S(1)}, u32[]{:S(2)}, u32[]{:S(2)}) collective-permute-start(bf16[8,16,8,128]{3,2,1,0:T(8,128)(2,1)S(1)} %reshape.42.t0), channel_id=1, source_target_pairs={{0,4},{4,8},{8,12},{12,16},{16,20},{20,24},{24,28},{28,32},{32,36}... | collective-permute-start | bytes 786440 | tf_op jit(solution)/shard_map/ppermute | solution.py:459
  51.5 18.1 %collective-permute-start.4 = (bf16[8,8,8,128]{3,2,1,0:T(8,128)(2,1)}, bf16[8,8,8,128]{3,2,1,0:T(8,128)(2,1)}, u32[]{:S(2)}, u32[]{:S(2)}) collective-permute-start(bf16[8,8,8,128]{3,2,1,0:T(8,128)(2,1)} %slice.4), channel_id=1, source_target_pairs={{0,8},{4,12},{8,16},{12,20},{16,24},{20,28},{24,32},{28,36},{32,40... | collective-permute-start | bytes 393224 | tf_op jit(solution)/shard_map/ppermute | solution.py:459
  52.8 13.6 %copy-start = (bf16[256,1536]{1,0:T(8,128)(2,1)S(1)}, bf16[256,1536]{1,0:T(8,128)(2,1)}, u32[]{:S(2)}) copy-start(bf16[256,1536]{1,0:T(8,128)(2,1)} %constant.115.clone.tables) | copy-start | bytes 2359300
  70.5 13.3 %copy-start.5 = (f32[8,64,256]{2,1,0:T(8,128)S(1)}, f32[8,64,256]{2,1,0:T(8,128)}, u32[]{:S(2)}) copy-start(f32[8,64,256]{2,1,0:T(8,128)} %pressure.1) | copy-start | bytes 1572868
  70.5 13.3 %copy-start.7 = (s32[256]{0:T(256)S(1)}, s32[256]{0:T(256)}, u32[]{:S(2)}) copy-start(s32[256]{0:T(256)} %lives.1) | copy-start | bytes 3076
  70.5 27.2 %all-to-all-start.2 = ((f16[256,8,128]{2,1,0:T(8,128)(2,1)}), f16[256,8,128]{2,1,0:T(8,128)(2,1)S(1)}, u32[]{:S(2)}, u32[]{:S(2)}) async-start(f16[256,8,128]{2,1,0:T(8,128)(2,1)} %convert_bitcast_fusion), calls=%async_computation.2 | async-start | bytes 1048576 | tf_op jit(solution)/shard_map/all_to_all | solution.py:476
  78.8 19.0 %copy-start.1 = (bf16[256,1536]{1,0:T(8,128)(2,1)S(1)}, bf16[256,1536]{1,0:T(8,128)(2,1)}, u32[]{:S(2)}) copy-start(bf16[256,1536]{1,0:T(8,128)(2,1)} %constant.117.clone.tables) | copy-start | bytes 2359300
  78.8 29.3 %collective-permute-start.5 = (f16[3,2,64,256]{3,2,1,0:T(8,128)(2,1)}, f16[3,2,64,256]{3,2,1,0:T(8,128)(2,1)}, u32[]{:S(2)}, u32[]{:S(2)}) collective-permute-start(f16[3,2,64,256]{3,2,1,0:T(8,128)(2,1)} %get-tuple-element.74), channel_id=1, source_target_pairs={{0,1},{1,2},{2,3},{3,0},{4,5},{5,6},{6,7},{7,4},{8,9},{9,10},{10,1... | collective-permute-start | bytes 589832 | tf_op jit(solution)/shard_map/ppermute | solution.py:459
  80.2 27.9 %collective-permute-start.6 = (f16[3,2,64,256]{3,2,1,0:T(8,128)(2,1)}, f16[3,2,64,256]{3,2,1,0:T(8,128)(2,1)}, u32[]{:S(2)}, u32[]{:S(2)}) collective-permute-start(f16[3,2,64,256]{3,2,1,0:T(8,128)(2,1)} %get-tuple-element.76), channel_id=1, source_target_pairs={{0,2},{1,3},{2,0},{3,1},{4,6},{5,7},{6,4},{7,5},{8,10},{9,11},{10,... | collective-permute-start | bytes 589832 | tf_op jit(solution)/shard_map/ppermute | solution.py:459
  82.6 25.5 %collective-permute-start.7 = (f16[3,2,64,256]{3,2,1,0:T(8,128)(2,1)}, f16[3,2,64,256]{3,2,1,0:T(8,128)(2,1)}, u32[]{:S(2)}, u32[]{:S(2)}) collective-permute-start(f16[3,2,64,256]{3,2,1,0:T(8,128)(2,1)} %get-tuple-element.75), channel_id=1, source_target_pairs={{0,3},{1,0},{2,1},{3,2},{4,7},{5,4},{6,5},{7,6},{8,11},{9,8},{10,9... | collective-permute-start | bytes 589832 | tf_op jit(solution)/shard_map/ppermute | solution.py:459
  87.5 35.9 %collective-permute-start.8 = (bf16[8,32,256]{2,1,0:T(8,128)(2,1)S(1)}, bf16[8,32,256]{2,1,0:T(8,128)(2,1)S(1)}, u32[]{:S(2)}, u32[]{:S(2)}) collective-permute-start(bf16[8,32,256]{2,1,0:T(8,128)(2,1)S(1)} %get-tuple-element.64), channel_id=1, source_target_pairs={{0,1},{1,2},{2,3},{3,0},{4,5},{5,6},{6,7},{7,4},{8,9},{9,10},{10,1... | collective-permute-start | bytes 393224 | tf_op jit(solution)/shard_map/ppermute | solution.py:459
  99.9 9.7 %copy-start.9 = (f32[3,8,64,256]{3,2,1,0:T(8,128)S(1)}, f32[3,8,64,256]{3,2,1,0:T(8,128)}, u32[]{:S(2)}) copy-start(f32[3,8,64,256]{3,2,1,0:T(8,128)} %param.14) | copy-start | bytes 4718596
  100.6 21.7 %all-to-all-start.3 = ((f16[256,4,128]{2,1,0:T(4,128)(2,1)}), f16[256,4,128]{2,1,0:T(4,128)(2,1)}, u32[]{:S(2)}, u32[]{:S(2)}) async-start(f16[256,4,128]{2,1,0:T(4,128)(2,1)} %bitcast.14), calls=%async_computation.3 | async-start | bytes 524288 | tf_op jit(solution)/shard_map/all_to_all | solution.py:476
  109.6 13.7 %copy-start.4 = (f32[8,64,256]{2,1,0:T(8,128)S(1)}, f32[8,64,256]{2,1,0:T(8,128)}, u32[]{:S(2)}) copy-start(f32[8,64,256]{2,1,0:T(8,128)} %bulk.1) | copy-start | bytes 1572868
  109.6 13.7 %copy-start.6 = (bf16[256,512]{1,0:T(8,128)(2,1)S(1)}, bf16[256,512]{1,0:T(8,128)(2,1)}, u32[]{:S(2)}) copy-start(bf16[256,512]{1,0:T(8,128)(2,1)} %constant.113.clone.x_ref) | copy-start | bytes 786436
  (1 other events, 8.4 us)
